TPU v7x, 32 devices: a whole 2x2x4 slice. The times are simulated.
32 devices in a mesh: grp: 2 (over y), row: 4 (over x, core), col: 4 (over z).
Axes of the slice: x: 2, y: 2, z: 4, core: 2. Of those that a mesh axis runs over, the one named last changes fastest.
Arguments:
- pair_map: float32 [256, 128, 128], P(('grp', 'row'), 'col'), parts along dimension 0, may hold values from -6 to 6
- pair_mask: int32 [256, 128], P(('grp', 'row'), 'col'), parts along dimension 0, may hold values from 0 to 1, as said below
- gain_in: float32 [2, 128], replicated, may hold values from 0.5 to 1.5
- proj_weight: bfloat16 [2, 128, 512], replicated, may hold values from -0.5 to 0.5
- gate_weight: bfloat16 [2, 128, 128], replicated, may hold values from -0.5 to 0.5
- gain_out: float32 [2, 128], replicated, may hold values from 0.5 to 1.5
- out_weight: bfloat16 [2, 128, 128], replicated, may hold values from -0.5 to 0.5
- trans_gain: float32 [128], replicated, may hold values from 0.5 to 1.5
- trans_up: bfloat16 [128, 1024], replicated, may hold values from -0.5 to 0.5
- trans_down: bfloat16 [512, 128], replicated, may hold values from -0.25 to 0.25
Outputs:
- pair_out: float32 [256, 128, 128], P(('grp', 'row'), 'col'), parts along dimension 0
There are 2 independent parts, one for each index of `grp`. A program takes and returns all parts, laid end to end along the dimension named above; an argument that names none is the same for every part. Nothing has to cross between parts.
Inputs may be any that keep to these rules, and one draw needn't show every extreme that they name: pair_mask[i, j] is 1 exactly when both i and j are below one valid length of the complex, which is at least 64.
All inputs are finite; a program needn't handle non-finite values.
Results may differ from a plain program's by a relative error of at most 0.0053.
Values may be sent and summed in bfloat16 or wider, within the bound.
No kernel may reach another device: no remote copies, remote signals or barrier semaphores. Data moves between devices by JAX's collectives and lax.ppermute only.
A program may use at most 128 MiB of HBM per device.

v0:
```python
import jax
import jax.numpy as jnp
from jax import lax
from jax.sharding import PartitionSpec as P


def layer_norm(values, gain):
    row_mean = jnp.mean(values, axis=-1, keepdims=True)
    centred = values - row_mean
    spread = jnp.mean(centred * centred, axis=-1, keepdims=True)
    return centred * lax.rsqrt(spread + 1e-05) * gain


def linear_map(values, weight):
    shape = values.shape
    flat = values.reshape(-1, shape[-1])
    result = jnp.dot(flat, weight, preferred_element_type=jnp.float32)
    return result.reshape(shape[:-1] + (weight.shape[1],))


def project(pair_map, pair_mask, gain, proj_weight, gate_weight):
    normed = layer_norm(pair_map, gain).astype(jnp.bfloat16)
    projected = linear_map(normed, proj_weight)
    width = proj_weight.shape[1] // 4
    keep_mask = pair_mask[..., None].astype(jnp.float32)
    left_act = (
        jax.nn.sigmoid(projected[..., :width]) * projected[..., width : 2 * width] * keep_mask
    ).astype(jnp.bfloat16)
    right_act = (
        jax.nn.sigmoid(projected[..., 2 * width : 3 * width])
        * projected[..., 3 * width :]
        * keep_mask
    ).astype(jnp.bfloat16)
    gate_act = jax.nn.sigmoid(linear_map(normed, gate_weight))
    return (left_act, right_act, gate_act)


def finish(pair_map, combined, gate_act, gain, out_weight):
    hidden = layer_norm(combined, gain).astype(jnp.bfloat16)
    return pair_map + gate_act * linear_map(hidden, out_weight)


def triangle(current, pair_mask, gain, proj_weight, gate_weight, gain_hidden, out_weight, outgoing):
    left_act, right_act, gate_act = project(current, pair_mask, gain, proj_weight, gate_weight)
    if outgoing:
        partial_value = jnp.einsum(
            "ikc,jkc->ijc",
            left_act,
            lax.all_gather(right_act, "row", axis=0, tiled=True),
            preferred_element_type=jnp.float32,
        )
        combined = lax.psum_scatter(partial_value, "col", scatter_dimension=1, tiled=True)
    else:
        partial_value = jnp.einsum(
            "kic,kjc->ijc",
            lax.all_gather(left_act, "col", axis=1, tiled=True),
            right_act,
            preferred_element_type=jnp.float32,
        )
        combined = lax.psum_scatter(partial_value, "row", scatter_dimension=0, tiled=True)
    return finish(current, combined, gate_act, gain_hidden, out_weight)


def per_device(
    pair_map,
    pair_mask,
    gain_in,
    proj_weight,
    gate_weight,
    gain_out,
    out_weight,
    trans_gain,
    trans_up,
    trans_down,
):
    current = triangle(
        pair_map,
        pair_mask,
        gain_in[0],
        proj_weight[0],
        gate_weight[0],
        gain_out[0],
        out_weight[0],
        True,
    )
    current = triangle(
        current,
        pair_mask,
        gain_in[1],
        proj_weight[1],
        gate_weight[1],
        gain_out[1],
        out_weight[1],
        False,
    )
    trans_in = layer_norm(current, trans_gain).astype(jnp.bfloat16)
    up_part = linear_map(trans_in, trans_up)
    half = trans_down.shape[0]
    trans_hidden = (jax.nn.silu(up_part[..., :half]) * up_part[..., half:]).astype(jnp.bfloat16)
    return current + linear_map(trans_hidden, trans_down)


def solution(mesh):
    in_specs = (
        P(("grp", "row"), "col", None),
        P(("grp", "row"), "col"),
        P(),
        P(),
        P(),
        P(),
        P(),
        P(),
        P(),
        P(),
    )
    out_specs = P(("grp", "row"), "col", None)
    return jax.shard_map(
        per_device, mesh=mesh, in_specs=in_specs, out_specs=out_specs, check_vma=False
    )
```

profile of v0, /device:TPU:0, one launch (start us, length us, event | category | flops | bytes accessed | tf_op | source)
XLA Modules:
  0.0 176.9 jit_solution(8020673670362392247)
XLA Ops:
  6.5 0.0 copy-start
  6.5 0.0 all-gather.3.cloned.1.call-start
  6.5 1.3 reduce_sum.90
  7.8 1.4 multiply_reduce_fusion.4
  9.3 0.8 slice_bitcast_fusion.1
  10.0 0.7 convert_element_type.36
  10.8 1.5 fusion.42
  12.3 1.0 fusion.21
  13.3 0.0 all-gather.3.cloned.1.call-update
  13.4 0.0 reduce-scatter.3.cloned.1.call-start
  13.4 1.4 copy.50
  14.9 18.1 %all-gather.3.cloned.1.call-done = bf16[128,32,128]{2,1,0:T(8,128)(2,1)} async-done(((bf16[32,32,128]{2,1,0:T(8,128)(2,1)}), bf16[128,32,128]{2,1,0:T(8,128)(2,1)}) %all-gather.3.cloned.1.call-update) | async-done | bytes 1048592 | tf_op jit(solution)/shard_map/all_gather | solution.py:49
  32.9 7.3 %copy.49 = bf16[128,32,128]{1,0,2:T(8,128)(2,1)} copy(bf16[128,32,128]{2,1,0:T(8,128)(2,1)} %all-gather.3.cloned.1.call-done) | data formatting | bytes 2097152 | tf_op jit(solution)/shard_map/all_gather | solution.py:49
  40.2 4.5 %convolution_bitcast_fusion.1 = f32[32,128,128]{1,0,2:T(8,128)S(1)} fusion(bf16[128,32,128]{1,0,2:T(8,128)(2,1)} %copy.49, bf16[32,32,128]{1,0,2:T(8,128)(2,1)S(1)} %copy.50), kind=kOutput, calls=%fused_computation.3 | convolution fusion | flops 33554432 | bytes 3407872 | tf_op jit(solution)/shard_map/ikc,jkc->ijc/dot_general | solution.py:46
  44.6 2.4 %copy.51 = f32[32,128,128]{2,0,1:T(8,128)} copy(f32[32,128,128]{1,0,2:T(8,128)S(1)} %convolution_bitcast_fusion.1) | data formatting | bytes 4194304 | tf_op jit(solution)/shard_map/ikc,jkc->ijc/transpose | solution.py:46
  47.0 0.0 copy-start.4
  47.0 0.0 copy-start.1
  47.0 0.0 copy-start.7
  47.0 0.0 reduce-scatter.3.cloned.1.call-update
  47.0 0.0 all-gather.5.cloned.1.call-start
  47.1 0.6 copy-done.4
  47.7 0.4 copy-done.1
  48.0 0.0 copy-done.7
  48.0 0.0 copy-start.3
  48.0 0.5 fusion.6
  48.5 42.5 %reduce-scatter.3.cloned.1.call-done = f32[32,32,128]{2,0,1:T(8,128)} async-done(((f32[32,128,128]{2,0,1:T(8,128)}), f32[32,32,128]{2,0,1:T(8,128)}) %reduce-scatter.3.cloned.1.call-update) | async-done | bytes 524304 | tf_op jit(solution)/shard_map/reduce_scatter | solution.py:52
  91.1 1.2 reduce_sum.92
  92.3 0.0 copy-start.2
  92.3 0.1 copy.52
  92.4 0.1 copy.53
  92.5 1.4 multiply_reduce_fusion.3
  93.9 0.1 copy.54
  94.0 0.1 copy.55
  94.1 1.4 multiply_convert_fusion.3
  95.5 0.0 copy-done.3
  95.5 0.4 fusion.55
  95.9 0.4 multiply_reduce_fusion.2
  96.2 0.0 copy-done.2
  96.3 0.5 fusion.40
  96.7 1.0 fusion.11
  97.8 0.0 all-gather.5.cloned.1.call-update
  97.8 0.2 reduce-scatter.5.cloned.1.call-start
  98.0 2.6 %copy.57 = bf16[32,32,128]{0,1,2:T(8,128)(2,1)} copy(bf16[32,32,128]{2,1,0:T(8,128)(2,1)S(1)} %get-tuple-element.6) | data formatting | bytes 524288 | tf_op jit(solution)/shard_map/convert_element_type | solution.py:33
  100.7 24.5 %all-gather.5.cloned.1.call-done = bf16[32,128,128]{2,1,0:T(8,128)(2,1)} async-done(((bf16[32,32,128]{2,1,0:T(8,128)(2,1)}), bf16[32,128,128]{2,1,0:T(8,128)(2,1)}) %all-gather.5.cloned.1.call-update) | async-done | bytes 1048592 | tf_op jit(solution)/shard_map/all_gather | solution.py:56
  125.2 2.7 %copy.58 = bf16[32,128,128]{1,0,2:T(8,128)(2,1)} copy(bf16[32,128,128]{2,1,0:T(8,128)(2,1)} %all-gather.5.cloned.1.call-done) | data formatting | bytes 2097152 | tf_op jit(solution)/shard_map/all_gather | solution.py:56
  127.8 2.0 %convolution_bitcast_fusion = f32[128,32,128]{0,1,2:T(8,128)S(1)} fusion(bf16[32,32,128]{0,1,2:T(8,128)(2,1)} %copy.57, bf16[32,128,128]{1,0,2:T(8,128)(2,1)} %copy.58), kind=kOutput, calls=%fused_computation.2 | convolution fusion | flops 33554432 | bytes 3407872 | tf_op jit(solution)/shard_map/kic,kjc->ijc/dot_general | solution.py:54
  129.8 2.3 %copy.59 = f32[128,32,128]{2,1,0:T(8,128)} copy(f32[128,32,128]{0,1,2:T(8,128)S(1)} %convolution_bitcast_fusion) | data formatting | bytes 4194304 | tf_op jit(solution)/shard_map/kic,kjc->ijc/transpose | solution.py:54
  132.1 0.0 reduce-scatter.5.cloned.1.call-update
  132.2 0.5 fusion.3
  132.6 0.0 copy-start.5
  132.6 30.6 %reduce-scatter.5.cloned.1.call-done = f32[32,32,128]{2,1,0:T(8,128)} async-done(((f32[128,32,128]{2,1,0:T(8,128)}), f32[32,32,128]{2,1,0:T(8,128)}) %reduce-scatter.5.cloned.1.call-update) | async-done | bytes 524304 | tf_op jit(solution)/shard_map/reduce_scatter | solution.py:60
  163.2 1.2 reduce_sum.96
  164.5 1.4 multiply_reduce_fusion.1
  165.9 1.6 fusion.56
  167.5 0.4 multiply_reduce_fusion
  167.9 0.0 copy-done
  167.9 0.0 copy-done.5
  168.0 0.0 copy-start.6
  168.0 0.8 fusion.30
  168.7 0.1 copy-done.6
  168.9 1.5 convolution_add_fusion
  (11 shorter events, 0.1 us)
Async XLA Ops:
  6.5 161.4 %copy-start = (bf16[128,1024]{1,0:T(8,128)(2,1)S(1)}, bf16[128,1024]{1,0:T(8,128)(2,1)}, u32[]{:S(2)}) copy-start(bf16[128,1024]{1,0:T(8,128)(2,1)} %param.18) | copy-start | bytes 786436
  6.5 26.4 %all-gather.3.cloned.1.call-start = ((), (), s32[]{:S(2)}) async-start(), calls=%async_computation.2 | async-start | bytes 1310720 | tf_op jit(solution)/shard_map/all_gather | solution.py:49
  13.4 77.7 %reduce-scatter.3.cloned.1.call-start = ((), (), s32[]{:S(2)}) async-start(), calls=%async_computation.3 | async-start | bytes 2621440 | tf_op jit(solution)/shard_map/reduce_scatter | solution.py:52
  47.0 0.7 copy-start.4
  47.0 1.1 copy-start.1
  47.0 1.1 copy-start.7
  47.0 78.2 %all-gather.5.cloned.1.call-start = ((), (), s32[]{:S(2)}) async-start(), calls=%async_computation.4 | async-start | bytes 1310720 | tf_op jit(solution)/shard_map/all_gather | solution.py:56
  48.0 47.4 %copy-start.3 = (bf16[2,128,128]{2,1,0:T(8,128)(2,1)S(1)}, bf16[2,128,128]{2,1,0:T(8,128)(2,1)}, u32[]{:S(2)}) copy-start(bf16[2,128,128]{2,1,0:T(8,128)(2,1)} %param.16) | copy-start | bytes 196612
  92.3 3.9 %copy-start.2 = (bf16[2,128,512]{2,1,0:T(8,128)(2,1)S(1)}, bf16[2,128,512]{2,1,0:T(8,128)(2,1)}, u32[]{:S(2)}) copy-start(bf16[2,128,512]{2,1,0:T(8,128)(2,1)} %param.13) | copy-start | bytes 786436
  97.8 65.4 %reduce-scatter.5.cloned.1.call-start = ((), (), s32[]{:S(2)}) async-start(), calls=%async_computation.5 | async-start | bytes 2621440 | tf_op jit(solution)/shard_map/reduce_scatter | solution.py:60
  132.6 35.3 %copy-start.5 = (f32[128]{0:T(128)S(1)}, f32[128]{0:T(128)}, u32[]{:S(2)}) copy-start(f32[128]{0:T(128)} %param.17) | copy-start | bytes 1540
  168.0 0.9 copy-start.6
Sparse Core Ops, SparseCore 0:
  13.5 19.4 all-gather.2
  47.1 43.8 reduce-scatter.2
  97.9 27.2 all-gather.4
  132.3 30.8 reduce-scatter.4
where the time goes:
time: 178 us; the launch traced here: 177 us
  waiting for transfers between devices  116 us (65%)
  local copies, waits for them, and re-layouts  20.9 us (12%)
  matrix products  13.6 us (8%)
  between operations  13.4 us (8%)
  other arithmetic  13 us (7%)
    reduce_scatter x1, waiting for transfers between devices, triangle(): lax.psum_scatter(partial_value, 'col', scatter_dimension=1, tiled=True)  42.5 us
    reduce_scatter x1, waiting for transfers between devices, triangle(): lax.psum_scatter(partial_value, 'row', scatter_dimension=0, tiled=True)  30.6 us
    all_gather x1, waiting for transfers between devices, triangle(): lax.all_gather(left_act, 'col', axis=1, tiled=True)  24.5 us
    all_gather x1, waiting for transfers between devices, triangle(): lax.all_gather(right_act, 'row', axis=0, tiled=True)  18.1 us
    all_gather x1, local copies, waits for them, and re-layouts, triangle(): lax.all_gather(right_act, 'row', axis=0, tiled=True)  7.25 us
    dot_general x8, matrix products, linear_map(): result = jnp.dot(flat, weight, preferred_element_type=jnp.float32)  7.17 us
    reduce_sum x5, other arithmetic, layer_norm(): spread = jnp.mean(centred * centred, axis=-1, keepdims=True)  5.02 us
    dot_general x1, matrix products, triangle(): jnp.einsum('ikc,jkc->ijc', left_act, lax.all_gather(right_act, 'row', axi...  4.45 us
  transfers between devices with their start and end apart: 4, of which 4 were waited for; matrix products, arithmetic and copies ran while one was open for 3% of the time, Pallas kernels for 0%

commit v1 on v0

v1 whole, which is shorter than its diff:
```python
import jax
import jax.numpy as jnp
from jax import lax
from jax.sharding import PartitionSpec as P

AXES = ("row", "col")


def channel_norm(values, gain):
    mean = jnp.mean(values, axis=0, keepdims=True)
    centred = values - mean
    spread = jnp.mean(centred * centred, axis=0, keepdims=True)
    return centred * lax.rsqrt(spread + 1e-05) * gain[:, None]


def apply_weight(weight, values):
    return lax.dot_general(
        weight, values, (((0,), (0,)), ((), ())), preferred_element_type=jnp.float32
    )


def project(current, keep_mask, gain, proj_weight, gate_weight, devices):
    normed = channel_norm(current, gain).astype(jnp.bfloat16)
    projected = apply_weight(proj_weight, normed)
    width = proj_weight.shape[1] // 4
    tokens = current.shape[1]
    left_act = (jax.nn.sigmoid(projected[:width]) * projected[width : 2 * width] * keep_mask).astype(jnp.bfloat16)
    right_act = (
        jax.nn.sigmoid(projected[2 * width : 3 * width]) * projected[3 * width :] * keep_mask
    ).astype(jnp.bfloat16)
    share = width // devices
    both = jnp.stack(
        [left_act.reshape(devices, share, tokens), right_act.reshape(devices, share, tokens)], axis=1
    )
    return both, jax.nn.sigmoid(apply_weight(gate_weight, normed))


def combine(both, rows, cols, height, breadth, outgoing):
    share = both.shape[2]

    def whole(part):
        blocks = part.reshape(rows, cols, share, height, breadth)
        return blocks.transpose(2, 0, 3, 1, 4).reshape(share, rows * height, cols * breadth)

    left, right = whole(both[:, 0]), whole(both[:, 1])
    spec = "cik,cjk->cij" if outgoing else "cki,ckj->cij"
    combined = jnp.einsum(spec, left, right, preferred_element_type=jnp.float32).astype(jnp.bfloat16)
    combined = combined.reshape(share, rows, height, cols, breadth).transpose(1, 3, 0, 2, 4)
    return combined.reshape(rows * cols, share, height * breadth)


def exchange(values):
    return lax.all_to_all(values, AXES, split_axis=0, concat_axis=0, tiled=True)


def per_device(
    rows,
    cols,
    pair_map,
    pair_mask,
    gain_in,
    proj_weight,
    gate_weight,
    gain_out,
    out_weight,
    trans_gain,
    trans_up,
    trans_down,
):
    height, breadth, channels = pair_map.shape
    current = pair_map.reshape(height * breadth, channels).T
    keep_mask = pair_mask.reshape(1, height * breadth).astype(jnp.float32)
    for update in range(2):
        both, gate_act = project(
            current, keep_mask, gain_in[update], proj_weight[update], gate_weight[update], rows * cols
        )
        combined = exchange(combine(exchange(both), rows, cols, height, breadth, update == 0))
        combined = combined.reshape(-1, height * breadth).astype(jnp.float32)
        hidden = channel_norm(combined, gain_out[update]).astype(jnp.bfloat16)
        current = current + gate_act * apply_weight(out_weight[update], hidden)
    trans_in = channel_norm(current, trans_gain).astype(jnp.bfloat16)
    up_part = apply_weight(trans_up, trans_in)
    half = trans_down.shape[0]
    trans_hidden = (jax.nn.silu(up_part[:half]) * up_part[half:]).astype(jnp.bfloat16)
    result = current + apply_weight(trans_down, trans_hidden)
    return result.T.reshape(height, breadth, channels)


def solution(mesh):
    rows, cols = mesh.shape["row"], mesh.shape["col"]
    spread = P(("grp", "row"), "col", None)
    in_specs = (spread, P(("grp", "row"), "col")) + (P(),) * 8

    def body(*args):
        return per_device(rows, cols, *args)

    return jax.shard_map(body, mesh=mesh, in_specs=in_specs, out_specs=spread, check_vma=False)
```

time: 178 us -> 97 us (0.54)
  waiting for transfers between devices: 116 us -> 19 us
  blocking collectives: 0 us -> 41.7 us
  between operations: 13.4 us -> 0.43 us
  matrix products: 13.6 us -> 6.57 us
  starting transfers between devices: 0.31 us -> 7.07 us
  other arithmetic: 13 us -> 6.48 us
  local copies, waits for them, and re-layouts: 20.9 us -> 15.2 us
    reduce_scatter x2 -> x0, waiting for transfers between devices: 73.1 us -> none  [the longest x1 42.5 us: triangle(): lax.psum_scatter(partial_value, 'col', scatter_dimension=1, tiled=True)]
    all_gather x2 -> x0, waiting for transfers between devices: 42.6 us -> none  [the longest x1 24.5 us: triangle(): lax.all_gather(left_act, 'col', axis=1, tiled=True)]
    all_to_all x0 -> x2, blocking collectives: none -> 41.7 us  [exchange(): return lax.all_to_all(values, AXES, split_axis=0, concat_axis=0, tiled=True)]
    all_to_all x0 -> x2, waiting for transfers between devices: none -> 19 us  [exchange(): return lax.all_to_all(values, AXES, split_axis=0, concat_axis=0, tiled=True)]
    all_gather x2 -> x0, local copies, waits for them, and re-layouts: 9.92 us -> none  [the longest x1 7.25 us: triangle(): lax.all_gather(right_act, 'row', axis=0, tiled=True)]
    all_to_all x0 -> x2, starting transfers between devices: none -> 7.07 us  [exchange(): return lax.all_to_all(values, AXES, split_axis=0, concat_axis=0, tiled=True)]
    dot_general x10, matrix products: 13.6 us -> 6.57 us  [the longest x8 6.04 us: apply_weight(): lax.dot_general(weight, values, (((0,), (0,)), ((), ())), preferred_eleme...]
    reshape x0 -> x10, local copies, waits for them, and re-layouts: none -> 6.87 us  [the longest x2 3.64 us: combine(): return combined.reshape(rows * cols, share, height * breadth)]
  transfers between devices with their start and end apart: 4 -> 2, of which waited for: 4 -> 2; matrix products, arithmetic and copies ran while one was open for 3% -> 1% of each run, Pallas kernels for 0% -> 0%
where the time goes in v1:
time: 97 us; the launch traced here: 96.4 us
  blocking collectives  41.7 us (43%)
  waiting for transfers between devices  19 us (20%)
  local copies, waits for them, and re-layouts  15.2 us (16%)
  starting transfers between devices  7.07 us (7%)
  matrix products  6.57 us (7%)
  other arithmetic  6.48 us (7%)
    all_to_all x2, blocking collectives, exchange(): return lax.all_to_all(values, AXES, split_axis=0, concat_axis=0, tiled=True)  41.7 us
    all_to_all x2, waiting for transfers between devices, exchange(): return lax.all_to_all(values, AXES, split_axis=0, concat_axis=0, tiled=True)  19 us
    all_to_all x2, starting transfers between devices, exchange(): return lax.all_to_all(values, AXES, split_axis=0, concat_axis=0, tiled=True)  7.07 us
    another operation x8, local copies, waits for them, and re-layouts, whole(): blocks = part.reshape(rows, cols, share, height, breadth)  6.25 us
    dot_general x8, matrix products, apply_weight(): lax.dot_general(weight, values, (((0,), (0,)), ((), ())), preferred_eleme...  6.04 us
    reshape x2, local copies, waits for them, and re-layouts, combine(): return combined.reshape(rows * cols, share, height * breadth)  3.64 us
    reduce_sum x5, other arithmetic, channel_norm(): spread = jnp.mean(centred * centred, axis=0, keepdims=True)  2.31 us
    reshape x4, local copies, waits for them, and re-layouts, whole(): blocks.transpose(2, 0, 3, 1, 4)  2.01 us
  transfers between devices with their start and end apart: 2, of which 2 were waited for; matrix products, arithmetic and copies ran while one was open for 1% of the time, Pallas kernels for 0%

profile of v1, /device:TPU:0, one launch (start us, length us, event | category | flops | bytes accessed | tf_op | source)
XLA Modules:
  0.0 96.4 jit_solution(10459118756186468143)
XLA Ops:
  0.0 0.8 slice_bitcast_fusion
  0.8 0.7 convert_element_type.66
  1.5 0.1 convert_element_type.67
  1.6 1.2 %reduce_sum.90 = f32[32,32]{1,0:T(8,128)S(1)} reduce(f32[32,32,128]{2,1,0:T(8,128)} %param.10, f32[]{:T(128)} %constant.17.clone.1), dimensions={2}, to_apply=%region_0.0 | reduce | flops 130048 | bytes 528388 | tf_op jit(solution)/shard_map/reduce_sum | solution.py:10
  2.8 0.1 div.63
  2.9 1.4 %multiply_reduce_fusion.2 = f32[1024]{0:T(1024)S(1)} fusion(f32[32,32,128]{2,1,0:T(8,128)} %param.10, f32[1024]{0:T(1024)S(1)} %div.63), kind=kLoop, calls=%fused_computation.75 | loop fusion | flops 392192 | bytes 532480 | tf_op jit(solution)/shard_map/reduce_sum | solution.py:12
  4.3 1.4 %multiply_convert_fusion.2 = bf16[1024,128]{1,0:T(8,128)(2,1)S(1)} fusion(f32[32,32,128]{2,1,0:T(8,128)} %param.10, f32[128]{0:T(128)S(1)} %get-tuple-element.16, f32[1024]{0:T(1024)S(1)} %add_rsqrt_fusion.4, f32[1024]{0:T(1024)S(1)} %div.63), kind=kLoop, calls=%fused_computation.74 | loop fusion | flops 524288 | bytes 795136 | tf_op jit(solution)/shard_map/convert_element_type | solution.py:23
  5.7 1.4 %convolution_bitcast_fusion.2 = f32[512,1024]{1,0:T(8,128)S(1)} fusion(bf16[1024,128]{1,0:T(8,128)(2,1)S(1)} %multiply_convert_fusion.2, bf16[2,128,512]{2,1,0:T(8,128)(2,1)} %param.13), kind=kOutput, calls=%fused_computation.4 | convolution fusion | flops 134217728 | bytes 2490368 | tf_op jit(solution)/shard_map/dot_general | solution.py:17
  7.1 0.3 fusion.53
  7.4 0.1 pad_maximum_fusion
  7.4 22.8 %all_to_all.20 = bf16[16,2,8,1024]{3,2,1,0:T(8,128)(2,1)S(1)} all-to-all(bf16[16,2,8,1024]{3,2,1,0:T(8,128)(2,1)S(1)} %pad_maximum_fusion), channel_id=1, replica_groups=mesh['grp'=2,'row'=4,'col'=4] {'row','col'}, dimensions={0} | all-to-all | bytes 1048576 | tf_op jit(solution)/shard_map/all_to_all | solution.py:53
  30.3 0.8 reshape_squeeze.13
  31.1 0.8 copy.39
  31.9 0.5 reshape.156
  32.4 0.8 reshape_squeeze.12
  33.2 0.8 copy.40
  34.0 0.5 reshape.155
  34.5 0.3 convolution_convert_fusion.1
  34.8 0.4 reshape.157
  35.3 0.0 copy-start.5
  35.3 0.0 copy-start.8
  35.3 0.2 copy.38
  35.5 0.0 copy-start.1
  35.5 0.0 copy-start.4
  35.5 1.8 %reshape.158 = bf16[16,8,1024]{2,1,0:T(8,128)(2,1)} reshape(bf16[4,4,8,32,32]{4,3,2,1,0:T(8,128)(2,1)S(1)} %bitcast.106) | data formatting | bytes 524288 | tf_op jit(solution)/shard_map/reshape | solution.py:49
  37.3 3.5 %all-to-all-start.1 = ((bf16[16,8,1024]{2,1,0:T(8,128)(2,1)}), bf16[16,8,1024]{2,1,0:T(8,128)(2,1)S(1)}, u32[]{:S(2)}, u32[]{:S(2)}) async-start(bf16[16,8,1024]{2,1,0:T(8,128)(2,1)} %reshape.158), calls=%async_computation.1 | async-start | bytes 524288 | tf_op jit(solution)/shard_map/all_to_all | solution.py:53
  40.9 0.1 mul.180
  41.0 0.0 copy-done.8
  41.0 0.0 copy-start.3
  41.0 0.3 fusion.6
  41.3 9.6 %all-to-all-done.1 = bf16[16,8,1024]{2,1,0:T(8,128)(2,1)S(1)} async-done(((bf16[16,8,1024]{2,1,0:T(8,128)(2,1)}), bf16[16,8,1024]{2,1,0:T(8,128)(2,1)S(1)}, u32[]{:S(2)}, u32[]{:S(2)}) %all-to-all-start.1) | async-done | bytes 262176 | tf_op jit(solution)/shard_map/all_to_all | solution.py:53
  50.9 0.1 convert_reduce_fusion.1
  51.0 0.1 fusion.17
  51.1 0.0 copy-done.1
  51.1 0.5 fusion.72
  51.6 0.4 multiply_reduce_fusion.1
  52.0 0.7 convolution_bitcast_fusion.1
  52.6 0.3 fusion.55
  52.9 0.1 pad_maximum_fusion.1
  53.0 18.8 %all_to_all.21 = bf16[16,2,8,1024]{3,2,1,0:T(8,128)(2,1)S(1)} all-to-all(bf16[16,2,8,1024]{3,2,1,0:T(8,128)(2,1)S(1)} %pad_maximum_fusion.1), channel_id=1, replica_groups=mesh['grp'=2,'row'=4,'col'=4] {'row','col'}, dimensions={0} | all-to-all | bytes 1048576 | tf_op jit(solution)/shard_map/all_to_all | solution.py:53
  71.8 0.7 fusion.70
  72.6 0.8 reshape_squeeze.15
  73.4 0.8 copy.37
  74.2 0.5 reshape.160
  74.7 0.8 reshape_squeeze.14
  75.5 0.7 copy.28
  76.2 0.5 reshape.159
  76.7 0.2 convolution_convert_fusion
  76.9 0.4 reshape.161
  77.4 0.2 copy.36
  77.6 1.8 %reshape.162 = bf16[16,8,1024]{2,1,0:T(8,128)(2,1)} reshape(bf16[4,4,8,32,32]{4,3,2,1,0:T(8,128)(2,1)S(1)} %bitcast.109) | data formatting | bytes 524288 | tf_op jit(solution)/shard_map/reshape | solution.py:49
  79.4 3.5 %all-to-all-start.3 = ((bf16[16,8,1024]{2,1,0:T(8,128)(2,1)}), bf16[16,8,1024]{2,1,0:T(8,128)(2,1)S(1)}, u32[]{:S(2)}, u32[]{:S(2)}) async-start(bf16[16,8,1024]{2,1,0:T(8,128)(2,1)} %reshape.162), calls=%async_computation.3 | async-start | bytes 524288 | tf_op jit(solution)/shard_map/all_to_all | solution.py:53
  82.9 0.1 mul.198
  83.0 0.5 fusion.3
  83.5 0.0 copy-start.6
  83.5 9.4 %all-to-all-done.3 = bf16[16,8,1024]{2,1,0:T(8,128)(2,1)S(1)} async-done(((bf16[16,8,1024]{2,1,0:T(8,128)(2,1)}), bf16[16,8,1024]{2,1,0:T(8,128)(2,1)S(1)}, u32[]{:S(2)}, u32[]{:S(2)}) %all-to-all-start.3) | async-done | bytes 262176 | tf_op jit(solution)/shard_map/all_to_all | solution.py:53
  92.9 0.1 convert_reduce_fusion
  93.0 0.1 fusion.14
  93.1 0.5 fusion.73
  93.6 0.4 multiply_reduce_fusion
  94.0 0.0 copy-start.7
  94.0 0.8 convolution_bitcast_fusion
  94.8 0.1 copy-done.7
  94.9 1.5 %convolution_add_fusion = f32[1024,128]{1,0:T(8,128)} fusion(f32[1024,128]{1,0:T(8,128)S(1)} %get-tuple-element.20, bf16[512,128]{1,0:T(8,128)(2,1)S(1)} %copy-done.7, f32[1024,1024]{0,1:T(8,128)S(1)} %convolution_bitcast_fusion), kind=kOutput, calls=%fused_computation.5 | convolution fusion | flops 137494528 | bytes 5373952 | tf_op jit(solution)/shard_map/dot_general | solution.py:17
  (20 shorter events, 0.1 us)
Async XLA Ops:
  0.0 94.0 %copy-start = (bf16[128,1024]{1,0:T(8,128)(2,1)S(1)}, bf16[128,1024]{1,0:T(8,128)(2,1)}, u32[]{:S(2)}) copy-start(bf16[128,1024]{1,0:T(8,128)(2,1)} %param.18) | copy-start | bytes 786436
  35.3 5.6 %copy-start.5 = (f32[2,128]{1,0:T(2,128)S(1)}, f32[2,128]{1,0:T(2,128)}, u32[]{:S(2)}) copy-start(f32[2,128]{1,0:T(2,128)} %param.15) | copy-start | bytes 3076
  35.3 5.7 %copy-start.8 = (bf16[2,128,128]{2,1,0:T(8,128)(2,1)S(1)}, bf16[2,128,128]{2,1,0:T(8,128)(2,1)}, u32[]{:S(2)}) copy-start(bf16[2,128,128]{2,1,0:T(8,128)(2,1)} %param.14) | copy-start | bytes 196612
  35.5 15.6 %copy-start.1 = (f32[32,32,128]{2,1,0:T(8,128)S(1)}, f32[32,32,128]{2,1,0:T(8,128)}, u32[]{:S(2)}) copy-start(f32[32,32,128]{2,1,0:T(8,128)} %param.10) | copy-start | bytes 1572868
  35.5 15.6 %copy-start.4 = (bf16[2,128,128]{2,1,0:T(8,128)(2,1)S(1)}, bf16[2,128,128]{2,1,0:T(8,128)(2,1)}, u32[]{:S(2)}) copy-start(bf16[2,128,128]{2,1,0:T(8,128)(2,1)} %param.16) | copy-start | bytes 196612
  37.3 13.6 %all-to-all-start.1 = ((bf16[16,8,1024]{2,1,0:T(8,128)(2,1)}), bf16[16,8,1024]{2,1,0:T(8,128)(2,1)S(1)}, u32[]{:S(2)}, u32[]{:S(2)}) async-start(bf16[16,8,1024]{2,1,0:T(8,128)(2,1)} %reshape.158), calls=%async_computation.1 | async-start | bytes 524288 | tf_op jit(solution)/shard_map/all_to_all | solution.py:53
  41.0 11.0 %copy-start.3 = (bf16[2,128,512]{2,1,0:T(8,128)(2,1)S(1)}, bf16[2,128,512]{2,1,0:T(8,128)(2,1)}, u32[]{:S(2)}) copy-start(bf16[2,128,512]{2,1,0:T(8,128)(2,1)} %param.13) | copy-start | bytes 786436
  72.6 2.1 %copy-start.2 = (bf16[16,1,8,1024]{3,2,1,0:T(8,128)(2,1)S(1)}, bf16[16,1,8,1024]{3,2,1,0:T(8,128)(2,1)}, u32[]{:S(2)}) copy-start(bf16[16,1,8,1024]{3,2,1,0:T(8,128)(2,1)} %get-tuple-element.12) | copy-start | bytes 786436
  79.4 13.6 %all-to-all-start.3 = ((bf16[16,8,1024]{2,1,0:T(8,128)(2,1)}), bf16[16,8,1024]{2,1,0:T(8,128)(2,1)S(1)}, u32[]{:S(2)}, u32[]{:S(2)}) async-start(bf16[16,8,1024]{2,1,0:T(8,128)(2,1)} %reshape.162), calls=%async_computation.3 | async-start | bytes 524288 | tf_op jit(solution)/shard_map/all_to_all | solution.py:53
  83.5 10.5 %copy-start.6 = (f32[128]{0:T(128)S(1)}, f32[128]{0:T(128)}, u32[]{:S(2)}) copy-start(f32[128]{0:T(128)} %param.17) | copy-start | bytes 1540
  94.0 0.9 copy-start.7

commit v2 on v1

v2 whole, which is shorter than its diff:
```python
import functools

import jax
import jax.numpy as jnp
from jax import lax
from jax.experimental import pallas as pl
from jax.experimental.pallas import tpu as pltpu
from jax.sharding import PartitionSpec as P

AXES = ("row", "col")
LANES = 128
VMEM_BYTES = 48 * 1024 * 1024
F32, BF16 = jnp.float32, jnp.bfloat16


def dot(left, right, contract=(1, 0)):
    return lax.dot_general(
        left, right, (((contract[0],), (contract[1],)), ((), ())), preferred_element_type=F32
    )


def sigmoid(values):
    return 0.5 * jnp.tanh(0.5 * values) + 0.5


def spread_gain(row, lanes):
    tile = jnp.broadcast_to(row, (LANES, row.shape[1])).T
    return jnp.concatenate([tile] * (lanes // LANES), axis=1)


def channel_norm(values, gain):
    centred = values - jnp.mean(values, axis=0, keepdims=True)
    spread = jnp.mean(centred * centred, axis=0, keepdims=True)
    return (centred * lax.rsqrt(spread + 1e-05) * gain).astype(BF16)


def token_mask(mask, lines, slots):
    height, breadth = mask.shape
    wide = jnp.concatenate([mask.astype(F32)] * slots, axis=1)
    row = lax.broadcasted_iota(jnp.int32, wide.shape, 0)
    lane = lax.broadcasted_iota(jnp.int32, wide.shape, 1)
    wide = jnp.where(row % slots == lane // breadth, wide, 0.0).astype(BF16)
    line = lax.broadcasted_iota(jnp.int32, (lines, height), 0)
    source = lax.broadcasted_iota(jnp.int32, (lines, height), 1)
    return dot((source // slots == line).astype(BF16), wide)


def emit_message(normed, weight_t, mask, line, message_ref, stage_ref, share):
    projected = dot(weight_t, normed)
    hid = weight_t.shape[0] // 4
    owners = hid // share
    for part in range(normed.shape[1] // LANES):
        here = projected[:, part * LANES : (part + 1) * LANES]
        keep = mask[line + part : line + part + 1]
        left = sigmoid(here[:hid]) * here[hid : 2 * hid] * keep
        right = sigmoid(here[2 * hid : 3 * hid]) * here[3 * hid :] * keep
        at = line + part
        if share % 8 == 0:
            for owner in range(owners):
                rows = slice(owner * share, (owner + 1) * share)
                both = jnp.concatenate([left[rows], right[rows]], axis=0).astype(BF16)
                message_ref[owner, 2 * share * at : 2 * share * (at + 1), :] = both
        else:
            lines = message_ref.shape[1] // 2
            stage_ref[pl.ds(2 * at, owners, stride=2 * lines), :] = left
            stage_ref[pl.ds(2 * at + 1, owners, stride=2 * lines), :] = right
    if share % 8 and line + normed.shape[1] // LANES == mask.shape[0]:
        message_ref[...] = stage_ref[...].astype(BF16).reshape(message_ref.shape)


def project_kernel(update, share, chunk, x_ref, mask_ref, gain_ref, weight_ref, message_ref, normed_ref, stage_ref):
    tokens = x_ref.shape[0]
    lines = tokens // LANES
    mask = token_mask(mask_ref[...], lines, LANES // mask_ref.shape[1])
    gain = spread_gain(gain_ref[update : update + 1, :], chunk)
    weight_t = weight_ref[...].T
    for start in range(0, tokens, chunk):
        current = x_ref[start : start + chunk, :].T
        normed = channel_norm(current, gain)
        normed_ref[:, start : start + chunk] = normed
        emit_message(normed, weight_t, mask, start // LANES, message_ref, stage_ref, share)


def gate_kernel(normed_ref, weight_ref, gate_ref):
    gate_ref[...] = sigmoid(dot(weight_ref[...].T, normed_ref[...]))


def gate_turn_kernel(normed_ref, weight_ref, x_ref, gate_ref, turned_ref):
    gate_ref[...] = sigmoid(dot(weight_ref[...].T, normed_ref[...]))
    turned_ref[...] = x_ref[...].T


def swap_slots(parts, breadth):
    parts = list(parts)
    slot = lax.broadcasted_iota(jnp.int32, parts[0].shape, 1) // breadth
    step = 1
    while step < len(parts):
        low = (slot // step) % 2 == 0
        for first in range(len(parts)):
            if first & step:
                continue
            a, b = parts[first], parts[first | step]
            parts[first] = jnp.where(low, a, pltpu.roll(b, step * breadth, 1))
            parts[first | step] = jnp.where(low, pltpu.roll(a, LANES - step * breadth, 1), b)
        step *= 2
    return parts


def combine_kernel(rows, cols, breadth, share, outgoing, both_ref, combined_ref, stage_ref, result_ref):
    slots = LANES // breadth
    span = both_ref.shape[1]
    lines = span // (2 * share)
    height = lines * slots
    tokens = rows * height
    group = rows * lines
    stage_ref[...] = both_ref[...].astype(F32).reshape(stage_ref.shape)

    natural = lax.broadcasted_iota(jnp.int32, (tokens, tokens), 0)
    held = lax.broadcasted_iota(jnp.int32, (tokens, tokens), 1)
    if not outgoing:
        natural, held = held, natural
    inner = held % group
    target = inner // lines * height + inner % lines * slots + held // group
    order = (natural == target).astype(BF16)

    def whole(side, channel):
        columns = [[] for _ in range(slots)]
        for high in range(cols // slots):
            parts = []
            for low in range(slots):
                col = high * slots + low
                parts.append(
                    jnp.concatenate(
                        [
                            stage_ref[
                                pl.ds((row * cols + col) * span + side * share + channel, lines, stride=2 * share), :
                            ]
                            for row in range(rows)
                        ],
                        axis=0,
                    )
                )
            for slot, part in enumerate(swap_slots(parts, breadth)):
                columns[slot].append(part)
        return jnp.concatenate([jnp.concatenate(column, axis=1) for column in columns], axis=0).astype(BF16)

    for channel in range(share):
        left, right = whole(0, channel), whole(1, channel)
        if outgoing:
            combined = dot(left, dot(order, right).astype(BF16), (1, 1))
        else:
            combined = dot(dot(order, left, (1, 1)).astype(BF16), right)
        for high in range(cols // slots):
            parts = [
                combined[slot * group : (slot + 1) * group, high * LANES : (high + 1) * LANES]
                for slot in range(slots)
            ]
            for low, part in enumerate(swap_slots(parts, breadth)):
                for row in range(rows):
                    base = (row * cols + high * slots + low) * lines * share + channel
                    result_ref[pl.ds(base, lines, stride=share), :] = part[row * lines : (row + 1) * lines]
    combined_ref[...] = result_ref[...].astype(BF16).reshape(combined_ref.shape)


def read_combined(stage_ref, owners, lines, share, first, count):
    columns = []
    for line in range(first, first + count):
        if share % 8 == 0:
            columns.append(
                jnp.concatenate(
                    [
                        stage_ref[(owner * lines + line) * share : (owner * lines + line + 1) * share, :]
                        for owner in range(owners)
                    ],
                    axis=0,
                )
            )
        else:
            columns.append(stage_ref[pl.ds(line, owners, stride=lines), :])
    return jnp.concatenate(columns, axis=1)


def middle_kernel(
    share,
    chunk,
    combined_ref,
    x_ref,
    gate_ref,
    gain_out_ref,
    out_weight_ref,
    mask_ref,
    gain_ref,
    weight_ref,
    message_ref,
    normed_ref,
    next_ref,
    stage_ref,
    message_stage_ref,
):
    tokens = x_ref.shape[1]
    lines = tokens // LANES
    owners = combined_ref.shape[0]
    stage_ref[...] = combined_ref[...].astype(F32).reshape(stage_ref.shape)
    mask = token_mask(mask_ref[...], lines, LANES // mask_ref.shape[1])
    gain_out = spread_gain(gain_out_ref[0:1, :], chunk)
    gain = spread_gain(gain_ref[1:2, :], chunk)
    out_t, weight_t = out_weight_ref[...].T, weight_ref[...].T
    for start in range(0, tokens, chunk):
        here = slice(start, start + chunk)
        combined = read_combined(stage_ref, owners, lines, share, start // LANES, chunk // LANES)
        hidden = channel_norm(combined, gain_out)
        current = x_ref[:, here] + gate_ref[:, here] * dot(out_t, hidden)
        next_ref[:, here] = current
        normed = channel_norm(current, gain)
        normed_ref[:, here] = normed
        emit_message(normed, weight_t, mask, start // LANES, message_ref, message_stage_ref, share)


def last_kernel(
    share,
    chunk,
    combined_ref,
    x_ref,
    gate_ref,
    gain_out_ref,
    out_weight_ref,
    gain_ref,
    up_ref,
    down_ref,
    result_ref,
    stage_ref,
):
    tokens = x_ref.shape[1]
    lines = tokens // LANES
    owners = combined_ref.shape[0]
    stage_ref[...] = combined_ref[...].astype(F32).reshape(stage_ref.shape)
    gain_out = spread_gain(gain_out_ref[1:2, :], chunk)
    gain = spread_gain(gain_ref[...], chunk)
    out_t, up_t, down_t = out_weight_ref[...].T, up_ref[...].T, down_ref[...].T
    half = down_t.shape[1]
    for start in range(0, tokens, chunk):
        here = slice(start, start + chunk)
        combined = read_combined(stage_ref, owners, lines, share, start // LANES, chunk // LANES)
        hidden = channel_norm(combined, gain_out)
        current = x_ref[:, here] + gate_ref[:, here] * dot(out_t, hidden)
        up_part = dot(up_t, channel_norm(current, gain))
        first = up_part[:half]
        trans_hidden = (first * sigmoid(first) * up_part[half:]).astype(BF16)
        result_ref[here, :] = (current + dot(down_t, trans_hidden)).T


def whole_spec(array):
    return pl.BlockSpec(array.shape, lambda step, dims=array.ndim: (0,) * dims)


def picked_spec(array, index):
    return pl.BlockSpec((None,) + array.shape[1:], lambda step: (index,) + (0,) * (array.ndim - 1))


def call(kernel, operands, picks, outs, scratch=()):
    specs = [
        picked_spec(array, picks[n]) if n in picks else whole_spec(array) for n, array in enumerate(operands)
    ]
    shapes = [jax.ShapeDtypeStruct(shape, dtype) for shape, dtype in outs]
    return pl.pallas_call(
        kernel,
        grid=(1,),
        in_specs=specs,
        out_specs=[whole_spec(shape) for shape in shapes],
        out_shape=shapes,
        scratch_shapes=[pltpu.VMEM(shape, F32) for shape in scratch],
        compiler_params=pltpu.CompilerParams(vmem_limit_bytes=VMEM_BYTES),
    )(*operands)


def exchange(values):
    return lax.all_to_all(values, AXES, split_axis=0, concat_axis=0, tiled=True)


def per_device(
    rows,
    cols,
    pair_map,
    pair_mask,
    gain_in,
    proj_weight,
    gate_weight,
    gain_out,
    out_weight,
    trans_gain,
    trans_up,
    trans_down,
):
    height, breadth, channels = pair_map.shape
    tokens = height * breadth
    lines = tokens // LANES
    hid = gain_out.shape[1]
    owners = rows * cols
    share = hid // owners
    chunk = min(2 * LANES, tokens)
    message = ((owners, 2 * share * lines, LANES), BF16)
    answer = ((owners, share * lines, LANES), BF16)
    staged = (owners * 2 * share * lines, LANES)
    result = (owners * share * lines, LANES)
    spare = (8, LANES) if share % 8 == 0 else staged
    flat = pair_map.reshape(tokens, channels)

    def combine(both, outgoing):
        (combined,) = call(
            functools.partial(combine_kernel, rows, cols, breadth, share, outgoing),
            (both,),
            {},
            [answer],
            (staged, result),
        )
        return combined

    both, normed = call(
        functools.partial(project_kernel, 0, share, chunk),
        (flat, pair_mask, gain_in, proj_weight),
        {3: 0},
        [message, ((channels, tokens), BF16)],
        (spare,),
    )
    both = exchange(both)
    gate, current = call(
        gate_turn_kernel,
        (normed, gate_weight, flat),
        {1: 0},
        [((channels, tokens), F32), ((channels, tokens), F32)],
    )
    combined = exchange(combine(both, True))
    both, normed, current = call(
        functools.partial(middle_kernel, share, chunk),
        (combined, current, gate, gain_out, out_weight, pair_mask, gain_in, proj_weight),
        {4: 0, 7: 1},
        [message, ((channels, tokens), BF16), ((channels, tokens), F32)],
        (result, spare),
    )
    both = exchange(both)
    (gate,) = call(gate_kernel, (normed, gate_weight), {1: 1}, [((channels, tokens), F32)])
    combined = exchange(combine(both, False))
    (pair_out,) = call(
        functools.partial(last_kernel, share, chunk),
        (combined, current, gate, gain_out, out_weight, trans_gain.reshape(1, -1), trans_up, trans_down),
        {4: 1},
        [((tokens, channels), F32)],
        (result,),
    )
    return pair_out.reshape(height, breadth, channels)


def solution(mesh):
    rows, cols = mesh.shape["row"], mesh.shape["col"]
    spread = P(("grp", "row"), "col", None)
    in_specs = (spread, P(("grp", "row"), "col")) + (P(),) * 8

    def body(*args):
        return per_device(rows, cols, *args)

    return jax.shard_map(body, mesh=mesh, in_specs=in_specs, out_specs=spread, check_vma=False)
```

time: 97 us -> 84.4 us (0.87)
  Pallas kernels: 0 us -> 10.6 us
  local copies, waits for them, and re-layouts: 15.2 us -> 4.74 us
  matrix products: 6.57 us -> 0 us
  other arithmetic: 6.48 us -> 0 us
    pallas_call x0 -> x7, Pallas kernels: none -> 10.6 us  [call(): pl.pallas_call(kernel, grid=(1,), in_specs=specs, out_specs=[whole_spec(s...]
    reshape x10 -> x0, local copies, waits for them, and re-layouts: 6.87 us -> none  [the longest x2 3.64 us: combine(): return combined.reshape(rows * cols, share, height * breadth)]
    dot_general x10 -> x0, matrix products: 6.57 us -> none  [the longest x8 6.04 us: apply_weight(): lax.dot_general(weight, values, (((0,), (0,)), ((), ())), preferred_eleme...]
    another operation x8 -> x0, local copies, waits for them, and re-layouts: 6.25 us -> none  [whole(): blocks = part.reshape(rows, cols, share, height, breadth)]
    unnamed x18 -> x26, local copies, waits for them, and re-layouts: 0.19 us -> 4.74 us
    reduce_sum x8 -> x0, other arithmetic: 3.66 us -> none  [the longest x5 2.31 us: channel_norm(): spread = jnp.mean(centred * centred, axis=0, keepdims=True)]
    convert_element_type x2 -> x0, other arithmetic: 2.1 us -> none  [the longest x1 1.38 us: project(): normed = channel_norm(current, gain).astype(jnp.bfloat16)]
  transfers between devices with their start and end apart: 2 -> 2, of which waited for: 2 -> 2; matrix products, arithmetic and copies ran while one was open for 1% -> 0% of each run, Pallas kernels for 0% -> 1%
where the time goes in v2:
time: 84.4 us; the launch traced here: 83.8 us
  blocking collectives  41.7 us (49%)
  waiting for transfers between devices  19.4 us (23%)
  Pallas kernels  10.6 us (13%)
  starting transfers between devices  7.2 us (9%)
  local copies, waits for them, and re-layouts  4.74 us (6%)
    all_to_all x2, blocking collectives, exchange(): return lax.all_to_all(values, AXES, split_axis=0, concat_axis=0, tiled=True)  41.7 us
    all_to_all x2, waiting for transfers between devices, exchange(): return lax.all_to_all(values, AXES, split_axis=0, concat_axis=0, tiled=True)  19.4 us
    pallas_call x7, Pallas kernels, call(): pl.pallas_call(kernel, grid=(1,), in_specs=specs, out_specs=[whole_spec(s...  10.6 us
    all_to_all x2, starting transfers between devices, exchange(): return lax.all_to_all(values, AXES, split_axis=0, concat_axis=0, tiled=True)  7.2 us
    unnamed x26, local copies, waits for them, and re-layouts  4.74 us
  transfers between devices with their start and end apart: 2, of which 2 were waited for; matrix products, arithmetic and copies ran while one was open for 0% of the time, Pallas kernels for 1%

profile of v2, /device:TPU:0, one launch (start us, length us, event | category | flops | bytes accessed | tf_op | source)
XLA Modules:
  0.0 83.8 jit_solution(15105902743199427092)
XLA Ops:
  0.0 0.0 copy-start.10
  0.0 0.7 copy-done.10
  0.7 0.0 copy-start
  0.7 1.0 %copy-done = f32[32,32,128]{2,1,0:T(8,128)S(1)} copy-done((f32[32,32,128]{2,1,0:T(8,128)S(1)}, f32[32,32,128]{2,1,0:T(8,128)}, u32[]{:S(2)}) %copy-start) | copy-done | bytes 524312
  1.7 0.0 copy-start.2
  1.7 0.9 %copy-done.2 = bf16[2,128,512]{2,1,0:T(8,128)(2,1)S(1)} copy-done((bf16[2,128,512]{2,1,0:T(8,128)(2,1)S(1)}, bf16[2,128,512]{2,1,0:T(8,128)(2,1)}, u32[]{:S(2)}) %copy-start.2) | copy-done | bytes 262168
  2.7 0.0 copy-start.8
  2.7 0.7 copy-done.8
  3.4 0.6 shard_map.100
  4.0 22.9 %all_to_all.20.both_ref = bf16[16,128,128]{2,1,0:T(8,128)(2,1)S(1)} all-to-all(bf16[16,128,128]{2,1,0:T(8,128)(2,1)S(1)} %get-tuple-element.12), channel_id=1, replica_groups=mesh['grp'=2,'row'=4,'col'=4] {'row','col'}, dimensions={0} | all-to-all | bytes 1048576 | tf_op jit(solution)/shard_map/all_to_all | solution.py:277
  26.9 0.0 copy-start.1
  26.9 2.1 %shard_map.101 = bf16[16,64,128]{2,1,0:T(8,128)(2,1)} custom-call(bf16[16,128,128]{2,1,0:T(8,128)(2,1)S(1)} %all_to_all.20.both_ref), custom_call_target="tpu_custom_call" | custom-call | tf_op jit(solution)/shard_map/pallas_call | solution.py:265
  28.9 0.0 copy-start.6
  28.9 3.7 %all-to-all-start.1 = ((bf16[16,64,128]{2,1,0:T(8,128)(2,1)}), bf16[16,64,128]{2,1,0:T(8,128)(2,1)S(1)}, u32[]{:S(2)}, u32[]{:S(2)}) async-start(bf16[16,64,128]{2,1,0:T(8,128)(2,1)} %shard_map.101), calls=%async_computation.1 | async-start | bytes 524288 | tf_op jit(solution)/shard_map/all_to_all | solution.py:277
  32.6 0.0 copy-done.1
  32.6 0.0 copy-done.6
  32.6 0.0 copy-start.3
  32.6 0.0 copy-start.5
  32.7 0.0 copy-start.9
  32.7 0.3 shard_map.102
  33.0 9.7 %all-to-all-done.1.combined_ref = bf16[16,64,128]{2,1,0:T(8,128)(2,1)S(1)} async-done(((bf16[16,64,128]{2,1,0:T(8,128)(2,1)}), bf16[16,64,128]{2,1,0:T(8,128)(2,1)S(1)}, u32[]{:S(2)}, u32[]{:S(2)}) %all-to-all-start.1) | async-done | bytes 262176 | tf_op jit(solution)/shard_map/all_to_all | solution.py:277
  42.6 0.0 copy-start.11
  42.6 0.0 copy-done.3
  42.6 0.0 copy-done.5
  42.6 0.0 copy-done.9
  42.6 0.7 copy-done.11
  43.3 1.0 %shard_map.103 = (bf16[16,128,128]{2,1,0:T(8,128)(2,1)S(1)}, bf16[128,1024]{1,0:T(8,128)(2,1)S(1)}, f32[128,1024]{1,0:T(8,128)S(1)}) custom-call(bf16[16,64,128]{2,1,0:T(8,128)(2,1)S(1)} %all-to-all-done.1.combined_ref, f32[128,1024]{1,0:T(8,128)S(1)} %get-tuple-element.14.x_ref, f32[128,1024]{1,0:T(8,128)S(1)} %get-tuple-element.15.gate_ref, ...), custom_call_target="tpu_custom_call" | custom-call | tf_op jit(solution)/shard_map/pallas_call | solution.py:265
  44.3 18.8 %all_to_all.21.both_ref = bf16[16,128,128]{2,1,0:T(8,128)(2,1)S(1)} all-to-all(bf16[16,128,128]{2,1,0:T(8,128)(2,1)S(1)} %get-tuple-element.16), channel_id=1, replica_groups=mesh['grp'=2,'row'=4,'col'=4] {'row','col'}, dimensions={0} | all-to-all | bytes 1048576 | tf_op jit(solution)/shard_map/all_to_all | solution.py:277
  63.2 2.7 %shard_map.104 = bf16[16,64,128]{2,1,0:T(8,128)(2,1)} custom-call(bf16[16,128,128]{2,1,0:T(8,128)(2,1)S(1)} %all_to_all.21.both_ref), custom_call_target="tpu_custom_call" | custom-call | tf_op jit(solution)/shard_map/pallas_call | solution.py:265
  65.9 3.5 %all-to-all-start.3 = ((bf16[16,64,128]{2,1,0:T(8,128)(2,1)}), bf16[16,64,128]{2,1,0:T(8,128)(2,1)S(1)}, u32[]{:S(2)}, u32[]{:S(2)}) async-start(bf16[16,64,128]{2,1,0:T(8,128)(2,1)} %shard_map.104), calls=%async_computation.3 | async-start | bytes 524288 | tf_op jit(solution)/shard_map/all_to_all | solution.py:277
  69.5 0.0 copy-start.4
  69.5 0.0 copy-start.7
  69.5 0.3 shard_map.105.gate_ref
  69.8 9.7 %all-to-all-done.3.combined_ref = bf16[16,64,128]{2,1,0:T(8,128)(2,1)S(1)} async-done(((bf16[16,64,128]{2,1,0:T(8,128)(2,1)}), bf16[16,64,128]{2,1,0:T(8,128)(2,1)S(1)}, u32[]{:S(2)}, u32[]{:S(2)}) %all-to-all-start.3) | async-done | bytes 262176 | tf_op jit(solution)/shard_map/all_to_all | solution.py:277
  79.5 0.0 copy-start.12
  79.5 0.0 copy-done.4
  79.5 0.0 copy-done.7
  79.5 0.6 copy-done.12
  80.1 3.6 %shard_map.106 = f32[1024,128]{1,0:T(8,128)} custom-call(bf16[16,64,128]{2,1,0:T(8,128)(2,1)S(1)} %all-to-all-done.3.combined_ref, f32[128,1024]{1,0:T(8,128)S(1)} %get-tuple-element.17.x_ref, f32[128,1024]{1,0:T(8,128)S(1)} %shard_map.105.gate_ref, f32[2,128]{1,0:T(2,128)S(1)} %copy-done.11, bf16[2,128,128]{2,1,0:T(8,128)(2,1)S(1)} %copy-done.5, ...), custom_call_target="tpu_custom_call" | custom-call | tf_op jit(solution)/shard_map/pallas_call | solution.py:265
Async XLA Ops:
  0.0 0.7 copy-start.10
  0.7 1.0 %copy-start = (f32[32,32,128]{2,1,0:T(8,128)S(1)}, f32[32,32,128]{2,1,0:T(8,128)}, u32[]{:S(2)}) copy-start(f32[32,32,128]{2,1,0:T(8,128)} %param.10) | copy-start | bytes 1572868
  1.7 0.9 %copy-start.2 = (bf16[2,128,512]{2,1,0:T(8,128)(2,1)S(1)}, bf16[2,128,512]{2,1,0:T(8,128)(2,1)}, u32[]{:S(2)}) copy-start(bf16[2,128,512]{2,1,0:T(8,128)(2,1)} %weight_ref.6) | copy-start | bytes 786436
  2.7 0.7 copy-start.8
  26.9 5.7 %copy-start.1 = (f32[32,32,128]{2,1,0:T(8,128)S(1)}, f32[32,32,128]{2,1,0:T(8,128)}, u32[]{:S(2)}) copy-start(f32[32,32,128]{2,1,0:T(8,128)} %param.10) | copy-start | bytes 1572868
  28.9 3.7 %copy-start.6 = (bf16[2,128,128]{2,1,0:T(8,128)(2,1)S(1)}, bf16[2,128,128]{2,1,0:T(8,128)(2,1)}, u32[]{:S(2)}) copy-start(bf16[2,128,128]{2,1,0:T(8,128)(2,1)} %weight_ref.7) | copy-start | bytes 196612
  28.9 13.7 %all-to-all-start.1 = ((bf16[16,64,128]{2,1,0:T(8,128)(2,1)}), bf16[16,64,128]{2,1,0:T(8,128)(2,1)S(1)}, u32[]{:S(2)}, u32[]{:S(2)}) async-start(bf16[16,64,128]{2,1,0:T(8,128)(2,1)} %shard_map.101), calls=%async_computation.1 | async-start | bytes 524288 | tf_op jit(solution)/shard_map/all_to_all | solution.py:277
  32.6 10.0 %copy-start.3 = (bf16[2,128,512]{2,1,0:T(8,128)(2,1)S(1)}, bf16[2,128,512]{2,1,0:T(8,128)(2,1)}, u32[]{:S(2)}) copy-start(bf16[2,128,512]{2,1,0:T(8,128)(2,1)} %weight_ref.6) | copy-start | bytes 786436
  32.6 10.0 %copy-start.5 = (bf16[2,128,128]{2,1,0:T(8,128)(2,1)S(1)}, bf16[2,128,128]{2,1,0:T(8,128)(2,1)}, u32[]{:S(2)}) copy-start(bf16[2,128,128]{2,1,0:T(8,128)(2,1)} %out_weight_ref.3) | copy-start | bytes 196612
  32.7 10.0 %copy-start.9 = (s32[32,32]{1,0:T(8,128)S(1)}, s32[32,32]{1,0:T(8,128)}, u32[]{:S(2)}) copy-start(s32[32,32]{1,0:T(8,128)} %mask_ref.3) | copy-start | bytes 12292
  42.6 0.7 copy-start.11
  65.9 13.6 %all-to-all-start.3 = ((bf16[16,64,128]{2,1,0:T(8,128)(2,1)}), bf16[16,64,128]{2,1,0:T(8,128)(2,1)S(1)}, u32[]{:S(2)}, u32[]{:S(2)}) async-start(bf16[16,64,128]{2,1,0:T(8,128)(2,1)} %shard_map.104), calls=%async_computation.3 | async-start | bytes 524288 | tf_op jit(solution)/shard_map/all_to_all | solution.py:277
  69.5 10.0 %copy-start.4 = (bf16[128,1024]{1,0:T(8,128)(2,1)S(1)}, bf16[128,1024]{1,0:T(8,128)(2,1)}, u32[]{:S(2)}) copy-start(bf16[128,1024]{1,0:T(8,128)(2,1)} %up_ref.1) | copy-start | bytes 786436
  69.5 10.0 %copy-start.7 = (bf16[512,128]{1,0:T(8,128)(2,1)S(1)}, bf16[512,128]{1,0:T(8,128)(2,1)}, u32[]{:S(2)}) copy-start(bf16[512,128]{1,0:T(8,128)(2,1)} %down_ref.1) | copy-start | bytes 393220
  79.5 0.7 copy-start.12

commit v3 on v2

--- a/solution.py
+++ b/solution.py
@@ -45,47 +45,69 @@
     return dot((source // slots == line).astype(BF16), wide)
 
 
-def emit_message(normed, weight_t, mask, line, message_ref, stage_ref, share):
+def pairwise(rows, cols, share):
+    owners = rows * cols
+    return owners <= 16 and owners & (owners - 1) == 0 and share % 8 == 0
+
+
+def partners(cols, refs, owners):
+    if len(refs) == 1:
+        return [(refs[0].at[n], n) for n in range(owners)]
+    own = lax.axis_index("row") * cols + lax.axis_index("col")
+    return [(ref, jnp.bitwise_xor(own, n)) for n, ref in enumerate(refs)]
+
+
+def project_act(normed, weight_t, mask, line, act_ref):
     projected = dot(weight_t, normed)
     hid = weight_t.shape[0] // 4
-    owners = hid // share
     for part in range(normed.shape[1] // LANES):
         here = projected[:, part * LANES : (part + 1) * LANES]
         keep = mask[line + part : line + part + 1]
-        left = sigmoid(here[:hid]) * here[hid : 2 * hid] * keep
-        right = sigmoid(here[2 * hid : 3 * hid]) * here[3 * hid :] * keep
-        at = line + part
-        if share % 8 == 0:
-            for owner in range(owners):
-                rows = slice(owner * share, (owner + 1) * share)
-                both = jnp.concatenate([left[rows], right[rows]], axis=0).astype(BF16)
-                message_ref[owner, 2 * share * at : 2 * share * (at + 1), :] = both
-        else:
-            lines = message_ref.shape[1] // 2
-            stage_ref[pl.ds(2 * at, owners, stride=2 * lines), :] = left
-            stage_ref[pl.ds(2 * at + 1, owners, stride=2 * lines), :] = right
-    if share % 8 and line + normed.shape[1] // LANES == mask.shape[0]:
-        message_ref[...] = stage_ref[...].astype(BF16).reshape(message_ref.shape)
-
-
-def project_kernel(update, share, chunk, x_ref, mask_ref, gain_ref, weight_ref, message_ref, normed_ref, stage_ref):
+        lanes = slice((line + part) * LANES, (line + part + 1) * LANES)
+        act_ref[:hid, lanes] = sigmoid(here[:hid]) * here[hid : 2 * hid] * keep
+        act_ref[hid:, lanes] = sigmoid(here[2 * hid : 3 * hid]) * here[3 * hid :] * keep
+
+
+def emit_messages(cols, share, act_ref, message_refs):
+    hid = act_ref.shape[0] // 2
+    lines = act_ref.shape[1] // LANES
+    for block_ref, owner in partners(cols, message_refs, hid // share):
+        slabs = [
+            act_ref[pl.ds(side * hid + owner * share, share), line * LANES : (line + 1) * LANES]
+            for line in range(lines)
+            for side in range(2)
+        ]
+        block_ref[...] = jnp.concatenate(slabs, axis=0).astype(BF16)
+
+
+def gather_blocks(cols, refs, owners, stage_ref):
+    for block_ref, owner in partners(cols, refs, owners):
+        span = block_ref.shape[0]
+        stage_ref[pl.ds(pl.multiple_of(owner * span, span), span), :] = block_ref[...].astype(F32)
+
+
+def project_kernel(update, cols, share, chunk, ins, outs, act_ref):
+    x_ref, mask_ref, gain_ref, weight_ref = ins
+    normed_ref, *message_refs = outs
     tokens = x_ref.shape[0]
-    lines = tokens // LANES
-    mask = token_mask(mask_ref[...], lines, LANES // mask_ref.shape[1])
+    mask = token_mask(mask_ref[...], tokens // LANES, LANES // mask_ref.shape[1])
     gain = spread_gain(gain_ref[update : update + 1, :], chunk)
     weight_t = weight_ref[...].T
     for start in range(0, tokens, chunk):
-        current = x_ref[start : start + chunk, :].T
-        normed = channel_norm(current, gain)
+        normed = channel_norm(x_ref[start : start + chunk, :].T, gain)
         normed_ref[:, start : start + chunk] = normed
-        emit_message(normed, weight_t, mask, start // LANES, message_ref, stage_ref, share)
-
-
-def gate_kernel(normed_ref, weight_ref, gate_ref):
-    gate_ref[...] = sigmoid(dot(weight_ref[...].T, normed_ref[...]))
-
-
-def gate_turn_kernel(normed_ref, weight_ref, x_ref, gate_ref, turned_ref):
+        project_act(normed, weight_t, mask, start // LANES, act_ref)
+    emit_messages(cols, share, act_ref, message_refs)
+
+
+def gate_kernel(ins, outs):
+    normed_ref, weight_ref = ins
+    outs[0][...] = sigmoid(dot(weight_ref[...].T, normed_ref[...]))
+
+
+def gate_turn_kernel(ins, outs):
+    normed_ref, weight_ref, x_ref = ins
+    gate_ref, turned_ref = outs
     gate_ref[...] = sigmoid(dot(weight_ref[...].T, normed_ref[...]))
     turned_ref[...] = x_ref[...].T
 
@@ -106,14 +128,14 @@
     return parts
 
 
-def combine_kernel(rows, cols, breadth, share, outgoing, both_ref, combined_ref, stage_ref, result_ref):
+def combine_kernel(rows, cols, breadth, share, outgoing, ins, outs, stage_ref, result_ref):
     slots = LANES // breadth
-    span = both_ref.shape[1]
+    span = stage_ref.shape[0] // (rows * cols)
     lines = span // (2 * share)
     height = lines * slots
     tokens = rows * height
     group = rows * lines
-    stage_ref[...] = both_ref[...].astype(F32).reshape(stage_ref.shape)
+    gather_blocks(cols, ins, rows * cols, stage_ref)
 
     natural = lax.broadcasted_iota(jnp.int32, (tokens, tokens), 0)
     held = lax.broadcasted_iota(jnp.int32, (tokens, tokens), 1)
@@ -159,7 +181,9 @@
                 for row in range(rows):
                     base = (row * cols + high * slots + low) * lines * share + channel
                     result_ref[pl.ds(base, lines, stride=share), :] = part[row * lines : (row + 1) * lines]
-    combined_ref[...] = result_ref[...].astype(BF16).reshape(combined_ref.shape)
+    for block_ref, owner in partners(cols, outs, rows * cols):
+        span = block_ref.shape[0]
+        block_ref[...] = result_ref[pl.ds(pl.multiple_of(owner * span, span), span), :].astype(BF16)
 
 
 def read_combined(stage_ref, owners, lines, share, first, count):
@@ -180,27 +204,13 @@
     return jnp.concatenate(columns, axis=1)
 
 
-def middle_kernel(
-    share,
-    chunk,
-    combined_ref,
-    x_ref,
-    gate_ref,
-    gain_out_ref,
-    out_weight_ref,
-    mask_ref,
-    gain_ref,
-    weight_ref,
-    message_ref,
-    normed_ref,
-    next_ref,
-    stage_ref,
-    message_stage_ref,
-):
+def middle_kernel(cols, share, chunk, ins, outs, stage_ref, act_ref):
+    x_ref, gate_ref, gain_out_ref, out_weight_ref, mask_ref, gain_ref, weight_ref, *combined_refs = ins
+    normed_ref, next_ref, *message_refs = outs
     tokens = x_ref.shape[1]
     lines = tokens // LANES
-    owners = combined_ref.shape[0]
-    stage_ref[...] = combined_ref[...].astype(F32).reshape(stage_ref.shape)
+    owners = x_ref.shape[0] // share
+    gather_blocks(cols, combined_refs, owners, stage_ref)
     mask = token_mask(mask_ref[...], lines, LANES // mask_ref.shape[1])
     gain_out = spread_gain(gain_out_ref[0:1, :], chunk)
     gain = spread_gain(gain_ref[1:2, :], chunk)
@@ -213,27 +223,17 @@
         next_ref[:, here] = current
         normed = channel_norm(current, gain)
         normed_ref[:, here] = normed
-        emit_message(normed, weight_t, mask, start // LANES, message_ref, message_stage_ref, share)
-
-
-def last_kernel(
-    share,
-    chunk,
-    combined_ref,
-    x_ref,
-    gate_ref,
-    gain_out_ref,
-    out_weight_ref,
-    gain_ref,
-    up_ref,
-    down_ref,
-    result_ref,
-    stage_ref,
-):
+        project_act(normed, weight_t, mask, start // LANES, act_ref)
+    emit_messages(cols, share, act_ref, message_refs)
+
+
+def last_kernel(cols, share, chunk, ins, outs, stage_ref):
+    x_ref, gate_ref, gain_out_ref, out_weight_ref, gain_ref, up_ref, down_ref, *combined_refs = ins
+    (result_ref,) = outs
     tokens = x_ref.shape[1]
     lines = tokens // LANES
-    owners = combined_ref.shape[0]
-    stage_ref[...] = combined_ref[...].astype(F32).reshape(stage_ref.shape)
+    owners = x_ref.shape[0] // share
+    gather_blocks(cols, combined_refs, owners, stage_ref)
     gain_out = spread_gain(gain_out_ref[1:2, :], chunk)
     gain = spread_gain(gain_ref[...], chunk)
     out_t, up_t, down_t = out_weight_ref[...].T, up_ref[...].T, down_ref[...].T
@@ -262,8 +262,13 @@
         picked_spec(array, picks[n]) if n in picks else whole_spec(array) for n, array in enumerate(operands)
     ]
     shapes = [jax.ShapeDtypeStruct(shape, dtype) for shape, dtype in outs]
+    count = len(operands)
+
+    def body(*refs):
+        kernel(refs[:count], refs[count : count + len(outs)], *refs[count + len(outs) :])
+
     return pl.pallas_call(
-        kernel,
+        body,
         grid=(1,),
         in_specs=specs,
         out_specs=[whole_spec(shape) for shape in shapes],
@@ -273,8 +278,14 @@
     )(*operands)
 
 
-def exchange(values):
-    return lax.all_to_all(values, AXES, split_axis=0, concat_axis=0, tiled=True)
+def exchange(cols, blocks):
+    if len(blocks) == 1:
+        return [lax.all_to_all(blocks[0], AXES, split_axis=0, concat_axis=0, tiled=True)]
+    owners = len(blocks)
+    received = list(blocks)
+    for n in sorted(range(1, owners), key=lambda n: (-(n % cols), n)):
+        received[n] = lax.ppermute(blocks[n], AXES, [(device, device ^ n) for device in range(owners)])
+    return received
 
 
 def per_device(
@@ -298,52 +309,47 @@
     owners = rows * cols
     share = hid // owners
     chunk = min(2 * LANES, tokens)
-    message = ((owners, 2 * share * lines, LANES), BF16)
-    answer = ((owners, share * lines, LANES), BF16)
+    flat = pair_map.reshape(tokens, channels)
+    act = (2 * hid, tokens)
     staged = (owners * 2 * share * lines, LANES)
     result = (owners * share * lines, LANES)
-    spare = (8, LANES) if share % 8 == 0 else staged
-    flat = pair_map.reshape(tokens, channels)
+    narrow, wide = ((channels, tokens), BF16), ((channels, tokens), F32)
+
+    def blocks(span):
+        if pairwise(rows, cols, share):
+            return [((span, LANES), BF16)] * owners
+        return [((owners, span, LANES), BF16)]
+
+    messages, answers = blocks(2 * share * lines), blocks(share * lines)
 
     def combine(both, outgoing):
-        (combined,) = call(
-            functools.partial(combine_kernel, rows, cols, breadth, share, outgoing),
-            (both,),
-            {},
-            [answer],
-            (staged, result),
-        )
-        return combined
-
-    both, normed = call(
-        functools.partial(project_kernel, 0, share, chunk),
+        kernel = functools.partial(combine_kernel, rows, cols, breadth, share, outgoing)
+        return exchange(cols, call(kernel, both, {}, answers, (staged, result)))
+
+    normed, *both = call(
+        functools.partial(project_kernel, 0, cols, share, chunk),
         (flat, pair_mask, gain_in, proj_weight),
         {3: 0},
-        [message, ((channels, tokens), BF16)],
-        (spare,),
+        [narrow] + messages,
+        (act,),
     )
-    both = exchange(both)
-    gate, current = call(
-        gate_turn_kernel,
-        (normed, gate_weight, flat),
-        {1: 0},
-        [((channels, tokens), F32), ((channels, tokens), F32)],
+    both = exchange(cols, both)
+    gate, current = call(gate_turn_kernel, (normed, gate_weight, flat), {1: 0}, [wide, wide])
+    combined = combine(both, True)
+    normed, current, *both = call(
+        functools.partial(middle_kernel, cols, share, chunk),
+        (current, gate, gain_out, out_weight, pair_mask, gain_in, proj_weight, *combined),
+        {3: 0, 6: 1},
+        [narrow, wide] + messages,
+        (result, act),
     )
-    combined = exchange(combine(both, True))
-    both, normed, current = call(
-        functools.partial(middle_kernel, share, chunk),
-        (combined, current, gate, gain_out, out_weight, pair_mask, gain_in, proj_weight),
-        {4: 0, 7: 1},
-        [message, ((channels, tokens), BF16), ((channels, tokens), F32)],
-        (result, spare),
-    )
-    both = exchange(both)
-    (gate,) = call(gate_kernel, (normed, gate_weight), {1: 1}, [((channels, tokens), F32)])
-    combined = exchange(combine(both, False))
+    both = exchange(cols, both)
+    (gate,) = call(gate_kernel, (normed, gate_weight), {1: 1}, [wide])
+    combined = combine(both, False)
     (pair_out,) = call(
-        functools.partial(last_kernel, share, chunk),
-        (combined, current, gate, gain_out, out_weight, trans_gain.reshape(1, -1), trans_up, trans_down),
-        {4: 1},
+        functools.partial(last_kernel, cols, share, chunk),
+        (current, gate, gain_out, out_weight, trans_gain.reshape(1, -1), trans_up, trans_down, *combined),
+        {3: 1},
         [((tokens, channels), F32)],
         (result,),
     )

time: 84.4 us -> 117 us (1.39)
  starting transfers between devices: 7.2 us -> 87.9 us
  blocking collectives: 41.7 us -> 0 us
  waiting for transfers between devices: 19.4 us -> 13 us
    ppermute x0 -> x60, starting transfers between devices: none -> 87.9 us  [exchange(): lax.ppermute(blocks[n], AXES, [(device, device ^ n) for device in range(o...]
    all_to_all x2 -> x0, blocking collectives: 41.7 us -> none  [exchange(): return lax.all_to_all(values, AXES, split_axis=0, concat_axis=0, tiled=True)]
    all_to_all x2 -> x0, waiting for transfers between devices: 19.4 us -> none  [exchange(): return lax.all_to_all(values, AXES, split_axis=0, concat_axis=0, tiled=True)]
    ppermute x0 -> x60, waiting for transfers between devices: none -> 13 us  [exchange(): lax.ppermute(blocks[n], AXES, [(device, device ^ n) for device in range(o...]
    all_to_all x2 -> x0, starting transfers between devices: 7.2 us -> none  [exchange(): return lax.all_to_all(values, AXES, split_axis=0, concat_axis=0, tiled=True)]
    pallas_call x7, Pallas kernels: 10.6 us -> 9.46 us  [call(): pl.pallas_call(body, grid=(1,), in_specs=specs, out_specs=[whole_spec(sha...]
  transfers between devices with their start and end apart: 2 -> 60, of which waited for: 2 -> 5; matrix products, arithmetic and copies ran while one was open for 0% -> 0% of each run, Pallas kernels for 1% -> 0%
where the time goes in v3:
time: 117 us; the launch traced here: 115 us
  starting transfers between devices  87.9 us (75%)
  waiting for transfers between devices  13 us (11%)
  Pallas kernels  9.46 us (8%)
  local copies, waits for them, and re-layouts  4.73 us (4%)
    ppermute x60, starting transfers between devices, exchange(): lax.ppermute(blocks[n], AXES, [(device, device ^ n) for device in range(o...  87.9 us
    ppermute x60, waiting for transfers between devices, exchange(): lax.ppermute(blocks[n], AXES, [(device, device ^ n) for device in range(o...  13 us
    pallas_call x7, Pallas kernels, call(): pl.pallas_call(body, grid=(1,), in_specs=specs, out_specs=[whole_spec(sha...  9.46 us
    unnamed x26, local copies, waits for them, and re-layouts  4.73 us
  transfers between devices with their start and end apart: 60, of which 5 were waited for; matrix products, arithmetic and copies ran while one was open for 0% of the time, Pallas kernels for 0%

profile of v3, /device:TPU:0, one launch (start us, length us, event | category | flops | bytes accessed | tf_op | source)
XLA Modules:
  0.0 115.4 jit_solution(4161542290505226402)
XLA Ops:
  0.0 0.7 copy-done.10
  0.7 1.0 copy-done
  1.7 0.9 copy-done.2
  2.7 0.7 copy-done.8
  3.4 0.7 shard_map.100
  4.1 3.1 %collective-permute-start = (bf16[128,128]{1,0:T(8,128)(2,1)S(1)}, bf16[128,128]{1,0:T(8,128)(2,1)S(1)}, u32[]{:S(2)}, u32[]{:S(2)}) collective-permute-start(bf16[128,128]{1,0:T(8,128)(2,1)S(1)} %get-tuple-element.78), channel_id=1, source_target_pairs={{0,1},{1,0},{2,3},{3,2},{4,5},{5,4},{6,7},{7,6},{8,9},{9,8},{10,11... | collective-permute-start | bytes 98312 | tf_op jit(solution)/shard_map/ppermute | solution.py:287
  7.2 2.6 %collective-permute-start.1 = (bf16[128,128]{1,0:T(8,128)(2,1)S(1)}, bf16[128,128]{1,0:T(8,128)(2,1)S(1)}, u32[]{:S(2)}, u32[]{:S(2)}) collective-permute-start(bf16[128,128]{1,0:T(8,128)(2,1)S(1)} %get-tuple-element.79), channel_id=1, source_target_pairs={{0,2},{1,3},{2,0},{3,1},{4,6},{5,7},{6,4},{7,5},{8,10},{9,11},{10,... | collective-permute-start | bytes 98312 | tf_op jit(solution)/shard_map/ppermute | solution.py:287
  9.8 1.0 collective-permute-start.4
  10.8 3.1 %collective-permute-start.5 = (bf16[128,128]{1,0:T(8,128)(2,1)S(1)}, bf16[128,128]{1,0:T(8,128)(2,1)S(1)}, u32[]{:S(2)}, u32[]{:S(2)}) collective-permute-start(bf16[128,128]{1,0:T(8,128)(2,1)S(1)} %get-tuple-element.83), channel_id=1, source_target_pairs={{0,6},{1,7},{2,4},{3,5},{4,2},{5,3},{6,0},{7,1},{8,14},{9,15},{10,... | collective-permute-start | bytes 98312 | tf_op jit(solution)/shard_map/ppermute | solution.py:287
  13.9 0.1 collective-permute-start.6
  14.0 1.9 %collective-permute-done.2.refs_3_ = bf16[128,128]{1,0:T(8,128)(2,1)S(1)} collective-permute-done((bf16[128,128]{1,0:T(8,128)(2,1)S(1)}, bf16[128,128]{1,0:T(8,128)(2,1)S(1)}, u32[]{:S(2)}, u32[]{:S(2)}) %collective-permute-start.2) | collective-permute-done | bytes 32800 | tf_op jit(solution)/shard_map/ppermute | solution.py:287
  15.9 1.5 %collective-permute-start.7 = (bf16[128,128]{1,0:T(8,128)(2,1)S(1)}, bf16[128,128]{1,0:T(8,128)(2,1)S(1)}, u32[]{:S(2)}, u32[]{:S(2)}) collective-permute-start(bf16[128,128]{1,0:T(8,128)(2,1)S(1)} %get-tuple-element.85), channel_id=1, source_target_pairs={{0,8},{1,9},{2,10},{3,11},{4,12},{5,13},{6,14},{7,15},{8,0},{9,1},... | collective-permute-start | bytes 98312 | tf_op jit(solution)/shard_map/ppermute | solution.py:287
  17.4 3.4 %collective-permute-start.9 = (bf16[128,128]{1,0:T(8,128)(2,1)S(1)}, bf16[128,128]{1,0:T(8,128)(2,1)S(1)}, u32[]{:S(2)}, u32[]{:S(2)}) collective-permute-start(bf16[128,128]{1,0:T(8,128)(2,1)S(1)} %get-tuple-element.87), channel_id=1, source_target_pairs={{0,10},{1,11},{2,8},{3,9},{4,14},{5,15},{6,12},{7,13},{8,2},{9,3},... | collective-permute-start | bytes 98312 | tf_op jit(solution)/shard_map/ppermute | solution.py:287
  20.8 1.9 %collective-permute-start.10 = (bf16[128,128]{1,0:T(8,128)(2,1)S(1)}, bf16[128,128]{1,0:T(8,128)(2,1)S(1)}, u32[]{:S(2)}, u32[]{:S(2)}) collective-permute-start(bf16[128,128]{1,0:T(8,128)(2,1)S(1)} %get-tuple-element.88), channel_id=1, source_target_pairs={{0,11},{1,10},{2,9},{3,8},{4,15},{5,14},{6,13},{7,12},{8,3},{9,2},... | collective-permute-start | bytes 98312 | tf_op jit(solution)/shard_map/ppermute | solution.py:287
  22.7 0.4 collective-permute-start.12
  23.1 2.8 %collective-permute-start.13 = (bf16[128,128]{1,0:T(8,128)(2,1)S(1)}, bf16[128,128]{1,0:T(8,128)(2,1)S(1)}, u32[]{:S(2)}, u32[]{:S(2)}) collective-permute-start(bf16[128,128]{1,0:T(8,128)(2,1)S(1)} %get-tuple-element.91), channel_id=1, source_target_pairs={{0,14},{1,15},{2,12},{3,13},{4,10},{5,11},{6,8},{7,9},{8,6},{9,7},... | collective-permute-start | bytes 98312 | tf_op jit(solution)/shard_map/ppermute | solution.py:287
  25.8 3.0 %collective-permute-start.14 = (bf16[128,128]{1,0:T(8,128)(2,1)S(1)}, bf16[128,128]{1,0:T(8,128)(2,1)S(1)}, u32[]{:S(2)}, u32[]{:S(2)}) collective-permute-start(bf16[128,128]{1,0:T(8,128)(2,1)S(1)} %get-tuple-element.92), channel_id=1, source_target_pairs={{0,15},{1,14},{2,13},{3,12},{4,11},{5,10},{6,9},{7,8},{8,7},{9,6},... | collective-permute-start | bytes 98312 | tf_op jit(solution)/shard_map/ppermute | solution.py:287
  28.9 3.0 %collective-permute-done.14.refs_15_ = bf16[128,128]{1,0:T(8,128)(2,1)S(1)} collective-permute-done((bf16[128,128]{1,0:T(8,128)(2,1)S(1)}, bf16[128,128]{1,0:T(8,128)(2,1)S(1)}, u32[]{:S(2)}, u32[]{:S(2)}) %collective-permute-start.14) | collective-permute-done | bytes 32800 | tf_op jit(solution)/shard_map/ppermute | solution.py:287
  31.9 1.4 %shard_map.102 = (bf16[64,128]{1,0:T(8,128)(2,1)S(1)}, bf16[64,128]{1,0:T(8,128)(2,1)S(1)}, bf16[64,128]{1,0:T(8,128)(2,1)S(1)}, bf16[64,128]{1,0:T(8,128)(2,1)S...) custom-call(bf16[128,128]{1,0:T(8,128)(2,1)S(1)} %get-tuple-element., ...), custom_call_target="tpu_custom_call" | custom-call | tf_op jit(solution)/shard_map/pallas_call | solution.py:270
  33.3 0.1 collective-permute-start.15
  33.3 2.5 %collective-permute-start.16 = (bf16[64,128]{1,0:T(8,128)(2,1)S(1)}, bf16[64,128]{1,0:T(8,128)(2,1)S(1)}, u32[]{:S(2)}, u32[]{:S(2)}) collective-permute-start(bf16[64,128]{1,0:T(8,128)(2,1)S(1)} %get-tuple-element.95), channel_id=1, source_target_pairs={{0,2},{1,3},{2,0},{3,1},{4,6},{5,7},{6,4},{7,5},{8,10},{9,11},{10,... | collective-permute-start | bytes 49160 | tf_op jit(solution)/shard_map/ppermute | solution.py:287
  35.8 1.9 %collective-permute-start.17 = (bf16[64,128]{1,0:T(8,128)(2,1)S(1)}, bf16[64,128]{1,0:T(8,128)(2,1)S(1)}, u32[]{:S(2)}, u32[]{:S(2)}) collective-permute-start(bf16[64,128]{1,0:T(8,128)(2,1)S(1)} %get-tuple-element.96), channel_id=1, source_target_pairs={{0,3},{1,2},{2,1},{3,0},{4,7},{5,6},{6,5},{7,4},{8,11},{9,10},{10,... | collective-permute-start | bytes 49160 | tf_op jit(solution)/shard_map/ppermute | solution.py:287
  37.7 0.7 collective-permute-start.18
  38.4 2.2 %collective-permute-start.20 = (bf16[64,128]{1,0:T(8,128)(2,1)S(1)}, bf16[64,128]{1,0:T(8,128)(2,1)S(1)}, u32[]{:S(2)}, u32[]{:S(2)}) collective-permute-start(bf16[64,128]{1,0:T(8,128)(2,1)S(1)} %get-tuple-element.99), channel_id=1, source_target_pairs={{0,6},{1,7},{2,4},{3,5},{4,2},{5,3},{6,0},{7,1},{8,14},{9,15},{10,... | collective-permute-start | bytes 49160 | tf_op jit(solution)/shard_map/ppermute | solution.py:287
  40.6 1.5 %collective-permute-start.21 = (bf16[64,128]{1,0:T(8,128)(2,1)S(1)}, bf16[64,128]{1,0:T(8,128)(2,1)S(1)}, u32[]{:S(2)}, u32[]{:S(2)}) collective-permute-start(bf16[64,128]{1,0:T(8,128)(2,1)S(1)} %get-tuple-element.100), channel_id=1, source_target_pairs={{0,7},{1,6},{2,5},{3,4},{4,3},{5,2},{6,1},{7,0},{8,15},{9,14},{10,... | collective-permute-start | bytes 49160 | tf_op jit(solution)/shard_map/ppermute | solution.py:287
  42.1 1.3 %collective-permute-start.22 = (bf16[64,128]{1,0:T(8,128)(2,1)S(1)}, bf16[64,128]{1,0:T(8,128)(2,1)S(1)}, u32[]{:S(2)}, u32[]{:S(2)}) collective-permute-start(bf16[64,128]{1,0:T(8,128)(2,1)S(1)} %get-tuple-element.101), channel_id=1, source_target_pairs={{0,8},{1,9},{2,10},{3,11},{4,12},{5,13},{6,14},{7,15},{8,0},{9,1},... | collective-permute-start | bytes 49160 | tf_op jit(solution)/shard_map/ppermute | solution.py:287
  43.5 3.4 %collective-permute-start.24 = (bf16[64,128]{1,0:T(8,128)(2,1)S(1)}, bf16[64,128]{1,0:T(8,128)(2,1)S(1)}, u32[]{:S(2)}, u32[]{:S(2)}) collective-permute-start(bf16[64,128]{1,0:T(8,128)(2,1)S(1)} %get-tuple-element.103), channel_id=1, source_target_pairs={{0,10},{1,11},{2,8},{3,9},{4,14},{5,15},{6,12},{7,13},{8,2},{9,3},... | collective-permute-start | bytes 49160 | tf_op jit(solution)/shard_map/ppermute | solution.py:287
  46.8 2.1 %collective-permute-start.25 = (bf16[64,128]{1,0:T(8,128)(2,1)S(1)}, bf16[64,128]{1,0:T(8,128)(2,1)S(1)}, u32[]{:S(2)}, u32[]{:S(2)}) collective-permute-start(bf16[64,128]{1,0:T(8,128)(2,1)S(1)} %get-tuple-element.104), channel_id=1, source_target_pairs={{0,11},{1,10},{2,9},{3,8},{4,15},{5,14},{6,13},{7,12},{8,3},{9,2},... | collective-permute-start | bytes 49160 | tf_op jit(solution)/shard_map/ppermute | solution.py:287
  48.9 0.2 collective-permute-start.27
  49.1 3.0 %collective-permute-start.28 = (bf16[64,128]{1,0:T(8,128)(2,1)S(1)}, bf16[64,128]{1,0:T(8,128)(2,1)S(1)}, u32[]{:S(2)}, u32[]{:S(2)}) collective-permute-start(bf16[64,128]{1,0:T(8,128)(2,1)S(1)} %get-tuple-element.107), channel_id=1, source_target_pairs={{0,14},{1,15},{2,12},{3,13},{4,10},{5,11},{6,8},{7,9},{8,6},{9,7},... | collective-permute-start | bytes 49160 | tf_op jit(solution)/shard_map/ppermute | solution.py:287
  52.1 3.0 %collective-permute-start.29 = (bf16[64,128]{1,0:T(8,128)(2,1)S(1)}, bf16[64,128]{1,0:T(8,128)(2,1)S(1)}, u32[]{:S(2)}, u32[]{:S(2)}) collective-permute-start(bf16[64,128]{1,0:T(8,128)(2,1)S(1)} %get-tuple-element.108), channel_id=1, source_target_pairs={{0,15},{1,14},{2,13},{3,12},{4,11},{5,10},{6,9},{7,8},{8,7},{9,6},... | collective-permute-start | bytes 49160 | tf_op jit(solution)/shard_map/ppermute | solution.py:287
  55.1 0.3 shard_map.101
  55.5 2.5 %collective-permute-done.29.refs_22_ = bf16[64,128]{1,0:T(8,128)(2,1)S(1)} collective-permute-done((bf16[64,128]{1,0:T(8,128)(2,1)S(1)}, bf16[64,128]{1,0:T(8,128)(2,1)S(1)}, u32[]{:S(2)}, u32[]{:S(2)}) %collective-permute-start.29) | collective-permute-done | bytes 16416 | tf_op jit(solution)/shard_map/ppermute | solution.py:287
  58.0 0.7 copy-done.11
  58.6 1.1 shard_map.103
  59.8 0.1 collective-permute-start.30
  59.8 2.5 %collective-permute-start.31 = (bf16[128,128]{1,0:T(8,128)(2,1)S(1)}, bf16[128,128]{1,0:T(8,128)(2,1)S(1)}, u32[]{:S(2)}, u32[]{:S(2)}) collective-permute-start(bf16[128,128]{1,0:T(8,128)(2,1)S(1)} %get-tuple-element.113), channel_id=1, source_target_pairs={{0,2},{1,3},{2,0},{3,1},{4,6},{5,7},{6,4},{7,5},{8,10},{9,11},{10,... | collective-permute-start | bytes 98312 | tf_op jit(solution)/shard_map/ppermute | solution.py:287
  62.3 1.9 %collective-permute-start.32 = (bf16[128,128]{1,0:T(8,128)(2,1)S(1)}, bf16[128,128]{1,0:T(8,128)(2,1)S(1)}, u32[]{:S(2)}, u32[]{:S(2)}) collective-permute-start(bf16[128,128]{1,0:T(8,128)(2,1)S(1)} %get-tuple-element.114), channel_id=1, source_target_pairs={{0,3},{1,2},{2,1},{3,0},{4,7},{5,6},{6,5},{7,4},{8,11},{9,10},{10,... | collective-permute-start | bytes 98312 | tf_op jit(solution)/shard_map/ppermute | solution.py:287
  64.2 0.5 collective-permute-start.33
  64.7 2.2 %collective-permute-start.35 = (bf16[128,128]{1,0:T(8,128)(2,1)S(1)}, bf16[128,128]{1,0:T(8,128)(2,1)S(1)}, u32[]{:S(2)}, u32[]{:S(2)}) collective-permute-start(bf16[128,128]{1,0:T(8,128)(2,1)S(1)} %get-tuple-element.117), channel_id=1, source_target_pairs={{0,6},{1,7},{2,4},{3,5},{4,2},{5,3},{6,0},{7,1},{8,14},{9,15},{10,... | collective-permute-start | bytes 98312 | tf_op jit(solution)/shard_map/ppermute | solution.py:287
  66.9 1.5 %collective-permute-start.36 = (bf16[128,128]{1,0:T(8,128)(2,1)S(1)}, bf16[128,128]{1,0:T(8,128)(2,1)S(1)}, u32[]{:S(2)}, u32[]{:S(2)}) collective-permute-start(bf16[128,128]{1,0:T(8,128)(2,1)S(1)} %get-tuple-element.118), channel_id=1, source_target_pairs={{0,7},{1,6},{2,5},{3,4},{4,3},{5,2},{6,1},{7,0},{8,15},{9,14},{10,... | collective-permute-start | bytes 98312 | tf_op jit(solution)/shard_map/ppermute | solution.py:287
  68.5 1.3 %collective-permute-start.37 = (bf16[128,128]{1,0:T(8,128)(2,1)S(1)}, bf16[128,128]{1,0:T(8,128)(2,1)S(1)}, u32[]{:S(2)}, u32[]{:S(2)}) collective-permute-start(bf16[128,128]{1,0:T(8,128)(2,1)S(1)} %get-tuple-element.119), channel_id=1, source_target_pairs={{0,8},{1,9},{2,10},{3,11},{4,12},{5,13},{6,14},{7,15},{8,0},{9,1},... | collective-permute-start | bytes 98312 | tf_op jit(solution)/shard_map/ppermute | solution.py:287
  69.8 3.4 %collective-permute-start.39 = (bf16[128,128]{1,0:T(8,128)(2,1)S(1)}, bf16[128,128]{1,0:T(8,128)(2,1)S(1)}, u32[]{:S(2)}, u32[]{:S(2)}) collective-permute-start(bf16[128,128]{1,0:T(8,128)(2,1)S(1)} %get-tuple-element.121), channel_id=1, source_target_pairs={{0,10},{1,11},{2,8},{3,9},{4,14},{5,15},{6,12},{7,13},{8,2},{9,3},... | collective-permute-start | bytes 98312 | tf_op jit(solution)/shard_map/ppermute | solution.py:287
  73.1 2.1 %collective-permute-start.40 = (bf16[128,128]{1,0:T(8,128)(2,1)S(1)}, bf16[128,128]{1,0:T(8,128)(2,1)S(1)}, u32[]{:S(2)}, u32[]{:S(2)}) collective-permute-start(bf16[128,128]{1,0:T(8,128)(2,1)S(1)} %get-tuple-element.122), channel_id=1, source_target_pairs={{0,11},{1,10},{2,9},{3,8},{4,15},{5,14},{6,13},{7,12},{8,3},{9,2},... | collective-permute-start | bytes 98312 | tf_op jit(solution)/shard_map/ppermute | solution.py:287
  75.2 0.2 collective-permute-start.42
  75.4 3.0 %collective-permute-start.43 = (bf16[128,128]{1,0:T(8,128)(2,1)S(1)}, bf16[128,128]{1,0:T(8,128)(2,1)S(1)}, u32[]{:S(2)}, u32[]{:S(2)}) collective-permute-start(bf16[128,128]{1,0:T(8,128)(2,1)S(1)} %get-tuple-element.125), channel_id=1, source_target_pairs={{0,14},{1,15},{2,12},{3,13},{4,10},{5,11},{6,8},{7,9},{8,6},{9,7},... | collective-permute-start | bytes 98312 | tf_op jit(solution)/shard_map/ppermute | solution.py:287
  78.4 3.0 %collective-permute-start.44 = (bf16[128,128]{1,0:T(8,128)(2,1)S(1)}, bf16[128,128]{1,0:T(8,128)(2,1)S(1)}, u32[]{:S(2)}, u32[]{:S(2)}) collective-permute-start(bf16[128,128]{1,0:T(8,128)(2,1)S(1)} %get-tuple-element.126), channel_id=1, source_target_pairs={{0,15},{1,14},{2,13},{3,12},{4,11},{5,10},{6,9},{7,8},{8,7},{9,6},... | collective-permute-start | bytes 98312 | tf_op jit(solution)/shard_map/ppermute | solution.py:287
  81.4 3.0 %collective-permute-done.44.refs_15_ = bf16[128,128]{1,0:T(8,128)(2,1)S(1)} collective-permute-done((bf16[128,128]{1,0:T(8,128)(2,1)S(1)}, bf16[128,128]{1,0:T(8,128)(2,1)S(1)}, u32[]{:S(2)}, u32[]{:S(2)}) %collective-permute-start.44) | collective-permute-done | bytes 32800 | tf_op jit(solution)/shard_map/ppermute | solution.py:287
  84.4 2.1 %shard_map.105 = (bf16[64,128]{1,0:T(8,128)(2,1)S(1)}, bf16[64,128]{1,0:T(8,128)(2,1)S(1)}, bf16[64,128]{1,0:T(8,128)(2,1)S(1)}, bf16[64,128]{1,0:T(8,128)(2,1)S...) custom-call(bf16[128,128]{1,0:T(8,128)(2,1)S(1)} %get-tuple-element., ...), custom_call_target="tpu_custom_call" | custom-call | tf_op jit(solution)/shard_map/pallas_call | solution.py:270
  86.6 2.5 %collective-permute-start.46 = (bf16[64,128]{1,0:T(8,128)(2,1)S(1)}, bf16[64,128]{1,0:T(8,128)(2,1)S(1)}, u32[]{:S(2)}, u32[]{:S(2)}) collective-permute-start(bf16[64,128]{1,0:T(8,128)(2,1)S(1)} %get-tuple-element.129), channel_id=1, source_target_pairs={{0,2},{1,3},{2,0},{3,1},{4,6},{5,7},{6,4},{7,5},{8,10},{9,11},{10,... | collective-permute-start | bytes 49160 | tf_op jit(solution)/shard_map/ppermute | solution.py:287
  89.1 1.9 %collective-permute-start.47 = (bf16[64,128]{1,0:T(8,128)(2,1)S(1)}, bf16[64,128]{1,0:T(8,128)(2,1)S(1)}, u32[]{:S(2)}, u32[]{:S(2)}) collective-permute-start(bf16[64,128]{1,0:T(8,128)(2,1)S(1)} %get-tuple-element.130), channel_id=1, source_target_pairs={{0,3},{1,2},{2,1},{3,0},{4,7},{5,6},{6,5},{7,4},{8,11},{9,10},{10,... | collective-permute-start | bytes 49160 | tf_op jit(solution)/shard_map/ppermute | solution.py:287
  91.0 0.5 collective-permute-start.48
  91.5 2.2 %collective-permute-start.50 = (bf16[64,128]{1,0:T(8,128)(2,1)S(1)}, bf16[64,128]{1,0:T(8,128)(2,1)S(1)}, u32[]{:S(2)}, u32[]{:S(2)}) collective-permute-start(bf16[64,128]{1,0:T(8,128)(2,1)S(1)} %get-tuple-element.133), channel_id=1, source_target_pairs={{0,6},{1,7},{2,4},{3,5},{4,2},{5,3},{6,0},{7,1},{8,14},{9,15},{10,... | collective-permute-start | bytes 49160 | tf_op jit(solution)/shard_map/ppermute | solution.py:287
  93.7 1.5 %collective-permute-start.51 = (bf16[64,128]{1,0:T(8,128)(2,1)S(1)}, bf16[64,128]{1,0:T(8,128)(2,1)S(1)}, u32[]{:S(2)}, u32[]{:S(2)}) collective-permute-start(bf16[64,128]{1,0:T(8,128)(2,1)S(1)} %get-tuple-element.134), channel_id=1, source_target_pairs={{0,7},{1,6},{2,5},{3,4},{4,3},{5,2},{6,1},{7,0},{8,15},{9,14},{10,... | collective-permute-start | bytes 49160 | tf_op jit(solution)/shard_map/ppermute | solution.py:287
  95.2 1.3 %collective-permute-start.52 = (bf16[64,128]{1,0:T(8,128)(2,1)S(1)}, bf16[64,128]{1,0:T(8,128)(2,1)S(1)}, u32[]{:S(2)}, u32[]{:S(2)}) collective-permute-start(bf16[64,128]{1,0:T(8,128)(2,1)S(1)} %get-tuple-element.135), channel_id=1, source_target_pairs={{0,8},{1,9},{2,10},{3,11},{4,12},{5,13},{6,14},{7,15},{8,0},{9,1},... | collective-permute-start | bytes 49160 | tf_op jit(solution)/shard_map/ppermute | solution.py:287
  96.5 3.4 %collective-permute-start.54 = (bf16[64,128]{1,0:T(8,128)(2,1)S(1)}, bf16[64,128]{1,0:T(8,128)(2,1)S(1)}, u32[]{:S(2)}, u32[]{:S(2)}) collective-permute-start(bf16[64,128]{1,0:T(8,128)(2,1)S(1)} %get-tuple-element.137), channel_id=1, source_target_pairs={{0,10},{1,11},{2,8},{3,9},{4,14},{5,15},{6,12},{7,13},{8,2},{9,3},... | collective-permute-start | bytes 49160 | tf_op jit(solution)/shard_map/ppermute | solution.py:287
  99.9 2.1 %collective-permute-start.55 = (bf16[64,128]{1,0:T(8,128)(2,1)S(1)}, bf16[64,128]{1,0:T(8,128)(2,1)S(1)}, u32[]{:S(2)}, u32[]{:S(2)}) collective-permute-start(bf16[64,128]{1,0:T(8,128)(2,1)S(1)} %get-tuple-element.138), channel_id=1, source_target_pairs={{0,11},{1,10},{2,9},{3,8},{4,15},{5,14},{6,13},{7,12},{8,3},{9,2},... | collective-permute-start | bytes 49160 | tf_op jit(solution)/shard_map/ppermute | solution.py:287
  102.0 0.2 collective-permute-start.57
  102.2 3.0 %collective-permute-start.58 = (bf16[64,128]{1,0:T(8,128)(2,1)S(1)}, bf16[64,128]{1,0:T(8,128)(2,1)S(1)}, u32[]{:S(2)}, u32[]{:S(2)}) collective-permute-start(bf16[64,128]{1,0:T(8,128)(2,1)S(1)} %get-tuple-element.141), channel_id=1, source_target_pairs={{0,14},{1,15},{2,12},{3,13},{4,10},{5,11},{6,8},{7,9},{8,6},{9,7},... | collective-permute-start | bytes 49160 | tf_op jit(solution)/shard_map/ppermute | solution.py:287
  105.2 3.0 %collective-permute-start.59 = (bf16[64,128]{1,0:T(8,128)(2,1)S(1)}, bf16[64,128]{1,0:T(8,128)(2,1)S(1)}, u32[]{:S(2)}, u32[]{:S(2)}) collective-permute-start(bf16[64,128]{1,0:T(8,128)(2,1)S(1)} %get-tuple-element.142), channel_id=1, source_target_pairs={{0,15},{1,14},{2,13},{3,12},{4,11},{5,10},{6,9},{7,8},{8,7},{9,6},... | collective-permute-start | bytes 49160 | tf_op jit(solution)/shard_map/ppermute | solution.py:287
  108.2 0.3 shard_map.104.refs_1_
  108.5 2.5 %collective-permute-done.59.refs_22_ = bf16[64,128]{1,0:T(8,128)(2,1)S(1)} collective-permute-done((bf16[64,128]{1,0:T(8,128)(2,1)S(1)}, bf16[64,128]{1,0:T(8,128)(2,1)S(1)}, u32[]{:S(2)}, u32[]{:S(2)}) %collective-permute-start.59) | collective-permute-done | bytes 16416 | tf_op jit(solution)/shard_map/ppermute | solution.py:287
  111.0 0.6 copy-done.12
  111.7 3.7 %shard_map.106 = f32[1024,128]{1,0:T(8,128)} custom-call(f32[128,1024]{1,0:T(8,128)S(1)} %get-tuple-element.109.refs_0_, f32[128,1024]{1,0:T(8,128)S(1)} %shard_map.104.refs_1_, f32[2,128]{1,0:T(2,128)S(1)} %copy-done.11, bf16[2,128,128]{2,1,0:T(8,128)(2,1)S(1)} %copy-done.5, f32[1,128]{1,0:T(1,128)S(1)} %bitcast.5, bf16[128,1024]{1,0:T(8,128)(2,1)S(1)} %copy-done.4, ...), custom_call_target="tpu_custom_call" | custom-call | tf_op jit(solution)/shard_map/pallas_call | solution.py:270
  (89 shorter events, 0.3 us)
Async XLA Ops:
  3.4 51.7 %copy-start.1 = (f32[32,32,128]{2,1,0:T(8,128)S(1)}, f32[32,32,128]{2,1,0:T(8,128)}, u32[]{:S(2)}) copy-start(f32[32,32,128]{2,1,0:T(8,128)} %param.10) | copy-start | bytes 1572868
  4.1 6.7 %collective-permute-start = (bf16[128,128]{1,0:T(8,128)(2,1)S(1)}, bf16[128,128]{1,0:T(8,128)(2,1)S(1)}, u32[]{:S(2)}, u32[]{:S(2)}) collective-permute-start(bf16[128,128]{1,0:T(8,128)(2,1)S(1)} %get-tuple-element.78), channel_id=1, source_target_pairs={{0,1},{1,0},{2,3},{3,2},{4,5},{5,4},{6,7},{7,6},{8,9},{9,8},{10,11... | collective-permute-start | bytes 98312 | tf_op jit(solution)/shard_map/ppermute | solution.py:287
  7.2 6.7 %collective-permute-start.1 = (bf16[128,128]{1,0:T(8,128)(2,1)S(1)}, bf16[128,128]{1,0:T(8,128)(2,1)S(1)}, u32[]{:S(2)}, u32[]{:S(2)}) collective-permute-start(bf16[128,128]{1,0:T(8,128)(2,1)S(1)} %get-tuple-element.79), channel_id=1, source_target_pairs={{0,2},{1,3},{2,0},{3,1},{4,6},{5,7},{6,4},{7,5},{8,10},{9,11},{10,... | collective-permute-start | bytes 98312 | tf_op jit(solution)/shard_map/ppermute | solution.py:287
  9.8 6.2 %collective-permute-start.2 = (bf16[128,128]{1,0:T(8,128)(2,1)S(1)}, bf16[128,128]{1,0:T(8,128)(2,1)S(1)}, u32[]{:S(2)}, u32[]{:S(2)}) collective-permute-start(bf16[128,128]{1,0:T(8,128)(2,1)S(1)} %get-tuple-element.80), channel_id=1, source_target_pairs={{0,3},{1,2},{2,1},{3,0},{4,7},{5,6},{6,5},{7,4},{8,11},{9,10},{10,... | collective-permute-start | bytes 98312 | tf_op jit(solution)/shard_map/ppermute | solution.py:287
  9.8 7.7 %collective-permute-start.3 = (bf16[128,128]{1,0:T(8,128)(2,1)S(1)}, bf16[128,128]{1,0:T(8,128)(2,1)S(1)}, u32[]{:S(2)}, u32[]{:S(2)}) collective-permute-start(bf16[128,128]{1,0:T(8,128)(2,1)S(1)} %get-tuple-element.81), channel_id=1, source_target_pairs={{0,4},{1,5},{2,6},{3,7},{4,0},{5,1},{6,2},{7,3},{8,12},{9,13},{10,... | collective-permute-start | bytes 98312 | tf_op jit(solution)/shard_map/ppermute | solution.py:287
  9.8 7.7 %collective-permute-start.4 = (bf16[128,128]{1,0:T(8,128)(2,1)S(1)}, bf16[128,128]{1,0:T(8,128)(2,1)S(1)}, u32[]{:S(2)}, u32[]{:S(2)}) collective-permute-start(bf16[128,128]{1,0:T(8,128)(2,1)S(1)} %get-tuple-element.82), channel_id=1, source_target_pairs={{0,5},{1,4},{2,7},{3,6},{4,1},{5,0},{6,3},{7,2},{8,13},{9,12},{10,... | collective-permute-start | bytes 98312 | tf_op jit(solution)/shard_map/ppermute | solution.py:287
  10.8 10.0 %collective-permute-start.5 = (bf16[128,128]{1,0:T(8,128)(2,1)S(1)}, bf16[128,128]{1,0:T(8,128)(2,1)S(1)}, u32[]{:S(2)}, u32[]{:S(2)}) collective-permute-start(bf16[128,128]{1,0:T(8,128)(2,1)S(1)} %get-tuple-element.83), channel_id=1, source_target_pairs={{0,6},{1,7},{2,4},{3,5},{4,2},{5,3},{6,0},{7,1},{8,14},{9,15},{10,... | collective-permute-start | bytes 98312 | tf_op jit(solution)/shard_map/ppermute | solution.py:287
  13.9 8.8 %collective-permute-start.6 = (bf16[128,128]{1,0:T(8,128)(2,1)S(1)}, bf16[128,128]{1,0:T(8,128)(2,1)S(1)}, u32[]{:S(2)}, u32[]{:S(2)}) collective-permute-start(bf16[128,128]{1,0:T(8,128)(2,1)S(1)} %get-tuple-element.84), channel_id=1, source_target_pairs={{0,7},{1,6},{2,5},{3,4},{4,3},{5,2},{6,1},{7,0},{8,15},{9,14},{10,... | collective-permute-start | bytes 98312 | tf_op jit(solution)/shard_map/ppermute | solution.py:287
  15.9 6.8 %collective-permute-start.7 = (bf16[128,128]{1,0:T(8,128)(2,1)S(1)}, bf16[128,128]{1,0:T(8,128)(2,1)S(1)}, u32[]{:S(2)}, u32[]{:S(2)}) collective-permute-start(bf16[128,128]{1,0:T(8,128)(2,1)S(1)} %get-tuple-element.85), channel_id=1, source_target_pairs={{0,8},{1,9},{2,10},{3,11},{4,12},{5,13},{6,14},{7,15},{8,0},{9,1},... | collective-permute-start | bytes 98312 | tf_op jit(solution)/shard_map/ppermute | solution.py:287
  17.4 5.7 %collective-permute-start.8 = (bf16[128,128]{1,0:T(8,128)(2,1)S(1)}, bf16[128,128]{1,0:T(8,128)(2,1)S(1)}, u32[]{:S(2)}, u32[]{:S(2)}) collective-permute-start(bf16[128,128]{1,0:T(8,128)(2,1)S(1)} %get-tuple-element.86), channel_id=1, source_target_pairs={{0,9},{1,8},{2,11},{3,10},{4,13},{5,12},{6,15},{7,14},{8,1},{9,0},... | collective-permute-start | bytes 98312 | tf_op jit(solution)/shard_map/ppermute | solution.py:287
  17.4 8.4 %collective-permute-start.9 = (bf16[128,128]{1,0:T(8,128)(2,1)S(1)}, bf16[128,128]{1,0:T(8,128)(2,1)S(1)}, u32[]{:S(2)}, u32[]{:S(2)}) collective-permute-start(bf16[128,128]{1,0:T(8,128)(2,1)S(1)} %get-tuple-element.87), channel_id=1, source_target_pairs={{0,10},{1,11},{2,8},{3,9},{4,14},{5,15},{6,12},{7,13},{8,2},{9,3},... | collective-permute-start | bytes 98312 | tf_op jit(solution)/shard_map/ppermute | solution.py:287
  20.8 8.1 %collective-permute-start.10 = (bf16[128,128]{1,0:T(8,128)(2,1)S(1)}, bf16[128,128]{1,0:T(8,128)(2,1)S(1)}, u32[]{:S(2)}, u32[]{:S(2)}) collective-permute-start(bf16[128,128]{1,0:T(8,128)(2,1)S(1)} %get-tuple-element.88), channel_id=1, source_target_pairs={{0,11},{1,10},{2,9},{3,8},{4,15},{5,14},{6,13},{7,12},{8,3},{9,2},... | collective-permute-start | bytes 98312 | tf_op jit(solution)/shard_map/ppermute | solution.py:287
  22.7 6.2 %collective-permute-start.11 = (bf16[128,128]{1,0:T(8,128)(2,1)S(1)}, bf16[128,128]{1,0:T(8,128)(2,1)S(1)}, u32[]{:S(2)}, u32[]{:S(2)}) collective-permute-start(bf16[128,128]{1,0:T(8,128)(2,1)S(1)} %get-tuple-element.89), channel_id=1, source_target_pairs={{0,12},{1,13},{2,14},{3,15},{4,8},{5,9},{6,10},{7,11},{8,4},{9,5},... | collective-permute-start | bytes 98312 | tf_op jit(solution)/shard_map/ppermute | solution.py:287
  22.7 6.2 %collective-permute-start.12 = (bf16[128,128]{1,0:T(8,128)(2,1)S(1)}, bf16[128,128]{1,0:T(8,128)(2,1)S(1)}, u32[]{:S(2)}, u32[]{:S(2)}) collective-permute-start(bf16[128,128]{1,0:T(8,128)(2,1)S(1)} %get-tuple-element.90), channel_id=1, source_target_pairs={{0,13},{1,12},{2,15},{3,14},{4,9},{5,8},{6,11},{7,10},{8,5},{9,4},... | collective-permute-start | bytes 98312 | tf_op jit(solution)/shard_map/ppermute | solution.py:287
  23.1 5.8 %collective-permute-start.13 = (bf16[128,128]{1,0:T(8,128)(2,1)S(1)}, bf16[128,128]{1,0:T(8,128)(2,1)S(1)}, u32[]{:S(2)}, u32[]{:S(2)}) collective-permute-start(bf16[128,128]{1,0:T(8,128)(2,1)S(1)} %get-tuple-element.91), channel_id=1, source_target_pairs={{0,14},{1,15},{2,12},{3,13},{4,10},{5,11},{6,8},{7,9},{8,6},{9,7},... | collective-permute-start | bytes 98312 | tf_op jit(solution)/shard_map/ppermute | solution.py:287
  25.8 6.0 %collective-permute-start.14 = (bf16[128,128]{1,0:T(8,128)(2,1)S(1)}, bf16[128,128]{1,0:T(8,128)(2,1)S(1)}, u32[]{:S(2)}, u32[]{:S(2)}) collective-permute-start(bf16[128,128]{1,0:T(8,128)(2,1)S(1)} %get-tuple-element.92), channel_id=1, source_target_pairs={{0,15},{1,14},{2,13},{3,12},{4,11},{5,10},{6,9},{7,8},{8,7},{9,6},... | collective-permute-start | bytes 98312 | tf_op jit(solution)/shard_map/ppermute | solution.py:287
  31.9 23.2 %copy-start.6 = (bf16[2,128,128]{2,1,0:T(8,128)(2,1)S(1)}, bf16[2,128,128]{2,1,0:T(8,128)(2,1)}, u32[]{:S(2)}) copy-start(bf16[2,128,128]{2,1,0:T(8,128)(2,1)} %refs_1_.5) | copy-start | bytes 196612
  33.3 5.2 %collective-permute-start.15 = (bf16[64,128]{1,0:T(8,128)(2,1)S(1)}, bf16[64,128]{1,0:T(8,128)(2,1)S(1)}, u32[]{:S(2)}, u32[]{:S(2)}) collective-permute-start(bf16[64,128]{1,0:T(8,128)(2,1)S(1)} %get-tuple-element.94), channel_id=1, source_target_pairs={{0,1},{1,0},{2,3},{3,2},{4,5},{5,4},{6,7},{7,6},{8,9},{9,8},{10,11... | collective-permute-start | bytes 49160 | tf_op jit(solution)/shard_map/ppermute | solution.py:287
  33.3 7.3 %collective-permute-start.16 = (bf16[64,128]{1,0:T(8,128)(2,1)S(1)}, bf16[64,128]{1,0:T(8,128)(2,1)S(1)}, u32[]{:S(2)}, u32[]{:S(2)}) collective-permute-start(bf16[64,128]{1,0:T(8,128)(2,1)S(1)} %get-tuple-element.95), channel_id=1, source_target_pairs={{0,2},{1,3},{2,0},{3,1},{4,6},{5,7},{6,4},{7,5},{8,10},{9,11},{10,... | collective-permute-start | bytes 49160 | tf_op jit(solution)/shard_map/ppermute | solution.py:287
  35.8 6.3 %collective-permute-start.17 = (bf16[64,128]{1,0:T(8,128)(2,1)S(1)}, bf16[64,128]{1,0:T(8,128)(2,1)S(1)}, u32[]{:S(2)}, u32[]{:S(2)}) collective-permute-start(bf16[64,128]{1,0:T(8,128)(2,1)S(1)} %get-tuple-element.96), channel_id=1, source_target_pairs={{0,3},{1,2},{2,1},{3,0},{4,7},{5,6},{6,5},{7,4},{8,11},{9,10},{10,... | collective-permute-start | bytes 49160 | tf_op jit(solution)/shard_map/ppermute | solution.py:287
  37.7 5.7 %collective-permute-start.18 = (bf16[64,128]{1,0:T(8,128)(2,1)S(1)}, bf16[64,128]{1,0:T(8,128)(2,1)S(1)}, u32[]{:S(2)}, u32[]{:S(2)}) collective-permute-start(bf16[64,128]{1,0:T(8,128)(2,1)S(1)} %get-tuple-element.97), channel_id=1, source_target_pairs={{0,4},{1,5},{2,6},{3,7},{4,0},{5,1},{6,2},{7,3},{8,12},{9,13},{10,... | collective-permute-start | bytes 49160 | tf_op jit(solution)/shard_map/ppermute | solution.py:287
  38.4 5.0 %collective-permute-start.19 = (bf16[64,128]{1,0:T(8,128)(2,1)S(1)}, bf16[64,128]{1,0:T(8,128)(2,1)S(1)}, u32[]{:S(2)}, u32[]{:S(2)}) collective-permute-start(bf16[64,128]{1,0:T(8,128)(2,1)S(1)} %get-tuple-element.98), channel_id=1, source_target_pairs={{0,5},{1,4},{2,7},{3,6},{4,1},{5,0},{6,3},{7,2},{8,13},{9,12},{10,... | collective-permute-start | bytes 49160 | tf_op jit(solution)/shard_map/ppermute | solution.py:287
  38.4 8.4 %collective-permute-start.20 = (bf16[64,128]{1,0:T(8,128)(2,1)S(1)}, bf16[64,128]{1,0:T(8,128)(2,1)S(1)}, u32[]{:S(2)}, u32[]{:S(2)}) collective-permute-start(bf16[64,128]{1,0:T(8,128)(2,1)S(1)} %get-tuple-element.99), channel_id=1, source_target_pairs={{0,6},{1,7},{2,4},{3,5},{4,2},{5,3},{6,0},{7,1},{8,14},{9,15},{10,... | collective-permute-start | bytes 49160 | tf_op jit(solution)/shard_map/ppermute | solution.py:287
  40.6 8.3 %collective-permute-start.21 = (bf16[64,128]{1,0:T(8,128)(2,1)S(1)}, bf16[64,128]{1,0:T(8,128)(2,1)S(1)}, u32[]{:S(2)}, u32[]{:S(2)}) collective-permute-start(bf16[64,128]{1,0:T(8,128)(2,1)S(1)} %get-tuple-element.100), channel_id=1, source_target_pairs={{0,7},{1,6},{2,5},{3,4},{4,3},{5,2},{6,1},{7,0},{8,15},{9,14},{10,... | collective-permute-start | bytes 49160 | tf_op jit(solution)/shard_map/ppermute | solution.py:287
  42.1 6.8 %collective-permute-start.22 = (bf16[64,128]{1,0:T(8,128)(2,1)S(1)}, bf16[64,128]{1,0:T(8,128)(2,1)S(1)}, u32[]{:S(2)}, u32[]{:S(2)}) collective-permute-start(bf16[64,128]{1,0:T(8,128)(2,1)S(1)} %get-tuple-element.101), channel_id=1, source_target_pairs={{0,8},{1,9},{2,10},{3,11},{4,12},{5,13},{6,14},{7,15},{8,0},{9,1},... | collective-permute-start | bytes 49160 | tf_op jit(solution)/shard_map/ppermute | solution.py:287
  43.4 5.7 %collective-permute-start.23 = (bf16[64,128]{1,0:T(8,128)(2,1)S(1)}, bf16[64,128]{1,0:T(8,128)(2,1)S(1)}, u32[]{:S(2)}, u32[]{:S(2)}) collective-permute-start(bf16[64,128]{1,0:T(8,128)(2,1)S(1)} %get-tuple-element.102), channel_id=1, source_target_pairs={{0,9},{1,8},{2,11},{3,10},{4,13},{5,12},{6,15},{7,14},{8,1},{9,0},... | collective-permute-start | bytes 49160 | tf_op jit(solution)/shard_map/ppermute | solution.py:287
  43.5 8.6 %collective-permute-start.24 = (bf16[64,128]{1,0:T(8,128)(2,1)S(1)}, bf16[64,128]{1,0:T(8,128)(2,1)S(1)}, u32[]{:S(2)}, u32[]{:S(2)}) collective-permute-start(bf16[64,128]{1,0:T(8,128)(2,1)S(1)} %get-tuple-element.103), channel_id=1, source_target_pairs={{0,10},{1,11},{2,8},{3,9},{4,14},{5,15},{6,12},{7,13},{8,2},{9,3},... | collective-permute-start | bytes 49160 | tf_op jit(solution)/shard_map/ppermute | solution.py:287
  46.8 8.6 %collective-permute-start.25 = (bf16[64,128]{1,0:T(8,128)(2,1)S(1)}, bf16[64,128]{1,0:T(8,128)(2,1)S(1)}, u32[]{:S(2)}, u32[]{:S(2)}) collective-permute-start(bf16[64,128]{1,0:T(8,128)(2,1)S(1)} %get-tuple-element.104), channel_id=1, source_target_pairs={{0,11},{1,10},{2,9},{3,8},{4,15},{5,14},{6,13},{7,12},{8,3},{9,2},... | collective-permute-start | bytes 49160 | tf_op jit(solution)/shard_map/ppermute | solution.py:287
  48.9 6.5 %collective-permute-start.26 = (bf16[64,128]{1,0:T(8,128)(2,1)S(1)}, bf16[64,128]{1,0:T(8,128)(2,1)S(1)}, u32[]{:S(2)}, u32[]{:S(2)}) collective-permute-start(bf16[64,128]{1,0:T(8,128)(2,1)S(1)} %get-tuple-element.105), channel_id=1, source_target_pairs={{0,12},{1,13},{2,14},{3,15},{4,8},{5,9},{6,10},{7,11},{8,4},{9,5},... | collective-permute-start | bytes 49160 | tf_op jit(solution)/shard_map/ppermute | solution.py:287
  48.9 6.5 %collective-permute-start.27 = (bf16[64,128]{1,0:T(8,128)(2,1)S(1)}, bf16[64,128]{1,0:T(8,128)(2,1)S(1)}, u32[]{:S(2)}, u32[]{:S(2)}) collective-permute-start(bf16[64,128]{1,0:T(8,128)(2,1)S(1)} %get-tuple-element.106), channel_id=1, source_target_pairs={{0,13},{1,12},{2,15},{3,14},{4,9},{5,8},{6,11},{7,10},{8,5},{9,4},... | collective-permute-start | bytes 49160 | tf_op jit(solution)/shard_map/ppermute | solution.py:287
  49.1 6.4 %collective-permute-start.28 = (bf16[64,128]{1,0:T(8,128)(2,1)S(1)}, bf16[64,128]{1,0:T(8,128)(2,1)S(1)}, u32[]{:S(2)}, u32[]{:S(2)}) collective-permute-start(bf16[64,128]{1,0:T(8,128)(2,1)S(1)} %get-tuple-element.107), channel_id=1, source_target_pairs={{0,14},{1,15},{2,12},{3,13},{4,10},{5,11},{6,8},{7,9},{8,6},{9,7},... | collective-permute-start | bytes 49160 | tf_op jit(solution)/shard_map/ppermute | solution.py:287
  52.1 5.9 %collective-permute-start.29 = (bf16[64,128]{1,0:T(8,128)(2,1)S(1)}, bf16[64,128]{1,0:T(8,128)(2,1)S(1)}, u32[]{:S(2)}, u32[]{:S(2)}) collective-permute-start(bf16[64,128]{1,0:T(8,128)(2,1)S(1)} %get-tuple-element.108), channel_id=1, source_target_pairs={{0,15},{1,14},{2,13},{3,12},{4,11},{5,10},{6,9},{7,8},{8,7},{9,6},... | collective-permute-start | bytes 49160 | tf_op jit(solution)/shard_map/ppermute | solution.py:287
  59.8 5.0 %collective-permute-start.30 = (bf16[128,128]{1,0:T(8,128)(2,1)S(1)}, bf16[128,128]{1,0:T(8,128)(2,1)S(1)}, u32[]{:S(2)}, u32[]{:S(2)}) collective-permute-start(bf16[128,128]{1,0:T(8,128)(2,1)S(1)} %get-tuple-element.112), channel_id=1, source_target_pairs={{0,1},{1,0},{2,3},{3,2},{4,5},{5,4},{6,7},{7,6},{8,9},{9,8},{10,11... | collective-permute-start | bytes 98312 | tf_op jit(solution)/shard_map/ppermute | solution.py:287
  59.8 7.1 %collective-permute-start.31 = (bf16[128,128]{1,0:T(8,128)(2,1)S(1)}, bf16[128,128]{1,0:T(8,128)(2,1)S(1)}, u32[]{:S(2)}, u32[]{:S(2)}) collective-permute-start(bf16[128,128]{1,0:T(8,128)(2,1)S(1)} %get-tuple-element.113), channel_id=1, source_target_pairs={{0,2},{1,3},{2,0},{3,1},{4,6},{5,7},{6,4},{7,5},{8,10},{9,11},{10,... | collective-permute-start | bytes 98312 | tf_op jit(solution)/shard_map/ppermute | solution.py:287
  62.3 6.2 %collective-permute-start.32 = (bf16[128,128]{1,0:T(8,128)(2,1)S(1)}, bf16[128,128]{1,0:T(8,128)(2,1)S(1)}, u32[]{:S(2)}, u32[]{:S(2)}) collective-permute-start(bf16[128,128]{1,0:T(8,128)(2,1)S(1)} %get-tuple-element.114), channel_id=1, source_target_pairs={{0,3},{1,2},{2,1},{3,0},{4,7},{5,6},{6,5},{7,4},{8,11},{9,10},{10,... | collective-permute-start | bytes 98312 | tf_op jit(solution)/shard_map/ppermute | solution.py:287
  64.2 5.5 %collective-permute-start.33 = (bf16[128,128]{1,0:T(8,128)(2,1)S(1)}, bf16[128,128]{1,0:T(8,128)(2,1)S(1)}, u32[]{:S(2)}, u32[]{:S(2)}) collective-permute-start(bf16[128,128]{1,0:T(8,128)(2,1)S(1)} %get-tuple-element.115), channel_id=1, source_target_pairs={{0,4},{1,5},{2,6},{3,7},{4,0},{5,1},{6,2},{7,3},{8,12},{9,13},{10,... | collective-permute-start | bytes 98312 | tf_op jit(solution)/shard_map/ppermute | solution.py:287
  64.7 5.0 %collective-permute-start.34 = (bf16[128,128]{1,0:T(8,128)(2,1)S(1)}, bf16[128,128]{1,0:T(8,128)(2,1)S(1)}, u32[]{:S(2)}, u32[]{:S(2)}) collective-permute-start(bf16[128,128]{1,0:T(8,128)(2,1)S(1)} %get-tuple-element.116), channel_id=1, source_target_pairs={{0,5},{1,4},{2,7},{3,6},{4,1},{5,0},{6,3},{7,2},{8,13},{9,12},{10,... | collective-permute-start | bytes 98312 | tf_op jit(solution)/shard_map/ppermute | solution.py:287
  64.7 8.4 %collective-permute-start.35 = (bf16[128,128]{1,0:T(8,128)(2,1)S(1)}, bf16[128,128]{1,0:T(8,128)(2,1)S(1)}, u32[]{:S(2)}, u32[]{:S(2)}) collective-permute-start(bf16[128,128]{1,0:T(8,128)(2,1)S(1)} %get-tuple-element.117), channel_id=1, source_target_pairs={{0,6},{1,7},{2,4},{3,5},{4,2},{5,3},{6,0},{7,1},{8,14},{9,15},{10,... | collective-permute-start | bytes 98312 | tf_op jit(solution)/shard_map/ppermute | solution.py:287
  66.9 8.3 %collective-permute-start.36 = (bf16[128,128]{1,0:T(8,128)(2,1)S(1)}, bf16[128,128]{1,0:T(8,128)(2,1)S(1)}, u32[]{:S(2)}, u32[]{:S(2)}) collective-permute-start(bf16[128,128]{1,0:T(8,128)(2,1)S(1)} %get-tuple-element.118), channel_id=1, source_target_pairs={{0,7},{1,6},{2,5},{3,4},{4,3},{5,2},{6,1},{7,0},{8,15},{9,14},{10,... | collective-permute-start | bytes 98312 | tf_op jit(solution)/shard_map/ppermute | solution.py:287
  68.5 6.8 %collective-permute-start.37 = (bf16[128,128]{1,0:T(8,128)(2,1)S(1)}, bf16[128,128]{1,0:T(8,128)(2,1)S(1)}, u32[]{:S(2)}, u32[]{:S(2)}) collective-permute-start(bf16[128,128]{1,0:T(8,128)(2,1)S(1)} %get-tuple-element.119), channel_id=1, source_target_pairs={{0,8},{1,9},{2,10},{3,11},{4,12},{5,13},{6,14},{7,15},{8,0},{9,1},... | collective-permute-start | bytes 98312 | tf_op jit(solution)/shard_map/ppermute | solution.py:287
  69.8 5.7 %collective-permute-start.38 = (bf16[128,128]{1,0:T(8,128)(2,1)S(1)}, bf16[128,128]{1,0:T(8,128)(2,1)S(1)}, u32[]{:S(2)}, u32[]{:S(2)}) collective-permute-start(bf16[128,128]{1,0:T(8,128)(2,1)S(1)} %get-tuple-element.120), channel_id=1, source_target_pairs={{0,9},{1,8},{2,11},{3,10},{4,13},{5,12},{6,15},{7,14},{8,1},{9,0},... | collective-permute-start | bytes 98312 | tf_op jit(solution)/shard_map/ppermute | solution.py:287
  69.8 8.6 %collective-permute-start.39 = (bf16[128,128]{1,0:T(8,128)(2,1)S(1)}, bf16[128,128]{1,0:T(8,128)(2,1)S(1)}, u32[]{:S(2)}, u32[]{:S(2)}) collective-permute-start(bf16[128,128]{1,0:T(8,128)(2,1)S(1)} %get-tuple-element.121), channel_id=1, source_target_pairs={{0,10},{1,11},{2,8},{3,9},{4,14},{5,15},{6,12},{7,13},{8,2},{9,3},... | collective-permute-start | bytes 98312 | tf_op jit(solution)/shard_map/ppermute | solution.py:287
  73.1 8.3 %collective-permute-start.40 = (bf16[128,128]{1,0:T(8,128)(2,1)S(1)}, bf16[128,128]{1,0:T(8,128)(2,1)S(1)}, u32[]{:S(2)}, u32[]{:S(2)}) collective-permute-start(bf16[128,128]{1,0:T(8,128)(2,1)S(1)} %get-tuple-element.122), channel_id=1, source_target_pairs={{0,11},{1,10},{2,9},{3,8},{4,15},{5,14},{6,13},{7,12},{8,3},{9,2},... | collective-permute-start | bytes 98312 | tf_op jit(solution)/shard_map/ppermute | solution.py:287
  75.2 6.2 %collective-permute-start.41 = (bf16[128,128]{1,0:T(8,128)(2,1)S(1)}, bf16[128,128]{1,0:T(8,128)(2,1)S(1)}, u32[]{:S(2)}, u32[]{:S(2)}) collective-permute-start(bf16[128,128]{1,0:T(8,128)(2,1)S(1)} %get-tuple-element.123), channel_id=1, source_target_pairs={{0,12},{1,13},{2,14},{3,15},{4,8},{5,9},{6,10},{7,11},{8,4},{9,5},... | collective-permute-start | bytes 98312 | tf_op jit(solution)/shard_map/ppermute | solution.py:287
  75.2 6.2 %collective-permute-start.42 = (bf16[128,128]{1,0:T(8,128)(2,1)S(1)}, bf16[128,128]{1,0:T(8,128)(2,1)S(1)}, u32[]{:S(2)}, u32[]{:S(2)}) collective-permute-start(bf16[128,128]{1,0:T(8,128)(2,1)S(1)} %get-tuple-element.124), channel_id=1, source_target_pairs={{0,13},{1,12},{2,15},{3,14},{4,9},{5,8},{6,11},{7,10},{8,5},{9,4},... | collective-permute-start | bytes 98312 | tf_op jit(solution)/shard_map/ppermute | solution.py:287
  75.4 6.0 %collective-permute-start.43 = (bf16[128,128]{1,0:T(8,128)(2,1)S(1)}, bf16[128,128]{1,0:T(8,128)(2,1)S(1)}, u32[]{:S(2)}, u32[]{:S(2)}) collective-permute-start(bf16[128,128]{1,0:T(8,128)(2,1)S(1)} %get-tuple-element.125), channel_id=1, source_target_pairs={{0,14},{1,15},{2,12},{3,13},{4,10},{5,11},{6,8},{7,9},{8,6},{9,7},... | collective-permute-start | bytes 98312 | tf_op jit(solution)/shard_map/ppermute | solution.py:287
  78.4 6.0 %collective-permute-start.44 = (bf16[128,128]{1,0:T(8,128)(2,1)S(1)}, bf16[128,128]{1,0:T(8,128)(2,1)S(1)}, u32[]{:S(2)}, u32[]{:S(2)}) collective-permute-start(bf16[128,128]{1,0:T(8,128)(2,1)S(1)} %get-tuple-element.126), channel_id=1, source_target_pairs={{0,15},{1,14},{2,13},{3,12},{4,11},{5,10},{6,9},{7,8},{8,7},{9,6},... | collective-permute-start | bytes 98312 | tf_op jit(solution)/shard_map/ppermute | solution.py:287
  86.5 5.0 %collective-permute-start.45 = (bf16[64,128]{1,0:T(8,128)(2,1)S(1)}, bf16[64,128]{1,0:T(8,128)(2,1)S(1)}, u32[]{:S(2)}, u32[]{:S(2)}) collective-permute-start(bf16[64,128]{1,0:T(8,128)(2,1)S(1)} %get-tuple-element.128), channel_id=1, source_target_pairs={{0,1},{1,0},{2,3},{3,2},{4,5},{5,4},{6,7},{7,6},{8,9},{9,8},{10,11... | collective-permute-start | bytes 49160 | tf_op jit(solution)/shard_map/ppermute | solution.py:287
  86.6 7.1 %collective-permute-start.46 = (bf16[64,128]{1,0:T(8,128)(2,1)S(1)}, bf16[64,128]{1,0:T(8,128)(2,1)S(1)}, u32[]{:S(2)}, u32[]{:S(2)}) collective-permute-start(bf16[64,128]{1,0:T(8,128)(2,1)S(1)} %get-tuple-element.129), channel_id=1, source_target_pairs={{0,2},{1,3},{2,0},{3,1},{4,6},{5,7},{6,4},{7,5},{8,10},{9,11},{10,... | collective-permute-start | bytes 49160 | tf_op jit(solution)/shard_map/ppermute | solution.py:287
  89.1 6.1 %collective-permute-start.47 = (bf16[64,128]{1,0:T(8,128)(2,1)S(1)}, bf16[64,128]{1,0:T(8,128)(2,1)S(1)}, u32[]{:S(2)}, u32[]{:S(2)}) collective-permute-start(bf16[64,128]{1,0:T(8,128)(2,1)S(1)} %get-tuple-element.130), channel_id=1, source_target_pairs={{0,3},{1,2},{2,1},{3,0},{4,7},{5,6},{6,5},{7,4},{8,11},{9,10},{10,... | collective-permute-start | bytes 49160 | tf_op jit(solution)/shard_map/ppermute | solution.py:287
  91.0 5.5 %collective-permute-start.48 = (bf16[64,128]{1,0:T(8,128)(2,1)S(1)}, bf16[64,128]{1,0:T(8,128)(2,1)S(1)}, u32[]{:S(2)}, u32[]{:S(2)}) collective-permute-start(bf16[64,128]{1,0:T(8,128)(2,1)S(1)} %get-tuple-element.131), channel_id=1, source_target_pairs={{0,4},{1,5},{2,6},{3,7},{4,0},{5,1},{6,2},{7,3},{8,12},{9,13},{10,... | collective-permute-start | bytes 49160 | tf_op jit(solution)/shard_map/ppermute | solution.py:287
  91.5 5.0 %collective-permute-start.49 = (bf16[64,128]{1,0:T(8,128)(2,1)S(1)}, bf16[64,128]{1,0:T(8,128)(2,1)S(1)}, u32[]{:S(2)}, u32[]{:S(2)}) collective-permute-start(bf16[64,128]{1,0:T(8,128)(2,1)S(1)} %get-tuple-element.132), channel_id=1, source_target_pairs={{0,5},{1,4},{2,7},{3,6},{4,1},{5,0},{6,3},{7,2},{8,13},{9,12},{10,... | collective-permute-start | bytes 49160 | tf_op jit(solution)/shard_map/ppermute | solution.py:287
  91.5 8.4 %collective-permute-start.50 = (bf16[64,128]{1,0:T(8,128)(2,1)S(1)}, bf16[64,128]{1,0:T(8,128)(2,1)S(1)}, u32[]{:S(2)}, u32[]{:S(2)}) collective-permute-start(bf16[64,128]{1,0:T(8,128)(2,1)S(1)} %get-tuple-element.133), channel_id=1, source_target_pairs={{0,6},{1,7},{2,4},{3,5},{4,2},{5,3},{6,0},{7,1},{8,14},{9,15},{10,... | collective-permute-start | bytes 49160 | tf_op jit(solution)/shard_map/ppermute | solution.py:287
  93.7 8.3 %collective-permute-start.51 = (bf16[64,128]{1,0:T(8,128)(2,1)S(1)}, bf16[64,128]{1,0:T(8,128)(2,1)S(1)}, u32[]{:S(2)}, u32[]{:S(2)}) collective-permute-start(bf16[64,128]{1,0:T(8,128)(2,1)S(1)} %get-tuple-element.134), channel_id=1, source_target_pairs={{0,7},{1,6},{2,5},{3,4},{4,3},{5,2},{6,1},{7,0},{8,15},{9,14},{10,... | collective-permute-start | bytes 49160 | tf_op jit(solution)/shard_map/ppermute | solution.py:287
  95.2 6.8 %collective-permute-start.52 = (bf16[64,128]{1,0:T(8,128)(2,1)S(1)}, bf16[64,128]{1,0:T(8,128)(2,1)S(1)}, u32[]{:S(2)}, u32[]{:S(2)}) collective-permute-start(bf16[64,128]{1,0:T(8,128)(2,1)S(1)} %get-tuple-element.135), channel_id=1, source_target_pairs={{0,8},{1,9},{2,10},{3,11},{4,12},{5,13},{6,14},{7,15},{8,0},{9,1},... | collective-permute-start | bytes 49160 | tf_op jit(solution)/shard_map/ppermute | solution.py:287
  96.5 5.7 %collective-permute-start.53 = (bf16[64,128]{1,0:T(8,128)(2,1)S(1)}, bf16[64,128]{1,0:T(8,128)(2,1)S(1)}, u32[]{:S(2)}, u32[]{:S(2)}) collective-permute-start(bf16[64,128]{1,0:T(8,128)(2,1)S(1)} %get-tuple-element.136), channel_id=1, source_target_pairs={{0,9},{1,8},{2,11},{3,10},{4,13},{5,12},{6,15},{7,14},{8,1},{9,0},... | collective-permute-start | bytes 49160 | tf_op jit(solution)/shard_map/ppermute | solution.py:287
  96.5 8.6 %collective-permute-start.54 = (bf16[64,128]{1,0:T(8,128)(2,1)S(1)}, bf16[64,128]{1,0:T(8,128)(2,1)S(1)}, u32[]{:S(2)}, u32[]{:S(2)}) collective-permute-start(bf16[64,128]{1,0:T(8,128)(2,1)S(1)} %get-tuple-element.137), channel_id=1, source_target_pairs={{0,10},{1,11},{2,8},{3,9},{4,14},{5,15},{6,12},{7,13},{8,2},{9,3},... | collective-permute-start | bytes 49160 | tf_op jit(solution)/shard_map/ppermute | solution.py:287
  99.9 8.5 %collective-permute-start.55 = (bf16[64,128]{1,0:T(8,128)(2,1)S(1)}, bf16[64,128]{1,0:T(8,128)(2,1)S(1)}, u32[]{:S(2)}, u32[]{:S(2)}) collective-permute-start(bf16[64,128]{1,0:T(8,128)(2,1)S(1)} %get-tuple-element.138), channel_id=1, source_target_pairs={{0,11},{1,10},{2,9},{3,8},{4,15},{5,14},{6,13},{7,12},{8,3},{9,2},... | collective-permute-start | bytes 49160 | tf_op jit(solution)/shard_map/ppermute | solution.py:287
  102.0 6.5 %collective-permute-start.56 = (bf16[64,128]{1,0:T(8,128)(2,1)S(1)}, bf16[64,128]{1,0:T(8,128)(2,1)S(1)}, u32[]{:S(2)}, u32[]{:S(2)}) collective-permute-start(bf16[64,128]{1,0:T(8,128)(2,1)S(1)} %get-tuple-element.139), channel_id=1, source_target_pairs={{0,12},{1,13},{2,14},{3,15},{4,8},{5,9},{6,10},{7,11},{8,4},{9,5},... | collective-permute-start | bytes 49160 | tf_op jit(solution)/shard_map/ppermute | solution.py:287
  102.0 6.5 %collective-permute-start.57 = (bf16[64,128]{1,0:T(8,128)(2,1)S(1)}, bf16[64,128]{1,0:T(8,128)(2,1)S(1)}, u32[]{:S(2)}, u32[]{:S(2)}) collective-permute-start(bf16[64,128]{1,0:T(8,128)(2,1)S(1)} %get-tuple-element.140), channel_id=1, source_target_pairs={{0,13},{1,12},{2,15},{3,14},{4,9},{5,8},{6,11},{7,10},{8,5},{9,4},... | collective-permute-start | bytes 49160 | tf_op jit(solution)/shard_map/ppermute | solution.py:287
  102.2 6.3 %collective-permute-start.58 = (bf16[64,128]{1,0:T(8,128)(2,1)S(1)}, bf16[64,128]{1,0:T(8,128)(2,1)S(1)}, u32[]{:S(2)}, u32[]{:S(2)}) collective-permute-start(bf16[64,128]{1,0:T(8,128)(2,1)S(1)} %get-tuple-element.141), channel_id=1, source_target_pairs={{0,14},{1,15},{2,12},{3,13},{4,10},{5,11},{6,8},{7,9},{8,6},{9,7},... | collective-permute-start | bytes 49160 | tf_op jit(solution)/shard_map/ppermute | solution.py:287
  105.2 5.9 %collective-permute-start.59 = (bf16[64,128]{1,0:T(8,128)(2,1)S(1)}, bf16[64,128]{1,0:T(8,128)(2,1)S(1)}, u32[]{:S(2)}, u32[]{:S(2)}) collective-permute-start(bf16[64,128]{1,0:T(8,128)(2,1)S(1)} %get-tuple-element.142), channel_id=1, source_target_pairs={{0,15},{1,14},{2,13},{3,12},{4,11},{5,10},{6,9},{7,8},{8,7},{9,6},... | collective-permute-start | bytes 49160 | tf_op jit(solution)/shard_map/ppermute | solution.py:287
  108.2 2.9 %copy-start.4 = (bf16[128,1024]{1,0:T(8,128)(2,1)S(1)}, bf16[128,1024]{1,0:T(8,128)(2,1)}, u32[]{:S(2)}) copy-start(bf16[128,1024]{1,0:T(8,128)(2,1)} %refs_5_.3) | copy-start | bytes 786436
  108.2 2.9 %copy-start.7 = (bf16[512,128]{1,0:T(8,128)(2,1)S(1)}, bf16[512,128]{1,0:T(8,128)(2,1)}, u32[]{:S(2)}) copy-start(bf16[512,128]{1,0:T(8,128)(2,1)} %refs_6_.3) | copy-start | bytes 393220
  (9 other events, 13.2 us)

commit v4 on v2

v4 whole, which is shorter than its diff:
```python
import functools

import jax
import jax.numpy as jnp
from jax import lax
from jax.experimental import pallas as pl
from jax.experimental.pallas import tpu as pltpu
from jax.sharding import PartitionSpec as P

AXES = ("row", "col")
LANES = 128
VMEM_BYTES = 48 * 1024 * 1024
FULL_VMEM_BYTES = 60 * 1024 * 1024
F32, BF16 = jnp.float32, jnp.bfloat16


def dot(left, right, contract=(1, 0)):
    return lax.dot_general(
        left, right, (((contract[0],), (contract[1],)), ((), ())), preferred_element_type=F32
    )


def sigmoid(values):
    return 0.5 * jnp.tanh(0.5 * values) + 0.5


def channel_norm(values, gain):
    wide = jnp.concatenate([gain] * (values.shape[1] // LANES), axis=1)
    centred = values - jnp.mean(values, axis=0, keepdims=True)
    spread = jnp.mean(centred * centred, axis=0, keepdims=True)
    return (centred * lax.rsqrt(spread + 1e-05) * wide).astype(BF16)


def spread_gain(row):
    return jnp.broadcast_to(row, (LANES, row.shape[1])).T


def token_mask(mask, lines):
    height, breadth = mask.shape
    wide = jnp.concatenate([mask.astype(F32)] * (LANES // breadth), axis=1)
    row = lax.broadcasted_iota(jnp.int32, wide.shape, 0)
    lane = lax.broadcasted_iota(jnp.int32, wide.shape, 1)
    wide = jnp.where(row // lines == lane // breadth, wide, 0.0).astype(BF16)
    line = lax.broadcasted_iota(jnp.int32, (lines, height), 0)
    source = lax.broadcasted_iota(jnp.int32, (lines, height), 1)
    return dot((source % lines == line).astype(BF16), wide)


def emit_message(normed, weight_t, mask, line, message_ref, stage_ref, share):
    projected = dot(weight_t, normed)
    hid = weight_t.shape[0] // 4
    owners = hid // share
    for part in range(normed.shape[1] // LANES):
        here = projected[:, part * LANES : (part + 1) * LANES]
        at = line + part
        keep = mask[at : at + 1]
        left = sigmoid(here[:hid]) * here[hid : 2 * hid] * keep
        right = sigmoid(here[2 * hid : 3 * hid]) * here[3 * hid :] * keep
        if share % 8 == 0:
            for owner in range(owners):
                rows = slice(owner * share, (owner + 1) * share)
                both = jnp.concatenate([left[rows], right[rows]], axis=0).astype(BF16)
                message_ref[owner, 2 * share * at : 2 * share * (at + 1), :] = both
        else:
            lines = message_ref.shape[1] // 2
            stage_ref[pl.ds(2 * at, owners, stride=2 * lines), :] = left
            stage_ref[pl.ds(2 * at + 1, owners, stride=2 * lines), :] = right
    if share % 8 and line + normed.shape[1] // LANES == mask.shape[0]:
        message_ref[...] = stage_ref[...].astype(BF16).reshape(message_ref.shape)


def project_kernel(share, chunk, ins, outs, stage_ref, x_ref, mask_ref, gain_ref, weight_ref, sems):
    message_ref, normed_ref, turned_ref, lines_ref = outs
    x_in, mask_in, gain_in, weight_in = ins
    pairs = [(gain_in, gain_ref), (mask_in, mask_ref), (weight_in.at[0], weight_ref), (x_in, x_ref)]
    copies = [pltpu.make_async_copy(src, dst, sems.at[n]) for n, (src, dst) in enumerate(pairs)]
    for copy in copies:
        copy.start()
    height, breadth, channels = x_ref.shape
    tokens = height * breadth
    lines = tokens // LANES
    copies[0].wait()
    copies[1].wait()
    mask = token_mask(mask_ref[...], lines)
    lines_ref[...] = mask
    gain = spread_gain(gain_ref[0:1, :])
    copies[2].wait()
    weight_t = weight_ref[...].T
    copies[3].wait()
    for start in range(0, tokens, chunk):
        first = start // LANES
        held = [
            x_ref[slot * lines + line]
            for line in range(first, first + chunk // LANES)
            for slot in range(LANES // breadth)
        ]
        current = jnp.concatenate(held, axis=0).T
        turned_ref[:, start : start + chunk] = current
        normed = channel_norm(current, gain)
        normed_ref[:, start : start + chunk] = normed
        emit_message(normed, weight_t, mask, first, message_ref, stage_ref, share)


def prepare_kernel(ins, outs):
    normed_ref, gate_ref, proj_ref, out_ref, up_ref, down_ref, gain_in_ref, gain_out_ref, trans_gain_ref = ins
    gate_out, proj_out, out_out, up_out, down_out, gains_out = outs
    gate_out[...] = sigmoid(dot(gate_ref[...].T, normed_ref[...]))
    proj_out[...] = proj_ref[...].T
    for update in range(2):
        out_out[update] = out_ref[update].T
    up_out[...] = up_ref[...].T
    down_out[...] = down_ref[...].T
    rows = [gain_out_ref[0:1, :], gain_in_ref[1:2, :], gain_out_ref[1:2, :], trans_gain_ref[...]]
    for n, row in enumerate(rows):
        gains_out[n] = spread_gain(row)


def gate_kernel(ins, outs):
    normed_ref, weight_ref = ins
    outs[0][...] = sigmoid(dot(weight_ref[...].T, normed_ref[...]))


def swap_slots(parts, breadth):
    parts = list(parts)
    slot = lax.broadcasted_iota(jnp.int32, parts[0].shape, 1) // breadth
    step = 1
    while step < len(parts):
        low = (slot // step) % 2 == 0
        for first in range(len(parts)):
            if first & step:
                continue
            a, b = parts[first], parts[first | step]
            parts[first] = jnp.where(low, a, pltpu.roll(b, step * breadth, 1))
            parts[first | step] = jnp.where(low, pltpu.roll(a, LANES - step * breadth, 1), b)
        step *= 2
    return parts


def combine_kernel(rows, cols, breadth, share, outgoing, ins, outs, stage_ref, result_ref):
    (both_ref,), (combined_ref,) = ins, outs
    slots = LANES // breadth
    span = both_ref.shape[1]
    lines = span // (2 * share)
    stage_ref[...] = both_ref[...].astype(F32).reshape(stage_ref.shape)

    def whole(side, channel):
        columns = []
        for high in range(cols // slots):
            parts = []
            for low in range(slots):
                base = (high * slots + low) * span + side * share + channel
                held = [
                    stage_ref[pl.ds(row * cols * span + base, lines, stride=2 * share), :] for row in range(rows)
                ]
                parts.append(jnp.concatenate(held, axis=0))
            parts = swap_slots(parts, breadth)
            columns.append(
                jnp.concatenate(
                    [part[row * lines : (row + 1) * lines] for row in range(rows) for part in parts], axis=0
                )
            )
        return jnp.concatenate(columns, axis=1).astype(BF16)

    for channel in range(share):
        left, right = whole(0, channel), whole(1, channel)
        combined = dot(left, right, (1, 1) if outgoing else (0, 0))
        for high in range(cols // slots):
            lanes = slice(high * LANES, (high + 1) * LANES)
            parts = [
                jnp.concatenate(
                    [
                        combined[(row * slots + slot) * lines : (row * slots + slot + 1) * lines, lanes]
                        for row in range(rows)
                    ],
                    axis=0,
                )
                for slot in range(slots)
            ]
            for low, part in enumerate(swap_slots(parts, breadth)):
                for row in range(rows):
                    base = (row * cols + high * slots + low) * lines * share + channel
                    result_ref[pl.ds(base, lines, stride=share), :] = part[row * lines : (row + 1) * lines]
    combined_ref[...] = result_ref[...].astype(BF16).reshape(combined_ref.shape)


def read_combined(stage_ref, owners, lines, share, first, count):
    columns = []
    for line in range(first, first + count):
        if share % 8 == 0:
            held = [
                stage_ref[(owner * lines + line) * share : (owner * lines + line + 1) * share, :]
                for owner in range(owners)
            ]
            columns.append(jnp.concatenate(held, axis=0))
        else:
            columns.append(stage_ref[pl.ds(line, owners, stride=lines), :])
    return jnp.concatenate(columns, axis=1)


def middle_kernel(share, chunk, ins, outs, stage_ref, message_stage_ref):
    combined_ref, x_ref, gate_ref, gains_ref, out_ref, mask_ref, weight_ref = ins
    message_ref, normed_ref, next_ref = outs
    tokens = x_ref.shape[1]
    lines = tokens // LANES
    owners = combined_ref.shape[0]
    stage_ref[...] = combined_ref[...].astype(F32).reshape(stage_ref.shape)
    mask = mask_ref[...]
    for start in range(0, tokens, chunk):
        here = slice(start, start + chunk)
        combined = read_combined(stage_ref, owners, lines, share, start // LANES, chunk // LANES)
        hidden = channel_norm(combined, gains_ref[0])
        current = x_ref[:, here] + gate_ref[:, here] * dot(out_ref[0], hidden)
        next_ref[:, here] = current
        normed = channel_norm(current, gains_ref[1])
        normed_ref[:, here] = normed
        emit_message(normed, weight_ref[...], mask, start // LANES, message_ref, message_stage_ref, share)


def last_kernel(share, chunk, ins, outs, stage_ref):
    combined_ref, x_ref, gate_ref, gains_ref, out_ref, up_ref, down_ref = ins
    (result_ref,) = outs
    height, breadth, channels = result_ref.shape
    tokens = x_ref.shape[1]
    lines = tokens // LANES
    owners = combined_ref.shape[0]
    half = down_ref.shape[1]
    stage_ref[...] = combined_ref[...].astype(F32).reshape(stage_ref.shape)
    for start in range(0, tokens, chunk):
        here = slice(start, start + chunk)
        combined = read_combined(stage_ref, owners, lines, share, start // LANES, chunk // LANES)
        hidden = channel_norm(combined, gains_ref[2])
        current = x_ref[:, here] + gate_ref[:, here] * dot(out_ref[1], hidden)
        up_part = dot(up_ref[...], channel_norm(current, gains_ref[3]))
        first = up_part[:half]
        trans_hidden = (first * sigmoid(first) * up_part[half:]).astype(BF16)
        result = (current + dot(down_ref[...], trans_hidden)).T
        for part in range(chunk // LANES):
            for slot in range(LANES // breadth):
                base = part * LANES + slot * breadth
                result_ref[slot * lines + start // LANES + part] = result[base : base + breadth]


def whole_spec(array):
    return pl.BlockSpec(array.shape, lambda step, dims=array.ndim: (0,) * dims)


def picked_spec(array, index):
    return pl.BlockSpec((None,) + array.shape[1:], lambda step: (index,) + (0,) * (array.ndim - 1))


def call(kernel, operands, picks, outs, scratch=(), in_place=False):
    limit = FULL_VMEM_BYTES if in_place else VMEM_BYTES
    specs = [
        picked_spec(array, picks[n]) if n in picks else whole_spec(array) for n, array in enumerate(operands)
    ]
    if in_place:
        specs = [pl.BlockSpec(memory_space=pltpu.HBM)] * len(operands)
    shapes = [jax.ShapeDtypeStruct(shape, dtype) for shape, dtype in outs]
    count = len(operands)

    def body(*refs):
        kernel(refs[:count], refs[count : count + len(outs)], *refs[count + len(outs) :])

    return pl.pallas_call(
        body,
        grid=(1,),
        in_specs=specs,
        out_specs=[whole_spec(shape) for shape in shapes],
        out_shape=shapes,
        scratch_shapes=list(scratch),
        compiler_params=pltpu.CompilerParams(vmem_limit_bytes=limit),
    )(*operands)


def exchange(values):
    return lax.all_to_all(values, AXES, split_axis=0, concat_axis=0, tiled=True)


def per_device(
    rows,
    cols,
    pair_map,
    pair_mask,
    gain_in,
    proj_weight,
    gate_weight,
    gain_out,
    out_weight,
    trans_gain,
    trans_up,
    trans_down,
):
    height, breadth, channels = pair_map.shape
    tokens = height * breadth
    lines = tokens // LANES
    hid = gain_out.shape[1]
    owners = rows * cols
    share = hid // owners
    chunk = min(2 * LANES, tokens)
    message = ((owners, 2 * share * lines, LANES), BF16)
    answer = ((owners, share * lines, LANES), BF16)
    staged = pltpu.VMEM((owners * 2 * share * lines, LANES), F32)
    result = pltpu.VMEM((owners * share * lines, LANES), F32)
    spare = pltpu.VMEM((8, LANES), F32) if share % 8 == 0 else staged
    narrow, wide = ((channels, tokens), BF16), ((channels, tokens), F32)

    def combine(both, outgoing):
        kernel = functools.partial(combine_kernel, rows, cols, breadth, share, outgoing)
        (combined,) = call(kernel, (both,), {}, [answer], (staged, result))
        return combined

    both, normed, current, mask = call(
        functools.partial(project_kernel, share, chunk),
        (pair_map, pair_mask, gain_in, proj_weight),
        {},
        [message, narrow, wide, ((lines, LANES), F32)],
        (
            spare,
            pltpu.VMEM(pair_map.shape, F32),
            pltpu.VMEM(pair_mask.shape, jnp.int32),
            pltpu.VMEM(gain_in.shape, F32),
            pltpu.VMEM(proj_weight.shape[1:], BF16),
            pltpu.SemaphoreType.DMA((4,)),
        ),
        in_place=True,
    )
    gate, proj_t, out_t, up_t, down_t, gains = call(
        prepare_kernel,
        (
            normed,
            gate_weight,
            proj_weight,
            out_weight,
            trans_up,
            trans_down,
            gain_in,
            gain_out,
            trans_gain.reshape(1, -1),
        ),
        {1: 0, 2: 1},
        [
            wide,
            (proj_weight.shape[:0:-1], BF16),
            ((2, out_weight.shape[2], hid), BF16),
            (trans_up.shape[::-1], BF16),
            (trans_down.shape[::-1], BF16),
            ((4, channels, LANES), F32),
        ],
    )
    combined = exchange(combine(exchange(both), True))
    both, normed, current = call(
        functools.partial(middle_kernel, share, chunk),
        (combined, current, gate, gains, out_t, mask, proj_t),
        {},
        [message, narrow, wide],
        (result, spare),
    )
    (gate,) = call(gate_kernel, (normed, gate_weight), {1: 1}, [wide])
    combined = exchange(combine(exchange(both), False))
    (pair_out,) = call(
        functools.partial(last_kernel, share, chunk),
        (combined, current, gate, gains, out_t, up_t, down_t),
        {},
        [(pair_map.shape, F32)],
        (result,),
    )
    return pair_out


def solution(mesh):
    rows, cols = mesh.shape["row"], mesh.shape["col"]
    spread = P(("grp", "row"), "col", None)
    in_specs = (spread, P(("grp", "row"), "col")) + (P(),) * 8

    def body(*args):
        return per_device(rows, cols, *args)

    return jax.shard_map(body, mesh=mesh, in_specs=in_specs, out_specs=spread, check_vma=False)
```

time: 84.4 us -> 82.3 us (0.975)
  local copies, waits for them, and re-layouts: 4.74 us -> 1.3 us
  Pallas kernels: 10.6 us -> 12.5 us
    unnamed x26 -> x22, local copies, waits for them, and re-layouts: 4.74 us -> 1.3 us
    pallas_call x7, Pallas kernels: 10.6 us -> 12.5 us  [call(): pl.pallas_call(body, grid=(1,), in_specs=specs, out_specs=[whole_spec(sha...]
where the time goes in v4:
time: 82.3 us; the launch traced here: 81.8 us
  blocking collectives  41.9 us (51%)
  waiting for transfers between devices  18.7 us (23%)
  Pallas kernels  12.5 us (15%)
  starting transfers between devices  7.2 us (9%)
  local copies, waits for them, and re-layouts  1.3 us (2%)
    all_to_all x2, blocking collectives, exchange(): return lax.all_to_all(values, AXES, split_axis=0, concat_axis=0, tiled=True)  41.9 us
    all_to_all x2, waiting for transfers between devices, exchange(): return lax.all_to_all(values, AXES, split_axis=0, concat_axis=0, tiled=True)  18.7 us
    pallas_call x7, Pallas kernels, call(): pl.pallas_call(body, grid=(1,), in_specs=specs, out_specs=[whole_spec(sha...  12.5 us
    all_to_all x2, starting transfers between devices, exchange(): return lax.all_to_all(values, AXES, split_axis=0, concat_axis=0, tiled=True)  7.2 us
  transfers between devices with their start and end apart: 2, of which 2 were waited for; matrix products, arithmetic and copies ran while one was open for 0% of the time, Pallas kernels for 1%

profile of v4, /device:TPU:0, one launch (start us, length us, event | category | flops | bytes accessed | tf_op | source)
XLA Modules:
  0.0 81.8 jit_solution(757038801796964748)
XLA Ops:
  0.0 2.6 %shard_map.100 = (bf16[16,128,128]{2,1,0:T(8,128)(2,1)}, bf16[128,1024]{1,0:T(8,128)(2,1)}, f32[128,1024]{1,0:T(8,128)}, f32[8,128]{1,0:T(8,128)}) custom-call(f32[32,32,128]{2,1,0:T(8,128)} %refs_0_.1, s32[32,32]{1,0:T(8,128)} %refs_1_.3, f32[2,128]{1,0:T(2,128)} %refs_6_.1, bf16[2,128,512]{2,1,0:T(8,128)(2,1)} %refs_2_.3), custom_call_target="tpu_custom_call" | custom-call | tf_op jit(solution)/shard_map/pallas_call | solution.py:264
  2.6 23.1 %all_to_all.20.refs_0_ = bf16[16,128,128]{2,1,0:T(8,128)(2,1)S(1)} all-to-all(bf16[16,128,128]{2,1,0:T(8,128)(2,1)} %get-tuple-element.18), channel_id=1, replica_groups=mesh['grp'=2,'row'=4,'col'=4] {'row','col'}, dimensions={0} | all-to-all | bytes 1048576 | tf_op jit(solution)/shard_map/all_to_all | solution.py:276
  25.7 0.0 copy-start.3
  25.7 0.0 copy-start.4
  25.7 0.0 copy-start.5
  25.7 0.0 copy-start.6
  25.7 2.1 %shard_map.101 = bf16[16,64,128]{2,1,0:T(8,128)(2,1)} custom-call(bf16[16,128,128]{2,1,0:T(8,128)(2,1)S(1)} %all_to_all.20.refs_0_), custom_call_target="tpu_custom_call" | custom-call | tf_op jit(solution)/shard_map/pallas_call | solution.py:264
  27.8 0.0 copy-start
  27.8 0.0 copy-start.2
  27.8 0.0 copy-start.9
  27.8 3.7 %all-to-all-start.1 = ((bf16[16,64,128]{2,1,0:T(8,128)(2,1)}), bf16[16,64,128]{2,1,0:T(8,128)(2,1)S(1)}, u32[]{:S(2)}, u32[]{:S(2)}) async-start(bf16[16,64,128]{2,1,0:T(8,128)(2,1)} %shard_map.101), calls=%async_computation.1 | async-start | bytes 524288 | tf_op jit(solution)/shard_map/all_to_all | solution.py:276
  31.5 0.0 copy-start.8
  31.5 0.0 copy-start.10
  31.5 0.0 copy-done.3
  31.5 0.0 copy-done.4
  31.5 0.0 copy-done.5
  31.6 0.0 copy-done.6
  31.6 0.0 copy-done
  31.6 0.0 copy-done.2
  31.6 0.0 copy-done.9
  31.6 0.6 copy-done.8
  32.2 0.0 copy-done.10
  32.2 0.0 copy-start.1
  32.2 0.3 shard_map.102
  32.5 9.0 %all-to-all-done.1.refs_0_ = bf16[16,64,128]{2,1,0:T(8,128)(2,1)S(1)} async-done(((bf16[16,64,128]{2,1,0:T(8,128)(2,1)}), bf16[16,64,128]{2,1,0:T(8,128)(2,1)S(1)}, u32[]{:S(2)}, u32[]{:S(2)}) %all-to-all-start.1) | async-done | bytes 262176 | tf_op jit(solution)/shard_map/all_to_all | solution.py:276
  41.5 0.0 copy-start.7
  41.5 0.0 copy-done.1
  41.5 0.7 copy-done.7
  42.2 1.0 %shard_map.103 = (bf16[16,128,128]{2,1,0:T(8,128)(2,1)S(1)}, bf16[128,1024]{1,0:T(8,128)(2,1)S(1)}, f32[128,1024]{1,0:T(8,128)S(1)}) custom-call(bf16[16,64,128]{2,1,0:T(8,128)(2,1)S(1)} %all-to-all-done.1.refs_0_, f32[128,1024]{1,0:T(8,128)S(1)} %copy-done.1, f32[128,1024]{1,0:T(8,128)S(1)} %get-tuple-element.21.refs_2_, ...), custom_call_target="tpu_custom_call" | custom-call | tf_op jit(solution)/shard_map/pallas_call | solution.py:264
  43.2 18.8 %all_to_all.21.refs_0_ = bf16[16,128,128]{2,1,0:T(8,128)(2,1)S(1)} all-to-all(bf16[16,128,128]{2,1,0:T(8,128)(2,1)S(1)} %get-tuple-element.26), channel_id=1, replica_groups=mesh['grp'=2,'row'=4,'col'=4] {'row','col'}, dimensions={0} | all-to-all | bytes 1048576 | tf_op jit(solution)/shard_map/all_to_all | solution.py:276
  62.0 2.6 %shard_map.104 = bf16[16,64,128]{2,1,0:T(8,128)(2,1)} custom-call(bf16[16,128,128]{2,1,0:T(8,128)(2,1)S(1)} %all_to_all.21.refs_0_), custom_call_target="tpu_custom_call" | custom-call | tf_op jit(solution)/shard_map/pallas_call | solution.py:264
  64.6 3.5 %all-to-all-start.3 = ((bf16[16,64,128]{2,1,0:T(8,128)(2,1)}), bf16[16,64,128]{2,1,0:T(8,128)(2,1)S(1)}, u32[]{:S(2)}, u32[]{:S(2)}) async-start(bf16[16,64,128]{2,1,0:T(8,128)(2,1)} %shard_map.104), calls=%async_computation.3 | async-start | bytes 524288 | tf_op jit(solution)/shard_map/all_to_all | solution.py:276
  68.1 0.3 shard_map.105.refs_2_
  68.4 9.8 %all-to-all-done.3.refs_0_ = bf16[16,64,128]{2,1,0:T(8,128)(2,1)S(1)} async-done(((bf16[16,64,128]{2,1,0:T(8,128)(2,1)}), bf16[16,64,128]{2,1,0:T(8,128)(2,1)S(1)}, u32[]{:S(2)}, u32[]{:S(2)}) %all-to-all-start.3) | async-done | bytes 262176 | tf_op jit(solution)/shard_map/all_to_all | solution.py:276
  78.2 3.6 %shard_map.106 = f32[32,32,128]{2,1,0:T(8,128)} custom-call(bf16[16,64,128]{2,1,0:T(8,128)(2,1)S(1)} %all-to-all-done.3.refs_0_, f32[128,1024]{1,0:T(8,128)S(1)} %get-tuple-element.27.refs_1_, f32[128,1024]{1,0:T(8,128)S(1)} %shard_map.105.refs_2_, f32[4,128,128]{2,1,0:T(8,128)S(1)} %get-tuple-element.22.refs_3_, ...), custom_call_target="tpu_custom_call" | custom-call | tf_op jit(solution)/shard_map/pallas_call | solution.py:264
Async XLA Ops:
  25.7 5.9 %copy-start.3 = (bf16[128,1024]{1,0:T(8,128)(2,1)S(1)}, bf16[128,1024]{1,0:T(8,128)(2,1)}, u32[]{:S(2)}) copy-start(bf16[128,1024]{1,0:T(8,128)(2,1)} %get-tuple-element.20.refs_0_) | copy-start | bytes 786436
  25.7 5.9 %copy-start.4 = (bf16[2,128,128]{2,1,0:T(8,128)(2,1)S(1)}, bf16[2,128,128]{2,1,0:T(8,128)(2,1)}, u32[]{:S(2)}) copy-start(bf16[2,128,128]{2,1,0:T(8,128)(2,1)} %refs_1_.5) | copy-start | bytes 196612
  25.7 5.9 %copy-start.5 = (bf16[512,128]{1,0:T(8,128)(2,1)S(1)}, bf16[512,128]{1,0:T(8,128)(2,1)}, u32[]{:S(2)}) copy-start(bf16[512,128]{1,0:T(8,128)(2,1)} %refs_5_.1) | copy-start | bytes 393220
  25.7 5.9 %copy-start.6 = (bf16[2,128,128]{2,1,0:T(8,128)(2,1)S(1)}, bf16[2,128,128]{2,1,0:T(8,128)(2,1)}, u32[]{:S(2)}) copy-start(bf16[2,128,128]{2,1,0:T(8,128)(2,1)} %refs_3_.3) | copy-start | bytes 196612
  27.8 3.7 %copy-start = (bf16[2,128,512]{2,1,0:T(8,128)(2,1)S(1)}, bf16[2,128,512]{2,1,0:T(8,128)(2,1)}, u32[]{:S(2)}) copy-start(bf16[2,128,512]{2,1,0:T(8,128)(2,1)} %refs_2_.3) | copy-start | bytes 786436
  27.8 3.8 %copy-start.2 = (bf16[128,1024]{1,0:T(8,128)(2,1)S(1)}, bf16[128,1024]{1,0:T(8,128)(2,1)}, u32[]{:S(2)}) copy-start(bf16[128,1024]{1,0:T(8,128)(2,1)} %refs_4_.1) | copy-start | bytes 786436
  27.8 3.8 %copy-start.9 = (f32[2,128]{1,0:T(2,128)S(1)}, f32[2,128]{1,0:T(2,128)}, u32[]{:S(2)}) copy-start(f32[2,128]{1,0:T(2,128)} %refs_7_.1) | copy-start | bytes 3076
  27.8 13.7 %all-to-all-start.1 = ((bf16[16,64,128]{2,1,0:T(8,128)(2,1)}), bf16[16,64,128]{2,1,0:T(8,128)(2,1)S(1)}, u32[]{:S(2)}, u32[]{:S(2)}) async-start(bf16[16,64,128]{2,1,0:T(8,128)(2,1)} %shard_map.101), calls=%async_computation.1 | async-start | bytes 524288 | tf_op jit(solution)/shard_map/all_to_all | solution.py:276
  31.5 0.7 copy-start.8
  31.5 0.7 copy-start.10
  32.2 9.3 %copy-start.1 = (f32[128,1024]{1,0:T(8,128)S(1)}, f32[128,1024]{1,0:T(8,128)}, u32[]{:S(2)}) copy-start(f32[128,1024]{1,0:T(8,128)} %get-tuple-element.19.refs_1_) | copy-start | bytes 1572868
  41.5 0.7 copy-start.7
  64.6 13.6 %all-to-all-start.3 = ((bf16[16,64,128]{2,1,0:T(8,128)(2,1)}), bf16[16,64,128]{2,1,0:T(8,128)(2,1)S(1)}, u32[]{:S(2)}, u32[]{:S(2)}) async-start(bf16[16,64,128]{2,1,0:T(8,128)(2,1)} %shard_map.104), calls=%async_computation.3 | async-start | bytes 524288 | tf_op jit(solution)/shard_map/all_to_all | solution.py:276

commit v5 on v4

--- a/solution.py
+++ b/solution.py
@@ -7,7 +7,7 @@
 from jax.experimental.pallas import tpu as pltpu
 from jax.sharding import PartitionSpec as P
 
-AXES = ("row", "col")
+AXES = ("col", "row")
 LANES = 128
 VMEM_BYTES = 48 * 1024 * 1024
 FULL_VMEM_BYTES = 60 * 1024 * 1024
@@ -148,9 +148,9 @@
         for high in range(cols // slots):
             parts = []
             for low in range(slots):
-                base = (high * slots + low) * span + side * share + channel
+                base = (high * slots + low) * rows * span + side * share + channel
                 held = [
-                    stage_ref[pl.ds(row * cols * span + base, lines, stride=2 * share), :] for row in range(rows)
+                    stage_ref[pl.ds(row * span + base, lines, stride=2 * share), :] for row in range(rows)
                 ]
                 parts.append(jnp.concatenate(held, axis=0))
             parts = swap_slots(parts, breadth)
@@ -178,7 +178,7 @@
             ]
             for low, part in enumerate(swap_slots(parts, breadth)):
                 for row in range(rows):
-                    base = (row * cols + high * slots + low) * lines * share + channel
+                    base = ((high * slots + low) * rows + row) * lines * share + channel
                     result_ref[pl.ds(base, lines, stride=share), :] = part[row * lines : (row + 1) * lines]
     combined_ref[...] = result_ref[...].astype(BF16).reshape(combined_ref.shape)
 

time: 82.3 us -> 80.7 us (0.981)
  blocking collectives: 41.9 us -> 39.1 us
  starting transfers between devices: 7.2 us -> 8.33 us
    all_to_all x2, blocking collectives: 41.9 us -> 39.1 us  [exchange(): return lax.all_to_all(values, AXES, split_axis=0, concat_axis=0, tiled=True)]
    all_to_all x2, starting transfers between devices: 7.2 us -> 8.33 us  [exchange(): return lax.all_to_all(values, AXES, split_axis=0, concat_axis=0, tiled=True)]
where the time goes in v5:
time: 80.7 us; the launch traced here: 80.1 us
  blocking collectives  39.1 us (48%)
  waiting for transfers between devices  18.8 us (23%)
  Pallas kernels  12.5 us (15%)
  starting transfers between devices  8.33 us (10%)
  local copies, waits for them, and re-layouts  1.3 us (2%)
    all_to_all x2, blocking collectives, exchange(): return lax.all_to_all(values, AXES, split_axis=0, concat_axis=0, tiled=True)  39.1 us
    all_to_all x2, waiting for transfers between devices, exchange(): return lax.all_to_all(values, AXES, split_axis=0, concat_axis=0, tiled=True)  18.8 us
    pallas_call x7, Pallas kernels, call(): pl.pallas_call(body, grid=(1,), in_specs=specs, out_specs=[whole_spec(sha...  12.5 us
    all_to_all x2, starting transfers between devices, exchange(): return lax.all_to_all(values, AXES, split_axis=0, concat_axis=0, tiled=True)  8.33 us
  transfers between devices with their start and end apart: 2, of which 2 were waited for; matrix products, arithmetic and copies ran while one was open for 0% of the time, Pallas kernels for 1%

profile of v5, /device:TPU:0, one launch (start us, length us, event | category | flops | bytes accessed | tf_op | source)
XLA Modules:
  0.0 80.1 jit_solution(13637025486869414310)
XLA Ops:
  0.0 2.6 %shard_map.100 = (bf16[16,128,128]{2,1,0:T(8,128)(2,1)}, bf16[128,1024]{1,0:T(8,128)(2,1)}, f32[128,1024]{1,0:T(8,128)}, f32[8,128]{1,0:T(8,128)}) custom-call(f32[32,32,128]{2,1,0:T(8,128)} %refs_0_.1, s32[32,32]{1,0:T(8,128)} %refs_1_.3, f32[2,128]{1,0:T(2,128)} %refs_6_.1, bf16[2,128,512]{2,1,0:T(8,128)(2,1)} %refs_2_.3), custom_call_target="tpu_custom_call" | custom-call | tf_op jit(solution)/shard_map/pallas_call | solution.py:264
  2.6 21.8 %all_to_all.20.refs_0_ = bf16[16,128,128]{2,1,0:T(8,128)(2,1)S(1)} all-to-all(bf16[16,128,128]{2,1,0:T(8,128)(2,1)} %get-tuple-element.18), channel_id=1, replica_groups=mesh['grp'=2,'row'=4,'col'=4] {'col','row'}, dimensions={0} | all-to-all | bytes 1048576 | tf_op jit(solution)/shard_map/all_to_all | solution.py:276
  24.4 0.0 copy-start.3
  24.4 0.0 copy-start.4
  24.4 0.0 copy-start.5
  24.5 0.0 copy-start.6
  24.5 2.1 %shard_map.101 = bf16[16,64,128]{2,1,0:T(8,128)(2,1)} custom-call(bf16[16,128,128]{2,1,0:T(8,128)(2,1)S(1)} %all_to_all.20.refs_0_), custom_call_target="tpu_custom_call" | custom-call | tf_op jit(solution)/shard_map/pallas_call | solution.py:264
  26.6 0.0 copy-start
  26.6 0.0 copy-start.2
  26.6 0.0 copy-start.9
  26.6 4.2 %all-to-all-start.1 = ((bf16[16,64,128]{2,1,0:T(8,128)(2,1)}), bf16[16,64,128]{2,1,0:T(8,128)(2,1)S(1)}, u32[]{:S(2)}, u32[]{:S(2)}) async-start(bf16[16,64,128]{2,1,0:T(8,128)(2,1)} %shard_map.101), calls=%async_computation.1 | async-start | bytes 524288 | tf_op jit(solution)/shard_map/all_to_all | solution.py:276
  30.8 0.0 copy-start.8
  30.9 0.0 copy-start.10
  30.9 0.0 copy-done.3
  30.9 0.0 copy-done.4
  30.9 0.0 copy-done.5
  30.9 0.0 copy-done.6
  30.9 0.0 copy-done
  30.9 0.0 copy-done.2
  30.9 0.0 copy-done.9
  30.9 0.6 copy-done.8
  31.5 0.0 copy-done.10
  31.5 0.0 copy-start.1
  31.5 0.3 shard_map.102
  31.9 9.0 %all-to-all-done.1.refs_0_ = bf16[16,64,128]{2,1,0:T(8,128)(2,1)S(1)} async-done(((bf16[16,64,128]{2,1,0:T(8,128)(2,1)}), bf16[16,64,128]{2,1,0:T(8,128)(2,1)S(1)}, u32[]{:S(2)}, u32[]{:S(2)}) %all-to-all-start.1) | async-done | bytes 262176 | tf_op jit(solution)/shard_map/all_to_all | solution.py:276
  40.9 0.0 copy-start.7
  40.9 0.0 copy-done.1
  40.9 0.7 copy-done.7
  41.6 1.0 %shard_map.103 = (bf16[16,128,128]{2,1,0:T(8,128)(2,1)S(1)}, bf16[128,1024]{1,0:T(8,128)(2,1)S(1)}, f32[128,1024]{1,0:T(8,128)S(1)}) custom-call(bf16[16,64,128]{2,1,0:T(8,128)(2,1)S(1)} %all-to-all-done.1.refs_0_, f32[128,1024]{1,0:T(8,128)S(1)} %copy-done.1, f32[128,1024]{1,0:T(8,128)S(1)} %get-tuple-element.21.refs_2_, ...), custom_call_target="tpu_custom_call" | custom-call | tf_op jit(solution)/shard_map/pallas_call | solution.py:264
  42.6 17.2 %all_to_all.21.refs_0_ = bf16[16,128,128]{2,1,0:T(8,128)(2,1)S(1)} all-to-all(bf16[16,128,128]{2,1,0:T(8,128)(2,1)S(1)} %get-tuple-element.26), channel_id=1, replica_groups=mesh['grp'=2,'row'=4,'col'=4] {'col','row'}, dimensions={0} | all-to-all | bytes 1048576 | tf_op jit(solution)/shard_map/all_to_all | solution.py:276
  59.8 2.6 %shard_map.104 = bf16[16,64,128]{2,1,0:T(8,128)(2,1)} custom-call(bf16[16,128,128]{2,1,0:T(8,128)(2,1)S(1)} %all_to_all.21.refs_0_), custom_call_target="tpu_custom_call" | custom-call | tf_op jit(solution)/shard_map/pallas_call | solution.py:264
  62.4 4.1 %all-to-all-start.3 = ((bf16[16,64,128]{2,1,0:T(8,128)(2,1)}), bf16[16,64,128]{2,1,0:T(8,128)(2,1)S(1)}, u32[]{:S(2)}, u32[]{:S(2)}) async-start(bf16[16,64,128]{2,1,0:T(8,128)(2,1)} %shard_map.104), calls=%async_computation.3 | async-start | bytes 524288 | tf_op jit(solution)/shard_map/all_to_all | solution.py:276
  66.5 0.3 shard_map.105.refs_2_
  66.8 9.8 %all-to-all-done.3.refs_0_ = bf16[16,64,128]{2,1,0:T(8,128)(2,1)S(1)} async-done(((bf16[16,64,128]{2,1,0:T(8,128)(2,1)}), bf16[16,64,128]{2,1,0:T(8,128)(2,1)S(1)}, u32[]{:S(2)}, u32[]{:S(2)}) %all-to-all-start.3) | async-done | bytes 262176 | tf_op jit(solution)/shard_map/all_to_all | solution.py:276
  76.5 3.6 %shard_map.106 = f32[32,32,128]{2,1,0:T(8,128)} custom-call(bf16[16,64,128]{2,1,0:T(8,128)(2,1)S(1)} %all-to-all-done.3.refs_0_, f32[128,1024]{1,0:T(8,128)S(1)} %get-tuple-element.27.refs_1_, f32[128,1024]{1,0:T(8,128)S(1)} %shard_map.105.refs_2_, f32[4,128,128]{2,1,0:T(8,128)S(1)} %get-tuple-element.22.refs_3_, ...), custom_call_target="tpu_custom_call" | custom-call | tf_op jit(solution)/shard_map/pallas_call | solution.py:264
Async XLA Ops:
  24.4 6.4 %copy-start.3 = (bf16[128,1024]{1,0:T(8,128)(2,1)S(1)}, bf16[128,1024]{1,0:T(8,128)(2,1)}, u32[]{:S(2)}) copy-start(bf16[128,1024]{1,0:T(8,128)(2,1)} %get-tuple-element.20.refs_0_) | copy-start | bytes 786436
  24.4 6.4 %copy-start.4 = (bf16[2,128,128]{2,1,0:T(8,128)(2,1)S(1)}, bf16[2,128,128]{2,1,0:T(8,128)(2,1)}, u32[]{:S(2)}) copy-start(bf16[2,128,128]{2,1,0:T(8,128)(2,1)} %refs_1_.5) | copy-start | bytes 196612
  24.4 6.4 %copy-start.5 = (bf16[512,128]{1,0:T(8,128)(2,1)S(1)}, bf16[512,128]{1,0:T(8,128)(2,1)}, u32[]{:S(2)}) copy-start(bf16[512,128]{1,0:T(8,128)(2,1)} %refs_5_.1) | copy-start | bytes 393220
  24.5 6.4 %copy-start.6 = (bf16[2,128,128]{2,1,0:T(8,128)(2,1)S(1)}, bf16[2,128,128]{2,1,0:T(8,128)(2,1)}, u32[]{:S(2)}) copy-start(bf16[2,128,128]{2,1,0:T(8,128)(2,1)} %refs_3_.3) | copy-start | bytes 196612
  26.6 4.3 %copy-start = (bf16[2,128,512]{2,1,0:T(8,128)(2,1)S(1)}, bf16[2,128,512]{2,1,0:T(8,128)(2,1)}, u32[]{:S(2)}) copy-start(bf16[2,128,512]{2,1,0:T(8,128)(2,1)} %refs_2_.3) | copy-start | bytes 786436
  26.6 4.3 %copy-start.2 = (bf16[128,1024]{1,0:T(8,128)(2,1)S(1)}, bf16[128,1024]{1,0:T(8,128)(2,1)}, u32[]{:S(2)}) copy-start(bf16[128,1024]{1,0:T(8,128)(2,1)} %refs_4_.1) | copy-start | bytes 786436
  26.6 4.3 %copy-start.9 = (f32[2,128]{1,0:T(2,128)S(1)}, f32[2,128]{1,0:T(2,128)}, u32[]{:S(2)}) copy-start(f32[2,128]{1,0:T(2,128)} %refs_7_.1) | copy-start | bytes 3076
  26.6 14.3 %all-to-all-start.1 = ((bf16[16,64,128]{2,1,0:T(8,128)(2,1)}), bf16[16,64,128]{2,1,0:T(8,128)(2,1)S(1)}, u32[]{:S(2)}, u32[]{:S(2)}) async-start(bf16[16,64,128]{2,1,0:T(8,128)(2,1)} %shard_map.101), calls=%async_computation.1 | async-start | bytes 524288 | tf_op jit(solution)/shard_map/all_to_all | solution.py:276
  30.8 0.7 copy-start.8
  30.9 0.7 copy-start.10
  31.5 9.4 %copy-start.1 = (f32[128,1024]{1,0:T(8,128)S(1)}, f32[128,1024]{1,0:T(8,128)}, u32[]{:S(2)}) copy-start(f32[128,1024]{1,0:T(8,128)} %get-tuple-element.19.refs_1_) | copy-start | bytes 1572868
  40.9 0.7 copy-start.7
  62.4 14.2 %all-to-all-start.3 = ((bf16[16,64,128]{2,1,0:T(8,128)(2,1)}), bf16[16,64,128]{2,1,0:T(8,128)(2,1)S(1)}, u32[]{:S(2)}, u32[]{:S(2)}) async-start(bf16[16,64,128]{2,1,0:T(8,128)(2,1)} %shard_map.104), calls=%async_computation.3 | async-start | bytes 524288 | tf_op jit(solution)/shard_map/all_to_all | solution.py:276

commit v6 on v5

--- a/solution.py
+++ b/solution.py
@@ -69,42 +69,60 @@
         message_ref[...] = stage_ref[...].astype(BF16).reshape(message_ref.shape)
 
 
-def project_kernel(share, chunk, ins, outs, stage_ref, x_ref, mask_ref, gain_ref, weight_ref, sems):
-    message_ref, normed_ref, turned_ref, lines_ref = outs
-    x_in, mask_in, gain_in, weight_in = ins
-    pairs = [(gain_in, gain_ref), (mask_in, mask_ref), (weight_in.at[0], weight_ref), (x_in, x_ref)]
-    copies = [pltpu.make_async_copy(src, dst, sems.at[n]) for n, (src, dst) in enumerate(pairs)]
+def start_all(pairs, sems, first=0):
+    copies = [pltpu.make_async_copy(src, dst, sems.at[first + n]) for n, (src, dst) in enumerate(pairs)]
     for copy in copies:
         copy.start()
-    height, breadth, channels = x_ref.shape
-    tokens = height * breadth
-    lines = tokens // LANES
-    copies[0].wait()
-    copies[1].wait()
+    return copies
+
+
+def line_tokens(x_ref, line):
+    return jnp.concatenate([x_ref[slot, line] for slot in range(x_ref.shape[0])], axis=0)
+
+
+def project_kernel(
+    share, chunk, ins, outs, stage_ref, x_ref, mask_ref, gain_ref, weight_ref, held_ref, in_sems, out_sems
+):
+    (message_out,) = outs
+    x_in, mask_in, gain_in, weight_in = ins
+    slots, lines, breadth, channels = x_ref.shape
+    count = chunk // LANES
+    steps = lines // count
+    pieces = [slice(n * count, (n + 1) * count) for n in range(steps)]
+    small = start_all([(gain_in, gain_ref), (mask_in, mask_ref), (weight_in.at[0], weight_ref)], in_sems)
+    large = start_all([(x_in.at[:, piece], x_ref.at[:, piece]) for piece in pieces], in_sems, 3)
+    small[0].wait()
+    small[1].wait()
     mask = token_mask(mask_ref[...], lines)
-    lines_ref[...] = mask
     gain = spread_gain(gain_ref[0:1, :])
-    copies[2].wait()
+    small[2].wait()
     weight_t = weight_ref[...].T
-    copies[3].wait()
-    for start in range(0, tokens, chunk):
-        first = start // LANES
-        held = [
-            x_ref[slot * lines + line]
-            for line in range(first, first + chunk // LANES)
-            for slot in range(LANES // breadth)
-        ]
-        current = jnp.concatenate(held, axis=0).T
-        turned_ref[:, start : start + chunk] = current
-        normed = channel_norm(current, gain)
-        normed_ref[:, start : start + chunk] = normed
-        emit_message(normed, weight_t, mask, first, message_ref, stage_ref, share)
-
-
-def prepare_kernel(ins, outs):
-    normed_ref, gate_ref, proj_ref, out_ref, up_ref, down_ref, gain_in_ref, gain_out_ref, trans_gain_ref = ins
-    gate_out, proj_out, out_out, up_out, down_out, gains_out = outs
-    gate_out[...] = sigmoid(dot(gate_ref[...].T, normed_ref[...]))
+    writes = []
+    for n, piece in enumerate(pieces):
+        large[n].wait()
+        current = jnp.concatenate([line_tokens(x_ref, line) for line in range(piece.start, piece.stop)], axis=0).T
+        emit_message(channel_norm(current, gain), weight_t, mask, piece.start, held_ref, stage_ref, share)
+        if share % 8 == 0:
+            rows = slice(2 * share * piece.start, 2 * share * piece.stop)
+            writes += start_all([(held_ref.at[:, rows], message_out.at[:, rows])], out_sems, n)
+        elif n == steps - 1:
+            writes += start_all([(held_ref, message_out)], out_sems)
+    for write in writes:
+        write.wait()
+
+
+def prepare(ins, outs):
+    x_ref, mask_ref, gate_ref, proj_ref, out_ref, up_ref, down_ref, gain_in_ref, gain_out_ref, trans_gain_ref = ins
+    gate_out, x_out, mask_out, gate_t_out, proj_out, out_out, up_out, down_out, gains_out = outs
+    lines = x_ref.shape[1]
+    gain, gate_t = spread_gain(gain_in_ref[0:1, :]), gate_ref[0].T
+    for line in range(lines):
+        lanes = slice(line * LANES, (line + 1) * LANES)
+        current = line_tokens(x_ref, line).T
+        x_out[:, lanes] = current
+        gate_out[:, lanes] = sigmoid(dot(gate_t, channel_norm(current, gain)))
+    mask_out[...] = token_mask(mask_ref[...], lines)
+    gate_t_out[...] = gate_ref[1].T
     proj_out[...] = proj_ref[...].T
     for update in range(2):
         out_out[update] = out_ref[update].T
@@ -113,11 +131,6 @@
     rows = [gain_out_ref[0:1, :], gain_in_ref[1:2, :], gain_out_ref[1:2, :], trans_gain_ref[...]]
     for n, row in enumerate(rows):
         gains_out[n] = spread_gain(row)
-
-
-def gate_kernel(ins, outs):
-    normed_ref, weight_ref = ins
-    outs[0][...] = sigmoid(dot(weight_ref[...].T, normed_ref[...]))
 
 
 def swap_slots(parts, breadth):
@@ -136,22 +149,41 @@
     return parts
 
 
+def pitch_of(share):
+    return share + 1 if share % 8 == 0 else share
+
+
 def combine_kernel(rows, cols, breadth, share, outgoing, ins, outs, stage_ref, result_ref):
-    (both_ref,), (combined_ref,) = ins, outs
+    both_ref, combined_ref = ins[0], outs[0]
+    if len(ins) > 1:
+        prepare(ins[1:], outs[1:])
     slots = LANES // breadth
-    span = both_ref.shape[1]
+    owners, span = both_ref.shape[:2]
     lines = span // (2 * share)
-    stage_ref[...] = both_ref[...].astype(F32).reshape(stage_ref.shape)
+    pitch = pitch_of(share)
+    padded = pitch != share
+    if padded:
+        for owner in range(owners):
+            for line in range(lines):
+                both = both_ref[owner, 2 * share * line : 2 * share * (line + 1), :].astype(F32)
+                for side in range(2):
+                    base = ((2 * owner + side) * lines + line) * pitch
+                    stage_ref[base : base + share, :] = both[side * share : (side + 1) * share]
+    else:
+        stage_ref[...] = both_ref[...].astype(F32).reshape(stage_ref.shape)
+
+    def line_rows(owner, side, channel):
+        if padded:
+            return pl.ds((2 * owner + side) * lines * pitch + channel, lines, stride=pitch)
+        return pl.ds(owner * span + side * share + channel, lines, stride=2 * share)
 
     def whole(side, channel):
         columns = []
         for high in range(cols // slots):
             parts = []
             for low in range(slots):
-                base = (high * slots + low) * rows * span + side * share + channel
-                held = [
-                    stage_ref[pl.ds(row * span + base, lines, stride=2 * share), :] for row in range(rows)
-                ]
+                col = high * slots + low
+                held = [stage_ref[line_rows(col * rows + row, side, channel), :] for row in range(rows)]
                 parts.append(jnp.concatenate(held, axis=0))
             parts = swap_slots(parts, breadth)
             columns.append(
@@ -178,9 +210,17 @@
             ]
             for low, part in enumerate(swap_slots(parts, breadth)):
                 for row in range(rows):
-                    base = ((high * slots + low) * rows + row) * lines * share + channel
-                    result_ref[pl.ds(base, lines, stride=share), :] = part[row * lines : (row + 1) * lines]
-    combined_ref[...] = result_ref[...].astype(BF16).reshape(combined_ref.shape)
+                    base = ((high * slots + low) * rows + row) * lines * pitch + channel
+                    result_ref[pl.ds(base, lines, stride=pitch), :] = part[row * lines : (row + 1) * lines]
+    if padded:
+        for owner in range(owners):
+            held = [
+                result_ref[(owner * lines + line) * pitch : (owner * lines + line) * pitch + share, :]
+                for line in range(lines)
+            ]
+            combined_ref[owner] = jnp.concatenate(held, axis=0).astype(BF16)
+    else:
+        combined_ref[...] = result_ref[...].astype(BF16).reshape(combined_ref.shape)
 
 
 def read_combined(stage_ref, owners, lines, share, first, count):
@@ -198,8 +238,8 @@
 
 
 def middle_kernel(share, chunk, ins, outs, stage_ref, message_stage_ref):
-    combined_ref, x_ref, gate_ref, gains_ref, out_ref, mask_ref, weight_ref = ins
-    message_ref, normed_ref, next_ref = outs
+    combined_ref, x_ref, gate_ref, mask_ref, gate_t_ref, weight_ref, out_ref, gains_ref = ins
+    message_ref, gate_out, next_ref = outs
     tokens = x_ref.shape[1]
     lines = tokens // LANES
     owners = combined_ref.shape[0]
@@ -212,32 +252,40 @@
         current = x_ref[:, here] + gate_ref[:, here] * dot(out_ref[0], hidden)
         next_ref[:, here] = current
         normed = channel_norm(current, gains_ref[1])
-        normed_ref[:, here] = normed
         emit_message(normed, weight_ref[...], mask, start // LANES, message_ref, message_stage_ref, share)
-
-
-def last_kernel(share, chunk, ins, outs, stage_ref):
-    combined_ref, x_ref, gate_ref, gains_ref, out_ref, up_ref, down_ref = ins
-    (result_ref,) = outs
-    height, breadth, channels = result_ref.shape
-    tokens = x_ref.shape[1]
-    lines = tokens // LANES
+        gate_out[:, here] = sigmoid(dot(gate_t_ref[...], normed))
+
+
+def last_kernel(share, chunk, ins, outs, stage_ref, result_ref, sems):
+    combined_ref, x_ref, gate_ref, out_ref, up_ref, down_ref, gains_ref = ins
+    (result_out,) = outs
+    slots, lines, breadth, channels = result_ref.shape
     owners = combined_ref.shape[0]
     half = down_ref.shape[1]
+    count = chunk // LANES
     stage_ref[...] = combined_ref[...].astype(F32).reshape(stage_ref.shape)
-    for start in range(0, tokens, chunk):
-        here = slice(start, start + chunk)
-        combined = read_combined(stage_ref, owners, lines, share, start // LANES, chunk // LANES)
+    writes = []
+    for first in range(0, lines, count):
+        here = slice(first * LANES, (first + count) * LANES)
+        combined = read_combined(stage_ref, owners, lines, share, first, count)
         hidden = channel_norm(combined, gains_ref[2])
         current = x_ref[:, here] + gate_ref[:, here] * dot(out_ref[1], hidden)
-        up_part = dot(up_ref[...], channel_norm(current, gains_ref[3]))
-        first = up_part[:half]
-        trans_hidden = (first * sigmoid(first) * up_part[half:]).astype(BF16)
-        result = (current + dot(down_ref[...], trans_hidden)).T
-        for part in range(chunk // LANES):
-            for slot in range(LANES // breadth):
+        trans_in = channel_norm(current, gains_ref[3])
+        block = min(256, half)
+        for base in range(0, half, block):
+            gate_part = dot(up_ref[base : base + block, :], trans_in)
+            up_part = dot(up_ref[half + base : half + base + block, :], trans_in)
+            trans_hidden = (gate_part * sigmoid(gate_part) * up_part).astype(BF16)
+            current = current + dot(down_ref[:, base : base + block], trans_hidden)
+        result = current.T
+        for part in range(count):
+            for slot in range(slots):
                 base = part * LANES + slot * breadth
-                result_ref[slot * lines + start // LANES + part] = result[base : base + breadth]
+                result_ref[slot, first + part] = result[base : base + breadth]
+        piece = slice(first, first + count)
+        writes += start_all([(result_ref.at[:, piece], result_out.at[:, piece])], sems, first // count)
+    for write in writes:
+        write.wait()
 
 
 def whole_spec(array):
@@ -248,13 +296,12 @@
     return pl.BlockSpec((None,) + array.shape[1:], lambda step: (index,) + (0,) * (array.ndim - 1))
 
 
-def call(kernel, operands, picks, outs, scratch=(), in_place=False):
-    limit = FULL_VMEM_BYTES if in_place else VMEM_BYTES
+def call(kernel, operands, outs, scratch=(), picks=None, in_hbm=False, out_hbm=False):
+    in_place = pl.BlockSpec(memory_space=pltpu.HBM)
     specs = [
-        picked_spec(array, picks[n]) if n in picks else whole_spec(array) for n, array in enumerate(operands)
+        picked_spec(array, picks[n]) if picks and n in picks else whole_spec(array)
+        for n, array in enumerate(operands)
     ]
-    if in_place:
-        specs = [pl.BlockSpec(memory_space=pltpu.HBM)] * len(operands)
     shapes = [jax.ShapeDtypeStruct(shape, dtype) for shape, dtype in outs]
     count = len(operands)
 
@@ -264,11 +311,11 @@
     return pl.pallas_call(
         body,
         grid=(1,),
-        in_specs=specs,
-        out_specs=[whole_spec(shape) for shape in shapes],
+        in_specs=[in_place] * count if in_hbm else specs,
+        out_specs=[in_place if out_hbm else whole_spec(shape) for shape in shapes],
         out_shape=shapes,
         scratch_shapes=list(scratch),
-        compiler_params=pltpu.CompilerParams(vmem_limit_bytes=limit),
+        compiler_params=pltpu.CompilerParams(vmem_limit_bytes=FULL_VMEM_BYTES if in_hbm else VMEM_BYTES),
     )(*operands)
 
 
@@ -297,37 +344,43 @@
     owners = rows * cols
     share = hid // owners
     chunk = min(2 * LANES, tokens)
+    steps = tokens // chunk
     message = ((owners, 2 * share * lines, LANES), BF16)
     answer = ((owners, share * lines, LANES), BF16)
-    staged = pltpu.VMEM((owners * 2 * share * lines, LANES), F32)
     result = pltpu.VMEM((owners * share * lines, LANES), F32)
-    spare = pltpu.VMEM((8, LANES), F32) if share % 8 == 0 else staged
-    narrow, wide = ((channels, tokens), BF16), ((channels, tokens), F32)
-
-    def combine(both, outgoing):
+    spare = pltpu.VMEM((8, LANES) if share % 8 == 0 else (owners * 2 * share * lines, LANES), F32)
+    wide = ((channels, tokens), F32)
+    held = ((LANES // breadth, lines, breadth, channels), F32)
+    grouped = pair_map.reshape(held[0])
+
+    def combine(operands, outs, outgoing):
         kernel = functools.partial(combine_kernel, rows, cols, breadth, share, outgoing)
-        (combined,) = call(kernel, (both,), {}, [answer], (staged, result))
-        return combined
-
-    both, normed, current, mask = call(
+        pitch = pitch_of(share)
+        scratch = [pltpu.VMEM((sides * owners * lines * pitch, LANES), F32) for sides in (2, 1)]
+        return call(kernel, operands, [answer] + outs, scratch, {4: 1})
+
+    (both,) = call(
         functools.partial(project_kernel, share, chunk),
-        (pair_map, pair_mask, gain_in, proj_weight),
-        {},
-        [message, narrow, wide, ((lines, LANES), F32)],
+        (grouped, pair_mask, gain_in, proj_weight),
+        [message],
         (
             spare,
-            pltpu.VMEM(pair_map.shape, F32),
+            pltpu.VMEM(*held),
             pltpu.VMEM(pair_mask.shape, jnp.int32),
             pltpu.VMEM(gain_in.shape, F32),
             pltpu.VMEM(proj_weight.shape[1:], BF16),
-            pltpu.SemaphoreType.DMA((4,)),
+            pltpu.VMEM(*message),
+            pltpu.SemaphoreType.DMA((3 + steps,)),
+            pltpu.SemaphoreType.DMA((steps,)),
         ),
-        in_place=True,
+        in_hbm=True,
+        out_hbm=True,
     )
-    gate, proj_t, out_t, up_t, down_t, gains = call(
-        prepare_kernel,
+    combined, gate, current, mask, gate_t, proj_t, out_t, up_t, down_t, gains = combine(
         (
-            normed,
+            exchange(both),
+            grouped,
+            pair_mask,
             gate_weight,
             proj_weight,
             out_weight,
@@ -337,34 +390,34 @@
             gain_out,
             trans_gain.reshape(1, -1),
         ),
-        {1: 0, 2: 1},
         [
             wide,
+            wide,
+            ((lines, LANES), F32),
+            ((channels, channels), BF16),
             (proj_weight.shape[:0:-1], BF16),
-            ((2, out_weight.shape[2], hid), BF16),
+            ((2, channels, hid), BF16),
             (trans_up.shape[::-1], BF16),
             (trans_down.shape[::-1], BF16),
             ((4, channels, LANES), F32),
         ],
+        True,
     )
-    combined = exchange(combine(exchange(both), True))
-    both, normed, current = call(
+    both, gate, current = call(
         functools.partial(middle_kernel, share, chunk),
-        (combined, current, gate, gains, out_t, mask, proj_t),
-        {},
-        [message, narrow, wide],
+        (exchange(combined), current, gate, mask, gate_t, proj_t, out_t, gains),
+        [message, wide, wide],
         (result, spare),
     )
-    (gate,) = call(gate_kernel, (normed, gate_weight), {1: 1}, [wide])
-    combined = exchange(combine(exchange(both), False))
+    (combined,) = combine((exchange(both),), [], False)
     (pair_out,) = call(
         functools.partial(last_kernel, share, chunk),
-        (combined, current, gate, gains, out_t, up_t, down_t),
-        {},
-        [(pair_map.shape, F32)],
-        (result,),
+        (exchange(combined), current, gate, out_t, up_t, down_t, gains),
+        [held],
+        (result, pltpu.VMEM(*held), pltpu.SemaphoreType.DMA((steps,))),
+        out_hbm=True,
     )
-    return pair_out
+    return pair_out.reshape(pair_map.shape)
 
 
 def solution(mesh):

time: 80.7 us -> 81.3 us (level)
  blocking collectives: 39.1 us -> 67.1 us
  waiting for transfers between devices: 18.8 us -> 0 us
  starting transfers between devices: 8.33 us -> 0 us
    all_to_all x2 -> x4, blocking collectives: 39.1 us -> 67.1 us  [exchange(): return lax.all_to_all(values, AXES, split_axis=0, concat_axis=0, tiled=True)]
    all_to_all x2 -> x0, waiting for transfers between devices: 18.8 us -> none  [exchange(): return lax.all_to_all(values, AXES, split_axis=0, concat_axis=0, tiled=True)]
    all_to_all x2 -> x0, starting transfers between devices: 8.33 us -> none  [exchange(): return lax.all_to_all(values, AXES, split_axis=0, concat_axis=0, tiled=True)]
    pallas_call x7 -> x5, Pallas kernels: 12.5 us -> 13 us  [call(): pl.pallas_call(body, grid=(1,), in_specs=[in_place] * count if in_hbm els...]
  transfers between devices with their start and end apart: 2 -> 0, of which waited for: 2 -> 0; matrix products, arithmetic and copies ran while one was open for 0% -> 0% of each run, Pallas kernels for 1% -> 0%
where the time goes in v6:
time: 81.3 us; the launch traced here: 80.9 us
  blocking collectives  67.1 us (83%)
  Pallas kernels  13 us (16%)
    all_to_all x4, blocking collectives, exchange(): return lax.all_to_all(values, AXES, split_axis=0, concat_axis=0, tiled=True)  67.1 us
    pallas_call x5, Pallas kernels, call(): pl.pallas_call(body, grid=(1,), in_specs=[in_place] * count if in_hbm els...  13 us

profile of v6, /device:TPU:0, one launch (start us, length us, event | category | flops | bytes accessed | tf_op | source)
XLA Modules:
  0.0 80.9 jit_solution(4660125910611672072)
XLA Ops:
  0.0 0.0 copy-start.3
  0.0 0.0 copy-start.4
  0.0 0.0 copy-start.5
  0.0 0.0 copy-start.6
  0.0 0.0 copy-start.8
  0.0 3.5 %shard_map.100 = bf16[16,128,128]{2,1,0:T(8,128)(2,1)} custom-call(f32[4,8,32,128]{3,2,1,0:T(8,128)} %bitcast.3, s32[32,32]{1,0:T(8,128)} %refs_2_.3, f32[2,128]{1,0:T(2,128)} %refs_8_.1, bf16[2,128,512]{2,1,0:T(8,128)(2,1)} %refs_4_.1), custom_call_target="tpu_custom_call" | custom-call | tf_op jit(solution)/shard_map/pallas_call | solution.py:311
  3.5 0.0 copy-start
  3.5 0.0 copy-start.1
  3.5 0.0 copy-start.2
  3.5 22.0 %all_to_all.20.refs_0_ = bf16[16,128,128]{2,1,0:T(8,128)(2,1)S(1)} all-to-all(bf16[16,128,128]{2,1,0:T(8,128)(2,1)} %shard_map.100), channel_id=1, replica_groups=mesh['grp'=2,'row'=4,'col'=4] {'col','row'}, dimensions={0} | all-to-all | bytes 1048576 | tf_op jit(solution)/shard_map/all_to_all | solution.py:323
  25.5 0.0 copy-start.7
  25.5 0.0 copy-start.9
  25.5 0.0 copy-done.3
  25.5 0.0 copy-done.4
  25.6 0.0 copy-done.5
  25.6 0.0 copy-done.6
  25.6 0.0 copy-done.8
  25.6 0.0 copy-done
  25.6 0.0 copy-done.1
  25.6 0.0 copy-done.2
  25.6 0.6 copy-done.7
  26.2 0.0 copy-done.9
  26.2 3.4 %shard_map.101 = (bf16[16,64,128]{2,1,0:T(8,128)(2,1)S(1)}, f32[128,1024]{1,0:T(8,128)S(1)}, f32[128,1024]{1,0:T(8,128)S(1)}, f32[8,128]{1,0:T(8,128)S(1)}, bf16...) custom-call(bf16[16,128,128]{2,1,0:T(8,128)(2,1)S(1)} %all_to_all.20, ...), custom_call_target="tpu_custom_call" | custom-call | tf_op jit(solution)/shard_map/pallas_call | solution.py:311
  29.6 13.9 %all_to_all.21.refs_0_ = bf16[16,64,128]{2,1,0:T(8,128)(2,1)S(1)} all-to-all(bf16[16,64,128]{2,1,0:T(8,128)(2,1)S(1)} %get-tuple-element.18), channel_id=1, replica_groups=mesh['grp'=2,'row'=4,'col'=4] {'col','row'}, dimensions={0} | all-to-all | bytes 524288 | tf_op jit(solution)/shard_map/all_to_all | solution.py:323
  43.6 1.4 %shard_map.102 = (bf16[16,128,128]{2,1,0:T(8,128)(2,1)S(1)}, f32[128,1024]{1,0:T(8,128)S(1)}, f32[128,1024]{1,0:T(8,128)S(1)}) custom-call(bf16[16,64,128]{2,1,0:T(8,128)(2,1)S(1)} %all_to_all.21.refs_0_, f32[128,1024]{1,0:T(8,128)S(1)} %get-tuple-element.19.refs_1_, f32[128,1024]{1,0:T(8,128)S(1)} %get-tuple-element.20.refs_2_, ...), custom_call_target="tpu_custom_call" | custom-call | tf_op jit(solution)/shard_map/pallas_call | solution.py:311
  45.0 17.2 %all_to_all.22.refs_0_ = bf16[16,128,128]{2,1,0:T(8,128)(2,1)S(1)} all-to-all(bf16[16,128,128]{2,1,0:T(8,128)(2,1)S(1)} %get-tuple-element.26), channel_id=1, replica_groups=mesh['grp'=2,'row'=4,'col'=4] {'col','row'}, dimensions={0} | all-to-all | bytes 1048576 | tf_op jit(solution)/shard_map/all_to_all | solution.py:323
  62.2 1.8 %shard_map.103 = bf16[16,64,128]{2,1,0:T(8,128)(2,1)S(1)} custom-call(bf16[16,128,128]{2,1,0:T(8,128)(2,1)S(1)} %all_to_all.22.refs_0_), custom_call_target="tpu_custom_call" | custom-call | tf_op jit(solution)/shard_map/pallas_call | solution.py:311
  64.0 13.9 %all_to_all.23.refs_0_ = bf16[16,64,128]{2,1,0:T(8,128)(2,1)S(1)} all-to-all(bf16[16,64,128]{2,1,0:T(8,128)(2,1)S(1)} %shard_map.103), channel_id=1, replica_groups=mesh['grp'=2,'row'=4,'col'=4] {'col','row'}, dimensions={0} | all-to-all | bytes 524288 | tf_op jit(solution)/shard_map/all_to_all | solution.py:323
  78.0 3.0 %shard_map.104 = f32[4,8,32,128]{3,2,1,0:T(8,128)} custom-call(bf16[16,64,128]{2,1,0:T(8,128)(2,1)S(1)} %all_to_all.23.refs_0_, f32[128,1024]{1,0:T(8,128)S(1)} %get-tuple-element.27.refs_1_, f32[128,1024]{1,0:T(8,128)S(1)} %get-tuple-element.28.refs_2_, bf16[2,128,128]{2,1,0:T(8,128)(2,1)S(1)} %get-tuple-element.24.refs_6_.refs_3_, ...), custom_call_target="tpu_custom_call" | custom-call | tf_op jit(solution)/shard_map/pallas_call | solution.py:311
Async XLA Ops:
  0.0 25.5 %copy-start.3 = (bf16[512,128]{1,0:T(8,128)(2,1)S(1)}, bf16[512,128]{1,0:T(8,128)(2,1)}, u32[]{:S(2)}) copy-start(bf16[512,128]{1,0:T(8,128)(2,1)} %refs_7_.1) | copy-start | bytes 393220
  0.0 25.5 %copy-start.4 = (s32[32,32]{1,0:T(8,128)S(1)}, s32[32,32]{1,0:T(8,128)}, u32[]{:S(2)}) copy-start(s32[32,32]{1,0:T(8,128)} %refs_2_.3) | copy-start | bytes 12292
  0.0 25.5 %copy-start.5 = (bf16[2,128,128]{2,1,0:T(8,128)(2,1)S(1)}, bf16[2,128,128]{2,1,0:T(8,128)(2,1)}, u32[]{:S(2)}) copy-start(bf16[2,128,128]{2,1,0:T(8,128)(2,1)} %refs_3_.3) | copy-start | bytes 196612
  0.0 25.6 %copy-start.6 = (bf16[2,128,128]{2,1,0:T(8,128)(2,1)S(1)}, bf16[2,128,128]{2,1,0:T(8,128)(2,1)}, u32[]{:S(2)}) copy-start(bf16[2,128,128]{2,1,0:T(8,128)(2,1)} %refs_5_.1) | copy-start | bytes 196612
  0.0 25.6 %copy-start.8 = (f32[2,128]{1,0:T(2,128)S(1)}, f32[2,128]{1,0:T(2,128)}, u32[]{:S(2)}) copy-start(f32[2,128]{1,0:T(2,128)} %refs_9_.1) | copy-start | bytes 3076
  3.5 22.1 %copy-start = (f32[32,32,128]{2,1,0:T(8,128)S(1)}, f32[32,32,128]{2,1,0:T(8,128)}, u32[]{:S(2)}) copy-start(f32[32,32,128]{2,1,0:T(8,128)} %param.10) | copy-start | bytes 1572868
  3.5 22.1 %copy-start.1 = (bf16[2,128,512]{2,1,0:T(8,128)(2,1)S(1)}, bf16[2,128,512]{2,1,0:T(8,128)(2,1)}, u32[]{:S(2)}) copy-start(bf16[2,128,512]{2,1,0:T(8,128)(2,1)} %refs_4_.1) | copy-start | bytes 786436
  3.5 22.1 %copy-start.2 = (bf16[128,1024]{1,0:T(8,128)(2,1)S(1)}, bf16[128,1024]{1,0:T(8,128)(2,1)}, u32[]{:S(2)}) copy-start(bf16[128,1024]{1,0:T(8,128)(2,1)} %refs_6_.1) | copy-start | bytes 786436
  25.5 0.7 copy-start.7
  25.5 0.7 copy-start.9

commit v7 on v6

--- a/solution.py
+++ b/solution.py
@@ -80,49 +80,28 @@
     return jnp.concatenate([x_ref[slot, line] for slot in range(x_ref.shape[0])], axis=0)
 
 
-def project_kernel(
-    share, chunk, ins, outs, stage_ref, x_ref, mask_ref, gain_ref, weight_ref, held_ref, in_sems, out_sems
-):
-    (message_out,) = outs
+def project_kernel(share, ins, outs, stage_ref, x_ref, mask_ref, gain_ref, weight_ref, sems):
+    message_ref, normed_ref = outs
     x_in, mask_in, gain_in, weight_in = ins
-    slots, lines, breadth, channels = x_ref.shape
-    count = chunk // LANES
-    steps = lines // count
-    pieces = [slice(n * count, (n + 1) * count) for n in range(steps)]
-    small = start_all([(gain_in, gain_ref), (mask_in, mask_ref), (weight_in.at[0], weight_ref)], in_sems)
-    large = start_all([(x_in.at[:, piece], x_ref.at[:, piece]) for piece in pieces], in_sems, 3)
-    small[0].wait()
-    small[1].wait()
+    lines = x_ref.shape[1]
+    pairs = [(weight_in.at[0], weight_ref), (x_in, x_ref), (gain_in, gain_ref), (mask_in, mask_ref)]
+    for copy in start_all(pairs, sems):
+        copy.wait()
     mask = token_mask(mask_ref[...], lines)
-    gain = spread_gain(gain_ref[0:1, :])
-    small[2].wait()
-    weight_t = weight_ref[...].T
-    writes = []
-    for n, piece in enumerate(pieces):
-        large[n].wait()
-        current = jnp.concatenate([line_tokens(x_ref, line) for line in range(piece.start, piece.stop)], axis=0).T
-        emit_message(channel_norm(current, gain), weight_t, mask, piece.start, held_ref, stage_ref, share)
-        if share % 8 == 0:
-            rows = slice(2 * share * piece.start, 2 * share * piece.stop)
-            writes += start_all([(held_ref.at[:, rows], message_out.at[:, rows])], out_sems, n)
-        elif n == steps - 1:
-            writes += start_all([(held_ref, message_out)], out_sems)
-    for write in writes:
-        write.wait()
-
-
-def prepare(ins, outs):
-    x_ref, mask_ref, gate_ref, proj_ref, out_ref, up_ref, down_ref, gain_in_ref, gain_out_ref, trans_gain_ref = ins
-    gate_out, x_out, mask_out, gate_t_out, proj_out, out_out, up_out, down_out, gains_out = outs
+    current = jnp.concatenate([line_tokens(x_ref, line).T for line in range(lines)], axis=1)
+    normed = channel_norm(current, spread_gain(gain_ref[0:1, :]))
+    emit_message(normed, weight_ref[...].T, mask, 0, message_ref, stage_ref, share)
+    normed_ref[...] = normed
+
+
+def prepare_kernel(ins, outs):
+    normed_ref, x_ref, mask_ref, gate_ref, proj_ref, out_ref, up_ref, down_ref, gain_in_ref, gain_out_ref, trans_gain_ref = ins
+    gate_out, x_out, mask_out, proj_out, out_out, up_out, down_out, gains_out = outs
     lines = x_ref.shape[1]
-    gain, gate_t = spread_gain(gain_in_ref[0:1, :]), gate_ref[0].T
+    gate_out[...] = sigmoid(dot(gate_ref[...].T, normed_ref[...]))
     for line in range(lines):
-        lanes = slice(line * LANES, (line + 1) * LANES)
-        current = line_tokens(x_ref, line).T
-        x_out[:, lanes] = current
-        gate_out[:, lanes] = sigmoid(dot(gate_t, channel_norm(current, gain)))
+        x_out[:, line * LANES : (line + 1) * LANES] = line_tokens(x_ref, line).T
     mask_out[...] = token_mask(mask_ref[...], lines)
-    gate_t_out[...] = gate_ref[1].T
     proj_out[...] = proj_ref[...].T
     for update in range(2):
         out_out[update] = out_ref[update].T
@@ -131,6 +110,11 @@
     rows = [gain_out_ref[0:1, :], gain_in_ref[1:2, :], gain_out_ref[1:2, :], trans_gain_ref[...]]
     for n, row in enumerate(rows):
         gains_out[n] = spread_gain(row)
+
+
+def gate_kernel(ins, outs):
+    normed_ref, weight_ref = ins
+    outs[0][...] = sigmoid(dot(weight_ref[...].T, normed_ref[...]))
 
 
 def swap_slots(parts, breadth):
@@ -154,9 +138,7 @@
 
 
 def combine_kernel(rows, cols, breadth, share, outgoing, ins, outs, stage_ref, result_ref):
-    both_ref, combined_ref = ins[0], outs[0]
-    if len(ins) > 1:
-        prepare(ins[1:], outs[1:])
+    (both_ref,), (combined_ref,) = ins, outs
     slots = LANES // breadth
     owners, span = both_ref.shape[:2]
     lines = span // (2 * share)
@@ -238,8 +220,8 @@
 
 
 def middle_kernel(share, chunk, ins, outs, stage_ref, message_stage_ref):
-    combined_ref, x_ref, gate_ref, mask_ref, gate_t_ref, weight_ref, out_ref, gains_ref = ins
-    message_ref, gate_out, next_ref = outs
+    combined_ref, x_ref, gate_ref, mask_ref, weight_ref, out_ref, gains_ref = ins
+    message_ref, normed_ref, next_ref = outs
     tokens = x_ref.shape[1]
     lines = tokens // LANES
     owners = combined_ref.shape[0]
@@ -253,7 +235,7 @@
         next_ref[:, here] = current
         normed = channel_norm(current, gains_ref[1])
         emit_message(normed, weight_ref[...], mask, start // LANES, message_ref, message_stage_ref, share)
-        gate_out[:, here] = sigmoid(dot(gate_t_ref[...], normed))
+        normed_ref[:, here] = normed
 
 
 def last_kernel(share, chunk, ins, outs, stage_ref, result_ref, sems):
@@ -343,42 +325,38 @@
     hid = gain_out.shape[1]
     owners = rows * cols
     share = hid // owners
-    chunk = min(2 * LANES, tokens)
-    steps = tokens // chunk
+    chunk = min(4 * LANES, tokens)
     message = ((owners, 2 * share * lines, LANES), BF16)
     answer = ((owners, share * lines, LANES), BF16)
     result = pltpu.VMEM((owners * share * lines, LANES), F32)
     spare = pltpu.VMEM((8, LANES) if share % 8 == 0 else (owners * 2 * share * lines, LANES), F32)
-    wide = ((channels, tokens), F32)
+    narrow, wide = ((channels, tokens), BF16), ((channels, tokens), F32)
     held = ((LANES // breadth, lines, breadth, channels), F32)
     grouped = pair_map.reshape(held[0])
 
-    def combine(operands, outs, outgoing):
+    def combine(both, outgoing):
         kernel = functools.partial(combine_kernel, rows, cols, breadth, share, outgoing)
-        pitch = pitch_of(share)
-        scratch = [pltpu.VMEM((sides * owners * lines * pitch, LANES), F32) for sides in (2, 1)]
-        return call(kernel, operands, [answer] + outs, scratch, {4: 1})
-
-    (both,) = call(
-        functools.partial(project_kernel, share, chunk),
+        scratch = [pltpu.VMEM((sides * owners * lines * pitch_of(share), LANES), F32) for sides in (2, 1)]
+        return call(kernel, (both,), [answer], scratch)[0]
+
+    both, normed = call(
+        functools.partial(project_kernel, share),
         (grouped, pair_mask, gain_in, proj_weight),
-        [message],
+        [message, narrow],
         (
             spare,
             pltpu.VMEM(*held),
             pltpu.VMEM(pair_mask.shape, jnp.int32),
             pltpu.VMEM(gain_in.shape, F32),
             pltpu.VMEM(proj_weight.shape[1:], BF16),
-            pltpu.VMEM(*message),
-            pltpu.SemaphoreType.DMA((3 + steps,)),
-            pltpu.SemaphoreType.DMA((steps,)),
+            pltpu.SemaphoreType.DMA((4,)),
         ),
         in_hbm=True,
-        out_hbm=True,
     )
-    combined, gate, current, mask, gate_t, proj_t, out_t, up_t, down_t, gains = combine(
+    gate, current, mask, proj_t, out_t, up_t, down_t, gains = call(
+        prepare_kernel,
         (
-            exchange(both),
+            normed,
             grouped,
             pair_mask,
             gate_weight,
@@ -394,27 +372,28 @@
             wide,
             wide,
             ((lines, LANES), F32),
-            ((channels, channels), BF16),
             (proj_weight.shape[:0:-1], BF16),
             ((2, channels, hid), BF16),
             (trans_up.shape[::-1], BF16),
             (trans_down.shape[::-1], BF16),
             ((4, channels, LANES), F32),
         ],
-        True,
+        picks={3: 0, 4: 1},
     )
-    both, gate, current = call(
+    combined = exchange(combine(exchange(both), True))
+    both, normed, current = call(
         functools.partial(middle_kernel, share, chunk),
-        (exchange(combined), current, gate, mask, gate_t, proj_t, out_t, gains),
-        [message, wide, wide],
+        (combined, current, gate, mask, proj_t, out_t, gains),
+        [message, narrow, wide],
         (result, spare),
     )
-    (combined,) = combine((exchange(both),), [], False)
+    (gate,) = call(gate_kernel, (normed, gate_weight), [wide], picks={1: 1})
+    combined = exchange(combine(exchange(both), False))
     (pair_out,) = call(
         functools.partial(last_kernel, share, chunk),
-        (exchange(combined), current, gate, out_t, up_t, down_t, gains),
+        (combined, current, gate, out_t, up_t, down_t, gains),
         [held],
-        (result, pltpu.VMEM(*held), pltpu.SemaphoreType.DMA((steps,))),
+        (result, pltpu.VMEM(*held), pltpu.SemaphoreType.DMA((tokens // chunk,))),
         out_hbm=True,
     )
     return pair_out.reshape(pair_map.shape)

time: 81.3 us -> 80.8 us (level)
  blocking collectives: 67.1 us -> 39.2 us
  waiting for transfers between devices: 0 us -> 15.9 us
  starting transfers between devices: 0 us -> 8.32 us
  local copies, waits for them, and re-layouts: 0.65 us -> 4.96 us
  Pallas kernels: 13 us -> 11.7 us
    all_to_all x4 -> x2, blocking collectives: 67.1 us -> 39.2 us  [exchange(): return lax.all_to_all(values, AXES, split_axis=0, concat_axis=0, tiled=True)]
    all_to_all x0 -> x2, waiting for transfers between devices: none -> 15.9 us  [exchange(): return lax.all_to_all(values, AXES, split_axis=0, concat_axis=0, tiled=True)]
    all_to_all x0 -> x2, starting transfers between devices: none -> 8.32 us  [exchange(): return lax.all_to_all(values, AXES, split_axis=0, concat_axis=0, tiled=True)]
    unnamed x20 -> x30, local copies, waits for them, and re-layouts: 0.65 us -> 4.96 us
    pallas_call x5 -> x7, Pallas kernels: 13 us -> 11.7 us  [call(): pl.pallas_call(body, grid=(1,), in_specs=[in_place] * count if in_hbm els...]
  transfers between devices with their start and end apart: 0 -> 2, of which waited for: 0 -> 2; matrix products, arithmetic and copies ran while one was open for 0% -> 0% of each run, Pallas kernels for 0% -> 1%
where the time goes in v7:
time: 80.8 us; the launch traced here: 80.2 us
  blocking collectives  39.2 us (49%)
  waiting for transfers between devices  15.9 us (20%)
  Pallas kernels  11.7 us (14%)
  starting transfers between devices  8.32 us (10%)
  local copies, waits for them, and re-layouts  4.96 us (6%)
    all_to_all x2, blocking collectives, exchange(): return lax.all_to_all(values, AXES, split_axis=0, concat_axis=0, tiled=True)  39.2 us
    all_to_all x2, waiting for transfers between devices, exchange(): return lax.all_to_all(values, AXES, split_axis=0, concat_axis=0, tiled=True)  15.9 us
    pallas_call x7, Pallas kernels, call(): pl.pallas_call(body, grid=(1,), in_specs=[in_place] * count if in_hbm els...  11.7 us
    all_to_all x2, starting transfers between devices, exchange(): return lax.all_to_all(values, AXES, split_axis=0, concat_axis=0, tiled=True)  8.32 us
    unnamed x30, local copies, waits for them, and re-layouts  4.96 us
  transfers between devices with their start and end apart: 2, of which 2 were waited for; matrix products, arithmetic and copies ran while one was open for 0% of the time, Pallas kernels for 1%

profile of v7, /device:TPU:0, one launch (start us, length us, event | category | flops | bytes accessed | tf_op | source)
XLA Modules:
  0.0 80.2 jit_solution(16987900632434294938)
XLA Ops:
  0.0 2.6 %shard_map.100 = (bf16[16,128,128]{2,1,0:T(8,128)(2,1)}, bf16[128,1024]{1,0:T(8,128)(2,1)}) custom-call(f32[4,8,32,128]{3,2,1,0:T(8,128)} %bitcast.3, s32[32,32]{1,0:T(8,128)} %refs_2_.3, f32[2,128]{1,0:T(2,128)} %refs_8_.1, bf16[2,128,512]{2,1,0:T(8,128)(2,1)} %refs_4_.1), custom_call_target="tpu_custom_call" | custom-call | tf_op jit(solution)/shard_map/pallas_call | solution.py:293
  2.6 0.0 copy-start.4
  2.6 0.0 copy-start.5
  2.6 0.0 copy-start.8
  2.6 22.0 %all_to_all.20.refs_0_ = bf16[16,128,128]{2,1,0:T(8,128)(2,1)S(1)} all-to-all(bf16[16,128,128]{2,1,0:T(8,128)(2,1)} %get-tuple-element.18), channel_id=1, replica_groups=mesh['grp'=2,'row'=4,'col'=4] {'col','row'}, dimensions={0} | all-to-all | bytes 1048576 | tf_op jit(solution)/shard_map/all_to_all | solution.py:305
  24.6 0.0 copy-start
  24.6 0.0 copy-start.3
  24.6 2.0 %shard_map.101 = bf16[16,64,128]{2,1,0:T(8,128)(2,1)} custom-call(bf16[16,128,128]{2,1,0:T(8,128)(2,1)S(1)} %all_to_all.20.refs_0_), custom_call_target="tpu_custom_call" | custom-call | tf_op jit(solution)/shard_map/pallas_call | solution.py:293
  26.7 0.0 copy-start.1
  26.7 0.0 copy-start.2
  26.7 4.2 %all-to-all-start.1 = ((bf16[16,64,128]{2,1,0:T(8,128)(2,1)}), bf16[16,64,128]{2,1,0:T(8,128)(2,1)S(1)}, u32[]{:S(2)}, u32[]{:S(2)}) async-start(bf16[16,64,128]{2,1,0:T(8,128)(2,1)} %shard_map.101), calls=%async_computation.1 | async-start | bytes 524288 | tf_op jit(solution)/shard_map/all_to_all | solution.py:305
  30.9 0.0 copy-start.12
  30.9 0.0 copy-start.14
  30.9 0.0 copy-done.4
  30.9 0.0 copy-done.5
  30.9 0.0 copy-done.8
  30.9 0.0 copy-done
  31.0 0.0 copy-done.3
  31.0 0.0 copy-done.1
  31.0 0.0 copy-done.2
  31.0 0.6 copy-done.12
  31.6 0.0 copy-done.14
  31.6 0.0 copy-start.9
  31.6 0.8 %copy-done.9 = bf16[2,128,128]{2,1,0:T(8,128)(2,1)S(1)} copy-done((bf16[2,128,128]{2,1,0:T(8,128)(2,1)S(1)}, bf16[2,128,128]{2,1,0:T(8,128)(2,1)}, u32[]{:S(2)}) %copy-start.9) | copy-done | bytes 65560
  32.4 0.0 copy-start.13
  32.4 0.7 copy-done.13
  33.1 0.5 shard_map.102
  33.6 0.0 copy-start.6
  33.6 0.6 copy-done.6
  34.3 0.0 copy-start.10
  34.3 0.6 copy-done.10
  34.9 6.1 %all-to-all-done.1.refs_0_ = bf16[16,64,128]{2,1,0:T(8,128)(2,1)S(1)} async-done(((bf16[16,64,128]{2,1,0:T(8,128)(2,1)}), bf16[16,64,128]{2,1,0:T(8,128)(2,1)S(1)}, u32[]{:S(2)}, u32[]{:S(2)}) %all-to-all-start.1) | async-done | bytes 262176 | tf_op jit(solution)/shard_map/all_to_all | solution.py:305
  40.9 0.0 copy-start.11
  40.9 0.7 copy-done.11
  41.6 0.0 copy-start.7
  41.6 0.9 %copy-done.7 = bf16[512,128]{1,0:T(8,128)(2,1)S(1)} copy-done((bf16[512,128]{1,0:T(8,128)(2,1)S(1)}, bf16[512,128]{1,0:T(8,128)(2,1)}, u32[]{:S(2)}) %copy-start.7) | copy-done | bytes 131096
  42.5 1.0 %shard_map.103 = (bf16[16,128,128]{2,1,0:T(8,128)(2,1)S(1)}, bf16[128,1024]{1,0:T(8,128)(2,1)S(1)}, f32[128,1024]{1,0:T(8,128)S(1)}) custom-call(bf16[16,64,128]{2,1,0:T(8,128)(2,1)S(1)} %all-to-all-done.1.refs_0_, f32[128,1024]{1,0:T(8,128)S(1)} %get-tuple-element.20.refs_1_, f32[128,1024]{1,0:T(8,128)S(1)} %get-tuple-element.21.refs_2_, ...), custom_call_target="tpu_custom_call" | custom-call | tf_op jit(solution)/shard_map/pallas_call | solution.py:293
  43.5 17.2 %all_to_all.21.refs_0_ = bf16[16,128,128]{2,1,0:T(8,128)(2,1)S(1)} all-to-all(bf16[16,128,128]{2,1,0:T(8,128)(2,1)S(1)} %get-tuple-element.26), channel_id=1, replica_groups=mesh['grp'=2,'row'=4,'col'=4] {'col','row'}, dimensions={0} | all-to-all | bytes 1048576 | tf_op jit(solution)/shard_map/all_to_all | solution.py:305
  60.8 2.5 %shard_map.104 = bf16[16,64,128]{2,1,0:T(8,128)(2,1)} custom-call(bf16[16,128,128]{2,1,0:T(8,128)(2,1)S(1)} %all_to_all.21.refs_0_), custom_call_target="tpu_custom_call" | custom-call | tf_op jit(solution)/shard_map/pallas_call | solution.py:293
  63.3 4.1 %all-to-all-start.3 = ((bf16[16,64,128]{2,1,0:T(8,128)(2,1)}), bf16[16,64,128]{2,1,0:T(8,128)(2,1)S(1)}, u32[]{:S(2)}, u32[]{:S(2)}) async-start(bf16[16,64,128]{2,1,0:T(8,128)(2,1)} %shard_map.104), calls=%async_computation.3 | async-start | bytes 524288 | tf_op jit(solution)/shard_map/all_to_all | solution.py:305
  67.4 0.3 shard_map.105.refs_2_
  67.7 9.8 %all-to-all-done.3.refs_0_ = bf16[16,64,128]{2,1,0:T(8,128)(2,1)S(1)} async-done(((bf16[16,64,128]{2,1,0:T(8,128)(2,1)}), bf16[16,64,128]{2,1,0:T(8,128)(2,1)S(1)}, u32[]{:S(2)}, u32[]{:S(2)}) %all-to-all-start.3) | async-done | bytes 262176 | tf_op jit(solution)/shard_map/all_to_all | solution.py:305
  77.5 2.8 %shard_map.106 = f32[4,8,32,128]{3,2,1,0:T(8,128)} custom-call(bf16[16,64,128]{2,1,0:T(8,128)(2,1)S(1)} %all-to-all-done.3.refs_0_, f32[128,1024]{1,0:T(8,128)S(1)} %get-tuple-element.27.refs_1_, f32[128,1024]{1,0:T(8,128)S(1)} %shard_map.105.refs_2_, bf16[2,128,128]{2,1,0:T(8,128)(2,1)S(1)} %get-tuple-element.24.refs_5_.refs_3_, ...), custom_call_target="tpu_custom_call" | custom-call | tf_op jit(solution)/shard_map/pallas_call | solution.py:293
Async XLA Ops:
  2.6 28.3 %copy-start.4 = (bf16[2,128,128]{2,1,0:T(8,128)(2,1)S(1)}, bf16[2,128,128]{2,1,0:T(8,128)(2,1)}, u32[]{:S(2)}) copy-start(bf16[2,128,128]{2,1,0:T(8,128)(2,1)} %refs_1_.3) | copy-start | bytes 196612
  2.6 28.3 %copy-start.5 = (bf16[512,128]{1,0:T(8,128)(2,1)S(1)}, bf16[512,128]{1,0:T(8,128)(2,1)}, u32[]{:S(2)}) copy-start(bf16[512,128]{1,0:T(8,128)(2,1)} %refs_7_.1) | copy-start | bytes 393220
  2.6 28.3 %copy-start.8 = (s32[32,32]{1,0:T(8,128)S(1)}, s32[32,32]{1,0:T(8,128)}, u32[]{:S(2)}) copy-start(s32[32,32]{1,0:T(8,128)} %refs_2_.3) | copy-start | bytes 12292
  24.6 6.3 %copy-start = (f32[32,32,128]{2,1,0:T(8,128)S(1)}, f32[32,32,128]{2,1,0:T(8,128)}, u32[]{:S(2)}) copy-start(f32[32,32,128]{2,1,0:T(8,128)} %param.10) | copy-start | bytes 1572868
  24.6 6.4 %copy-start.3 = (bf16[128,1024]{1,0:T(8,128)(2,1)S(1)}, bf16[128,1024]{1,0:T(8,128)(2,1)}, u32[]{:S(2)}) copy-start(bf16[128,1024]{1,0:T(8,128)(2,1)} %get-tuple-element.19.refs_0_) | copy-start | bytes 786436
  26.7 4.3 %copy-start.1 = (bf16[2,128,512]{2,1,0:T(8,128)(2,1)S(1)}, bf16[2,128,512]{2,1,0:T(8,128)(2,1)}, u32[]{:S(2)}) copy-start(bf16[2,128,512]{2,1,0:T(8,128)(2,1)} %refs_4_.1) | copy-start | bytes 786436
  26.7 4.3 %copy-start.2 = (bf16[128,1024]{1,0:T(8,128)(2,1)S(1)}, bf16[128,1024]{1,0:T(8,128)(2,1)}, u32[]{:S(2)}) copy-start(bf16[128,1024]{1,0:T(8,128)(2,1)} %refs_6_.1) | copy-start | bytes 786436
  26.7 14.3 %all-to-all-start.1 = ((bf16[16,64,128]{2,1,0:T(8,128)(2,1)}), bf16[16,64,128]{2,1,0:T(8,128)(2,1)S(1)}, u32[]{:S(2)}, u32[]{:S(2)}) async-start(bf16[16,64,128]{2,1,0:T(8,128)(2,1)} %shard_map.101), calls=%async_computation.1 | async-start | bytes 524288 | tf_op jit(solution)/shard_map/all_to_all | solution.py:305
  30.9 0.7 copy-start.12
  30.9 0.7 copy-start.14
  31.6 0.8 %copy-start.9 = (bf16[2,128,128]{2,1,0:T(8,128)(2,1)S(1)}, bf16[2,128,128]{2,1,0:T(8,128)(2,1)}, u32[]{:S(2)}) copy-start(bf16[2,128,128]{2,1,0:T(8,128)(2,1)} %refs_5_.1) | copy-start | bytes 196612
  32.4 0.7 copy-start.13
  33.6 0.6 copy-start.6
  34.3 0.6 copy-start.10
  40.9 0.7 copy-start.11
  41.6 0.9 %copy-start.7 = (bf16[512,128]{1,0:T(8,128)(2,1)S(1)}, bf16[512,128]{1,0:T(8,128)(2,1)}, u32[]{:S(2)}) copy-start(bf16[512,128]{1,0:T(8,128)(2,1)} %copy-done.6) | copy-start | bytes 393220
  63.3 14.2 %all-to-all-start.3 = ((bf16[16,64,128]{2,1,0:T(8,128)(2,1)}), bf16[16,64,128]{2,1,0:T(8,128)(2,1)S(1)}, u32[]{:S(2)}, u32[]{:S(2)}) async-start(bf16[16,64,128]{2,1,0:T(8,128)(2,1)} %shard_map.104), calls=%async_computation.3 | async-start | bytes 524288 | tf_op jit(solution)/shard_map/all_to_all | solution.py:305

commit v8 on v7

v8 whole, which is shorter than its diff:
```python
import functools

import jax
import jax.numpy as jnp
from jax import lax
from jax.experimental import pallas as pl
from jax.experimental.pallas import tpu as pltpu
from jax.sharding import PartitionSpec as P

AXES = ("col", "row")
LANES = 128
VMEM_BYTES = 24 * 1024 * 1024
FULL_VMEM_BYTES = 60 * 1024 * 1024
F32, BF16 = jnp.float32, jnp.bfloat16


def dot(left, right, contract=(1, 0)):
    return lax.dot_general(
        left, right, (((contract[0],), (contract[1],)), ((), ())), preferred_element_type=F32
    )


def sigmoid(values):
    return 0.5 * jnp.tanh(0.5 * values) + 0.5


def channel_norm(values, gain):
    wide = jnp.concatenate([gain] * (values.shape[1] // LANES), axis=1)
    centred = values - jnp.mean(values, axis=0, keepdims=True)
    spread = jnp.mean(centred * centred, axis=0, keepdims=True)
    return (centred * lax.rsqrt(spread + 1e-05) * wide).astype(BF16)


def spread_gain(row):
    return jnp.broadcast_to(row, (LANES, row.shape[1])).T


def token_mask(mask, lines):
    height, breadth = mask.shape
    wide = jnp.concatenate([mask.astype(F32)] * (LANES // breadth), axis=1)
    row = lax.broadcasted_iota(jnp.int32, wide.shape, 0)
    lane = lax.broadcasted_iota(jnp.int32, wide.shape, 1)
    wide = jnp.where(row // lines == lane // breadth, wide, 0.0).astype(BF16)
    line = lax.broadcasted_iota(jnp.int32, (lines, height), 0)
    source = lax.broadcasted_iota(jnp.int32, (lines, height), 1)
    return dot((source % lines == line).astype(BF16), wide)


def arrange(weight, parts, take):
    width = weight.shape[1]
    hid = width // 4
    row = lax.broadcasted_iota(jnp.int32, (width, width), 0)
    source = lax.broadcasted_iota(jnp.int32, (width, width), 1)
    block = 2 * hid // parts
    owners = hid // (parts * take)
    inner = row % block
    channel = (row // (2 * block) * take + inner % take) * owners + inner // (2 * take)
    wanted = inner // take % 2 * (2 * hid) + row // block % 2 * hid + channel
    return dot((source == wanted).astype(BF16), weight, (1, 1)).astype(BF16)


def emit_messages(normed, weight_t, mask, line, message_refs, take):
    block = weight_t.shape[0] // (2 * len(message_refs))
    size = 2 * take
    count = normed.shape[1] // LANES
    group = max(1, 16 // size)
    for part, message_ref in enumerate(message_refs):
        projected = dot(weight_t[2 * part * block : 2 * (part + 1) * block], normed)
        act = sigmoid(projected[:block]) * projected[block:]
        acts = [act[:, n * LANES : (n + 1) * LANES] * mask[line + n : line + n + 1] for n in range(count)]
        for owner in range(block // size):
            rows = slice(owner * size, (owner + 1) * size)
            for first in range(0, count, group):
                held = jnp.concatenate([act[rows] for act in acts[first : first + group]], axis=0).astype(BF16)
                message_ref[owner, size * (line + first) : size * (line + first + group), :] = held


def start_all(pairs, sems, first=0):
    copies = [pltpu.make_async_copy(src, dst, sems.at[first + n]) for n, (src, dst) in enumerate(pairs)]
    for copy in copies:
        copy.start()
    return copies


def line_tokens(x_ref, line):
    return jnp.concatenate([x_ref[slot, line] for slot in range(x_ref.shape[0])], axis=0)


def project_kernel(parts, take, ins, outs, x_ref, mask_ref, gain_ref, weight_ref, sems):
    normed_ref, *message_refs = outs
    x_in, mask_in, gain_in, weight_in = ins
    lines = x_ref.shape[1]
    pairs = [(weight_in.at[0], weight_ref), (x_in, x_ref), (gain_in, gain_ref), (mask_in, mask_ref)]
    for copy in start_all(pairs, sems):
        copy.wait()
    mask = token_mask(mask_ref[...], lines)
    current = jnp.concatenate([line_tokens(x_ref, line).T for line in range(lines)], axis=1)
    normed = channel_norm(current, spread_gain(gain_ref[0:1, :]))
    emit_messages(normed, arrange(weight_ref[...], parts, take), mask, 0, message_refs, take)
    normed_ref[...] = normed


def prepare_kernel(parts, take, ins, outs):
    normed_ref, x_ref, mask_ref, gate_ref, proj_ref, out_ref, up_ref, down_ref, gain_in_ref, gain_out_ref, trans_gain_ref = ins
    gate_out, x_out, mask_out, proj_out, out_out, up_out, down_out, gains_out = outs
    lines = x_ref.shape[1]
    gate_out[...] = sigmoid(dot(gate_ref[...].T, normed_ref[...]))
    for line in range(lines):
        x_out[:, line * LANES : (line + 1) * LANES] = line_tokens(x_ref, line).T
    mask_out[...] = token_mask(mask_ref[...], lines)
    proj_out[...] = arrange(proj_ref[...], parts, take)
    for update in range(2):
        out_out[update] = out_ref[update].T
    up_out[...] = up_ref[...].T
    down_out[...] = down_ref[...].T
    rows = [gain_out_ref[0:1, :], gain_in_ref[1:2, :], gain_out_ref[1:2, :], trans_gain_ref[...]]
    for n, row in enumerate(rows):
        gains_out[n] = spread_gain(row)


def gate_kernel(ins, outs):
    normed_ref, weight_ref = ins
    outs[0][...] = sigmoid(dot(weight_ref[...].T, normed_ref[...]))


def swap_slots(parts, breadth):
    parts = list(parts)
    slot = lax.broadcasted_iota(jnp.int32, parts[0].shape, 1) // breadth
    step = 1
    while step < len(parts):
        low = (slot // step) % 2 == 0
        for first in range(len(parts)):
            if first & step:
                continue
            a, b = parts[first], parts[first | step]
            parts[first] = jnp.where(low, a, pltpu.roll(b, step * breadth, 1))
            parts[first | step] = jnp.where(low, pltpu.roll(a, LANES - step * breadth, 1), b)
        step *= 2
    return parts


def combine_kernel(rows, cols, breadth, take, outgoing, ins, outs, stage_ref):
    (both_ref,), (combined_ref,) = ins, outs
    slots = LANES // breadth
    owners, span = both_ref.shape[:2]
    size = 2 * take
    lines = span // size
    pitch = size + 1
    for owner in range(owners):
        both = both_ref[owner].astype(F32)
        for line in range(lines):
            base = (owner * lines + line) * pitch
            stage_ref[base : base + size, :] = both[line * size : (line + 1) * size]

    def whole(side, channel):
        columns = []
        for high in range(cols // slots):
            parts = []
            for low in range(slots):
                first = (high * slots + low) * rows
                held = [
                    stage_ref[pl.ds((first + row) * lines * pitch + side * take + channel, lines, stride=pitch), :]
                    for row in range(rows)
                ]
                parts.append(jnp.concatenate(held, axis=0))
            parts = swap_slots(parts, breadth)
            columns.append(
                jnp.concatenate(
                    [part[row * lines : (row + 1) * lines] for row in range(rows) for part in parts], axis=0
                )
            )
        return jnp.concatenate(columns, axis=1).astype(BF16)

    group = min(take, max(1, 16 // lines))
    for channel in range(0, take, group):
        answers = [[] for _ in range(owners)]
        for n in range(channel, channel + group):
            left, right = whole(0, n), whole(1, n)
            combined = dot(left, right, (1, 1) if outgoing else (0, 0))
            for high in range(cols // slots):
                lanes = slice(high * LANES, (high + 1) * LANES)
                parts = [
                    jnp.concatenate(
                        [
                            combined[(row * slots + slot) * lines : (row * slots + slot + 1) * lines, lanes]
                            for row in range(rows)
                        ],
                        axis=0,
                    )
                    for slot in range(slots)
                ]
                for low, part in enumerate(swap_slots(parts, breadth)):
                    for row in range(rows):
                        owner = (high * slots + low) * rows + row
                        answers[owner].append(part[row * lines : (row + 1) * lines])
        for owner, held in enumerate(answers):
            at = slice(channel * lines, (channel + group) * lines)
            combined_ref[owner, at, :] = jnp.concatenate(held, axis=0).astype(BF16)


def hold_answers(combined_refs, stage_ref):
    for part, combined_ref in enumerate(combined_refs):
        owners, span = combined_ref.shape[:2]
        for owner in range(owners):
            base = (part * owners + owner) * (span + 1)
            stage_ref[base : base + span, :] = combined_ref[owner].astype(F32)


def read_combined(stage_ref, parts, owners, take, lines, first, count):
    span = take * lines
    columns = []
    for line in range(first, first + count):
        held = [
            stage_ref[pl.ds(part * owners * (span + 1) + n * lines + line, owners, stride=span + 1), :]
            for part in range(parts)
            for n in range(take)
        ]
        columns.append(jnp.concatenate(held, axis=0))
    return jnp.concatenate(columns, axis=1)


def middle_kernel(parts, take, chunk, ins, outs, stage_ref):
    x_ref, gate_ref, mask_ref, weight_ref, out_ref, gains_ref, *combined_refs = ins
    normed_ref, next_ref, *message_refs = outs
    tokens = x_ref.shape[1]
    lines = tokens // LANES
    owners = combined_refs[0].shape[0]
    hold_answers(combined_refs, stage_ref)
    mask, weight_t = mask_ref[...], weight_ref[...]
    for start in range(0, tokens, chunk):
        here = slice(start, start + chunk)
        combined = read_combined(stage_ref, parts, owners, take, lines, start // LANES, chunk // LANES)
        hidden = channel_norm(combined, gains_ref[0])
        current = x_ref[:, here] + gate_ref[:, here] * dot(out_ref[0], hidden)
        next_ref[:, here] = current
        normed = channel_norm(current, gains_ref[1])
        normed_ref[:, here] = normed
        emit_messages(normed, weight_t, mask, start // LANES, message_refs, take)


def last_kernel(parts, take, chunk, ins, outs, stage_ref, result_ref, sems):
    x_ref, gate_ref, out_ref, up_ref, down_ref, gains_ref, *combined_refs = ins
    (result_out,) = outs
    slots, lines, breadth, channels = result_ref.shape
    owners = combined_refs[0].shape[0]
    half = down_ref.shape[1]
    count = chunk // LANES
    hold_answers(combined_refs, stage_ref)
    writes = []
    for first in range(0, lines, count):
        here = slice(first * LANES, (first + count) * LANES)
        combined = read_combined(stage_ref, parts, owners, take, lines, first, count)
        hidden = channel_norm(combined, gains_ref[2])
        current = x_ref[:, here] + gate_ref[:, here] * dot(out_ref[1], hidden)
        trans_in = channel_norm(current, gains_ref[3])
        block = min(256, half)
        for base in range(0, half, block):
            gate_part = dot(up_ref[base : base + block, :], trans_in)
            up_part = dot(up_ref[half + base : half + base + block, :], trans_in)
            trans_hidden = (gate_part * sigmoid(gate_part) * up_part).astype(BF16)
            current = current + dot(down_ref[:, base : base + block], trans_hidden)
        result = current.T
        for part in range(count):
            for slot in range(slots):
                base = part * LANES + slot * breadth
                result_ref[slot, first + part] = result[base : base + breadth]
        piece = slice(first, first + count)
        writes += start_all([(result_ref.at[:, piece], result_out.at[:, piece])], sems, first // count)
    for write in writes:
        write.wait()


def whole_spec(array):
    return pl.BlockSpec(array.shape, lambda step, dims=array.ndim: (0,) * dims)


def picked_spec(array, index):
    return pl.BlockSpec((None,) + array.shape[1:], lambda step: (index,) + (0,) * (array.ndim - 1))


def call(kernel, operands, outs, scratch=(), picks=None, in_hbm=False, out_hbm=False):
    in_place = pl.BlockSpec(memory_space=pltpu.HBM)
    specs = [
        picked_spec(array, picks[n]) if picks and n in picks else whole_spec(array)
        for n, array in enumerate(operands)
    ]
    shapes = [jax.ShapeDtypeStruct(shape, dtype) for shape, dtype in outs]
    count = len(operands)

    def body(*refs):
        kernel(refs[:count], refs[count : count + len(outs)], *refs[count + len(outs) :])

    return pl.pallas_call(
        body,
        grid=(1,),
        in_specs=[in_place] * count if in_hbm else specs,
        out_specs=[in_place if out_hbm else whole_spec(shape) for shape in shapes],
        out_shape=shapes,
        scratch_shapes=list(scratch),
        compiler_params=pltpu.CompilerParams(vmem_limit_bytes=FULL_VMEM_BYTES if in_hbm else VMEM_BYTES),
    )(*operands)


def exchange(values):
    return lax.all_to_all(values, AXES, split_axis=0, concat_axis=0, tiled=True)


def per_device(
    rows,
    cols,
    pair_map,
    pair_mask,
    gain_in,
    proj_weight,
    gate_weight,
    gain_out,
    out_weight,
    trans_gain,
    trans_up,
    trans_down,
):
    height, breadth, channels = pair_map.shape
    tokens = height * breadth
    lines = tokens // LANES
    hid = gain_out.shape[1]
    owners = rows * cols
    share = hid // owners
    parts = 2 if share % 8 == 0 else 1
    take = share // parts
    chunk = min(max(4, 8 // take) * LANES, tokens)
    messages = [((owners, 2 * take * lines, LANES), BF16)] * parts
    answer = ((owners, take * lines, LANES), BF16)
    answers = pltpu.VMEM((parts * owners * (take * lines + 1), LANES), F32)
    narrow, wide = ((channels, tokens), BF16), ((channels, tokens), F32)
    held = ((LANES // breadth, lines, breadth, channels), F32)
    grouped = pair_map.reshape(held[0])

    def combine(messages, outgoing):
        kernel = functools.partial(combine_kernel, rows, cols, breadth, take, outgoing)
        scratch = [pltpu.VMEM((owners * lines * (2 * take + 1), LANES), F32)]
        received = [exchange(both) for both in messages]
        return [exchange(call(kernel, (both,), [answer], scratch)[0]) for both in received]

    normed, *both = call(
        functools.partial(project_kernel, parts, take),
        (grouped, pair_mask, gain_in, proj_weight),
        [narrow] + messages,
        (
            pltpu.VMEM(*held),
            pltpu.VMEM(pair_mask.shape, jnp.int32),
            pltpu.VMEM(gain_in.shape, F32),
            pltpu.VMEM(proj_weight.shape[1:], BF16),
            pltpu.SemaphoreType.DMA((4,)),
        ),
        in_hbm=True,
    )
    gate, current, mask, proj_t, out_t, up_t, down_t, gains = call(
        functools.partial(prepare_kernel, parts, take),
        (
            normed,
            grouped,
            pair_mask,
            gate_weight,
            proj_weight,
            out_weight,
            trans_up,
            trans_down,
            gain_in,
            gain_out,
            trans_gain.reshape(1, -1),
        ),
        [
            wide,
            wide,
            ((lines, LANES), F32),
            (proj_weight.shape[:0:-1], BF16),
            ((2, channels, hid), BF16),
            (trans_up.shape[::-1], BF16),
            (trans_down.shape[::-1], BF16),
            ((4, channels, LANES), F32),
        ],
        picks={3: 0, 4: 1},
    )
    combined = combine(both, True)
    normed, current, *both = call(
        functools.partial(middle_kernel, parts, take, chunk),
        (current, gate, mask, proj_t, out_t, gains, *combined),
        [narrow, wide] + messages,
        (answers,),
    )
    (gate,) = call(gate_kernel, (normed, gate_weight), [wide], picks={1: 1})
    combined = combine(both, False)
    (pair_out,) = call(
        functools.partial(last_kernel, parts, take, chunk),
        (current, gate, out_t, up_t, down_t, gains, *combined),
        [held],
        (answers, pltpu.VMEM(*held), pltpu.SemaphoreType.DMA((tokens // chunk,))),
        out_hbm=True,
    )
    return pair_out.reshape(pair_map.shape)


def solution(mesh):
    rows, cols = mesh.shape["row"], mesh.shape["col"]
    spread = P(("grp", "row"), "col", None)
    in_specs = (spread, P(("grp", "row"), "col")) + (P(),) * 8

    def body(*args):
        return per_device(rows, cols, *args)

    return jax.shard_map(body, mesh=mesh, in_specs=in_specs, out_specs=spread, check_vma=False)
```

time: 80.8 us -> 113 us (1.40)
  waiting for transfers between devices: 15.9 us -> 41.3 us
  starting transfers between devices: 8.32 us -> 21.2 us
  blocking collectives: 39.2 us -> 30 us
  Pallas kernels: 11.7 us -> 14.1 us
    all_to_all x2 -> x6, waiting for transfers between devices: 15.9 us -> 41.3 us  [exchange(): return lax.all_to_all(values, AXES, split_axis=0, concat_axis=0, tiled=True)]
    all_to_all x2 -> x6, starting transfers between devices: 8.32 us -> 21.2 us  [exchange(): return lax.all_to_all(values, AXES, split_axis=0, concat_axis=0, tiled=True)]
    all_to_all x2, blocking collectives: 39.2 us -> 30 us  [exchange(): return lax.all_to_all(values, AXES, split_axis=0, concat_axis=0, tiled=True)]
    pallas_call x7 -> x9, Pallas kernels: 11.7 us -> 14.1 us  [call(): pl.pallas_call(body, grid=(1,), in_specs=[in_place] * count if in_hbm els...]
  transfers between devices with their start and end apart: 2 -> 6, of which waited for: 2 -> 6; matrix products, arithmetic and copies ran while one was open for 0% -> 0% of each run, Pallas kernels for 1% -> 6%
where the time goes in v8:
time: 113 us; the launch traced here: 112 us
  waiting for transfers between devices  41.3 us (37%)
  blocking collectives  30 us (27%)
  starting transfers between devices  21.2 us (19%)
  Pallas kernels  14.1 us (12%)
  local copies, waits for them, and re-layouts  4.95 us (4%)
    all_to_all x6, waiting for transfers between devices, exchange(): return lax.all_to_all(values, AXES, split_axis=0, concat_axis=0, tiled=True)  41.3 us
    all_to_all x2, blocking collectives, exchange(): return lax.all_to_all(values, AXES, split_axis=0, concat_axis=0, tiled=True)  30 us
    all_to_all x6, starting transfers between devices, exchange(): return lax.all_to_all(values, AXES, split_axis=0, concat_axis=0, tiled=True)  21.2 us
    pallas_call x9, Pallas kernels, call(): pl.pallas_call(body, grid=(1,), in_specs=[in_place] * count if in_hbm els...  14.1 us
    unnamed x30, local copies, waits for them, and re-layouts  4.95 us
  transfers between devices with their start and end apart: 6, of which 6 were waited for; matrix products, arithmetic and copies ran while one was open for 0% of the time, Pallas kernels for 6%

profile of v8, /device:TPU:0, one launch (start us, length us, event | category | flops | bytes accessed | tf_op | source)
XLA Modules:
  0.0 111.8 jit_solution(11538564445719675156)
XLA Ops:
  0.0 2.8 %shard_map.100 = (bf16[128,1024]{1,0:T(8,128)(2,1)}, bf16[16,64,128]{2,1,0:T(8,128)(2,1)}, bf16[16,64,128]{2,1,0:T(8,128)(2,1)}) custom-call(f32[4,8,32,128]{3,2,1,0:T(8,128)} %bitcast.3, s32[32,32]{1,0:T(8,128)} %refs_2_.3, f32[2,128]{1,0:T(2,128)} %refs_8_.1, bf16[2,128,512]{2,1,0:T(8,128)(2,1)} %refs_4_.1), custom_call_target="tpu_custom_call" | custom-call | tf_op jit(solution)/shard_map/pallas_call | solution.py:293
  2.8 17.4 %all_to_all.40.refs_0_ = bf16[16,64,128]{2,1,0:T(8,128)(2,1)S(1)} all-to-all(bf16[16,64,128]{2,1,0:T(8,128)(2,1)} %get-tuple-element.27), channel_id=1, replica_groups=mesh['grp'=2,'row'=4,'col'=4] {'col','row'}, dimensions={0} | all-to-all | bytes 524288 | tf_op jit(solution)/shard_map/all_to_all | solution.py:305
  20.2 0.0 copy-start.4
  20.2 0.0 copy-start.5
  20.2 0.0 copy-start.8
  20.2 3.7 %all-to-all-start.2 = ((bf16[16,64,128]{2,1,0:T(8,128)(2,1)}), bf16[16,64,128]{2,1,0:T(8,128)(2,1)S(1)}, u32[]{:S(2)}, u32[]{:S(2)}) async-start(bf16[16,64,128]{2,1,0:T(8,128)(2,1)} %get-tuple-element.28), calls=%async_computation.2 | async-start | bytes 524288 | tf_op jit(solution)/shard_map/all_to_all | solution.py:305
  23.9 0.0 copy-start.2
  23.9 0.0 copy-start.3
  23.9 1.6 %shard_map.102 = bf16[16,32,128]{2,1,0:T(8,128)(2,1)} custom-call(bf16[16,64,128]{2,1,0:T(8,128)(2,1)S(1)} %all_to_all.40.refs_0_), custom_call_target="tpu_custom_call" | custom-call | tf_op jit(solution)/shard_map/pallas_call | solution.py:293
  25.6 0.0 copy-start
  25.6 8.3 %all-to-all-done.2.refs_0_ = bf16[16,64,128]{2,1,0:T(8,128)(2,1)S(1)} async-done(((bf16[16,64,128]{2,1,0:T(8,128)(2,1)}), bf16[16,64,128]{2,1,0:T(8,128)(2,1)S(1)}, u32[]{:S(2)}, u32[]{:S(2)}) %all-to-all-start.2) | async-done | bytes 262176 | tf_op jit(solution)/shard_map/all_to_all | solution.py:305
  33.9 3.5 %all-to-all-start.1 = ((bf16[16,32,128]{2,1,0:T(8,128)(2,1)}), bf16[16,32,128]{2,1,0:T(8,128)(2,1)S(1)}, u32[]{:S(2)}, u32[]{:S(2)}) async-start(bf16[16,32,128]{2,1,0:T(8,128)(2,1)} %shard_map.102), calls=%async_computation.1 | async-start | bytes 262144 | tf_op jit(solution)/shard_map/all_to_all | solution.py:305
  37.4 0.0 copy-start.1
  37.4 1.7 %shard_map.103 = bf16[16,32,128]{2,1,0:T(8,128)(2,1)} custom-call(bf16[16,64,128]{2,1,0:T(8,128)(2,1)S(1)} %all-to-all-done.2.refs_0_), custom_call_target="tpu_custom_call" | custom-call | tf_op jit(solution)/shard_map/pallas_call | solution.py:293
  39.1 6.2 %all-to-all-done.1.refs_6_ = bf16[16,32,128]{2,1,0:T(8,128)(2,1)S(1)} async-done(((bf16[16,32,128]{2,1,0:T(8,128)(2,1)}), bf16[16,32,128]{2,1,0:T(8,128)(2,1)S(1)}, u32[]{:S(2)}, u32[]{:S(2)}) %all-to-all-start.1) | async-done | bytes 131104 | tf_op jit(solution)/shard_map/all_to_all | solution.py:305
  45.3 3.5 %all-to-all-start.3 = ((bf16[16,32,128]{2,1,0:T(8,128)(2,1)}), bf16[16,32,128]{2,1,0:T(8,128)(2,1)S(1)}, u32[]{:S(2)}, u32[]{:S(2)}) async-start(bf16[16,32,128]{2,1,0:T(8,128)(2,1)} %shard_map.103), calls=%async_computation.3 | async-start | bytes 262144 | tf_op jit(solution)/shard_map/all_to_all | solution.py:305
  48.8 0.0 copy-start.12
  48.9 0.0 copy-start.14
  48.9 0.0 copy-done.4
  48.9 0.0 copy-done.5
  48.9 0.0 copy-done.8
  48.9 0.0 copy-done.2
  48.9 0.0 copy-done.3
  48.9 0.0 copy-done
  48.9 0.0 copy-done.1
  48.9 0.6 copy-done.12
  49.5 0.0 copy-done.14
  49.5 0.0 copy-start.9
  49.5 0.8 copy-done.9
  50.4 0.0 copy-start.13
  50.4 0.7 copy-done.13
  51.0 0.6 shard_map.101
  51.7 0.0 copy-start.6
  51.7 0.6 copy-done.6
  52.3 0.0 copy-start.10
  52.3 0.6 copy-done.10
  52.9 3.8 %all-to-all-done.3.refs_7_ = bf16[16,32,128]{2,1,0:T(8,128)(2,1)S(1)} async-done(((bf16[16,32,128]{2,1,0:T(8,128)(2,1)}), bf16[16,32,128]{2,1,0:T(8,128)(2,1)S(1)}, u32[]{:S(2)}, u32[]{:S(2)}) %all-to-all-start.3) | async-done | bytes 131104 | tf_op jit(solution)/shard_map/all_to_all | solution.py:305
  56.7 0.0 copy-start.11
  56.7 0.7 copy-done.11
  57.4 0.0 copy-start.7
  57.4 0.9 copy-done.7
  58.3 1.7 %shard_map.104 = (bf16[128,1024]{1,0:T(8,128)(2,1)S(1)}, f32[128,1024]{1,0:T(8,128)S(1)}, bf16[16,64,128]{2,1,0:T(8,128)(2,1)S(1)}, bf16[16,64,128]{2,1,0:T(8,128)(2,1)}) custom-call(f32[128,1024]{1,0:T(8,128)S(1)} %get-tuple-element.21.refs_0_, f32[128,1024]{1,0:T(8,128)S(1)} %get-tuple-element.22.refs_1_, f32[8,128]{1,0:T(8,128)S(1)} %copy-done.11, ...), custom_call_target="tpu_custom_call" | custom-call | tf_op jit(solution)/shard_map/pallas_call | solution.py:293
  60.0 12.6 %all_to_all.41.refs_0_ = bf16[16,64,128]{2,1,0:T(8,128)(2,1)S(1)} all-to-all(bf16[16,64,128]{2,1,0:T(8,128)(2,1)S(1)} %get-tuple-element.33), channel_id=1, replica_groups=mesh['grp'=2,'row'=4,'col'=4] {'col','row'}, dimensions={0} | all-to-all | bytes 524288 | tf_op jit(solution)/shard_map/all_to_all | solution.py:305
  72.7 3.5 %all-to-all-start.6 = ((bf16[16,64,128]{2,1,0:T(8,128)(2,1)}), bf16[16,64,128]{2,1,0:T(8,128)(2,1)S(1)}, u32[]{:S(2)}, u32[]{:S(2)}) async-start(bf16[16,64,128]{2,1,0:T(8,128)(2,1)} %get-tuple-element.34), calls=%async_computation.6 | async-start | bytes 524288 | tf_op jit(solution)/shard_map/all_to_all | solution.py:305
  76.2 1.3 %shard_map.106 = bf16[16,32,128]{2,1,0:T(8,128)(2,1)} custom-call(bf16[16,64,128]{2,1,0:T(8,128)(2,1)S(1)} %all_to_all.41.refs_0_), custom_call_target="tpu_custom_call" | custom-call | tf_op jit(solution)/shard_map/pallas_call | solution.py:293
  77.5 8.7 %all-to-all-done.6.refs_0_ = bf16[16,64,128]{2,1,0:T(8,128)(2,1)S(1)} async-done(((bf16[16,64,128]{2,1,0:T(8,128)(2,1)}), bf16[16,64,128]{2,1,0:T(8,128)(2,1)S(1)}, u32[]{:S(2)}, u32[]{:S(2)}) %all-to-all-start.6) | async-done | bytes 262176 | tf_op jit(solution)/shard_map/all_to_all | solution.py:305
  86.2 3.5 %all-to-all-start.5 = ((bf16[16,32,128]{2,1,0:T(8,128)(2,1)}), bf16[16,32,128]{2,1,0:T(8,128)(2,1)S(1)}, u32[]{:S(2)}, u32[]{:S(2)}) async-start(bf16[16,32,128]{2,1,0:T(8,128)(2,1)} %shard_map.106), calls=%async_computation.5 | async-start | bytes 262144 | tf_op jit(solution)/shard_map/all_to_all | solution.py:305
  89.7 1.3 %shard_map.107 = bf16[16,32,128]{2,1,0:T(8,128)(2,1)} custom-call(bf16[16,64,128]{2,1,0:T(8,128)(2,1)S(1)} %all-to-all-done.6.refs_0_), custom_call_target="tpu_custom_call" | custom-call | tf_op jit(solution)/shard_map/pallas_call | solution.py:293
  91.0 6.6 %all-to-all-done.5.refs_6_ = bf16[16,32,128]{2,1,0:T(8,128)(2,1)S(1)} async-done(((bf16[16,32,128]{2,1,0:T(8,128)(2,1)}), bf16[16,32,128]{2,1,0:T(8,128)(2,1)S(1)}, u32[]{:S(2)}, u32[]{:S(2)}) %all-to-all-start.5) | async-done | bytes 131104 | tf_op jit(solution)/shard_map/all_to_all | solution.py:305
  97.6 3.5 %all-to-all-start.7 = ((bf16[16,32,128]{2,1,0:T(8,128)(2,1)}), bf16[16,32,128]{2,1,0:T(8,128)(2,1)S(1)}, u32[]{:S(2)}, u32[]{:S(2)}) async-start(bf16[16,32,128]{2,1,0:T(8,128)(2,1)} %shard_map.107), calls=%async_computation.7 | async-start | bytes 262144 | tf_op jit(solution)/shard_map/all_to_all | solution.py:305
  101.2 0.3 shard_map.105.refs_1_
  101.4 7.6 %all-to-all-done.7.refs_7_ = bf16[16,32,128]{2,1,0:T(8,128)(2,1)S(1)} async-done(((bf16[16,32,128]{2,1,0:T(8,128)(2,1)}), bf16[16,32,128]{2,1,0:T(8,128)(2,1)S(1)}, u32[]{:S(2)}, u32[]{:S(2)}) %all-to-all-start.7) | async-done | bytes 131104 | tf_op jit(solution)/shard_map/all_to_all | solution.py:305
  109.1 2.8 %shard_map.108 = f32[4,8,32,128]{3,2,1,0:T(8,128)} custom-call(f32[128,1024]{1,0:T(8,128)S(1)} %get-tuple-element.29.refs_0_, f32[128,1024]{1,0:T(8,128)S(1)} %shard_map.105.refs_1_, bf16[2,128,128]{2,1,0:T(8,128)(2,1)S(1)} %get-tuple-element.25.refs_4_.refs_2_, bf16[1024,128]{1,0:T(8,128)(2,1)S(1)} %get-tuple-element.31.refs_3_, ...), custom_call_target="tpu_custom_call" | custom-call | tf_op jit(solution)/shard_map/pallas_call | solution.py:293
Async XLA Ops:
  20.2 28.6 %copy-start.4 = (bf16[2,128,128]{2,1,0:T(8,128)(2,1)S(1)}, bf16[2,128,128]{2,1,0:T(8,128)(2,1)}, u32[]{:S(2)}) copy-start(bf16[2,128,128]{2,1,0:T(8,128)(2,1)} %refs_1_.3) | copy-start | bytes 196612
  20.2 28.7 %copy-start.5 = (bf16[512,128]{1,0:T(8,128)(2,1)S(1)}, bf16[512,128]{1,0:T(8,128)(2,1)}, u32[]{:S(2)}) copy-start(bf16[512,128]{1,0:T(8,128)(2,1)} %refs_7_.1) | copy-start | bytes 393220
  20.2 28.7 %copy-start.8 = (s32[32,32]{1,0:T(8,128)S(1)}, s32[32,32]{1,0:T(8,128)}, u32[]{:S(2)}) copy-start(s32[32,32]{1,0:T(8,128)} %refs_2_.3) | copy-start | bytes 12292
  20.2 13.7 %all-to-all-start.2 = ((bf16[16,64,128]{2,1,0:T(8,128)(2,1)}), bf16[16,64,128]{2,1,0:T(8,128)(2,1)S(1)}, u32[]{:S(2)}, u32[]{:S(2)}) async-start(bf16[16,64,128]{2,1,0:T(8,128)(2,1)} %get-tuple-element.28), calls=%async_computation.2 | async-start | bytes 524288 | tf_op jit(solution)/shard_map/all_to_all | solution.py:305
  23.9 25.0 %copy-start.2 = (bf16[128,1024]{1,0:T(8,128)(2,1)S(1)}, bf16[128,1024]{1,0:T(8,128)(2,1)}, u32[]{:S(2)}) copy-start(bf16[128,1024]{1,0:T(8,128)(2,1)} %refs_6_.1) | copy-start | bytes 786436
  23.9 25.0 %copy-start.3 = (bf16[128,1024]{1,0:T(8,128)(2,1)S(1)}, bf16[128,1024]{1,0:T(8,128)(2,1)}, u32[]{:S(2)}) copy-start(bf16[128,1024]{1,0:T(8,128)(2,1)} %get-tuple-element.20.refs_0_) | copy-start | bytes 786436
  25.6 23.3 %copy-start = (f32[32,32,128]{2,1,0:T(8,128)S(1)}, f32[32,32,128]{2,1,0:T(8,128)}, u32[]{:S(2)}) copy-start(f32[32,32,128]{2,1,0:T(8,128)} %param.10) | copy-start | bytes 1572868
  33.9 11.4 %all-to-all-start.1 = ((bf16[16,32,128]{2,1,0:T(8,128)(2,1)}), bf16[16,32,128]{2,1,0:T(8,128)(2,1)S(1)}, u32[]{:S(2)}, u32[]{:S(2)}) async-start(bf16[16,32,128]{2,1,0:T(8,128)(2,1)} %shard_map.102), calls=%async_computation.1 | async-start | bytes 262144 | tf_op jit(solution)/shard_map/all_to_all | solution.py:305
  37.4 11.5 %copy-start.1 = (bf16[2,128,512]{2,1,0:T(8,128)(2,1)S(1)}, bf16[2,128,512]{2,1,0:T(8,128)(2,1)}, u32[]{:S(2)}) copy-start(bf16[2,128,512]{2,1,0:T(8,128)(2,1)} %refs_4_.1) | copy-start | bytes 786436
  45.3 11.4 %all-to-all-start.3 = ((bf16[16,32,128]{2,1,0:T(8,128)(2,1)}), bf16[16,32,128]{2,1,0:T(8,128)(2,1)S(1)}, u32[]{:S(2)}, u32[]{:S(2)}) async-start(bf16[16,32,128]{2,1,0:T(8,128)(2,1)} %shard_map.103), calls=%async_computation.3 | async-start | bytes 262144 | tf_op jit(solution)/shard_map/all_to_all | solution.py:305
  48.8 0.7 copy-start.12
  48.9 0.7 copy-start.14
  49.5 0.8 copy-start.9
  50.4 0.7 copy-start.13
  51.7 0.7 copy-start.6
  52.3 0.6 copy-start.10
  56.7 0.7 copy-start.11
  57.4 0.9 copy-start.7
  72.7 13.5 %all-to-all-start.6 = ((bf16[16,64,128]{2,1,0:T(8,128)(2,1)}), bf16[16,64,128]{2,1,0:T(8,128)(2,1)S(1)}, u32[]{:S(2)}, u32[]{:S(2)}) async-start(bf16[16,64,128]{2,1,0:T(8,128)(2,1)} %get-tuple-element.34), calls=%async_computation.6 | async-start | bytes 524288 | tf_op jit(solution)/shard_map/all_to_all | solution.py:305
  86.2 11.4 %all-to-all-start.5 = ((bf16[16,32,128]{2,1,0:T(8,128)(2,1)}), bf16[16,32,128]{2,1,0:T(8,128)(2,1)S(1)}, u32[]{:S(2)}, u32[]{:S(2)}) async-start(bf16[16,32,128]{2,1,0:T(8,128)(2,1)} %shard_map.106), calls=%async_computation.5 | async-start | bytes 262144 | tf_op jit(solution)/shard_map/all_to_all | solution.py:305
  97.6 11.4 %all-to-all-start.7 = ((bf16[16,32,128]{2,1,0:T(8,128)(2,1)}), bf16[16,32,128]{2,1,0:T(8,128)(2,1)S(1)}, u32[]{:S(2)}, u32[]{:S(2)}) async-start(bf16[16,32,128]{2,1,0:T(8,128)(2,1)} %shard_map.107), calls=%async_computation.7 | async-start | bytes 262144 | tf_op jit(solution)/shard_map/all_to_all | solution.py:305

commit v9 on v7

--- a/solution.py
+++ b/solution.py
@@ -9,7 +9,7 @@
 
 AXES = ("col", "row")
 LANES = 128
-VMEM_BYTES = 48 * 1024 * 1024
+VMEM_BYTES = 24 * 1024 * 1024
 FULL_VMEM_BYTES = 60 * 1024 * 1024
 F32, BF16 = jnp.float32, jnp.bfloat16
 
@@ -95,26 +95,15 @@
 
 
 def prepare_kernel(ins, outs):
-    normed_ref, x_ref, mask_ref, gate_ref, proj_ref, out_ref, up_ref, down_ref, gain_in_ref, gain_out_ref, trans_gain_ref = ins
-    gate_out, x_out, mask_out, proj_out, out_out, up_out, down_out, gains_out = outs
+    normed_ref, x_ref, mask_ref, gate_ref, gain_in_ref, gain_out_ref, trans_gain_ref = ins
+    gate_out, x_out, mask_out, gains_out = outs
     lines = x_ref.shape[1]
     gate_out[...] = sigmoid(dot(gate_ref[...].T, normed_ref[...]))
     for line in range(lines):
         x_out[:, line * LANES : (line + 1) * LANES] = line_tokens(x_ref, line).T
     mask_out[...] = token_mask(mask_ref[...], lines)
-    proj_out[...] = proj_ref[...].T
-    for update in range(2):
-        out_out[update] = out_ref[update].T
-    up_out[...] = up_ref[...].T
-    down_out[...] = down_ref[...].T
     rows = [gain_out_ref[0:1, :], gain_in_ref[1:2, :], gain_out_ref[1:2, :], trans_gain_ref[...]]
-    for n, row in enumerate(rows):
-        gains_out[n] = spread_gain(row)
-
-
-def gate_kernel(ins, outs):
-    normed_ref, weight_ref = ins
-    outs[0][...] = sigmoid(dot(weight_ref[...].T, normed_ref[...]))
+    gains_out[...] = jnp.concatenate(rows + rows, axis=0)
 
 
 def swap_slots(parts, breadth):
@@ -138,7 +127,7 @@
 
 
 def combine_kernel(rows, cols, breadth, share, outgoing, ins, outs, stage_ref, result_ref):
-    (both_ref,), (combined_ref,) = ins, outs
+    both_ref, combined_ref = ins[0], outs[0]
     slots = LANES // breadth
     owners, span = both_ref.shape[:2]
     lines = span // (2 * share)
@@ -220,45 +209,49 @@
 
 
 def middle_kernel(share, chunk, ins, outs, stage_ref, message_stage_ref):
-    combined_ref, x_ref, gate_ref, mask_ref, weight_ref, out_ref, gains_ref = ins
-    message_ref, normed_ref, next_ref = outs
+    combined_ref, x_ref, gate_ref, mask_ref, gains_ref, proj_ref, gate_weight_ref, out_ref = ins
+    message_ref, gate_out, next_ref = outs
     tokens = x_ref.shape[1]
     lines = tokens // LANES
     owners = combined_ref.shape[0]
     stage_ref[...] = combined_ref[...].astype(F32).reshape(stage_ref.shape)
     mask = mask_ref[...]
+    gain_out, gain = [spread_gain(gains_ref[n : n + 1, :]) for n in (0, 1)]
+    out_t, proj_t, gate_t = out_ref[...].T, proj_ref[...].T, gate_weight_ref[...].T
     for start in range(0, tokens, chunk):
         here = slice(start, start + chunk)
         combined = read_combined(stage_ref, owners, lines, share, start // LANES, chunk // LANES)
-        hidden = channel_norm(combined, gains_ref[0])
-        current = x_ref[:, here] + gate_ref[:, here] * dot(out_ref[0], hidden)
+        hidden = channel_norm(combined, gain_out)
+        current = x_ref[:, here] + gate_ref[:, here] * dot(out_t, hidden)
         next_ref[:, here] = current
-        normed = channel_norm(current, gains_ref[1])
-        emit_message(normed, weight_ref[...], mask, start // LANES, message_ref, message_stage_ref, share)
-        normed_ref[:, here] = normed
+        normed = channel_norm(current, gain)
+        emit_message(normed, proj_t, mask, start // LANES, message_ref, message_stage_ref, share)
+        gate_out[:, here] = sigmoid(dot(gate_t, normed))
 
 
 def last_kernel(share, chunk, ins, outs, stage_ref, result_ref, sems):
-    combined_ref, x_ref, gate_ref, out_ref, up_ref, down_ref, gains_ref = ins
+    combined_ref, x_ref, gate_ref, gains_ref, out_ref, up_ref, down_ref = ins
     (result_out,) = outs
     slots, lines, breadth, channels = result_ref.shape
     owners = combined_ref.shape[0]
-    half = down_ref.shape[1]
+    half = down_ref.shape[0]
     count = chunk // LANES
+    gain_out, gain = [spread_gain(gains_ref[n : n + 1, :]) for n in (2, 3)]
+    out_t, up_t, down_t = out_ref[...].T, up_ref[...].T, down_ref[...].T
     stage_ref[...] = combined_ref[...].astype(F32).reshape(stage_ref.shape)
     writes = []
     for first in range(0, lines, count):
         here = slice(first * LANES, (first + count) * LANES)
         combined = read_combined(stage_ref, owners, lines, share, first, count)
-        hidden = channel_norm(combined, gains_ref[2])
-        current = x_ref[:, here] + gate_ref[:, here] * dot(out_ref[1], hidden)
-        trans_in = channel_norm(current, gains_ref[3])
+        hidden = channel_norm(combined, gain_out)
+        current = x_ref[:, here] + gate_ref[:, here] * dot(out_t, hidden)
+        trans_in = channel_norm(current, gain)
         block = min(256, half)
         for base in range(0, half, block):
-            gate_part = dot(up_ref[base : base + block, :], trans_in)
-            up_part = dot(up_ref[half + base : half + base + block, :], trans_in)
+            gate_part = dot(up_t[base : base + block], trans_in)
+            up_part = dot(up_t[half + base : half + base + block], trans_in)
             trans_hidden = (gate_part * sigmoid(gate_part) * up_part).astype(BF16)
-            current = current + dot(down_ref[:, base : base + block], trans_hidden)
+            current = current + dot(down_t[:, base : base + block], trans_hidden)
         result = current.T
         for part in range(count):
             for slot in range(slots):
@@ -334,10 +327,10 @@
     held = ((LANES // breadth, lines, breadth, channels), F32)
     grouped = pair_map.reshape(held[0])
 
-    def combine(both, outgoing):
+    def combine(operands, outgoing):
         kernel = functools.partial(combine_kernel, rows, cols, breadth, share, outgoing)
         scratch = [pltpu.VMEM((sides * owners * lines * pitch_of(share), LANES), F32) for sides in (2, 1)]
-        return call(kernel, (both,), [answer], scratch)[0]
+        return call(kernel, operands, [answer], scratch)[0]
 
     both, normed = call(
         functools.partial(project_kernel, share),
@@ -353,47 +346,27 @@
         ),
         in_hbm=True,
     )
-    gate, current, mask, proj_t, out_t, up_t, down_t, gains = call(
+    gate, current, mask, gains = call(
         prepare_kernel,
-        (
-            normed,
-            grouped,
-            pair_mask,
-            gate_weight,
-            proj_weight,
-            out_weight,
-            trans_up,
-            trans_down,
-            gain_in,
-            gain_out,
-            trans_gain.reshape(1, -1),
-        ),
-        [
-            wide,
-            wide,
-            ((lines, LANES), F32),
-            (proj_weight.shape[:0:-1], BF16),
-            ((2, channels, hid), BF16),
-            (trans_up.shape[::-1], BF16),
-            (trans_down.shape[::-1], BF16),
-            ((4, channels, LANES), F32),
-        ],
-        picks={3: 0, 4: 1},
-    )
-    combined = exchange(combine(exchange(both), True))
-    both, normed, current = call(
+        (normed, grouped, pair_mask, gate_weight, gain_in, gain_out, trans_gain.reshape(1, -1)),
+        [wide, wide, ((lines, LANES), F32), ((8, channels), F32)],
+        picks={3: 0},
+    )
+    combined = exchange(combine((exchange(both), mask), True))
+    both, gate, current = call(
         functools.partial(middle_kernel, share, chunk),
-        (combined, current, gate, mask, proj_t, out_t, gains),
-        [message, narrow, wide],
+        (combined, current, gate, mask, gains, proj_weight, gate_weight, out_weight),
+        [message, wide, wide],
         (result, spare),
-    )
-    (gate,) = call(gate_kernel, (normed, gate_weight), [wide], picks={1: 1})
-    combined = exchange(combine(exchange(both), False))
+        picks={5: 1, 6: 1, 7: 0},
+    )
+    combined = exchange(combine((exchange(both),), False))
     (pair_out,) = call(
         functools.partial(last_kernel, share, chunk),
-        (combined, current, gate, out_t, up_t, down_t, gains),
+        (combined, current, gate, gains, out_weight, trans_up, trans_down),
         [held],
         (result, pltpu.VMEM(*held), pltpu.SemaphoreType.DMA((tokens // chunk,))),
+        picks={4: 1},
         out_hbm=True,
     )
     return pair_out.reshape(pair_map.shape)

time: 80.8 us -> 77.5 us (0.959)
  blocking collectives: 39.2 us -> 45.4 us
  local copies, waits for them, and re-layouts: 4.96 us -> 0.67 us
  waiting for transfers between devices: 15.9 us -> 13.5 us
  Pallas kernels: 11.7 us -> 9.86 us
  starting transfers between devices: 8.32 us -> 7.51 us
    all_to_all x2 -> x3, blocking collectives: 39.2 us -> 45.4 us  [exchange(): return lax.all_to_all(values, AXES, split_axis=0, concat_axis=0, tiled=True)]
    unnamed x30 -> x22, local copies, waits for them, and re-layouts: 4.96 us -> 0.67 us
    all_to_all x2 -> x1, waiting for transfers between devices: 15.9 us -> 13.5 us  [exchange(): return lax.all_to_all(values, AXES, split_axis=0, concat_axis=0, tiled=True)]
    pallas_call x7 -> x6, Pallas kernels: 11.7 us -> 9.86 us  [call(): pl.pallas_call(body, grid=(1,), in_specs=[in_place] * count if in_hbm els...]
    all_to_all x2 -> x1, starting transfers between devices: 8.32 us -> 7.51 us  [exchange(): return lax.all_to_all(values, AXES, split_axis=0, concat_axis=0, tiled=True)]
  transfers between devices with their start and end apart: 2 -> 1, of which waited for: 2 -> 1; matrix products, arithmetic and copies ran while one was open for 0% -> 0% of each run, Pallas kernels for 1% -> 0%
where the time goes in v9:
time: 77.5 us; the launch traced here: 77.1 us
  blocking collectives  45.4 us (59%)
  waiting for transfers between devices  13.5 us (17%)
  Pallas kernels  9.86 us (13%)
  starting transfers between devices  7.51 us (10%)
    all_to_all x3, blocking collectives, exchange(): return lax.all_to_all(values, AXES, split_axis=0, concat_axis=0, tiled=True)  45.4 us
    all_to_all x1, waiting for transfers between devices, exchange(): return lax.all_to_all(values, AXES, split_axis=0, concat_axis=0, tiled=True)  13.5 us
    pallas_call x6, Pallas kernels, call(): pl.pallas_call(body, grid=(1,), in_specs=[in_place] * count if in_hbm els...  9.86 us
    all_to_all x1, starting transfers between devices, exchange(): return lax.all_to_all(values, AXES, split_axis=0, concat_axis=0, tiled=True)  7.51 us
  transfers between devices with their start and end apart: 1, of which 1 were waited for; matrix products, arithmetic and copies ran while one was open for 0% of the time, Pallas kernels for 0%

profile of v9, /device:TPU:0, one launch (start us, length us, event | category | flops | bytes accessed | tf_op | source)
XLA Modules:
  0.0 77.1 jit_solution(14290911603316883822)
XLA Ops:
  0.0 2.6 %shard_map.100 = (bf16[16,128,128]{2,1,0:T(8,128)(2,1)}, bf16[128,1024]{1,0:T(8,128)(2,1)}) custom-call(f32[4,8,32,128]{3,2,1,0:T(8,128)} %bitcast.3, s32[32,32]{1,0:T(8,128)} %refs_2_.3, f32[2,128]{1,0:T(2,128)} %refs_4_.2, bf16[2,128,512]{2,1,0:T(8,128)(2,1)} %refs_5_.4), custom_call_target="tpu_custom_call" | custom-call | tf_op jit(solution)/shard_map/pallas_call | solution.py:286
  2.6 0.0 copy-start
  2.6 0.0 copy-start.3
  2.6 0.0 copy-start.4
  2.6 0.0 copy-start.7
  2.6 0.0 copy-start.9
  2.6 7.5 %all-to-all-start = ((bf16[16,128,128]{2,1,0:T(8,128)(2,1)}), bf16[16,128,128]{2,1,0:T(8,128)(2,1)S(1)}, u32[]{:S(2)}, u32[]{:S(2)}) async-start(bf16[16,128,128]{2,1,0:T(8,128)(2,1)} %get-tuple-element.14), calls=%async_computation | async-start | bytes 1048576 | tf_op jit(solution)/shard_map/all_to_all | solution.py:298
  10.2 0.0 copy-start.8
  10.2 0.0 copy-start.10
  10.2 0.0 copy-done
  10.2 0.0 copy-done.3
  10.2 0.0 copy-done.4
  10.2 0.0 copy-done.7
  10.2 0.0 copy-done.9
  10.2 0.6 copy-done.8
  10.8 0.0 copy-done.10
  10.8 0.3 shard_map.101
  11.1 13.5 %all-to-all-done.refs_0_ = bf16[16,128,128]{2,1,0:T(8,128)(2,1)S(1)} async-done(((bf16[16,128,128]{2,1,0:T(8,128)(2,1)}), bf16[16,128,128]{2,1,0:T(8,128)(2,1)S(1)}, u32[]{:S(2)}, u32[]{:S(2)}) %all-to-all-start) | async-done | bytes 524320 | tf_op jit(solution)/shard_map/all_to_all | solution.py:298
  24.6 1.3 %shard_map.102 = bf16[16,64,128]{2,1,0:T(8,128)(2,1)S(1)} custom-call(bf16[16,128,128]{2,1,0:T(8,128)(2,1)S(1)} %all-to-all-done.refs_0_, f32[8,128]{1,0:T(8,128)S(1)} %get-tuple-element.16.refs_1_.refs_3_), custom_call_target="tpu_custom_call" | custom-call | tf_op jit(solution)/shard_map/pallas_call | solution.py:286
  26.0 0.0 copy-start.1
  26.0 0.0 copy-start.5
  26.0 14.1 %all_to_all.20.refs_0_ = bf16[16,64,128]{2,1,0:T(8,128)(2,1)S(1)} all-to-all(bf16[16,64,128]{2,1,0:T(8,128)(2,1)S(1)} %shard_map.102), channel_id=1, replica_groups=mesh['grp'=2,'row'=4,'col'=4] {'col','row'}, dimensions={0} | all-to-all | bytes 524288 | tf_op jit(solution)/shard_map/all_to_all | solution.py:298
  40.1 0.0 copy-done.1
  40.1 0.0 copy-done.5
  40.1 1.1 %shard_map.103 = (bf16[16,128,128]{2,1,0:T(8,128)(2,1)S(1)}, f32[128,1024]{1,0:T(8,128)S(1)}, f32[128,1024]{1,0:T(8,128)S(1)}) custom-call(bf16[16,64,128]{2,1,0:T(8,128)(2,1)S(1)} %all_to_all.20.refs_0_, f32[128,1024]{1,0:T(8,128)S(1)} %get-tuple-element.17.refs_1_, f32[128,1024]{1,0:T(8,128)S(1)} %get-tuple-element.18.refs_2_, ...), custom_call_target="tpu_custom_call" | custom-call | tf_op jit(solution)/shard_map/pallas_call | solution.py:286
  41.2 17.2 %all_to_all.21.refs_0_ = bf16[16,128,128]{2,1,0:T(8,128)(2,1)S(1)} all-to-all(bf16[16,128,128]{2,1,0:T(8,128)(2,1)S(1)} %get-tuple-element.20), channel_id=1, replica_groups=mesh['grp'=2,'row'=4,'col'=4] {'col','row'}, dimensions={0} | all-to-all | bytes 1048576 | tf_op jit(solution)/shard_map/all_to_all | solution.py:298
  58.4 1.8 %shard_map.104 = bf16[16,64,128]{2,1,0:T(8,128)(2,1)S(1)} custom-call(bf16[16,128,128]{2,1,0:T(8,128)(2,1)S(1)} %all_to_all.21.refs_0_), custom_call_target="tpu_custom_call" | custom-call | tf_op jit(solution)/shard_map/pallas_call | solution.py:286
  60.2 0.0 copy-start.2
  60.3 0.0 copy-start.6
  60.3 14.1 %all_to_all.22.refs_0_ = bf16[16,64,128]{2,1,0:T(8,128)(2,1)S(1)} all-to-all(bf16[16,64,128]{2,1,0:T(8,128)(2,1)S(1)} %shard_map.104), channel_id=1, replica_groups=mesh['grp'=2,'row'=4,'col'=4] {'col','row'}, dimensions={0} | all-to-all | bytes 524288 | tf_op jit(solution)/shard_map/all_to_all | solution.py:298
  74.4 0.0 copy-done.2
  74.4 0.0 copy-done.6
  74.4 2.8 %shard_map.105 = f32[4,8,32,128]{3,2,1,0:T(8,128)} custom-call(bf16[16,64,128]{2,1,0:T(8,128)(2,1)S(1)} %all_to_all.22.refs_0_, f32[128,1024]{1,0:T(8,128)S(1)} %get-tuple-element.21.refs_1_, f32[128,1024]{1,0:T(8,128)S(1)} %get-tuple-element.22.refs_2_, f32[8,128]{1,0:T(8,128)S(1)} %get-tuple-element.19.refs_4_.refs_3_, bf16[2,128,128]{2,1,0:T(8,128)(2,1)S(1)} %copy-done.5, ...), custom_call_target="tpu_custom_call" | custom-call | tf_op jit(solution)/shard_map/pallas_call | solution.py:286
Async XLA Ops:
  2.6 7.6 %copy-start = (f32[32,32,128]{2,1,0:T(8,128)S(1)}, f32[32,32,128]{2,1,0:T(8,128)}, u32[]{:S(2)}) copy-start(f32[32,32,128]{2,1,0:T(8,128)} %param.10) | copy-start | bytes 1572868
  2.6 7.6 %copy-start.3 = (bf16[128,1024]{1,0:T(8,128)(2,1)S(1)}, bf16[128,1024]{1,0:T(8,128)(2,1)}, u32[]{:S(2)}) copy-start(bf16[128,1024]{1,0:T(8,128)(2,1)} %get-tuple-element.15.refs_0_) | copy-start | bytes 786436
  2.6 7.6 %copy-start.4 = (bf16[2,128,128]{2,1,0:T(8,128)(2,1)S(1)}, bf16[2,128,128]{2,1,0:T(8,128)(2,1)}, u32[]{:S(2)}) copy-start(bf16[2,128,128]{2,1,0:T(8,128)(2,1)} %refs_6_.2) | copy-start | bytes 196612
  2.6 7.6 %copy-start.7 = (s32[32,32]{1,0:T(8,128)S(1)}, s32[32,32]{1,0:T(8,128)}, u32[]{:S(2)}) copy-start(s32[32,32]{1,0:T(8,128)} %refs_2_.3) | copy-start | bytes 12292
  2.6 7.6 %copy-start.9 = (f32[2,128]{1,0:T(2,128)S(1)}, f32[2,128]{1,0:T(2,128)}, u32[]{:S(2)}) copy-start(f32[2,128]{1,0:T(2,128)} %refs_5_.3) | copy-start | bytes 3076
  2.6 22.0 %all-to-all-start = ((bf16[16,128,128]{2,1,0:T(8,128)(2,1)}), bf16[16,128,128]{2,1,0:T(8,128)(2,1)S(1)}, u32[]{:S(2)}, u32[]{:S(2)}) async-start(bf16[16,128,128]{2,1,0:T(8,128)(2,1)} %get-tuple-element.14), calls=%async_computation | async-start | bytes 1048576 | tf_op jit(solution)/shard_map/all_to_all | solution.py:298
  10.2 0.7 copy-start.8
  10.2 0.7 copy-start.10
  26.0 14.1 %copy-start.1 = (bf16[2,128,512]{2,1,0:T(8,128)(2,1)S(1)}, bf16[2,128,512]{2,1,0:T(8,128)(2,1)}, u32[]{:S(2)}) copy-start(bf16[2,128,512]{2,1,0:T(8,128)(2,1)} %refs_5_.4) | copy-start | bytes 786436
  26.0 14.1 %copy-start.5 = (bf16[2,128,128]{2,1,0:T(8,128)(2,1)S(1)}, bf16[2,128,128]{2,1,0:T(8,128)(2,1)}, u32[]{:S(2)}) copy-start(bf16[2,128,128]{2,1,0:T(8,128)(2,1)} %refs_4_.3) | copy-start | bytes 196612
  60.2 14.1 %copy-start.2 = (bf16[128,1024]{1,0:T(8,128)(2,1)S(1)}, bf16[128,1024]{1,0:T(8,128)(2,1)}, u32[]{:S(2)}) copy-start(bf16[128,1024]{1,0:T(8,128)(2,1)} %refs_5_.5) | copy-start | bytes 786436
  60.3 14.1 %copy-start.6 = (bf16[512,128]{1,0:T(8,128)(2,1)S(1)}, bf16[512,128]{1,0:T(8,128)(2,1)}, u32[]{:S(2)}) copy-start(bf16[512,128]{1,0:T(8,128)(2,1)} %refs_6_.3) | copy-start | bytes 393220

commit v10 on v9

--- a/solution.py
+++ b/solution.py
@@ -5,9 +5,11 @@
 from jax import lax
 from jax.experimental import pallas as pl
 from jax.experimental.pallas import tpu as pltpu
+from jax.sharding import Mesh
 from jax.sharding import PartitionSpec as P
 
-AXES = ("col", "row")
+NEAR_AXES = ("near", "row")
+ALL_AXES = ("half", "near", "row")
 LANES = 128
 VMEM_BYTES = 24 * 1024 * 1024
 FULL_VMEM_BYTES = 60 * 1024 * 1024
@@ -126,7 +128,7 @@
     return share + 1 if share % 8 == 0 else share
 
 
-def combine_kernel(rows, cols, breadth, share, outgoing, ins, outs, stage_ref, result_ref):
+def combine_kernel(rows, cols, near, breadth, share, outgoing, ins, outs, stage_ref, result_ref):
     both_ref, combined_ref = ins[0], outs[0]
     slots = LANES // breadth
     owners, span = both_ref.shape[:2]
@@ -148,12 +150,12 @@
             return pl.ds((2 * owner + side) * lines * pitch + channel, lines, stride=pitch)
         return pl.ds(owner * span + side * share + channel, lines, stride=2 * share)
 
-    def whole(side, channel):
+    def whole(side, wanted):
+        places = [(channel, col) for channel in wanted for col in range(near)]
         columns = []
-        for high in range(cols // slots):
+        for first in range(0, len(places), slots):
             parts = []
-            for low in range(slots):
-                col = high * slots + low
+            for channel, col in places[first : first + slots]:
                 held = [stage_ref[line_rows(col * rows + row, side, channel), :] for row in range(rows)]
                 parts.append(jnp.concatenate(held, axis=0))
             parts = swap_slots(parts, breadth)
@@ -164,27 +166,34 @@
             )
         return jnp.concatenate(columns, axis=1).astype(BF16)
 
-    for channel in range(share):
-        left, right = whole(0, channel), whole(1, channel)
-        combined = dot(left, right, (1, 1) if outgoing else (0, 0))
-        for high in range(cols // slots):
-            lanes = slice(high * LANES, (high + 1) * LANES)
-            parts = [
-                jnp.concatenate(
-                    [
-                        combined[(row * slots + slot) * lines : (row * slots + slot + 1) * lines, lanes]
-                        for row in range(rows)
-                    ],
-                    axis=0,
-                )
-                for slot in range(slots)
-            ]
-            for low, part in enumerate(swap_slots(parts, breadth)):
-                for row in range(rows):
-                    base = ((high * slots + low) * rows + row) * lines * pitch + channel
-                    result_ref[pl.ds(base, lines, stride=pitch), :] = part[row * lines : (row + 1) * lines]
+    group = max(1, slots // near)
+    for base in range(0, share, group):
+        wanted = range(base, base + group)
+        left, right = whole(0, wanted), whole(1, wanted)
+        for place, channel in enumerate(wanted):
+            mine = left
+            if group > 1:
+                lane = lax.broadcasted_iota(jnp.int32, left.shape, 1)
+                mine = jnp.where(lane // (near * breadth) == place, left, jnp.zeros_like(left))
+            combined = dot(mine, right, (1, 1) if outgoing else (0, 0))
+            for high in range(cols // slots):
+                lanes = slice(high * LANES, (high + 1) * LANES)
+                parts = [
+                    jnp.concatenate(
+                        [
+                            combined[(row * slots + slot) * lines : (row * slots + slot + 1) * lines, lanes]
+                            for row in range(rows)
+                        ],
+                        axis=0,
+                    )
+                    for slot in range(slots)
+                ]
+                for low, part in enumerate(swap_slots(parts, breadth)):
+                    for row in range(rows):
+                        at = ((high * slots + low) * rows + row) * lines * pitch + channel
+                        result_ref[pl.ds(at, lines, stride=pitch), :] = part[row * lines : (row + 1) * lines]
     if padded:
-        for owner in range(owners):
+        for owner in range(rows * cols):
             held = [
                 result_ref[(owner * lines + line) * pitch : (owner * lines + line) * pitch + share, :]
                 for line in range(lines)
@@ -192,6 +201,14 @@
             combined_ref[owner] = jnp.concatenate(held, axis=0).astype(BF16)
     else:
         combined_ref[...] = result_ref[...].astype(BF16).reshape(combined_ref.shape)
+
+
+def hold_combined(combined_ref, stage_ref):
+    owners = stage_ref.shape[0] // combined_ref.shape[1]
+    total = combined_ref[:owners].astype(F32)
+    for first in range(owners, combined_ref.shape[0], owners):
+        total = total + combined_ref[first : first + owners].astype(F32)
+    stage_ref[...] = total.reshape(stage_ref.shape)
 
 
 def read_combined(stage_ref, owners, lines, share, first, count):
@@ -208,13 +225,13 @@
     return jnp.concatenate(columns, axis=1)
 
 
-def middle_kernel(share, chunk, ins, outs, stage_ref, message_stage_ref):
+def middle_kernel(share, next_share, chunk, ins, outs, stage_ref, message_stage_ref):
     combined_ref, x_ref, gate_ref, mask_ref, gains_ref, proj_ref, gate_weight_ref, out_ref = ins
     message_ref, gate_out, next_ref = outs
     tokens = x_ref.shape[1]
     lines = tokens // LANES
-    owners = combined_ref.shape[0]
-    stage_ref[...] = combined_ref[...].astype(F32).reshape(stage_ref.shape)
+    owners = x_ref.shape[0] // share
+    hold_combined(combined_ref, stage_ref)
     mask = mask_ref[...]
     gain_out, gain = [spread_gain(gains_ref[n : n + 1, :]) for n in (0, 1)]
     out_t, proj_t, gate_t = out_ref[...].T, proj_ref[...].T, gate_weight_ref[...].T
@@ -225,7 +242,7 @@
         current = x_ref[:, here] + gate_ref[:, here] * dot(out_t, hidden)
         next_ref[:, here] = current
         normed = channel_norm(current, gain)
-        emit_message(normed, proj_t, mask, start // LANES, message_ref, message_stage_ref, share)
+        emit_message(normed, proj_t, mask, start // LANES, message_ref, message_stage_ref, next_share)
         gate_out[:, here] = sigmoid(dot(gate_t, normed))
 
 
@@ -233,12 +250,12 @@
     combined_ref, x_ref, gate_ref, gains_ref, out_ref, up_ref, down_ref = ins
     (result_out,) = outs
     slots, lines, breadth, channels = result_ref.shape
-    owners = combined_ref.shape[0]
+    owners = x_ref.shape[0] // share
     half = down_ref.shape[0]
     count = chunk // LANES
     gain_out, gain = [spread_gain(gains_ref[n : n + 1, :]) for n in (2, 3)]
     out_t, up_t, down_t = out_ref[...].T, up_ref[...].T, down_ref[...].T
-    stage_ref[...] = combined_ref[...].astype(F32).reshape(stage_ref.shape)
+    hold_combined(combined_ref, stage_ref)
     writes = []
     for first in range(0, lines, count):
         here = slice(first * LANES, (first + count) * LANES)
@@ -294,13 +311,14 @@
     )(*operands)
 
 
-def exchange(values):
-    return lax.all_to_all(values, AXES, split_axis=0, concat_axis=0, tiled=True)
+def exchange(values, axes):
+    return lax.all_to_all(values, axes, split_axis=0, concat_axis=0, tiled=True)
 
 
 def per_device(
     rows,
-    cols,
+    halves,
+    nears,
     pair_map,
     pair_mask,
     gain_in,
@@ -316,26 +334,33 @@
     tokens = height * breadth
     lines = tokens // LANES
     hid = gain_out.shape[1]
+    cols = halves * nears
     owners = rows * cols
     share = hid // owners
     chunk = min(4 * LANES, tokens)
-    message = ((owners, 2 * share * lines, LANES), BF16)
-    answer = ((owners, share * lines, LANES), BF16)
+    split = halves if share % 8 == 0 else 1
+    first_share = split * share
+    held = ((LANES // breadth, lines, breadth, channels), F32)
+    grouped = pair_map.reshape(held[0])
+    wide, narrow = ((channels, tokens), F32), ((channels, tokens), BF16)
     result = pltpu.VMEM((owners * share * lines, LANES), F32)
     spare = pltpu.VMEM((8, LANES) if share % 8 == 0 else (owners * 2 * share * lines, LANES), F32)
-    narrow, wide = ((channels, tokens), BF16), ((channels, tokens), F32)
-    held = ((LANES // breadth, lines, breadth, channels), F32)
-    grouped = pair_map.reshape(held[0])
-
-    def combine(operands, outgoing):
-        kernel = functools.partial(combine_kernel, rows, cols, breadth, share, outgoing)
-        scratch = [pltpu.VMEM((sides * owners * lines * pitch_of(share), LANES), F32) for sides in (2, 1)]
-        return call(kernel, operands, [answer], scratch)[0]
+
+    def message(own):
+        return ((hid // own, 2 * own * lines, LANES), BF16)
+
+    def combine(operands, own, outgoing):
+        near = cols * share // own
+        kernel = functools.partial(combine_kernel, rows, cols, near, breadth, own, outgoing)
+        block = lines * pitch_of(own)
+        scratch = [pltpu.VMEM((count * block, LANES), F32) for count in (2 * rows * near, owners)]
+        answer = ((owners, own * lines, LANES), BF16)
+        return exchange(call(kernel, operands, [answer], scratch)[0], ALL_AXES)
 
     both, normed = call(
-        functools.partial(project_kernel, share),
+        functools.partial(project_kernel, first_share),
         (grouped, pair_mask, gain_in, proj_weight),
-        [message, narrow],
+        [message(first_share), narrow],
         (
             spare,
             pltpu.VMEM(*held),
@@ -352,15 +377,16 @@
         [wide, wide, ((lines, LANES), F32), ((8, channels), F32)],
         picks={3: 0},
     )
-    combined = exchange(combine((exchange(both), mask), True))
+    both = exchange(both, NEAR_AXES if split > 1 else ALL_AXES)
+    combined = combine((both, mask), first_share, True)
     both, gate, current = call(
-        functools.partial(middle_kernel, share, chunk),
+        functools.partial(middle_kernel, first_share, share, chunk),
         (combined, current, gate, mask, gains, proj_weight, gate_weight, out_weight),
-        [message, wide, wide],
+        [message(share), wide, wide],
         (result, spare),
         picks={5: 1, 6: 1, 7: 0},
     )
-    combined = exchange(combine((exchange(both),), False))
+    combined = combine((exchange(both, ALL_AXES),), share, False)
     (pair_out,) = call(
         functools.partial(last_kernel, share, chunk),
         (combined, current, gate, gains, out_weight, trans_up, trans_down),
@@ -373,11 +399,14 @@
 
 
 def solution(mesh):
-    rows, cols = mesh.shape["row"], mesh.shape["col"]
-    spread = P(("grp", "row"), "col", None)
-    in_specs = (spread, P(("grp", "row"), "col")) + (P(),) * 8
+    groups, rows, cols = (mesh.shape[name] for name in ("grp", "row", "col"))
+    halves = 2 if cols % 2 == 0 else 1
+    nears = cols // halves
+    folded = Mesh(mesh.devices.reshape(groups, rows, halves, nears), ("grp", "row", "half", "near"))
+    tokens = (("grp", "row"), ("half", "near"))
+    in_specs = (P(*tokens, None), P(*tokens)) + (P(),) * 8
 
     def body(*args):
-        return per_device(rows, cols, *args)
-
-    return jax.shard_map(body, mesh=mesh, in_specs=in_specs, out_specs=spread, check_vma=False)
+        return per_device(rows, halves, nears, *args)
+
+    return jax.shard_map(body, mesh=folded, in_specs=in_specs, out_specs=P(*tokens, None), check_vma=False)

time: 77.5 us -> 76.9 us (level)
  blocking collectives: 45.4 us -> 51.7 us
  waiting for transfers between devices: 13.5 us -> 7.87 us
  starting transfers between devices: 7.51 us -> 5.37 us
  Pallas kernels: 9.86 us -> 10.7 us
    all_to_all x3, blocking collectives: 45.4 us -> 51.7 us  [exchange(): return lax.all_to_all(values, axes, split_axis=0, concat_axis=0, tiled=True)]
    all_to_all x1, waiting for transfers between devices: 13.5 us -> 7.87 us  [exchange(): return lax.all_to_all(values, axes, split_axis=0, concat_axis=0, tiled=True)]
    all_to_all x1, starting transfers between devices: 7.51 us -> 5.37 us  [exchange(): return lax.all_to_all(values, axes, split_axis=0, concat_axis=0, tiled=True)]
    pallas_call x6, Pallas kernels: 9.86 us -> 10.7 us  [call(): pl.pallas_call(body, grid=(1,), in_specs=[in_place] * count if in_hbm els...]
where the time goes in v10:
time: 76.9 us; the launch traced here: 76.5 us
  blocking collectives  51.7 us (67%)
  Pallas kernels  10.7 us (14%)
  waiting for transfers between devices  7.87 us (10%)
  starting transfers between devices  5.37 us (7%)
    all_to_all x3, blocking collectives, exchange(): return lax.all_to_all(values, axes, split_axis=0, concat_axis=0, tiled=True)  51.7 us
    pallas_call x6, Pallas kernels, call(): pl.pallas_call(body, grid=(1,), in_specs=[in_place] * count if in_hbm els...  10.7 us
    all_to_all x1, waiting for transfers between devices, exchange(): return lax.all_to_all(values, axes, split_axis=0, concat_axis=0, tiled=True)  7.87 us
    all_to_all x1, starting transfers between devices, exchange(): return lax.all_to_all(values, axes, split_axis=0, concat_axis=0, tiled=True)  5.37 us
  transfers between devices with their start and end apart: 1, of which 1 were waited for; matrix products, arithmetic and copies ran while one was open for 0% of the time, Pallas kernels for 0%

profile of v10, /device:TPU:0, one launch (start us, length us, event | category | flops | bytes accessed | tf_op | source)
XLA Modules:
  0.0 76.5 jit_solution(4540999795138167696)
XLA Ops:
  0.0 2.6 %shard_map.100 = (bf16[8,256,128]{2,1,0:T(8,128)(2,1)}, bf16[128,1024]{1,0:T(8,128)(2,1)}) custom-call(f32[4,8,32,128]{3,2,1,0:T(8,128)} %bitcast.3, s32[32,32]{1,0:T(8,128)} %refs_2_.3, f32[2,128]{1,0:T(2,128)} %refs_4_.2, bf16[2,128,512]{2,1,0:T(8,128)(2,1)} %refs_5_.4), custom_call_target="tpu_custom_call" | custom-call | tf_op jit(solution)/shard_map/pallas_call | solution.py:303
  2.6 0.0 copy-start
  2.6 0.0 copy-start.3
  2.6 0.0 copy-start.4
  2.6 0.0 copy-start.7
  2.6 0.0 copy-start.9
  2.6 5.4 %all-to-all-start = ((bf16[8,256,128]{2,1,0:T(8,128)(2,1)}), bf16[8,256,128]{2,1,0:T(8,128)(2,1)S(1)}, u32[]{:S(2)}, u32[]{:S(2)}) async-start(bf16[8,256,128]{2,1,0:T(8,128)(2,1)} %get-tuple-element.14), calls=%async_computation | async-start | bytes 1048576 | tf_op jit(solution)/shard_map/all_to_all | solution.py:315
  8.0 0.0 copy-start.8
  8.0 0.0 copy-start.10
  8.0 0.0 copy-done
  8.0 0.0 copy-done.3
  8.1 0.0 copy-done.4
  8.1 0.0 copy-done.7
  8.1 0.0 copy-done.9
  8.1 0.6 copy-done.8
  8.7 0.0 copy-done.10
  8.7 0.3 shard_map.101
  9.0 7.9 %all-to-all-done.refs_0_ = bf16[8,256,128]{2,1,0:T(8,128)(2,1)S(1)} async-done(((bf16[8,256,128]{2,1,0:T(8,128)(2,1)}), bf16[8,256,128]{2,1,0:T(8,128)(2,1)S(1)}, u32[]{:S(2)}, u32[]{:S(2)}) %all-to-all-start) | async-done | bytes 524320 | tf_op jit(solution)/shard_map/all_to_all | solution.py:315
  16.9 2.2 %shard_map.102 = bf16[16,128,128]{2,1,0:T(8,128)(2,1)S(1)} custom-call(bf16[8,256,128]{2,1,0:T(8,128)(2,1)S(1)} %all-to-all-done.refs_0_, f32[8,128]{1,0:T(8,128)S(1)} %get-tuple-element.16.refs_1_.refs_3_), custom_call_target="tpu_custom_call" | custom-call | tf_op jit(solution)/shard_map/pallas_call | solution.py:303
  19.1 0.0 copy-start.1
  19.1 0.0 copy-start.5
  19.1 19.3 %all_to_all.20.refs_0_ = bf16[16,128,128]{2,1,0:T(8,128)(2,1)S(1)} all-to-all(bf16[16,128,128]{2,1,0:T(8,128)(2,1)S(1)} %shard_map.102), channel_id=1, replica_groups=mesh['grp'=2,'row'=4,'half'=2,'near'=2] {'half','near','row'}, dimensions={0} | all-to-all | bytes 1048576 | tf_op jit(solution)/shard_map/all_to_all | solution.py:315
  38.4 0.0 copy-done.1
  38.4 0.0 copy-done.5
  38.4 1.1 %shard_map.103 = (bf16[16,128,128]{2,1,0:T(8,128)(2,1)S(1)}, f32[128,1024]{1,0:T(8,128)S(1)}, f32[128,1024]{1,0:T(8,128)S(1)}) custom-call(bf16[16,128,128]{2,1,0:T(8,128)(2,1)S(1)} %all_to_all.20.refs_0_, f32[128,1024]{1,0:T(8,128)S(1)} %get-tuple-element.17.refs_1_, f32[128,1024]{1,0:T(8,128)S(1)} %get-tuple-element.18.refs_2_, ...), custom_call_target="tpu_custom_call" | custom-call | tf_op jit(solution)/shard_map/pallas_call | solution.py:303
  39.5 18.4 %all_to_all.21.refs_0_ = bf16[16,128,128]{2,1,0:T(8,128)(2,1)S(1)} all-to-all(bf16[16,128,128]{2,1,0:T(8,128)(2,1)S(1)} %get-tuple-element.20), channel_id=1, replica_groups=mesh['grp'=2,'row'=4,'half'=2,'near'=2] {'half','near','row'}, dimensions={0} | all-to-all | bytes 1048576 | tf_op jit(solution)/shard_map/all_to_all | solution.py:315
  57.8 1.8 %shard_map.104 = bf16[16,64,128]{2,1,0:T(8,128)(2,1)S(1)} custom-call(bf16[16,128,128]{2,1,0:T(8,128)(2,1)S(1)} %all_to_all.21.refs_0_), custom_call_target="tpu_custom_call" | custom-call | tf_op jit(solution)/shard_map/pallas_call | solution.py:303
  59.7 0.0 copy-start.2
  59.7 0.0 copy-start.6
  59.7 14.1 %all_to_all.22.refs_0_ = bf16[16,64,128]{2,1,0:T(8,128)(2,1)S(1)} all-to-all(bf16[16,64,128]{2,1,0:T(8,128)(2,1)S(1)} %shard_map.104), channel_id=1, replica_groups=mesh['grp'=2,'row'=4,'half'=2,'near'=2] {'half','near','row'}, dimensions={0} | all-to-all | bytes 524288 | tf_op jit(solution)/shard_map/all_to_all | solution.py:315
  73.8 0.0 copy-done.2
  73.8 0.0 copy-done.6
  73.8 2.8 %shard_map.105 = f32[4,8,32,128]{3,2,1,0:T(8,128)} custom-call(bf16[16,64,128]{2,1,0:T(8,128)(2,1)S(1)} %all_to_all.22.refs_0_, f32[128,1024]{1,0:T(8,128)S(1)} %get-tuple-element.21.refs_1_, f32[128,1024]{1,0:T(8,128)S(1)} %get-tuple-element.22.refs_2_, f32[8,128]{1,0:T(8,128)S(1)} %get-tuple-element.19.refs_4_.refs_3_, bf16[2,128,128]{2,1,0:T(8,128)(2,1)S(1)} %copy-done.5, ...), custom_call_target="tpu_custom_call" | custom-call | tf_op jit(solution)/shard_map/pallas_call | solution.py:303
Async XLA Ops:
  2.6 5.4 %copy-start = (f32[32,32,128]{2,1,0:T(8,128)S(1)}, f32[32,32,128]{2,1,0:T(8,128)}, u32[]{:S(2)}) copy-start(f32[32,32,128]{2,1,0:T(8,128)} %param.10) | copy-start | bytes 1572868
  2.6 5.4 %copy-start.3 = (bf16[128,1024]{1,0:T(8,128)(2,1)S(1)}, bf16[128,1024]{1,0:T(8,128)(2,1)}, u32[]{:S(2)}) copy-start(bf16[128,1024]{1,0:T(8,128)(2,1)} %get-tuple-element.15.refs_0_) | copy-start | bytes 786436
  2.6 5.4 %copy-start.4 = (bf16[2,128,128]{2,1,0:T(8,128)(2,1)S(1)}, bf16[2,128,128]{2,1,0:T(8,128)(2,1)}, u32[]{:S(2)}) copy-start(bf16[2,128,128]{2,1,0:T(8,128)(2,1)} %refs_6_.2) | copy-start | bytes 196612
  2.6 5.4 %copy-start.7 = (s32[32,32]{1,0:T(8,128)S(1)}, s32[32,32]{1,0:T(8,128)}, u32[]{:S(2)}) copy-start(s32[32,32]{1,0:T(8,128)} %refs_2_.3) | copy-start | bytes 12292
  2.6 5.4 %copy-start.9 = (f32[2,128]{1,0:T(2,128)S(1)}, f32[2,128]{1,0:T(2,128)}, u32[]{:S(2)}) copy-start(f32[2,128]{1,0:T(2,128)} %refs_5_.3) | copy-start | bytes 3076
  2.6 14.2 %all-to-all-start = ((bf16[8,256,128]{2,1,0:T(8,128)(2,1)}), bf16[8,256,128]{2,1,0:T(8,128)(2,1)S(1)}, u32[]{:S(2)}, u32[]{:S(2)}) async-start(bf16[8,256,128]{2,1,0:T(8,128)(2,1)} %get-tuple-element.14), calls=%async_computation | async-start | bytes 1048576 | tf_op jit(solution)/shard_map/all_to_all | solution.py:315
  8.0 0.7 copy-start.8
  8.0 0.7 copy-start.10
  19.1 19.3 %copy-start.1 = (bf16[2,128,512]{2,1,0:T(8,128)(2,1)S(1)}, bf16[2,128,512]{2,1,0:T(8,128)(2,1)}, u32[]{:S(2)}) copy-start(bf16[2,128,512]{2,1,0:T(8,128)(2,1)} %refs_5_.4) | copy-start | bytes 786436
  19.1 19.3 %copy-start.5 = (bf16[2,128,128]{2,1,0:T(8,128)(2,1)S(1)}, bf16[2,128,128]{2,1,0:T(8,128)(2,1)}, u32[]{:S(2)}) copy-start(bf16[2,128,128]{2,1,0:T(8,128)(2,1)} %refs_4_.3) | copy-start | bytes 196612
  59.7 14.1 %copy-start.2 = (bf16[128,1024]{1,0:T(8,128)(2,1)S(1)}, bf16[128,1024]{1,0:T(8,128)(2,1)}, u32[]{:S(2)}) copy-start(bf16[128,1024]{1,0:T(8,128)(2,1)} %refs_5_.5) | copy-start | bytes 786436
  59.7 14.1 %copy-start.6 = (bf16[512,128]{1,0:T(8,128)(2,1)S(1)}, bf16[512,128]{1,0:T(8,128)(2,1)}, u32[]{:S(2)}) copy-start(bf16[512,128]{1,0:T(8,128)(2,1)} %refs_6_.3) | copy-start | bytes 393220

commit v11 on v10

--- a/solution.py
+++ b/solution.py
@@ -108,107 +108,97 @@
     gains_out[...] = jnp.concatenate(rows + rows, axis=0)
 
 
-def swap_slots(parts, breadth):
-    parts = list(parts)
-    slot = lax.broadcasted_iota(jnp.int32, parts[0].shape, 1) // breadth
-    step = 1
-    while step < len(parts):
-        low = (slot // step) % 2 == 0
-        for first in range(len(parts)):
-            if first & step:
-                continue
-            a, b = parts[first], parts[first | step]
-            parts[first] = jnp.where(low, a, pltpu.roll(b, step * breadth, 1))
-            parts[first | step] = jnp.where(low, pltpu.roll(a, LANES - step * breadth, 1), b)
-        step *= 2
-    return parts
-
-
-def pitch_of(share):
-    return share + 1 if share % 8 == 0 else share
-
-
-def combine_kernel(rows, cols, near, breadth, share, outgoing, ins, outs, stage_ref, result_ref):
+def one_hot(rows, columns, wanted):
+    row = lax.broadcasted_iota(jnp.int32, (rows, columns), 0)
+    column = lax.broadcasted_iota(jnp.int32, (rows, columns), 1)
+    return (wanted(row) == column).astype(BF16)
+
+
+def swap_matrix(slots, breadth):
+    size = slots * LANES
+    return one_hot(
+        size, size, lambda lane: lane // breadth % slots * LANES + lane // LANES * breadth + lane % breadth
+    )
+
+
+def combine_kernel(rows, cols, near, breadth, share, outgoing, ins, outs):
     both_ref, combined_ref = ins[0], outs[0]
     slots = LANES // breadth
-    owners, span = both_ref.shape[:2]
+    span = both_ref.shape[1]
     lines = span // (2 * share)
-    pitch = pitch_of(share)
-    padded = pitch != share
-    if padded:
-        for owner in range(owners):
-            for line in range(lines):
-                both = both_ref[owner, 2 * share * line : 2 * share * (line + 1), :].astype(F32)
-                for side in range(2):
-                    base = ((2 * owner + side) * lines + line) * pitch
-                    stage_ref[base : base + share, :] = both[side * share : (side + 1) * share]
-    else:
-        stage_ref[...] = both_ref[...].astype(F32).reshape(stage_ref.shape)
-
-    def line_rows(owner, side, channel):
-        if padded:
-            return pl.ds((2 * owner + side) * lines * pitch + channel, lines, stride=pitch)
-        return pl.ds(owner * span + side * share + channel, lines, stride=2 * share)
-
-    def whole(side, wanted):
-        places = [(channel, col) for channel in wanted for col in range(near)]
+    pack = max(1, slots // near)
+    groups = share // pack
+    size = span // pack
+    swap = swap_matrix(slots, breadth)
+
+    def source(row):
+        channel = row // size * groups + row // lines % groups
+        return row % lines * (2 * share) + row // (groups * lines) % 2 * share + channel
+
+    order = one_hot(span, span, source)
+    wide = []
+    for row in range(rows):
+        here = jnp.concatenate([both_ref[col * rows + row] for col in range(near)], axis=1)
+        here = dot(order, here).astype(BF16)
+        wide.append(jnp.concatenate([here[n * size : (n + 1) * size] for n in range(pack)], axis=1))
+    wide = jnp.concatenate(wide, axis=0)
+    block = slots * LANES
+    swapped = [dot(wide[:, first : first + block], swap) for first in range(0, wide.shape[1], block)]
+
+    def whole(side, group):
         columns = []
-        for first in range(0, len(places), slots):
-            parts = []
-            for channel, col in places[first : first + slots]:
-                held = [stage_ref[line_rows(col * rows + row, side, channel), :] for row in range(rows)]
-                parts.append(jnp.concatenate(held, axis=0))
-            parts = swap_slots(parts, breadth)
-            columns.append(
-                jnp.concatenate(
-                    [part[row * lines : (row + 1) * lines] for row in range(rows) for part in parts], axis=0
-                )
-            )
+        for part in swapped:
+            held = []
+            for row in range(rows):
+                first = row * size + (side * groups + group) * lines
+                held += [part[first : first + lines, slot * LANES : (slot + 1) * LANES] for slot in range(slots)]
+            columns.append(jnp.concatenate(held, axis=0))
         return jnp.concatenate(columns, axis=1).astype(BF16)
 
-    group = max(1, slots // near)
-    for base in range(0, share, group):
-        wanted = range(base, base + group)
-        left, right = whole(0, wanted), whole(1, wanted)
-        for place, channel in enumerate(wanted):
+    products = [None] * share
+    for group in range(groups):
+        left, right = whole(0, group), whole(1, group)
+        for place in range(pack):
             mine = left
-            if group > 1:
+            if pack > 1:
                 lane = lax.broadcasted_iota(jnp.int32, left.shape, 1)
                 mine = jnp.where(lane // (near * breadth) == place, left, jnp.zeros_like(left))
-            combined = dot(mine, right, (1, 1) if outgoing else (0, 0))
-            for high in range(cols // slots):
-                lanes = slice(high * LANES, (high + 1) * LANES)
+            products[place * groups + group] = dot(mine, right, (1, 1) if outgoing else (0, 0))
+
+    for high in range(cols // slots):
+        lanes = slice(high * LANES, (high + 1) * LANES)
+        held = []
+        for row in range(rows):
+            for product in products:
                 parts = [
-                    jnp.concatenate(
-                        [
-                            combined[(row * slots + slot) * lines : (row * slots + slot + 1) * lines, lanes]
-                            for row in range(rows)
-                        ],
-                        axis=0,
-                    )
+                    product[(row * slots + slot) * lines : (row * slots + slot + 1) * lines, lanes]
                     for slot in range(slots)
                 ]
-                for low, part in enumerate(swap_slots(parts, breadth)):
-                    for row in range(rows):
-                        at = ((high * slots + low) * rows + row) * lines * pitch + channel
-                        result_ref[pl.ds(at, lines, stride=pitch), :] = part[row * lines : (row + 1) * lines]
-    if padded:
-        for owner in range(rows * cols):
-            held = [
-                result_ref[(owner * lines + line) * pitch : (owner * lines + line) * pitch + share, :]
-                for line in range(lines)
-            ]
-            combined_ref[owner] = jnp.concatenate(held, axis=0).astype(BF16)
-    else:
-        combined_ref[...] = result_ref[...].astype(BF16).reshape(combined_ref.shape)
-
-
-def hold_combined(combined_ref, stage_ref):
-    owners = stage_ref.shape[0] // combined_ref.shape[1]
-    total = combined_ref[:owners].astype(F32)
-    for first in range(owners, combined_ref.shape[0], owners):
-        total = total + combined_ref[first : first + owners].astype(F32)
-    stage_ref[...] = total.reshape(stage_ref.shape)
+                held.append(jnp.concatenate(parts, axis=1))
+        back = dot(jnp.concatenate(held, axis=0).astype(BF16), swap).astype(BF16)
+        for low in range(slots):
+            for row in range(rows):
+                first = row * share * lines
+                combined_ref[(high * slots + low) * rows + row] = back[
+                    first : first + share * lines, low * LANES : (low + 1) * LANES
+                ]
+
+
+def hold_combined(combined_ref, stage_ref, share):
+    span = combined_ref.shape[1]
+    lines = span // share
+    owners = stage_ref.shape[0] // span
+    halves = combined_ref.shape[0] // owners
+    order = one_hot(span, span, lambda row: row % share * lines + row // share)
+    order = jnp.concatenate([order] * halves, axis=1)
+    for first in range(0, owners, 2):
+        blocks = [
+            jnp.concatenate([combined_ref[half * owners + owner] for half in range(halves)], axis=0)
+            for owner in (first, first + 1)
+        ]
+        ordered = dot(order, jnp.concatenate(blocks, axis=1))
+        for n in range(2):
+            stage_ref[(first + n) * span : (first + n + 1) * span, :] = ordered[:, n * LANES : (n + 1) * LANES]
 
 
 def read_combined(stage_ref, owners, lines, share, first, count):
@@ -231,7 +221,7 @@
     tokens = x_ref.shape[1]
     lines = tokens // LANES
     owners = x_ref.shape[0] // share
-    hold_combined(combined_ref, stage_ref)
+    hold_combined(combined_ref, stage_ref, share)
     mask = mask_ref[...]
     gain_out, gain = [spread_gain(gains_ref[n : n + 1, :]) for n in (0, 1)]
     out_t, proj_t, gate_t = out_ref[...].T, proj_ref[...].T, gate_weight_ref[...].T
@@ -255,7 +245,7 @@
     count = chunk // LANES
     gain_out, gain = [spread_gain(gains_ref[n : n + 1, :]) for n in (2, 3)]
     out_t, up_t, down_t = out_ref[...].T, up_ref[...].T, down_ref[...].T
-    hold_combined(combined_ref, stage_ref)
+    hold_combined(combined_ref, stage_ref, share)
     writes = []
     for first in range(0, lines, count):
         here = slice(first * LANES, (first + count) * LANES)
@@ -352,10 +342,8 @@
     def combine(operands, own, outgoing):
         near = cols * share // own
         kernel = functools.partial(combine_kernel, rows, cols, near, breadth, own, outgoing)
-        block = lines * pitch_of(own)
-        scratch = [pltpu.VMEM((count * block, LANES), F32) for count in (2 * rows * near, owners)]
         answer = ((owners, own * lines, LANES), BF16)
-        return exchange(call(kernel, operands, [answer], scratch)[0], ALL_AXES)
+        return exchange(call(kernel, operands, [answer])[0], ALL_AXES)
 
     both, normed = call(
         functools.partial(project_kernel, first_share),

time: 76.9 us -> 75.8 us (0.986)
  Pallas kernels: 10.7 us -> 9.63 us
    pallas_call x6, Pallas kernels: 10.7 us -> 9.63 us  [call(): pl.pallas_call(body, grid=(1,), in_specs=[in_place] * count if in_hbm els...]
where the time goes in v11:
time: 75.8 us; the launch traced here: 75.4 us
  blocking collectives  51.7 us (68%)
  Pallas kernels  9.63 us (13%)
  waiting for transfers between devices  7.87 us (10%)
  starting transfers between devices  5.37 us (7%)
    all_to_all x3, blocking collectives, exchange(): return lax.all_to_all(values, axes, split_axis=0, concat_axis=0, tiled=True)  51.7 us
    pallas_call x6, Pallas kernels, call(): pl.pallas_call(body, grid=(1,), in_specs=[in_place] * count if in_hbm els...  9.63 us
    all_to_all x1, waiting for transfers between devices, exchange(): return lax.all_to_all(values, axes, split_axis=0, concat_axis=0, tiled=True)  7.87 us
    all_to_all x1, starting transfers between devices, exchange(): return lax.all_to_all(values, axes, split_axis=0, concat_axis=0, tiled=True)  5.37 us
  transfers between devices with their start and end apart: 1, of which 1 were waited for; matrix products, arithmetic and copies ran while one was open for 0% of the time, Pallas kernels for 0%

profile of v11, /device:TPU:0, one launch (start us, length us, event | category | flops | bytes accessed | tf_op | source)
XLA Modules:
  0.0 75.4 jit_solution(17616287201458260971)
XLA Ops:
  0.0 2.6 %shard_map.100 = (bf16[8,256,128]{2,1,0:T(8,128)(2,1)}, bf16[128,1024]{1,0:T(8,128)(2,1)}) custom-call(f32[4,8,32,128]{3,2,1,0:T(8,128)} %bitcast.3, s32[32,32]{1,0:T(8,128)} %refs_2_.3, f32[2,128]{1,0:T(2,128)} %refs_4_.2, bf16[2,128,512]{2,1,0:T(8,128)(2,1)} %refs_5_.4), custom_call_target="tpu_custom_call" | custom-call | tf_op jit(solution)/shard_map/pallas_call | solution.py:293
  2.6 0.0 copy-start
  2.6 0.0 copy-start.3
  2.6 0.0 copy-start.4
  2.6 0.0 copy-start.7
  2.6 0.0 copy-start.9
  2.6 5.4 %all-to-all-start = ((bf16[8,256,128]{2,1,0:T(8,128)(2,1)}), bf16[8,256,128]{2,1,0:T(8,128)(2,1)S(1)}, u32[]{:S(2)}, u32[]{:S(2)}) async-start(bf16[8,256,128]{2,1,0:T(8,128)(2,1)} %get-tuple-element.14), calls=%async_computation | async-start | bytes 1048576 | tf_op jit(solution)/shard_map/all_to_all | solution.py:305
  8.0 0.0 copy-start.8
  8.0 0.0 copy-start.10
  8.0 0.0 copy-done
  8.0 0.0 copy-done.3
  8.1 0.0 copy-done.4
  8.1 0.0 copy-done.7
  8.1 0.0 copy-done.9
  8.1 0.6 copy-done.8
  8.7 0.0 copy-done.10
  8.7 0.3 shard_map.101
  9.0 7.9 %all-to-all-done.refs_0_ = bf16[8,256,128]{2,1,0:T(8,128)(2,1)S(1)} async-done(((bf16[8,256,128]{2,1,0:T(8,128)(2,1)}), bf16[8,256,128]{2,1,0:T(8,128)(2,1)S(1)}, u32[]{:S(2)}, u32[]{:S(2)}) %all-to-all-start) | async-done | bytes 524320 | tf_op jit(solution)/shard_map/all_to_all | solution.py:305
  16.9 1.5 %shard_map.102 = bf16[16,128,128]{2,1,0:T(8,128)(2,1)S(1)} custom-call(bf16[8,256,128]{2,1,0:T(8,128)(2,1)S(1)} %all-to-all-done.refs_0_, f32[8,128]{1,0:T(8,128)S(1)} %get-tuple-element.16.refs_1_.refs_3_), custom_call_target="tpu_custom_call" | custom-call | tf_op jit(solution)/shard_map/pallas_call | solution.py:293
  18.4 0.0 copy-start.1
  18.4 0.0 copy-start.5
  18.4 19.3 %all_to_all.20.refs_0_ = bf16[16,128,128]{2,1,0:T(8,128)(2,1)S(1)} all-to-all(bf16[16,128,128]{2,1,0:T(8,128)(2,1)S(1)} %shard_map.102), channel_id=1, replica_groups=mesh['grp'=2,'row'=4,'half'=2,'near'=2] {'half','near','row'}, dimensions={0} | all-to-all | bytes 1048576 | tf_op jit(solution)/shard_map/all_to_all | solution.py:305
  37.7 0.0 copy-done.1
  37.7 0.0 copy-done.5
  37.7 1.3 %shard_map.103 = (bf16[16,128,128]{2,1,0:T(8,128)(2,1)S(1)}, f32[128,1024]{1,0:T(8,128)S(1)}, f32[128,1024]{1,0:T(8,128)S(1)}) custom-call(bf16[16,128,128]{2,1,0:T(8,128)(2,1)S(1)} %all_to_all.20.refs_0_, f32[128,1024]{1,0:T(8,128)S(1)} %get-tuple-element.17.refs_1_, f32[128,1024]{1,0:T(8,128)S(1)} %get-tuple-element.18.refs_2_, ...), custom_call_target="tpu_custom_call" | custom-call | tf_op jit(solution)/shard_map/pallas_call | solution.py:293
  38.9 18.4 %all_to_all.21.refs_0_ = bf16[16,128,128]{2,1,0:T(8,128)(2,1)S(1)} all-to-all(bf16[16,128,128]{2,1,0:T(8,128)(2,1)S(1)} %get-tuple-element.20), channel_id=1, replica_groups=mesh['grp'=2,'row'=4,'half'=2,'near'=2] {'half','near','row'}, dimensions={0} | all-to-all | bytes 1048576 | tf_op jit(solution)/shard_map/all_to_all | solution.py:305
  57.3 1.1 %shard_map.104 = bf16[16,64,128]{2,1,0:T(8,128)(2,1)S(1)} custom-call(bf16[16,128,128]{2,1,0:T(8,128)(2,1)S(1)} %all_to_all.21.refs_0_), custom_call_target="tpu_custom_call" | custom-call | tf_op jit(solution)/shard_map/pallas_call | solution.py:293
  58.4 0.0 copy-start.2
  58.4 0.0 copy-start.6
  58.4 14.1 %all_to_all.22.refs_0_ = bf16[16,64,128]{2,1,0:T(8,128)(2,1)S(1)} all-to-all(bf16[16,64,128]{2,1,0:T(8,128)(2,1)S(1)} %shard_map.104), channel_id=1, replica_groups=mesh['grp'=2,'row'=4,'half'=2,'near'=2] {'half','near','row'}, dimensions={0} | all-to-all | bytes 524288 | tf_op jit(solution)/shard_map/all_to_all | solution.py:305
  72.5 0.0 copy-done.2
  72.5 0.0 copy-done.6
  72.5 2.9 %shard_map.105 = f32[4,8,32,128]{3,2,1,0:T(8,128)} custom-call(bf16[16,64,128]{2,1,0:T(8,128)(2,1)S(1)} %all_to_all.22.refs_0_, f32[128,1024]{1,0:T(8,128)S(1)} %get-tuple-element.21.refs_1_, f32[128,1024]{1,0:T(8,128)S(1)} %get-tuple-element.22.refs_2_, f32[8,128]{1,0:T(8,128)S(1)} %get-tuple-element.19.refs_4_.refs_3_, bf16[2,128,128]{2,1,0:T(8,128)(2,1)S(1)} %copy-done.5, ...), custom_call_target="tpu_custom_call" | custom-call | tf_op jit(solution)/shard_map/pallas_call | solution.py:293
Async XLA Ops:
  2.6 5.4 %copy-start = (f32[32,32,128]{2,1,0:T(8,128)S(1)}, f32[32,32,128]{2,1,0:T(8,128)}, u32[]{:S(2)}) copy-start(f32[32,32,128]{2,1,0:T(8,128)} %param.10) | copy-start | bytes 1572868
  2.6 5.4 %copy-start.3 = (bf16[128,1024]{1,0:T(8,128)(2,1)S(1)}, bf16[128,1024]{1,0:T(8,128)(2,1)}, u32[]{:S(2)}) copy-start(bf16[128,1024]{1,0:T(8,128)(2,1)} %get-tuple-element.15.refs_0_) | copy-start | bytes 786436
  2.6 5.4 %copy-start.4 = (bf16[2,128,128]{2,1,0:T(8,128)(2,1)S(1)}, bf16[2,128,128]{2,1,0:T(8,128)(2,1)}, u32[]{:S(2)}) copy-start(bf16[2,128,128]{2,1,0:T(8,128)(2,1)} %refs_6_.2) | copy-start | bytes 196612
  2.6 5.4 %copy-start.7 = (s32[32,32]{1,0:T(8,128)S(1)}, s32[32,32]{1,0:T(8,128)}, u32[]{:S(2)}) copy-start(s32[32,32]{1,0:T(8,128)} %refs_2_.3) | copy-start | bytes 12292
  2.6 5.4 %copy-start.9 = (f32[2,128]{1,0:T(2,128)S(1)}, f32[2,128]{1,0:T(2,128)}, u32[]{:S(2)}) copy-start(f32[2,128]{1,0:T(2,128)} %refs_5_.3) | copy-start | bytes 3076
  2.6 14.2 %all-to-all-start = ((bf16[8,256,128]{2,1,0:T(8,128)(2,1)}), bf16[8,256,128]{2,1,0:T(8,128)(2,1)S(1)}, u32[]{:S(2)}, u32[]{:S(2)}) async-start(bf16[8,256,128]{2,1,0:T(8,128)(2,1)} %get-tuple-element.14), calls=%async_computation | async-start | bytes 1048576 | tf_op jit(solution)/shard_map/all_to_all | solution.py:305
  8.0 0.7 copy-start.8
  8.0 0.7 copy-start.10
  18.4 19.3 %copy-start.1 = (bf16[2,128,512]{2,1,0:T(8,128)(2,1)S(1)}, bf16[2,128,512]{2,1,0:T(8,128)(2,1)}, u32[]{:S(2)}) copy-start(bf16[2,128,512]{2,1,0:T(8,128)(2,1)} %refs_5_.4) | copy-start | bytes 786436
  18.4 19.3 %copy-start.5 = (bf16[2,128,128]{2,1,0:T(8,128)(2,1)S(1)}, bf16[2,128,128]{2,1,0:T(8,128)(2,1)}, u32[]{:S(2)}) copy-start(bf16[2,128,128]{2,1,0:T(8,128)(2,1)} %refs_4_.3) | copy-start | bytes 196612
  58.4 14.1 %copy-start.2 = (bf16[128,1024]{1,0:T(8,128)(2,1)S(1)}, bf16[128,1024]{1,0:T(8,128)(2,1)}, u32[]{:S(2)}) copy-start(bf16[128,1024]{1,0:T(8,128)(2,1)} %refs_5_.5) | copy-start | bytes 786436
  58.4 14.1 %copy-start.6 = (bf16[512,128]{1,0:T(8,128)(2,1)S(1)}, bf16[512,128]{1,0:T(8,128)(2,1)}, u32[]{:S(2)}) copy-start(bf16[512,128]{1,0:T(8,128)(2,1)} %refs_6_.3) | copy-start | bytes 393220

commit v12 on v11

--- a/solution.py
+++ b/solution.py
@@ -22,8 +22,12 @@
     )
 
 
-def sigmoid(values):
-    return 0.5 * jnp.tanh(0.5 * values) + 0.5
+def halved(weight):
+    return weight.T * 0.5
+
+
+def twice_sigmoid(half):
+    return jnp.tanh(half) + 1.0
 
 
 def channel_norm(values, gain):
@@ -56,8 +60,8 @@
         here = projected[:, part * LANES : (part + 1) * LANES]
         at = line + part
         keep = mask[at : at + 1]
-        left = sigmoid(here[:hid]) * here[hid : 2 * hid] * keep
-        right = sigmoid(here[2 * hid : 3 * hid]) * here[3 * hid :] * keep
+        left = twice_sigmoid(here[:hid]) * here[hid : 2 * hid] * keep
+        right = twice_sigmoid(here[2 * hid : 3 * hid]) * here[3 * hid :] * keep
         if share % 8 == 0:
             for owner in range(owners):
                 rows = slice(owner * share, (owner + 1) * share)
@@ -83,7 +87,7 @@
 
 
 def project_kernel(share, ins, outs, stage_ref, x_ref, mask_ref, gain_ref, weight_ref, sems):
-    message_ref, normed_ref = outs
+    (message_ref,) = outs
     x_in, mask_in, gain_in, weight_in = ins
     lines = x_ref.shape[1]
     pairs = [(weight_in.at[0], weight_ref), (x_in, x_ref), (gain_in, gain_ref), (mask_in, mask_ref)]
@@ -92,17 +96,17 @@
     mask = token_mask(mask_ref[...], lines)
     current = jnp.concatenate([line_tokens(x_ref, line).T for line in range(lines)], axis=1)
     normed = channel_norm(current, spread_gain(gain_ref[0:1, :]))
-    emit_message(normed, weight_ref[...].T, mask, 0, message_ref, stage_ref, share)
-    normed_ref[...] = normed
+    emit_message(normed, halved(weight_ref[...]), mask, 0, message_ref, stage_ref, share)
 
 
 def prepare_kernel(ins, outs):
-    normed_ref, x_ref, mask_ref, gate_ref, gain_in_ref, gain_out_ref, trans_gain_ref = ins
+    x_ref, mask_ref, gate_ref, gain_in_ref, gain_out_ref, trans_gain_ref = ins
     gate_out, x_out, mask_out, gains_out = outs
     lines = x_ref.shape[1]
-    gate_out[...] = sigmoid(dot(gate_ref[...].T, normed_ref[...]))
-    for line in range(lines):
-        x_out[:, line * LANES : (line + 1) * LANES] = line_tokens(x_ref, line).T
+    current = jnp.concatenate([line_tokens(x_ref, line).T for line in range(lines)], axis=1)
+    x_out[...] = current
+    normed = channel_norm(current, spread_gain(gain_in_ref[0:1, :]))
+    gate_out[...] = twice_sigmoid(dot(halved(gate_ref[0]), normed))
     mask_out[...] = token_mask(mask_ref[...], lines)
     rows = [gain_out_ref[0:1, :], gain_in_ref[1:2, :], gain_out_ref[1:2, :], trans_gain_ref[...]]
     gains_out[...] = jnp.concatenate(rows + rows, axis=0)
@@ -224,7 +228,7 @@
     hold_combined(combined_ref, stage_ref, share)
     mask = mask_ref[...]
     gain_out, gain = [spread_gain(gains_ref[n : n + 1, :]) for n in (0, 1)]
-    out_t, proj_t, gate_t = out_ref[...].T, proj_ref[...].T, gate_weight_ref[...].T
+    out_t, proj_t, gate_t = halved(out_ref[0]), halved(proj_ref[1]), halved(gate_weight_ref[1])
     for start in range(0, tokens, chunk):
         here = slice(start, start + chunk)
         combined = read_combined(stage_ref, owners, lines, share, start // LANES, chunk // LANES)
@@ -233,7 +237,7 @@
         next_ref[:, here] = current
         normed = channel_norm(current, gain)
         emit_message(normed, proj_t, mask, start // LANES, message_ref, message_stage_ref, next_share)
-        gate_out[:, here] = sigmoid(dot(gate_t, normed))
+        gate_out[:, here] = twice_sigmoid(dot(gate_t, normed))
 
 
 def last_kernel(share, chunk, ins, outs, stage_ref, result_ref, sems):
@@ -244,7 +248,8 @@
     half = down_ref.shape[0]
     count = chunk // LANES
     gain_out, gain = [spread_gain(gains_ref[n : n + 1, :]) for n in (2, 3)]
-    out_t, up_t, down_t = out_ref[...].T, up_ref[...].T, down_ref[...].T
+    out_t, down_t = halved(out_ref[1]), down_ref[...].T
+    gate_t, up_t = halved(up_ref[:, :half]), up_ref[:, half:].T
     hold_combined(combined_ref, stage_ref, share)
     writes = []
     for first in range(0, lines, count):
@@ -255,9 +260,9 @@
         trans_in = channel_norm(current, gain)
         block = min(256, half)
         for base in range(0, half, block):
-            gate_part = dot(up_t[base : base + block], trans_in)
-            up_part = dot(up_t[half + base : half + base + block], trans_in)
-            trans_hidden = (gate_part * sigmoid(gate_part) * up_part).astype(BF16)
+            gate_part = dot(gate_t[base : base + block], trans_in)
+            up_part = dot(up_t[base : base + block], trans_in)
+            trans_hidden = (gate_part * twice_sigmoid(gate_part) * up_part).astype(BF16)
             current = current + dot(down_t[:, base : base + block], trans_hidden)
         result = current.T
         for part in range(count):
@@ -270,21 +275,8 @@
         write.wait()
 
 
-def whole_spec(array):
-    return pl.BlockSpec(array.shape, lambda step, dims=array.ndim: (0,) * dims)
-
-
-def picked_spec(array, index):
-    return pl.BlockSpec((None,) + array.shape[1:], lambda step: (index,) + (0,) * (array.ndim - 1))
-
-
-def call(kernel, operands, outs, scratch=(), picks=None, in_hbm=False, out_hbm=False):
-    in_place = pl.BlockSpec(memory_space=pltpu.HBM)
-    specs = [
-        picked_spec(array, picks[n]) if picks and n in picks else whole_spec(array)
-        for n, array in enumerate(operands)
-    ]
-    shapes = [jax.ShapeDtypeStruct(shape, dtype) for shape, dtype in outs]
+def call(kernel, operands, outs, scratch=(), in_hbm=False, out_hbm=False):
+    in_place, held = pl.BlockSpec(memory_space=pltpu.HBM), pl.BlockSpec(memory_space=pltpu.VMEM)
     count = len(operands)
 
     def body(*refs):
@@ -292,10 +284,9 @@
 
     return pl.pallas_call(
         body,
-        grid=(1,),
-        in_specs=[in_place] * count if in_hbm else specs,
-        out_specs=[in_place if out_hbm else whole_spec(shape) for shape in shapes],
-        out_shape=shapes,
+        in_specs=[in_place if in_hbm else held] * count,
+        out_specs=[in_place if out_hbm else held] * len(outs),
+        out_shape=[jax.ShapeDtypeStruct(shape, dtype) for shape, dtype in outs],
         scratch_shapes=list(scratch),
         compiler_params=pltpu.CompilerParams(vmem_limit_bytes=FULL_VMEM_BYTES if in_hbm else VMEM_BYTES),
     )(*operands)
@@ -332,7 +323,7 @@
     first_share = split * share
     held = ((LANES // breadth, lines, breadth, channels), F32)
     grouped = pair_map.reshape(held[0])
-    wide, narrow = ((channels, tokens), F32), ((channels, tokens), BF16)
+    wide = ((channels, tokens), F32)
     result = pltpu.VMEM((owners * share * lines, LANES), F32)
     spare = pltpu.VMEM((8, LANES) if share % 8 == 0 else (owners * 2 * share * lines, LANES), F32)
 
@@ -345,10 +336,10 @@
         answer = ((owners, own * lines, LANES), BF16)
         return exchange(call(kernel, operands, [answer])[0], ALL_AXES)
 
-    both, normed = call(
+    (both,) = call(
         functools.partial(project_kernel, first_share),
         (grouped, pair_mask, gain_in, proj_weight),
-        [message(first_share), narrow],
+        [message(first_share)],
         (
             spare,
             pltpu.VMEM(*held),
@@ -361,9 +352,8 @@
     )
     gate, current, mask, gains = call(
         prepare_kernel,
-        (normed, grouped, pair_mask, gate_weight, gain_in, gain_out, trans_gain.reshape(1, -1)),
+        (grouped, pair_mask, gate_weight, gain_in, gain_out, trans_gain.reshape(1, -1)),
         [wide, wide, ((lines, LANES), F32), ((8, channels), F32)],
-        picks={3: 0},
     )
     both = exchange(both, NEAR_AXES if split > 1 else ALL_AXES)
     combined = combine((both, mask), first_share, True)
@@ -372,7 +362,6 @@
         (combined, current, gate, mask, gains, proj_weight, gate_weight, out_weight),
         [message(share), wide, wide],
         (result, spare),
-        picks={5: 1, 6: 1, 7: 0},
     )
     combined = combine((exchange(both, ALL_AXES),), share, False)
     (pair_out,) = call(
@@ -380,7 +369,6 @@
         (combined, current, gate, gains, out_weight, trans_up, trans_down),
         [held],
         (result, pltpu.VMEM(*held), pltpu.SemaphoreType.DMA((tokens // chunk,))),
-        picks={4: 1},
         out_hbm=True,
     )
     return pair_out.reshape(pair_map.shape)

time: 75.8 us -> 75.8 us (level)
  transfers between devices with their start and end apart: 1 -> 1, of which waited for: 1 -> 1; matrix products, arithmetic and copies ran while one was open for 0% -> 0% of each run, Pallas kernels for 0% -> 1%
where the time goes in v12:
time: 75.8 us; the launch traced here: 75.4 us
  blocking collectives  51.7 us (68%)
  Pallas kernels  9.76 us (13%)
  waiting for transfers between devices  7.71 us (10%)
  starting transfers between devices  5.37 us (7%)
    all_to_all x3, blocking collectives, exchange(): return lax.all_to_all(values, axes, split_axis=0, concat_axis=0, tiled=True)  51.7 us
    pallas_call x6, Pallas kernels, call(): pl.pallas_call(body, in_specs=[in_place if in_hbm else held] * count, out...  9.76 us
    all_to_all x1, waiting for transfers between devices, exchange(): return lax.all_to_all(values, axes, split_axis=0, concat_axis=0, tiled=True)  7.71 us
    all_to_all x1, starting transfers between devices, exchange(): return lax.all_to_all(values, axes, split_axis=0, concat_axis=0, tiled=True)  5.37 us
  transfers between devices with their start and end apart: 1, of which 1 were waited for; matrix products, arithmetic and copies ran while one was open for 0% of the time, Pallas kernels for 1%

profile of v12, /device:TPU:0, one launch (start us, length us, event | category | flops | bytes accessed | tf_op | source)
XLA Modules:
  0.0 75.4 jit_solution(12534261704237158741)
XLA Ops:
  0.0 2.6 %shard_map.100 = bf16[8,256,128]{2,1,0:T(8,128)(2,1)} custom-call(f32[4,8,32,128]{3,2,1,0:T(8,128)} %bitcast.3, s32[32,32]{1,0:T(8,128)} %refs_1_.3, f32[2,128]{1,0:T(2,128)} %refs_3_.3, bf16[2,128,512]{2,1,0:T(8,128)(2,1)} %refs_5_.2), custom_call_target="tpu_custom_call" | custom-call | tf_op jit(solution)/shard_map/pallas_call | solution.py:285
  2.6 0.0 copy-start
  2.6 0.0 copy-start.4
  2.6 0.0 copy-start.6
  2.6 0.0 copy-start.8
  2.6 5.4 %all-to-all-start = ((bf16[8,256,128]{2,1,0:T(8,128)(2,1)}), bf16[8,256,128]{2,1,0:T(8,128)(2,1)S(1)}, u32[]{:S(2)}, u32[]{:S(2)}) async-start(bf16[8,256,128]{2,1,0:T(8,128)(2,1)} %shard_map.100), calls=%async_computation | async-start | bytes 1048576 | tf_op jit(solution)/shard_map/all_to_all | solution.py:296
  8.0 0.0 copy-start.7
  8.0 0.0 copy-start.9
  8.0 0.0 copy-done
  8.0 0.0 copy-done.4
  8.0 0.0 copy-done.6
  8.1 0.0 copy-done.8
  8.1 0.6 copy-done.7
  8.7 0.0 copy-done.9
  8.7 0.4 shard_map.101
  9.1 7.7 %all-to-all-done.refs_0_ = bf16[8,256,128]{2,1,0:T(8,128)(2,1)S(1)} async-done(((bf16[8,256,128]{2,1,0:T(8,128)(2,1)}), bf16[8,256,128]{2,1,0:T(8,128)(2,1)S(1)}, u32[]{:S(2)}, u32[]{:S(2)}) %all-to-all-start) | async-done | bytes 524320 | tf_op jit(solution)/shard_map/all_to_all | solution.py:296
  16.9 1.5 %shard_map.102 = bf16[16,128,128]{2,1,0:T(8,128)(2,1)S(1)} custom-call(bf16[8,256,128]{2,1,0:T(8,128)(2,1)S(1)} %all-to-all-done.refs_0_, f32[8,128]{1,0:T(8,128)S(1)} %get-tuple-element.12.refs_1_.refs_3_), custom_call_target="tpu_custom_call" | custom-call | tf_op jit(solution)/shard_map/pallas_call | solution.py:285
  18.3 0.0 copy-start.1
  18.3 0.0 copy-start.3
  18.4 19.3 %all_to_all.20.refs_0_ = bf16[16,128,128]{2,1,0:T(8,128)(2,1)S(1)} all-to-all(bf16[16,128,128]{2,1,0:T(8,128)(2,1)S(1)} %shard_map.102), channel_id=1, replica_groups=mesh['grp'=2,'row'=4,'half'=2,'near'=2] {'half','near','row'}, dimensions={0} | all-to-all | bytes 1048576 | tf_op jit(solution)/shard_map/all_to_all | solution.py:296
  37.6 0.0 copy-done.1
  37.6 0.0 copy-done.3
  37.6 1.3 %shard_map.103 = (bf16[16,128,128]{2,1,0:T(8,128)(2,1)S(1)}, f32[128,1024]{1,0:T(8,128)S(1)}, f32[128,1024]{1,0:T(8,128)S(1)}) custom-call(bf16[16,128,128]{2,1,0:T(8,128)(2,1)S(1)} %all_to_all.20.refs_0_, f32[128,1024]{1,0:T(8,128)S(1)} %get-tuple-element.13.refs_1_, f32[128,1024]{1,0:T(8,128)S(1)} %get-tuple-element.14.refs_2_, ...), custom_call_target="tpu_custom_call" | custom-call | tf_op jit(solution)/shard_map/pallas_call | solution.py:285
  38.9 18.4 %all_to_all.21.refs_0_ = bf16[16,128,128]{2,1,0:T(8,128)(2,1)S(1)} all-to-all(bf16[16,128,128]{2,1,0:T(8,128)(2,1)S(1)} %get-tuple-element.16), channel_id=1, replica_groups=mesh['grp'=2,'row'=4,'half'=2,'near'=2] {'half','near','row'}, dimensions={0} | all-to-all | bytes 1048576 | tf_op jit(solution)/shard_map/all_to_all | solution.py:296
  57.3 1.1 %shard_map.104 = bf16[16,64,128]{2,1,0:T(8,128)(2,1)S(1)} custom-call(bf16[16,128,128]{2,1,0:T(8,128)(2,1)S(1)} %all_to_all.21.refs_0_), custom_call_target="tpu_custom_call" | custom-call | tf_op jit(solution)/shard_map/pallas_call | solution.py:285
  58.4 0.0 copy-start.2
  58.4 0.0 copy-start.5
  58.4 14.1 %all_to_all.22.refs_0_ = bf16[16,64,128]{2,1,0:T(8,128)(2,1)S(1)} all-to-all(bf16[16,64,128]{2,1,0:T(8,128)(2,1)S(1)} %shard_map.104), channel_id=1, replica_groups=mesh['grp'=2,'row'=4,'half'=2,'near'=2] {'half','near','row'}, dimensions={0} | all-to-all | bytes 524288 | tf_op jit(solution)/shard_map/all_to_all | solution.py:296
  72.5 0.0 copy-done.2
  72.5 0.0 copy-done.5
  72.5 2.9 %shard_map.105 = f32[4,8,32,128]{3,2,1,0:T(8,128)} custom-call(bf16[16,64,128]{2,1,0:T(8,128)(2,1)S(1)} %all_to_all.22.refs_0_, f32[128,1024]{1,0:T(8,128)S(1)} %get-tuple-element.17.refs_1_, f32[128,1024]{1,0:T(8,128)S(1)} %get-tuple-element.18.refs_2_, f32[8,128]{1,0:T(8,128)S(1)} %get-tuple-element.15.refs_4_.refs_3_, bf16[2,128,128]{2,1,0:T(8,128)(2,1)S(1)} %copy-done.3, ...), custom_call_target="tpu_custom_call" | custom-call | tf_op jit(solution)/shard_map/pallas_call | solution.py:285
Async XLA Ops:
  2.6 5.4 %copy-start = (f32[32,32,128]{2,1,0:T(8,128)S(1)}, f32[32,32,128]{2,1,0:T(8,128)}, u32[]{:S(2)}) copy-start(f32[32,32,128]{2,1,0:T(8,128)} %param.10) | copy-start | bytes 1572868
  2.6 5.4 %copy-start.4 = (bf16[2,128,128]{2,1,0:T(8,128)(2,1)S(1)}, bf16[2,128,128]{2,1,0:T(8,128)(2,1)}, u32[]{:S(2)}) copy-start(bf16[2,128,128]{2,1,0:T(8,128)(2,1)} %refs_6_.2) | copy-start | bytes 196612
  2.6 5.4 %copy-start.6 = (s32[32,32]{1,0:T(8,128)S(1)}, s32[32,32]{1,0:T(8,128)}, u32[]{:S(2)}) copy-start(s32[32,32]{1,0:T(8,128)} %refs_1_.3) | copy-start | bytes 12292
  2.6 5.4 %copy-start.8 = (f32[2,128]{1,0:T(2,128)S(1)}, f32[2,128]{1,0:T(2,128)}, u32[]{:S(2)}) copy-start(f32[2,128]{1,0:T(2,128)} %refs_4_.2) | copy-start | bytes 3076
  2.6 14.2 %all-to-all-start = ((bf16[8,256,128]{2,1,0:T(8,128)(2,1)}), bf16[8,256,128]{2,1,0:T(8,128)(2,1)S(1)}, u32[]{:S(2)}, u32[]{:S(2)}) async-start(bf16[8,256,128]{2,1,0:T(8,128)(2,1)} %shard_map.100), calls=%async_computation | async-start | bytes 1048576 | tf_op jit(solution)/shard_map/all_to_all | solution.py:296
  8.0 0.7 copy-start.7
  8.0 0.7 copy-start.9
  18.3 19.3 %copy-start.1 = (bf16[2,128,512]{2,1,0:T(8,128)(2,1)S(1)}, bf16[2,128,512]{2,1,0:T(8,128)(2,1)}, u32[]{:S(2)}) copy-start(bf16[2,128,512]{2,1,0:T(8,128)(2,1)} %refs_5_.2) | copy-start | bytes 786436
  18.3 19.3 %copy-start.3 = (bf16[2,128,128]{2,1,0:T(8,128)(2,1)S(1)}, bf16[2,128,128]{2,1,0:T(8,128)(2,1)}, u32[]{:S(2)}) copy-start(bf16[2,128,128]{2,1,0:T(8,128)(2,1)} %refs_4_.3) | copy-start | bytes 196612
  58.4 14.1 %copy-start.2 = (bf16[128,1024]{1,0:T(8,128)(2,1)S(1)}, bf16[128,1024]{1,0:T(8,128)(2,1)}, u32[]{:S(2)}) copy-start(bf16[128,1024]{1,0:T(8,128)(2,1)} %refs_5_.3) | copy-start | bytes 786436
  58.4 14.1 %copy-start.5 = (bf16[512,128]{1,0:T(8,128)(2,1)S(1)}, bf16[512,128]{1,0:T(8,128)(2,1)}, u32[]{:S(2)}) copy-start(bf16[512,128]{1,0:T(8,128)(2,1)} %refs_6_.3) | copy-start | bytes 393220

commit v13 on v12

--- a/solution.py
+++ b/solution.py
@@ -9,11 +9,23 @@
 from jax.sharding import PartitionSpec as P
 
 NEAR_AXES = ("near", "row")
-ALL_AXES = ("half", "near", "row")
+ALL_AXES = ("near", "row", "half")
 LANES = 128
 VMEM_BYTES = 24 * 1024 * 1024
 FULL_VMEM_BYTES = 60 * 1024 * 1024
 F32, BF16 = jnp.float32, jnp.bfloat16
+
+
+def count_devices(axes, sizes):
+    found = {}
+    for half in range(sizes["half"]):
+        for near in range(sizes["near"]):
+            for row in range(sizes["row"]):
+                index, at = 0, {"half": half, "near": near, "row": row}
+                for axis in axes:
+                    index = index * sizes[axis] + at[axis]
+                found[half, near, row] = index
+    return found
 
 
 def dot(left, right, contract=(1, 0)):
@@ -86,17 +98,22 @@
     return jnp.concatenate([x_ref[slot, line] for slot in range(x_ref.shape[0])], axis=0)
 
 
-def project_kernel(share, ins, outs, stage_ref, x_ref, mask_ref, gain_ref, weight_ref, sems):
-    (message_ref,) = outs
+def project_kernel(share, ins, outs, stage_ref, x_ref, mask_ref, gain_ref, weight_ref, message_ref, sems, out_sems):
+    (message_out,) = outs
     x_in, mask_in, gain_in, weight_in = ins
     lines = x_ref.shape[1]
-    pairs = [(weight_in.at[0], weight_ref), (x_in, x_ref), (gain_in, gain_ref), (mask_in, mask_ref)]
+    pairs = [(gain_in, gain_ref), (mask_in, mask_ref), (weight_in.at[0], weight_ref)]
+    pairs += [(x_in.at[slot], x_ref.at[slot]) for slot in range(x_ref.shape[0])]
     for copy in start_all(pairs, sems):
         copy.wait()
     mask = token_mask(mask_ref[...], lines)
     current = jnp.concatenate([line_tokens(x_ref, line).T for line in range(lines)], axis=1)
     normed = channel_norm(current, spread_gain(gain_ref[0:1, :]))
     emit_message(normed, halved(weight_ref[...]), mask, 0, message_ref, stage_ref, share)
+    size = message_ref.shape[0] // out_sems.shape[0]
+    blocks = [pl.ds(first, size) for first in range(0, message_ref.shape[0], size)]
+    for copy in start_all([(message_ref.at[block], message_out.at[block]) for block in blocks], out_sems):
+        copy.wait()
 
 
 def prepare_kernel(ins, outs):
@@ -125,7 +142,9 @@
     )
 
 
-def combine_kernel(rows, cols, near, breadth, share, outgoing, ins, outs):
+def combine_kernel(sizes, sources, owners, breadth, share, outgoing, ins, outs):
+    rows, cols = sizes["row"], sizes["half"] * sizes["near"]
+    near = len(sources) // rows
     both_ref, combined_ref = ins[0], outs[0]
     slots = LANES // breadth
     span = both_ref.shape[1]
@@ -142,7 +161,7 @@
     order = one_hot(span, span, source)
     wide = []
     for row in range(rows):
-        here = jnp.concatenate([both_ref[col * rows + row] for col in range(near)], axis=1)
+        here = jnp.concatenate([both_ref[sources[col, row]] for col in range(near)], axis=1)
         here = dot(order, here).astype(BF16)
         wide.append(jnp.concatenate([here[n * size : (n + 1) * size] for n in range(pack)], axis=1))
     wide = jnp.concatenate(wide, axis=0)
@@ -183,21 +202,19 @@
         for low in range(slots):
             for row in range(rows):
                 first = row * share * lines
-                combined_ref[(high * slots + low) * rows + row] = back[
+                combined_ref[owners[high * slots + low, row]] = back[
                     first : first + share * lines, low * LANES : (low + 1) * LANES
                 ]
 
 
-def hold_combined(combined_ref, stage_ref, share):
+def hold_combined(combined_ref, stage_ref, share, sources):
     span = combined_ref.shape[1]
     lines = span // share
-    owners = stage_ref.shape[0] // span
-    halves = combined_ref.shape[0] // owners
     order = one_hot(span, span, lambda row: row % share * lines + row // share)
-    order = jnp.concatenate([order] * halves, axis=1)
-    for first in range(0, owners, 2):
+    order = jnp.concatenate([order] * len(sources[0]), axis=1)
+    for first in range(0, len(sources), 2):
         blocks = [
-            jnp.concatenate([combined_ref[half * owners + owner] for half in range(halves)], axis=0)
+            jnp.concatenate([combined_ref[source] for source in sources[owner]], axis=0)
             for owner in (first, first + 1)
         ]
         ordered = dot(order, jnp.concatenate(blocks, axis=1))
@@ -219,13 +236,13 @@
     return jnp.concatenate(columns, axis=1)
 
 
-def middle_kernel(share, next_share, chunk, ins, outs, stage_ref, message_stage_ref):
+def middle_kernel(share, sources, next_share, chunk, ins, outs, stage_ref, message_stage_ref):
     combined_ref, x_ref, gate_ref, mask_ref, gains_ref, proj_ref, gate_weight_ref, out_ref = ins
     message_ref, gate_out, next_ref = outs
     tokens = x_ref.shape[1]
     lines = tokens // LANES
     owners = x_ref.shape[0] // share
-    hold_combined(combined_ref, stage_ref, share)
+    hold_combined(combined_ref, stage_ref, share, sources)
     mask = mask_ref[...]
     gain_out, gain = [spread_gain(gains_ref[n : n + 1, :]) for n in (0, 1)]
     out_t, proj_t, gate_t = halved(out_ref[0]), halved(proj_ref[1]), halved(gate_weight_ref[1])
@@ -240,7 +257,7 @@
         gate_out[:, here] = twice_sigmoid(dot(gate_t, normed))
 
 
-def last_kernel(share, chunk, ins, outs, stage_ref, result_ref, sems):
+def last_kernel(share, sources, chunk, ins, outs, stage_ref, result_ref, sems):
     combined_ref, x_ref, gate_ref, gains_ref, out_ref, up_ref, down_ref = ins
     (result_out,) = outs
     slots, lines, breadth, channels = result_ref.shape
@@ -250,7 +267,7 @@
     gain_out, gain = [spread_gain(gains_ref[n : n + 1, :]) for n in (2, 3)]
     out_t, down_t = halved(out_ref[1]), down_ref[...].T
     gate_t, up_t = halved(up_ref[:, :half]), up_ref[:, half:].T
-    hold_combined(combined_ref, stage_ref, share)
+    hold_combined(combined_ref, stage_ref, share, sources)
     writes = []
     for first in range(0, lines, count):
         here = slice(first * LANES, (first + count) * LANES)
@@ -270,7 +287,8 @@
                 base = part * LANES + slot * breadth
                 result_ref[slot, first + part] = result[base : base + breadth]
         piece = slice(first, first + count)
-        writes += start_all([(result_ref.at[:, piece], result_out.at[:, piece])], sems, first // count)
+        pairs = [(result_ref.at[slot, piece], result_out.at[slot, piece]) for slot in range(slots)]
+        writes += start_all(pairs, sems, first // count * slots)
     for write in writes:
         write.wait()
 
@@ -297,9 +315,7 @@
 
 
 def per_device(
-    rows,
-    halves,
-    nears,
+    sizes,
     pair_map,
     pair_mask,
     gain_in,
@@ -315,11 +331,11 @@
     tokens = height * breadth
     lines = tokens // LANES
     hid = gain_out.shape[1]
-    cols = halves * nears
+    rows, cols = sizes["row"], sizes["half"] * sizes["near"]
     owners = rows * cols
     share = hid // owners
     chunk = min(4 * LANES, tokens)
-    split = halves if share % 8 == 0 else 1
+    split = sizes["half"] if share % 8 == 0 else 1
     first_share = split * share
     held = ((LANES // breadth, lines, breadth, channels), F32)
     grouped = pair_map.reshape(held[0])
@@ -330,9 +346,17 @@
     def message(own):
         return ((hid // own, 2 * own * lines, LANES), BF16)
 
-    def combine(operands, own, outgoing):
-        near = cols * share // own
-        kernel = functools.partial(combine_kernel, rows, cols, near, breadth, own, outgoing)
+    nears = sizes["near"]
+    by_all, by_near = count_devices(ALL_AXES, sizes), count_devices(NEAR_AXES, sizes)
+    everyone = {(half * nears + near, row): n for (half, near, row), n in by_all.items()}
+    beside = {(near, row): n for (half, near, row), n in by_near.items()} if split > 1 else everyone
+    single = [[n] for n in range(owners)]
+    paired = [[] for _ in range(owners // split)]
+    for at, n in by_all.items():
+        paired[by_near[at] if split > 1 else n].append(n)
+
+    def combine(operands, own, sources, outgoing):
+        kernel = functools.partial(combine_kernel, sizes, sources, everyone, breadth, own, outgoing)
         answer = ((owners, own * lines, LANES), BF16)
         return exchange(call(kernel, operands, [answer])[0], ALL_AXES)
 
@@ -346,9 +370,12 @@
             pltpu.VMEM(pair_mask.shape, jnp.int32),
             pltpu.VMEM(gain_in.shape, F32),
             pltpu.VMEM(proj_weight.shape[1:], BF16),
-            pltpu.SemaphoreType.DMA((4,)),
+            pltpu.VMEM(*message(first_share)),
+            pltpu.SemaphoreType.DMA((3 + LANES // breadth,)),
+            pltpu.SemaphoreType.DMA((8,)),
         ),
         in_hbm=True,
+        out_hbm=True,
     )
     gate, current, mask, gains = call(
         prepare_kernel,
@@ -356,19 +383,19 @@
         [wide, wide, ((lines, LANES), F32), ((8, channels), F32)],
     )
     both = exchange(both, NEAR_AXES if split > 1 else ALL_AXES)
-    combined = combine((both, mask), first_share, True)
+    combined = combine((both, mask), first_share, beside, True)
     both, gate, current = call(
-        functools.partial(middle_kernel, first_share, share, chunk),
+        functools.partial(middle_kernel, first_share, paired, share, chunk),
         (combined, current, gate, mask, gains, proj_weight, gate_weight, out_weight),
         [message(share), wide, wide],
         (result, spare),
     )
-    combined = combine((exchange(both, ALL_AXES),), share, False)
+    combined = combine((exchange(both, ALL_AXES),), share, everyone, False)
     (pair_out,) = call(
-        functools.partial(last_kernel, share, chunk),
+        functools.partial(last_kernel, share, single, chunk),
         (combined, current, gate, gains, out_weight, trans_up, trans_down),
         [held],
-        (result, pltpu.VMEM(*held), pltpu.SemaphoreType.DMA((tokens // chunk,))),
+        (result, pltpu.VMEM(*held), pltpu.SemaphoreType.DMA((tokens // chunk * (LANES // breadth),))),
         out_hbm=True,
     )
     return pair_out.reshape(pair_map.shape)
@@ -377,12 +404,12 @@
 def solution(mesh):
     groups, rows, cols = (mesh.shape[name] for name in ("grp", "row", "col"))
     halves = 2 if cols % 2 == 0 else 1
-    nears = cols // halves
-    folded = Mesh(mesh.devices.reshape(groups, rows, halves, nears), ("grp", "row", "half", "near"))
+    sizes = {"half": halves, "near": cols // halves, "row": rows}
+    folded = Mesh(mesh.devices.reshape(groups, rows, halves, cols // halves), ("grp", "row", "half", "near"))
     tokens = (("grp", "row"), ("half", "near"))
     in_specs = (P(*tokens, None), P(*tokens)) + (P(),) * 8
 
     def body(*args):
-        return per_device(rows, halves, nears, *args)
+        return per_device(sizes, *args)
 
     return jax.shard_map(body, mesh=folded, in_specs=in_specs, out_specs=P(*tokens, None), check_vma=False)

time: 75.8 us -> 76.3 us (level)
  no operation moved by 1% of the time
where the time goes in v13:
time: 76.3 us; the launch traced here: 75.9 us
  blocking collectives  52.1 us (68%)
  Pallas kernels  9.96 us (13%)
  waiting for transfers between devices  7.71 us (10%)
  starting transfers between devices  5.37 us (7%)
    all_to_all x3, blocking collectives, exchange(): return lax.all_to_all(values, axes, split_axis=0, concat_axis=0, tiled=True)  52.1 us
    pallas_call x6, Pallas kernels, call(): pl.pallas_call(body, in_specs=[in_place if in_hbm else held] * count, out...  9.96 us
    all_to_all x1, waiting for transfers between devices, exchange(): return lax.all_to_all(values, axes, split_axis=0, concat_axis=0, tiled=True)  7.71 us
    all_to_all x1, starting transfers between devices, exchange(): return lax.all_to_all(values, axes, split_axis=0, concat_axis=0, tiled=True)  5.37 us
  transfers between devices with their start and end apart: 1, of which 1 were waited for; matrix products, arithmetic and copies ran while one was open for 0% of the time, Pallas kernels for 1%

profile of v13, /device:TPU:0, one launch (start us, length us, event | category | flops | bytes accessed | tf_op | source)
XLA Modules:
  0.0 75.9 jit_solution(13936927841327118605)
XLA Ops:
  0.0 2.7 %shard_map.100 = bf16[8,256,128]{2,1,0:T(8,128)(2,1)} custom-call(f32[4,8,32,128]{3,2,1,0:T(8,128)} %bitcast.3, s32[32,32]{1,0:T(8,128)} %refs_1_.3, f32[2,128]{1,0:T(2,128)} %refs_3_.3, bf16[2,128,512]{2,1,0:T(8,128)(2,1)} %refs_5_.2), custom_call_target="tpu_custom_call" | custom-call | tf_op jit(solution)/shard_map/pallas_call | solution.py:303
  2.7 0.0 copy-start
  2.7 0.0 copy-start.4
  2.8 0.0 copy-start.6
  2.8 0.0 copy-start.8
  2.8 5.4 %all-to-all-start = ((bf16[8,256,128]{2,1,0:T(8,128)(2,1)}), bf16[8,256,128]{2,1,0:T(8,128)(2,1)S(1)}, u32[]{:S(2)}, u32[]{:S(2)}) async-start(bf16[8,256,128]{2,1,0:T(8,128)(2,1)} %shard_map.100), calls=%async_computation | async-start | bytes 1048576 | tf_op jit(solution)/shard_map/all_to_all | solution.py:314
  8.2 0.0 copy-start.7
  8.2 0.0 copy-start.9
  8.2 0.0 copy-done
  8.2 0.0 copy-done.4
  8.2 0.0 copy-done.6
  8.2 0.0 copy-done.8
  8.2 0.6 copy-done.7
  8.8 0.0 copy-done.9
  8.8 0.4 shard_map.101
  9.3 7.7 %all-to-all-done.refs_0_ = bf16[8,256,128]{2,1,0:T(8,128)(2,1)S(1)} async-done(((bf16[8,256,128]{2,1,0:T(8,128)(2,1)}), bf16[8,256,128]{2,1,0:T(8,128)(2,1)S(1)}, u32[]{:S(2)}, u32[]{:S(2)}) %all-to-all-start) | async-done | bytes 524320 | tf_op jit(solution)/shard_map/all_to_all | solution.py:314
  17.0 1.5 %shard_map.102 = bf16[16,128,128]{2,1,0:T(8,128)(2,1)S(1)} custom-call(bf16[8,256,128]{2,1,0:T(8,128)(2,1)S(1)} %all-to-all-done.refs_0_, f32[8,128]{1,0:T(8,128)S(1)} %get-tuple-element.12.refs_1_.refs_3_), custom_call_target="tpu_custom_call" | custom-call | tf_op jit(solution)/shard_map/pallas_call | solution.py:303
  18.5 0.0 copy-start.1
  18.5 0.0 copy-start.3
  18.5 20.1 %all_to_all.20.refs_0_ = bf16[16,128,128]{2,1,0:T(8,128)(2,1)S(1)} all-to-all(bf16[16,128,128]{2,1,0:T(8,128)(2,1)S(1)} %shard_map.102), channel_id=1, replica_groups=mesh['grp'=2,'row'=4,'half'=2,'near'=2] {'near','row','half'}, dimensions={0} | all-to-all | bytes 1048576 | tf_op jit(solution)/shard_map/all_to_all | solution.py:314
  38.6 0.0 copy-done.1
  38.6 0.0 copy-done.3
  38.6 1.3 %shard_map.103 = (bf16[16,128,128]{2,1,0:T(8,128)(2,1)S(1)}, f32[128,1024]{1,0:T(8,128)S(1)}, f32[128,1024]{1,0:T(8,128)S(1)}) custom-call(bf16[16,128,128]{2,1,0:T(8,128)(2,1)S(1)} %all_to_all.20.refs_0_, f32[128,1024]{1,0:T(8,128)S(1)} %get-tuple-element.13.refs_1_, f32[128,1024]{1,0:T(8,128)S(1)} %get-tuple-element.14.refs_2_, ...), custom_call_target="tpu_custom_call" | custom-call | tf_op jit(solution)/shard_map/pallas_call | solution.py:303
  39.9 18.5 %all_to_all.21.refs_0_ = bf16[16,128,128]{2,1,0:T(8,128)(2,1)S(1)} all-to-all(bf16[16,128,128]{2,1,0:T(8,128)(2,1)S(1)} %get-tuple-element.16), channel_id=1, replica_groups=mesh['grp'=2,'row'=4,'half'=2,'near'=2] {'near','row','half'}, dimensions={0} | all-to-all | bytes 1048576 | tf_op jit(solution)/shard_map/all_to_all | solution.py:314
  58.3 1.1 %shard_map.104 = bf16[16,64,128]{2,1,0:T(8,128)(2,1)S(1)} custom-call(bf16[16,128,128]{2,1,0:T(8,128)(2,1)S(1)} %all_to_all.21.refs_0_), custom_call_target="tpu_custom_call" | custom-call | tf_op jit(solution)/shard_map/pallas_call | solution.py:303
  59.4 0.0 copy-start.2
  59.5 0.0 copy-start.5
  59.5 13.5 %all_to_all.22.refs_0_ = bf16[16,64,128]{2,1,0:T(8,128)(2,1)S(1)} all-to-all(bf16[16,64,128]{2,1,0:T(8,128)(2,1)S(1)} %shard_map.104), channel_id=1, replica_groups=mesh['grp'=2,'row'=4,'half'=2,'near'=2] {'near','row','half'}, dimensions={0} | all-to-all | bytes 524288 | tf_op jit(solution)/shard_map/all_to_all | solution.py:314
  73.0 0.0 copy-done.2
  73.0 0.0 copy-done.5
  73.0 2.9 %shard_map.105 = f32[4,8,32,128]{3,2,1,0:T(8,128)} custom-call(bf16[16,64,128]{2,1,0:T(8,128)(2,1)S(1)} %all_to_all.22.refs_0_, f32[128,1024]{1,0:T(8,128)S(1)} %get-tuple-element.17.refs_1_, f32[128,1024]{1,0:T(8,128)S(1)} %get-tuple-element.18.refs_2_, f32[8,128]{1,0:T(8,128)S(1)} %get-tuple-element.15.refs_4_.refs_3_, bf16[2,128,128]{2,1,0:T(8,128)(2,1)S(1)} %copy-done.3, ...), custom_call_target="tpu_custom_call" | custom-call | tf_op jit(solution)/shard_map/pallas_call | solution.py:303
Async XLA Ops:
  2.7 5.4 %copy-start = (f32[32,32,128]{2,1,0:T(8,128)S(1)}, f32[32,32,128]{2,1,0:T(8,128)}, u32[]{:S(2)}) copy-start(f32[32,32,128]{2,1,0:T(8,128)} %param.10) | copy-start | bytes 1572868
  2.7 5.4 %copy-start.4 = (bf16[2,128,128]{2,1,0:T(8,128)(2,1)S(1)}, bf16[2,128,128]{2,1,0:T(8,128)(2,1)}, u32[]{:S(2)}) copy-start(bf16[2,128,128]{2,1,0:T(8,128)(2,1)} %refs_6_.2) | copy-start | bytes 196612
  2.8 5.4 %copy-start.6 = (s32[32,32]{1,0:T(8,128)S(1)}, s32[32,32]{1,0:T(8,128)}, u32[]{:S(2)}) copy-start(s32[32,32]{1,0:T(8,128)} %refs_1_.3) | copy-start | bytes 12292
  2.8 5.4 %copy-start.8 = (f32[2,128]{1,0:T(2,128)S(1)}, f32[2,128]{1,0:T(2,128)}, u32[]{:S(2)}) copy-start(f32[2,128]{1,0:T(2,128)} %refs_4_.2) | copy-start | bytes 3076
  2.8 14.2 %all-to-all-start = ((bf16[8,256,128]{2,1,0:T(8,128)(2,1)}), bf16[8,256,128]{2,1,0:T(8,128)(2,1)S(1)}, u32[]{:S(2)}, u32[]{:S(2)}) async-start(bf16[8,256,128]{2,1,0:T(8,128)(2,1)} %shard_map.100), calls=%async_computation | async-start | bytes 1048576 | tf_op jit(solution)/shard_map/all_to_all | solution.py:314
  8.2 0.7 copy-start.7
  8.2 0.7 copy-start.9
  18.5 20.1 %copy-start.1 = (bf16[2,128,512]{2,1,0:T(8,128)(2,1)S(1)}, bf16[2,128,512]{2,1,0:T(8,128)(2,1)}, u32[]{:S(2)}) copy-start(bf16[2,128,512]{2,1,0:T(8,128)(2,1)} %refs_5_.2) | copy-start | bytes 786436
  18.5 20.1 %copy-start.3 = (bf16[2,128,128]{2,1,0:T(8,128)(2,1)S(1)}, bf16[2,128,128]{2,1,0:T(8,128)(2,1)}, u32[]{:S(2)}) copy-start(bf16[2,128,128]{2,1,0:T(8,128)(2,1)} %refs_4_.3) | copy-start | bytes 196612
  59.4 13.6 %copy-start.2 = (bf16[128,1024]{1,0:T(8,128)(2,1)S(1)}, bf16[128,1024]{1,0:T(8,128)(2,1)}, u32[]{:S(2)}) copy-start(bf16[128,1024]{1,0:T(8,128)(2,1)} %refs_5_.3) | copy-start | bytes 786436
  59.5 13.6 %copy-start.5 = (bf16[512,128]{1,0:T(8,128)(2,1)S(1)}, bf16[512,128]{1,0:T(8,128)(2,1)}, u32[]{:S(2)}) copy-start(bf16[512,128]{1,0:T(8,128)(2,1)} %refs_6_.3) | copy-start | bytes 393220

commit v14 on v12

--- a/solution.py
+++ b/solution.py
@@ -12,7 +12,6 @@
 ALL_AXES = ("half", "near", "row")
 LANES = 128
 VMEM_BYTES = 24 * 1024 * 1024
-FULL_VMEM_BYTES = 60 * 1024 * 1024
 F32, BF16 = jnp.float32, jnp.bfloat16
 
 
@@ -86,28 +85,28 @@
     return jnp.concatenate([x_ref[slot, line] for slot in range(x_ref.shape[0])], axis=0)
 
 
-def project_kernel(share, ins, outs, stage_ref, x_ref, mask_ref, gain_ref, weight_ref, sems):
-    (message_ref,) = outs
-    x_in, mask_in, gain_in, weight_in = ins
+def project_kernel(share, ins, outs, stage_ref, x_ref, mask_ref, weight_ref, gate_ref, gain_in_ref, gain_out_ref, trans_gain_ref, sems):
+    message_ref, gate_out, turned_out, mask_out, gains_out = outs
+    x_in, mask_in, weight_in, gate_in, gain_in, gain_out, trans_gain = ins
     lines = x_ref.shape[1]
-    pairs = [(weight_in.at[0], weight_ref), (x_in, x_ref), (gain_in, gain_ref), (mask_in, mask_ref)]
+    pairs = [
+        (weight_in.at[0], weight_ref),
+        (x_in, x_ref),
+        (gain_in, gain_in_ref),
+        (mask_in, mask_ref),
+        (gate_in.at[0], gate_ref),
+        (gain_out, gain_out_ref),
+        (trans_gain, trans_gain_ref),
+    ]
     for copy in start_all(pairs, sems):
         copy.wait()
     mask = token_mask(mask_ref[...], lines)
     current = jnp.concatenate([line_tokens(x_ref, line).T for line in range(lines)], axis=1)
-    normed = channel_norm(current, spread_gain(gain_ref[0:1, :]))
+    normed = channel_norm(current, spread_gain(gain_in_ref[0:1, :]))
     emit_message(normed, halved(weight_ref[...]), mask, 0, message_ref, stage_ref, share)
-
-
-def prepare_kernel(ins, outs):
-    x_ref, mask_ref, gate_ref, gain_in_ref, gain_out_ref, trans_gain_ref = ins
-    gate_out, x_out, mask_out, gains_out = outs
-    lines = x_ref.shape[1]
-    current = jnp.concatenate([line_tokens(x_ref, line).T for line in range(lines)], axis=1)
-    x_out[...] = current
-    normed = channel_norm(current, spread_gain(gain_in_ref[0:1, :]))
-    gate_out[...] = twice_sigmoid(dot(halved(gate_ref[0]), normed))
-    mask_out[...] = token_mask(mask_ref[...], lines)
+    gate_out[...] = twice_sigmoid(dot(halved(gate_ref[...]), normed))
+    turned_out[...] = current
+    mask_out[...] = mask
     rows = [gain_out_ref[0:1, :], gain_in_ref[1:2, :], gain_out_ref[1:2, :], trans_gain_ref[...]]
     gains_out[...] = jnp.concatenate(rows + rows, axis=0)
 
@@ -126,7 +125,7 @@
 
 
 def combine_kernel(rows, cols, near, breadth, share, outgoing, ins, outs):
-    both_ref, combined_ref = ins[0], outs[0]
+    (both_ref,), (combined_ref,) = ins, outs
     slots = LANES // breadth
     span = both_ref.shape[1]
     lines = span // (2 * share)
@@ -288,8 +287,8 @@
         out_specs=[in_place if out_hbm else held] * len(outs),
         out_shape=[jax.ShapeDtypeStruct(shape, dtype) for shape, dtype in outs],
         scratch_shapes=list(scratch),
-        compiler_params=pltpu.CompilerParams(vmem_limit_bytes=FULL_VMEM_BYTES if in_hbm else VMEM_BYTES),
-    )(*operands)
+        compiler_params=pltpu.CompilerParams(vmem_limit_bytes=VMEM_BYTES),
+    )(*[pltpu.with_memory_space_constraint(array, pltpu.HBM) if in_hbm else array for array in operands])
 
 
 def exchange(values, axes):
@@ -330,40 +329,36 @@
     def message(own):
         return ((hid // own, 2 * own * lines, LANES), BF16)
 
-    def combine(operands, own, outgoing):
+    def combine(both, own, outgoing):
         near = cols * share // own
         kernel = functools.partial(combine_kernel, rows, cols, near, breadth, own, outgoing)
         answer = ((owners, own * lines, LANES), BF16)
-        return exchange(call(kernel, operands, [answer])[0], ALL_AXES)
-
-    (both,) = call(
+        return exchange(call(kernel, (both,), [answer])[0], ALL_AXES)
+
+    operands = (grouped, pair_mask, proj_weight, gate_weight, gain_in, gain_out, trans_gain.reshape(1, -1))
+    both, gate, current, mask, gains = call(
         functools.partial(project_kernel, first_share),
-        (grouped, pair_mask, gain_in, proj_weight),
-        [message(first_share)],
+        operands,
+        [message(first_share), wide, wide, ((lines, LANES), F32), ((8, channels), F32)],
         (
             spare,
-            pltpu.VMEM(*held),
-            pltpu.VMEM(pair_mask.shape, jnp.int32),
-            pltpu.VMEM(gain_in.shape, F32),
-            pltpu.VMEM(proj_weight.shape[1:], BF16),
-            pltpu.SemaphoreType.DMA((4,)),
+            *[
+                pltpu.VMEM(array.shape[1:] if array.ndim == 3 else array.shape, array.dtype)
+                for array in operands
+            ],
+            pltpu.SemaphoreType.DMA((len(operands),)),
         ),
         in_hbm=True,
     )
-    gate, current, mask, gains = call(
-        prepare_kernel,
-        (grouped, pair_mask, gate_weight, gain_in, gain_out, trans_gain.reshape(1, -1)),
-        [wide, wide, ((lines, LANES), F32), ((8, channels), F32)],
-    )
     both = exchange(both, NEAR_AXES if split > 1 else ALL_AXES)
-    combined = combine((both, mask), first_share, True)
+    combined = combine(both, first_share, True)
     both, gate, current = call(
         functools.partial(middle_kernel, first_share, share, chunk),
         (combined, current, gate, mask, gains, proj_weight, gate_weight, out_weight),
         [message(share), wide, wide],
         (result, spare),
     )
-    combined = combine((exchange(both, ALL_AXES),), share, False)
+    combined = combine(exchange(both, ALL_AXES), share, False)
     (pair_out,) = call(
         functools.partial(last_kernel, share, chunk),
         (combined, current, gate, gains, out_weight, trans_up, trans_down),

time: 75.8 us -> 74.7 us (0.985)
  blocking collectives: 51.7 us -> 65.7 us
  waiting for transfers between devices: 7.71 us -> 0 us
  starting transfers between devices: 5.37 us -> 0 us
  Pallas kernels: 9.76 us -> 8.62 us
    all_to_all x3 -> x4, blocking collectives: 51.7 us -> 65.7 us  [exchange(): return lax.all_to_all(values, axes, split_axis=0, concat_axis=0, tiled=True)]
    all_to_all x1 -> x0, waiting for transfers between devices: 7.71 us -> none  [exchange(): return lax.all_to_all(values, axes, split_axis=0, concat_axis=0, tiled=True)]
    all_to_all x1 -> x0, starting transfers between devices: 5.37 us -> none  [exchange(): return lax.all_to_all(values, axes, split_axis=0, concat_axis=0, tiled=True)]
    pallas_call x6 -> x5, Pallas kernels: 9.76 us -> 8.62 us  [call(): pl.pallas_call(body, in_specs=[in_place if in_hbm else held] * count, out...]
  transfers between devices with their start and end apart: 1 -> 0, of which waited for: 1 -> 0; matrix products, arithmetic and copies ran while one was open for 0% -> 0% of each run, Pallas kernels for 1% -> 0%
where the time goes in v14:
time: 74.7 us; the launch traced here: 74.4 us
  blocking collectives  65.7 us (88%)
  Pallas kernels  8.62 us (12%)
    all_to_all x4, blocking collectives, exchange(): return lax.all_to_all(values, axes, split_axis=0, concat_axis=0, tiled=True)  65.7 us
    pallas_call x5, Pallas kernels, call(): pl.pallas_call(body, in_specs=[in_place if in_hbm else held] * count, out...  8.62 us

profile of v14, /device:TPU:0, one launch (start us, length us, event | category | flops | bytes accessed | tf_op | source)
XLA Modules:
  0.0 74.4 jit_solution(16831316704205599132)
XLA Ops:
  0.0 1.9 %shard_map.100 = (bf16[8,256,128]{2,1,0:T(8,128)(2,1)S(1)}, f32[128,1024]{1,0:T(8,128)S(1)}, f32[128,1024]{1,0:T(8,128)S(1)}, f32[8,128]{1,0:T(8,128)S(1)}, f32[8,128]{1,0:T(8,128)S(1)}) custom-call(f32[4,8,32,128]{3,2,1,0:T(8,128)} %bitcast.3, s32[32,32]{1,0:T(8,128)} %refs_1_.1, bf16[2,128,512]{2,1,0:T(8,128)(2,1)} %refs_5_.4, ...), custom_call_target="tpu_custom_call" | custom-call | tf_op jit(solution)/shard_map/pallas_call | solution.py:284
  1.9 13.9 %all_to_all.20.refs_0_ = bf16[8,256,128]{2,1,0:T(8,128)(2,1)S(1)} all-to-all(bf16[8,256,128]{2,1,0:T(8,128)(2,1)S(1)} %get-tuple-element.13), channel_id=1, replica_groups=mesh['grp'=2,'row'=4,'half'=2,'near'=2] {'near','row'}, dimensions={0} | all-to-all | bytes 1048576 | tf_op jit(solution)/shard_map/all_to_all | solution.py:295
  15.8 1.5 %shard_map.101 = bf16[16,128,128]{2,1,0:T(8,128)(2,1)S(1)} custom-call(bf16[8,256,128]{2,1,0:T(8,128)(2,1)S(1)} %all_to_all.20.refs_0_), custom_call_target="tpu_custom_call" | custom-call | tf_op jit(solution)/shard_map/pallas_call | solution.py:284
  17.3 0.0 copy-start
  17.3 0.0 copy-start.2
  17.3 0.0 copy-start.3
  17.3 19.3 %all_to_all.21.refs_0_ = bf16[16,128,128]{2,1,0:T(8,128)(2,1)S(1)} all-to-all(bf16[16,128,128]{2,1,0:T(8,128)(2,1)S(1)} %shard_map.101), channel_id=1, replica_groups=mesh['grp'=2,'row'=4,'half'=2,'near'=2] {'half','near','row'}, dimensions={0} | all-to-all | bytes 1048576 | tf_op jit(solution)/shard_map/all_to_all | solution.py:295
  36.7 0.0 copy-done
  36.7 0.0 copy-done.2
  36.7 0.0 copy-done.3
  36.7 1.3 %shard_map.102 = (bf16[16,128,128]{2,1,0:T(8,128)(2,1)S(1)}, f32[128,1024]{1,0:T(8,128)S(1)}, f32[128,1024]{1,0:T(8,128)S(1)}) custom-call(bf16[16,128,128]{2,1,0:T(8,128)(2,1)S(1)} %all_to_all.21.refs_0_, f32[128,1024]{1,0:T(8,128)S(1)} %get-tuple-element.14.refs_1_, f32[128,1024]{1,0:T(8,128)S(1)} %get-tuple-element.15.refs_2_, ...), custom_call_target="tpu_custom_call" | custom-call | tf_op jit(solution)/shard_map/pallas_call | solution.py:284
  37.9 18.4 %all_to_all.22.refs_0_ = bf16[16,128,128]{2,1,0:T(8,128)(2,1)S(1)} all-to-all(bf16[16,128,128]{2,1,0:T(8,128)(2,1)S(1)} %get-tuple-element.18), channel_id=1, replica_groups=mesh['grp'=2,'row'=4,'half'=2,'near'=2] {'half','near','row'}, dimensions={0} | all-to-all | bytes 1048576 | tf_op jit(solution)/shard_map/all_to_all | solution.py:295
  56.3 1.1 %shard_map.103 = bf16[16,64,128]{2,1,0:T(8,128)(2,1)S(1)} custom-call(bf16[16,128,128]{2,1,0:T(8,128)(2,1)S(1)} %all_to_all.22.refs_0_), custom_call_target="tpu_custom_call" | custom-call | tf_op jit(solution)/shard_map/pallas_call | solution.py:284
  57.4 0.0 copy-start.1
  57.4 0.0 copy-start.4
  57.4 14.1 %all_to_all.23.refs_0_ = bf16[16,64,128]{2,1,0:T(8,128)(2,1)S(1)} all-to-all(bf16[16,64,128]{2,1,0:T(8,128)(2,1)S(1)} %shard_map.103), channel_id=1, replica_groups=mesh['grp'=2,'row'=4,'half'=2,'near'=2] {'half','near','row'}, dimensions={0} | all-to-all | bytes 524288 | tf_op jit(solution)/shard_map/all_to_all | solution.py:295
  71.5 0.0 copy-done.1
  71.5 0.0 copy-done.4
  71.5 2.9 %shard_map.104 = f32[4,8,32,128]{3,2,1,0:T(8,128)} custom-call(bf16[16,64,128]{2,1,0:T(8,128)(2,1)S(1)} %all_to_all.23.refs_0_, f32[128,1024]{1,0:T(8,128)S(1)} %get-tuple-element.19.refs_1_, f32[128,1024]{1,0:T(8,128)S(1)} %get-tuple-element.20.refs_2_, f32[8,128]{1,0:T(8,128)S(1)} %get-tuple-element.17.refs_4_.refs_3_, bf16[2,128,128]{2,1,0:T(8,128)(2,1)S(1)} %copy-done.3, ...), custom_call_target="tpu_custom_call" | custom-call | tf_op jit(solution)/shard_map/pallas_call | solution.py:284
Async XLA Ops:
  17.3 19.3 %copy-start = (bf16[2,128,512]{2,1,0:T(8,128)(2,1)S(1)}, bf16[2,128,512]{2,1,0:T(8,128)(2,1)}, u32[]{:S(2)}) copy-start(bf16[2,128,512]{2,1,0:T(8,128)(2,1)} %refs_5_.4) | copy-start | bytes 786436
  17.3 19.3 %copy-start.2 = (bf16[2,128,128]{2,1,0:T(8,128)(2,1)S(1)}, bf16[2,128,128]{2,1,0:T(8,128)(2,1)}, u32[]{:S(2)}) copy-start(bf16[2,128,128]{2,1,0:T(8,128)(2,1)} %refs_6_.2) | copy-start | bytes 196612
  17.3 19.3 %copy-start.3 = (bf16[2,128,128]{2,1,0:T(8,128)(2,1)S(1)}, bf16[2,128,128]{2,1,0:T(8,128)(2,1)}, u32[]{:S(2)}) copy-start(bf16[2,128,128]{2,1,0:T(8,128)(2,1)} %refs_4_.3) | copy-start | bytes 196612
  57.4 14.1 %copy-start.1 = (bf16[128,1024]{1,0:T(8,128)(2,1)S(1)}, bf16[128,1024]{1,0:T(8,128)(2,1)}, u32[]{:S(2)}) copy-start(bf16[128,1024]{1,0:T(8,128)(2,1)} %refs_5_.5) | copy-start | bytes 786436
  57.4 14.1 %copy-start.4 = (bf16[512,128]{1,0:T(8,128)(2,1)S(1)}, bf16[512,128]{1,0:T(8,128)(2,1)}, u32[]{:S(2)}) copy-start(bf16[512,128]{1,0:T(8,128)(2,1)} %refs_6_.3) | copy-start | bytes 393220

commit v15 on v14

--- a/solution.py
+++ b/solution.py
@@ -250,17 +250,18 @@
     out_t, down_t = halved(out_ref[1]), down_ref[...].T
     gate_t, up_t = halved(up_ref[:, :half]), up_ref[:, half:].T
     hold_combined(combined_ref, stage_ref, share)
+    combined = read_combined(stage_ref, owners, lines, share, 0, lines)
+    hidden = channel_norm(combined, gain_out)
+    whole = x_ref[...] + gate_ref[...] * dot(out_t, hidden)
+    trans_in = channel_norm(whole, gain)
     writes = []
     for first in range(0, lines, count):
         here = slice(first * LANES, (first + count) * LANES)
-        combined = read_combined(stage_ref, owners, lines, share, first, count)
-        hidden = channel_norm(combined, gain_out)
-        current = x_ref[:, here] + gate_ref[:, here] * dot(out_t, hidden)
-        trans_in = channel_norm(current, gain)
+        current = whole[:, here]
         block = min(256, half)
         for base in range(0, half, block):
-            gate_part = dot(gate_t[base : base + block], trans_in)
-            up_part = dot(up_t[base : base + block], trans_in)
+            gate_part = dot(gate_t[base : base + block], trans_in[:, here])
+            up_part = dot(up_t[base : base + block], trans_in[:, here])
             trans_hidden = (gate_part * twice_sigmoid(gate_part) * up_part).astype(BF16)
             current = current + dot(down_t[:, base : base + block], trans_hidden)
         result = current.T
@@ -317,7 +318,7 @@
     cols = halves * nears
     owners = rows * cols
     share = hid // owners
-    chunk = min(4 * LANES, tokens)
+    chunk = min(2 * LANES, tokens)
     split = halves if share % 8 == 0 else 1
     first_share = split * share
     held = ((LANES // breadth, lines, breadth, channels), F32)
@@ -353,7 +354,7 @@
     both = exchange(both, NEAR_AXES if split > 1 else ALL_AXES)
     combined = combine(both, first_share, True)
     both, gate, current = call(
-        functools.partial(middle_kernel, first_share, share, chunk),
+        functools.partial(middle_kernel, first_share, share, tokens),
         (combined, current, gate, mask, gains, proj_weight, gate_weight, out_weight),
         [message(share), wide, wide],
         (result, spare),

time: 74.7 us -> 74.9 us (level)
  no operation moved by 1% of the time
where the time goes in v15:
time: 74.9 us; the launch traced here: 74.6 us
  blocking collectives  65.7 us (88%)
  Pallas kernels  8.82 us (12%)
    all_to_all x4, blocking collectives, exchange(): return lax.all_to_all(values, axes, split_axis=0, concat_axis=0, tiled=True)  65.7 us
    pallas_call x5, Pallas kernels, call(): pl.pallas_call(body, in_specs=[in_place if in_hbm else held] * count, out...  8.82 us

profile of v15, /device:TPU:0, one launch (start us, length us, event | category | flops | bytes accessed | tf_op | source)
XLA Modules:
  0.0 74.6 jit_solution(6618981025762971450)
XLA Ops:
  0.0 1.9 %shard_map.100 = (bf16[8,256,128]{2,1,0:T(8,128)(2,1)S(1)}, f32[128,1024]{1,0:T(8,128)S(1)}, f32[128,1024]{1,0:T(8,128)S(1)}, f32[8,128]{1,0:T(8,128)S(1)}, f32[8,128]{1,0:T(8,128)S(1)}) custom-call(f32[4,8,32,128]{3,2,1,0:T(8,128)} %bitcast.3, s32[32,32]{1,0:T(8,128)} %refs_1_.1, bf16[2,128,512]{2,1,0:T(8,128)(2,1)} %refs_5_.4, ...), custom_call_target="tpu_custom_call" | custom-call | tf_op jit(solution)/shard_map/pallas_call | solution.py:285
  1.9 13.9 %all_to_all.20.refs_0_ = bf16[8,256,128]{2,1,0:T(8,128)(2,1)S(1)} all-to-all(bf16[8,256,128]{2,1,0:T(8,128)(2,1)S(1)} %get-tuple-element.13), channel_id=1, replica_groups=mesh['grp'=2,'row'=4,'half'=2,'near'=2] {'near','row'}, dimensions={0} | all-to-all | bytes 1048576 | tf_op jit(solution)/shard_map/all_to_all | solution.py:296
  15.8 1.5 %shard_map.101 = bf16[16,128,128]{2,1,0:T(8,128)(2,1)S(1)} custom-call(bf16[8,256,128]{2,1,0:T(8,128)(2,1)S(1)} %all_to_all.20.refs_0_), custom_call_target="tpu_custom_call" | custom-call | tf_op jit(solution)/shard_map/pallas_call | solution.py:285
  17.3 0.0 copy-start
  17.3 0.0 copy-start.2
  17.3 0.0 copy-start.3
  17.3 19.3 %all_to_all.21.refs_0_ = bf16[16,128,128]{2,1,0:T(8,128)(2,1)S(1)} all-to-all(bf16[16,128,128]{2,1,0:T(8,128)(2,1)S(1)} %shard_map.101), channel_id=1, replica_groups=mesh['grp'=2,'row'=4,'half'=2,'near'=2] {'half','near','row'}, dimensions={0} | all-to-all | bytes 1048576 | tf_op jit(solution)/shard_map/all_to_all | solution.py:296
  36.7 0.0 copy-done
  36.7 0.0 copy-done.2
  36.7 0.0 copy-done.3
  36.7 1.1 %shard_map.102 = (bf16[16,128,128]{2,1,0:T(8,128)(2,1)S(1)}, f32[128,1024]{1,0:T(8,128)S(1)}, f32[128,1024]{1,0:T(8,128)S(1)}) custom-call(bf16[16,128,128]{2,1,0:T(8,128)(2,1)S(1)} %all_to_all.21.refs_0_, f32[128,1024]{1,0:T(8,128)S(1)} %get-tuple-element.14.refs_1_, f32[128,1024]{1,0:T(8,128)S(1)} %get-tuple-element.15.refs_2_, ...), custom_call_target="tpu_custom_call" | custom-call | tf_op jit(solution)/shard_map/pallas_call | solution.py:285
  37.8 18.4 %all_to_all.22.refs_0_ = bf16[16,128,128]{2,1,0:T(8,128)(2,1)S(1)} all-to-all(bf16[16,128,128]{2,1,0:T(8,128)(2,1)S(1)} %get-tuple-element.18), channel_id=1, replica_groups=mesh['grp'=2,'row'=4,'half'=2,'near'=2] {'half','near','row'}, dimensions={0} | all-to-all | bytes 1048576 | tf_op jit(solution)/shard_map/all_to_all | solution.py:296
  56.1 1.1 %shard_map.103 = bf16[16,64,128]{2,1,0:T(8,128)(2,1)S(1)} custom-call(bf16[16,128,128]{2,1,0:T(8,128)(2,1)S(1)} %all_to_all.22.refs_0_), custom_call_target="tpu_custom_call" | custom-call | tf_op jit(solution)/shard_map/pallas_call | solution.py:285
  57.3 0.0 copy-start.1
  57.3 0.0 copy-start.4
  57.3 14.1 %all_to_all.23.refs_0_ = bf16[16,64,128]{2,1,0:T(8,128)(2,1)S(1)} all-to-all(bf16[16,64,128]{2,1,0:T(8,128)(2,1)S(1)} %shard_map.103), channel_id=1, replica_groups=mesh['grp'=2,'row'=4,'half'=2,'near'=2] {'half','near','row'}, dimensions={0} | all-to-all | bytes 524288 | tf_op jit(solution)/shard_map/all_to_all | solution.py:296
  71.3 0.0 copy-done.1
  71.3 0.0 copy-done.4
  71.3 3.2 %shard_map.104 = f32[4,8,32,128]{3,2,1,0:T(8,128)} custom-call(bf16[16,64,128]{2,1,0:T(8,128)(2,1)S(1)} %all_to_all.23.refs_0_, f32[128,1024]{1,0:T(8,128)S(1)} %get-tuple-element.19.refs_1_, f32[128,1024]{1,0:T(8,128)S(1)} %get-tuple-element.20.refs_2_, f32[8,128]{1,0:T(8,128)S(1)} %get-tuple-element.17.refs_4_.refs_3_, bf16[2,128,128]{2,1,0:T(8,128)(2,1)S(1)} %copy-done.3, ...), custom_call_target="tpu_custom_call" | custom-call | tf_op jit(solution)/shard_map/pallas_call | solution.py:285
Async XLA Ops:
  17.3 19.3 %copy-start = (bf16[2,128,512]{2,1,0:T(8,128)(2,1)S(1)}, bf16[2,128,512]{2,1,0:T(8,128)(2,1)}, u32[]{:S(2)}) copy-start(bf16[2,128,512]{2,1,0:T(8,128)(2,1)} %refs_5_.4) | copy-start | bytes 786436
  17.3 19.3 %copy-start.2 = (bf16[2,128,128]{2,1,0:T(8,128)(2,1)S(1)}, bf16[2,128,128]{2,1,0:T(8,128)(2,1)}, u32[]{:S(2)}) copy-start(bf16[2,128,128]{2,1,0:T(8,128)(2,1)} %refs_6_.2) | copy-start | bytes 196612
  17.3 19.3 %copy-start.3 = (bf16[2,128,128]{2,1,0:T(8,128)(2,1)S(1)}, bf16[2,128,128]{2,1,0:T(8,128)(2,1)}, u32[]{:S(2)}) copy-start(bf16[2,128,128]{2,1,0:T(8,128)(2,1)} %refs_4_.3) | copy-start | bytes 196612
  57.3 14.1 %copy-start.1 = (bf16[128,1024]{1,0:T(8,128)(2,1)S(1)}, bf16[128,1024]{1,0:T(8,128)(2,1)}, u32[]{:S(2)}) copy-start(bf16[128,1024]{1,0:T(8,128)(2,1)} %refs_5_.5) | copy-start | bytes 786436
  57.3 14.1 %copy-start.4 = (bf16[512,128]{1,0:T(8,128)(2,1)S(1)}, bf16[512,128]{1,0:T(8,128)(2,1)}, u32[]{:S(2)}) copy-start(bf16[512,128]{1,0:T(8,128)(2,1)} %refs_6_.3) | copy-start | bytes 393220

commit v16 on v15

--- a/solution.py
+++ b/solution.py
@@ -252,23 +252,20 @@
     hold_combined(combined_ref, stage_ref, share)
     combined = read_combined(stage_ref, owners, lines, share, 0, lines)
     hidden = channel_norm(combined, gain_out)
-    whole = x_ref[...] + gate_ref[...] * dot(out_t, hidden)
-    trans_in = channel_norm(whole, gain)
+    current = x_ref[...] + gate_ref[...] * dot(out_t, hidden)
+    trans_in = channel_norm(current, gain)
+    block = min(256, half)
+    for base in range(0, half, block):
+        gate_part = dot(gate_t[base : base + block], trans_in)
+        up_part = dot(up_t[base : base + block], trans_in)
+        trans_hidden = (gate_part * twice_sigmoid(gate_part) * up_part).astype(BF16)
+        current = current + dot(down_t[:, base : base + block], trans_hidden)
     writes = []
     for first in range(0, lines, count):
-        here = slice(first * LANES, (first + count) * LANES)
-        current = whole[:, here]
-        block = min(256, half)
-        for base in range(0, half, block):
-            gate_part = dot(gate_t[base : base + block], trans_in[:, here])
-            up_part = dot(up_t[base : base + block], trans_in[:, here])
-            trans_hidden = (gate_part * twice_sigmoid(gate_part) * up_part).astype(BF16)
-            current = current + dot(down_t[:, base : base + block], trans_hidden)
-        result = current.T
-        for part in range(count):
+        for line in range(first, first + count):
+            result = current[:, line * LANES : (line + 1) * LANES].T
             for slot in range(slots):
-                base = part * LANES + slot * breadth
-                result_ref[slot, first + part] = result[base : base + breadth]
+                result_ref[slot, line] = result[slot * breadth : (slot + 1) * breadth]
         piece = slice(first, first + count)
         writes += start_all([(result_ref.at[:, piece], result_out.at[:, piece])], sems, first // count)
     for write in writes:
@@ -318,7 +315,7 @@
     cols = halves * nears
     owners = rows * cols
     share = hid // owners
-    chunk = min(2 * LANES, tokens)
+    chunk = min(4 * LANES, tokens)
     split = halves if share % 8 == 0 else 1
     first_share = split * share
     held = ((LANES // breadth, lines, breadth, channels), F32)

time: 74.9 us -> 74.1 us (0.989)
  Pallas kernels: 8.82 us -> 7.99 us
    pallas_call x5, Pallas kernels: 8.82 us -> 7.99 us  [call(): pl.pallas_call(body, in_specs=[in_place if in_hbm else held] * count, out...]
where the time goes in v16:
time: 74.1 us; the launch traced here: 73.8 us
  blocking collectives  65.7 us (89%)
  Pallas kernels  7.99 us (11%)
    all_to_all x4, blocking collectives, exchange(): return lax.all_to_all(values, axes, split_axis=0, concat_axis=0, tiled=True)  65.7 us
    pallas_call x5, Pallas kernels, call(): pl.pallas_call(body, in_specs=[in_place if in_hbm else held] * count, out...  7.99 us

profile of v16, /device:TPU:0, one launch (start us, length us, event | category | flops | bytes accessed | tf_op | source)
XLA Modules:
  0.0 73.8 jit_solution(9902159104234974648)
XLA Ops:
  0.0 1.9 %shard_map.100 = (bf16[8,256,128]{2,1,0:T(8,128)(2,1)S(1)}, f32[128,1024]{1,0:T(8,128)S(1)}, f32[128,1024]{1,0:T(8,128)S(1)}, f32[8,128]{1,0:T(8,128)S(1)}, f32[8,128]{1,0:T(8,128)S(1)}) custom-call(f32[4,8,32,128]{3,2,1,0:T(8,128)} %bitcast.3, s32[32,32]{1,0:T(8,128)} %refs_1_.1, bf16[2,128,512]{2,1,0:T(8,128)(2,1)} %refs_5_.4, ...), custom_call_target="tpu_custom_call" | custom-call | tf_op jit(solution)/shard_map/pallas_call | solution.py:282
  1.9 13.9 %all_to_all.20.refs_0_ = bf16[8,256,128]{2,1,0:T(8,128)(2,1)S(1)} all-to-all(bf16[8,256,128]{2,1,0:T(8,128)(2,1)S(1)} %get-tuple-element.13), channel_id=1, replica_groups=mesh['grp'=2,'row'=4,'half'=2,'near'=2] {'near','row'}, dimensions={0} | all-to-all | bytes 1048576 | tf_op jit(solution)/shard_map/all_to_all | solution.py:293
  15.8 1.5 %shard_map.101 = bf16[16,128,128]{2,1,0:T(8,128)(2,1)S(1)} custom-call(bf16[8,256,128]{2,1,0:T(8,128)(2,1)S(1)} %all_to_all.20.refs_0_), custom_call_target="tpu_custom_call" | custom-call | tf_op jit(solution)/shard_map/pallas_call | solution.py:282
  17.3 0.0 copy-start
  17.3 0.0 copy-start.2
  17.3 0.0 copy-start.3
  17.3 19.3 %all_to_all.21.refs_0_ = bf16[16,128,128]{2,1,0:T(8,128)(2,1)S(1)} all-to-all(bf16[16,128,128]{2,1,0:T(8,128)(2,1)S(1)} %shard_map.101), channel_id=1, replica_groups=mesh['grp'=2,'row'=4,'half'=2,'near'=2] {'half','near','row'}, dimensions={0} | all-to-all | bytes 1048576 | tf_op jit(solution)/shard_map/all_to_all | solution.py:293
  36.7 0.0 copy-done
  36.7 0.0 copy-done.2
  36.7 0.0 copy-done.3
  36.7 1.1 %shard_map.102 = (bf16[16,128,128]{2,1,0:T(8,128)(2,1)S(1)}, f32[128,1024]{1,0:T(8,128)S(1)}, f32[128,1024]{1,0:T(8,128)S(1)}) custom-call(bf16[16,128,128]{2,1,0:T(8,128)(2,1)S(1)} %all_to_all.21.refs_0_, f32[128,1024]{1,0:T(8,128)S(1)} %get-tuple-element.14.refs_1_, f32[128,1024]{1,0:T(8,128)S(1)} %get-tuple-element.15.refs_2_, ...), custom_call_target="tpu_custom_call" | custom-call | tf_op jit(solution)/shard_map/pallas_call | solution.py:282
  37.8 18.4 %all_to_all.22.refs_0_ = bf16[16,128,128]{2,1,0:T(8,128)(2,1)S(1)} all-to-all(bf16[16,128,128]{2,1,0:T(8,128)(2,1)S(1)} %get-tuple-element.18), channel_id=1, replica_groups=mesh['grp'=2,'row'=4,'half'=2,'near'=2] {'half','near','row'}, dimensions={0} | all-to-all | bytes 1048576 | tf_op jit(solution)/shard_map/all_to_all | solution.py:293
  56.1 1.1 %shard_map.103 = bf16[16,64,128]{2,1,0:T(8,128)(2,1)S(1)} custom-call(bf16[16,128,128]{2,1,0:T(8,128)(2,1)S(1)} %all_to_all.22.refs_0_), custom_call_target="tpu_custom_call" | custom-call | tf_op jit(solution)/shard_map/pallas_call | solution.py:282
  57.3 0.0 copy-start.1
  57.3 0.0 copy-start.4
  57.3 14.1 %all_to_all.23.refs_0_ = bf16[16,64,128]{2,1,0:T(8,128)(2,1)S(1)} all-to-all(bf16[16,64,128]{2,1,0:T(8,128)(2,1)S(1)} %shard_map.103), channel_id=1, replica_groups=mesh['grp'=2,'row'=4,'half'=2,'near'=2] {'half','near','row'}, dimensions={0} | all-to-all | bytes 524288 | tf_op jit(solution)/shard_map/all_to_all | solution.py:293
  71.3 0.0 copy-done.1
  71.3 0.0 copy-done.4
  71.3 2.4 %shard_map.104 = f32[4,8,32,128]{3,2,1,0:T(8,128)} custom-call(bf16[16,64,128]{2,1,0:T(8,128)(2,1)S(1)} %all_to_all.23.refs_0_, f32[128,1024]{1,0:T(8,128)S(1)} %get-tuple-element.19.refs_1_, f32[128,1024]{1,0:T(8,128)S(1)} %get-tuple-element.20.refs_2_, f32[8,128]{1,0:T(8,128)S(1)} %get-tuple-element.17.refs_4_.refs_3_, bf16[2,128,128]{2,1,0:T(8,128)(2,1)S(1)} %copy-done.3, ...), custom_call_target="tpu_custom_call" | custom-call | tf_op jit(solution)/shard_map/pallas_call | solution.py:282
Async XLA Ops:
  17.3 19.3 %copy-start = (bf16[2,128,512]{2,1,0:T(8,128)(2,1)S(1)}, bf16[2,128,512]{2,1,0:T(8,128)(2,1)}, u32[]{:S(2)}) copy-start(bf16[2,128,512]{2,1,0:T(8,128)(2,1)} %refs_5_.4) | copy-start | bytes 786436
  17.3 19.3 %copy-start.2 = (bf16[2,128,128]{2,1,0:T(8,128)(2,1)S(1)}, bf16[2,128,128]{2,1,0:T(8,128)(2,1)}, u32[]{:S(2)}) copy-start(bf16[2,128,128]{2,1,0:T(8,128)(2,1)} %refs_6_.2) | copy-start | bytes 196612
  17.3 19.3 %copy-start.3 = (bf16[2,128,128]{2,1,0:T(8,128)(2,1)S(1)}, bf16[2,128,128]{2,1,0:T(8,128)(2,1)}, u32[]{:S(2)}) copy-start(bf16[2,128,128]{2,1,0:T(8,128)(2,1)} %refs_4_.3) | copy-start | bytes 196612
  57.3 14.1 %copy-start.1 = (bf16[128,1024]{1,0:T(8,128)(2,1)S(1)}, bf16[128,1024]{1,0:T(8,128)(2,1)}, u32[]{:S(2)}) copy-start(bf16[128,1024]{1,0:T(8,128)(2,1)} %refs_5_.5) | copy-start | bytes 786436
  57.3 14.1 %copy-start.4 = (bf16[512,128]{1,0:T(8,128)(2,1)S(1)}, bf16[512,128]{1,0:T(8,128)(2,1)}, u32[]{:S(2)}) copy-start(bf16[512,128]{1,0:T(8,128)(2,1)} %refs_6_.3) | copy-start | bytes 393220

commit v17 on v16

--- a/solution.py
+++ b/solution.py
@@ -124,7 +124,8 @@
     )
 
 
-def combine_kernel(rows, cols, near, breadth, share, outgoing, ins, outs):
+def combine_kernel(sources, owners, breadth, share, outgoing, ins, outs):
+    near, cols, rows = len(sources), len(owners), len(owners[0])
     (both_ref,), (combined_ref,) = ins, outs
     slots = LANES // breadth
     span = both_ref.shape[1]
@@ -141,7 +142,7 @@
     order = one_hot(span, span, source)
     wide = []
     for row in range(rows):
-        here = jnp.concatenate([both_ref[col * rows + row] for col in range(near)], axis=1)
+        here = jnp.concatenate([both_ref[sources[col][row]] for col in range(near)], axis=1)
         here = dot(order, here).astype(BF16)
         wide.append(jnp.concatenate([here[n * size : (n + 1) * size] for n in range(pack)], axis=1))
     wide = jnp.concatenate(wide, axis=0)
@@ -182,21 +183,19 @@
         for low in range(slots):
             for row in range(rows):
                 first = row * share * lines
-                combined_ref[(high * slots + low) * rows + row] = back[
+                combined_ref[owners[high * slots + low][row]] = back[
                     first : first + share * lines, low * LANES : (low + 1) * LANES
                 ]
 
 
-def hold_combined(combined_ref, stage_ref, share):
+def hold_combined(combined_ref, stage_ref, share, sources):
     span = combined_ref.shape[1]
     lines = span // share
-    owners = stage_ref.shape[0] // span
-    halves = combined_ref.shape[0] // owners
     order = one_hot(span, span, lambda row: row % share * lines + row // share)
-    order = jnp.concatenate([order] * halves, axis=1)
-    for first in range(0, owners, 2):
+    order = jnp.concatenate([order] * len(sources[0]), axis=1)
+    for first in range(0, len(sources), 2):
         blocks = [
-            jnp.concatenate([combined_ref[half * owners + owner] for half in range(halves)], axis=0)
+            jnp.concatenate([combined_ref[source] for source in sources[owner]], axis=0)
             for owner in (first, first + 1)
         ]
         ordered = dot(order, jnp.concatenate(blocks, axis=1))
@@ -218,13 +217,13 @@
     return jnp.concatenate(columns, axis=1)
 
 
-def middle_kernel(share, next_share, chunk, ins, outs, stage_ref, message_stage_ref):
+def middle_kernel(share, sources, next_share, chunk, ins, outs, stage_ref, message_stage_ref):
     combined_ref, x_ref, gate_ref, mask_ref, gains_ref, proj_ref, gate_weight_ref, out_ref = ins
     message_ref, gate_out, next_ref = outs
     tokens = x_ref.shape[1]
     lines = tokens // LANES
     owners = x_ref.shape[0] // share
-    hold_combined(combined_ref, stage_ref, share)
+    hold_combined(combined_ref, stage_ref, share, sources)
     mask = mask_ref[...]
     gain_out, gain = [spread_gain(gains_ref[n : n + 1, :]) for n in (0, 1)]
     out_t, proj_t, gate_t = halved(out_ref[0]), halved(proj_ref[1]), halved(gate_weight_ref[1])
@@ -239,7 +238,7 @@
         gate_out[:, here] = twice_sigmoid(dot(gate_t, normed))
 
 
-def last_kernel(share, chunk, ins, outs, stage_ref, result_ref, sems):
+def last_kernel(share, sources, chunk, ins, outs, stage_ref, result_ref, sems):
     combined_ref, x_ref, gate_ref, gains_ref, out_ref, up_ref, down_ref = ins
     (result_out,) = outs
     slots, lines, breadth, channels = result_ref.shape
@@ -249,7 +248,7 @@
     gain_out, gain = [spread_gain(gains_ref[n : n + 1, :]) for n in (2, 3)]
     out_t, down_t = halved(out_ref[1]), down_ref[...].T
     gate_t, up_t = halved(up_ref[:, :half]), up_ref[:, half:].T
-    hold_combined(combined_ref, stage_ref, share)
+    hold_combined(combined_ref, stage_ref, share, sources)
     combined = read_combined(stage_ref, owners, lines, share, 0, lines)
     hidden = channel_norm(combined, gain_out)
     current = x_ref[...] + gate_ref[...] * dot(out_t, hidden)
@@ -289,8 +288,9 @@
     )(*[pltpu.with_memory_space_constraint(array, pltpu.HBM) if in_hbm else array for array in operands])
 
 
-def exchange(values, axes):
-    return lax.all_to_all(values, axes, split_axis=0, concat_axis=0, tiled=True)
+def exchange(values, axes, order=None):
+    groups = [order] if order else None
+    return lax.all_to_all(values, axes, split_axis=0, concat_axis=0, axis_index_groups=groups, tiled=True)
 
 
 def per_device(
@@ -327,11 +327,20 @@
     def message(own):
         return ((hid // own, 2 * own * lines, LANES), BF16)
 
-    def combine(both, own, outgoing):
-        near = cols * share // own
-        kernel = functools.partial(combine_kernel, rows, cols, near, breadth, own, outgoing)
+    blocks = list(range(cols))
+    blocks.insert(0, blocks.pop((cols - 1) // 2))
+    order = [col * rows + row for col in blocks for row in range(rows)]
+    everyone = [[order.index(col * rows + row) for row in range(rows)] for col in range(cols)]
+    beside = [[near * rows + row for row in range(rows)] for near in range(nears)] if split > 1 else everyone
+    single = [[n] for n in range(owners)]
+    paired = single if split == 1 else [
+        [everyone[half * nears + near][row] for half in range(halves)] for near in range(nears) for row in range(rows)
+    ]
+
+    def combine(both, own, sources, outgoing):
+        kernel = functools.partial(combine_kernel, sources, everyone, breadth, own, outgoing)
         answer = ((owners, own * lines, LANES), BF16)
-        return exchange(call(kernel, (both,), [answer])[0], ALL_AXES)
+        return exchange(call(kernel, (both,), [answer])[0], ALL_AXES, order)
 
     operands = (grouped, pair_mask, proj_weight, gate_weight, gain_in, gain_out, trans_gain.reshape(1, -1))
     both, gate, current, mask, gains = call(
@@ -348,17 +357,17 @@
         ),
         in_hbm=True,
     )
-    both = exchange(both, NEAR_AXES if split > 1 else ALL_AXES)
-    combined = combine(both, first_share, True)
+    both = exchange(both, NEAR_AXES) if split > 1 else exchange(both, ALL_AXES, order)
+    combined = combine(both, first_share, beside, True)
     both, gate, current = call(
-        functools.partial(middle_kernel, first_share, share, tokens),
+        functools.partial(middle_kernel, first_share, paired, share, tokens),
         (combined, current, gate, mask, gains, proj_weight, gate_weight, out_weight),
         [message(share), wide, wide],
         (result, spare),
     )
-    combined = combine(exchange(both, ALL_AXES), share, False)
+    combined = combine(exchange(both, ALL_AXES, order), share, everyone, False)
     (pair_out,) = call(
-        functools.partial(last_kernel, share, chunk),
+        functools.partial(last_kernel, share, single, chunk),
         (combined, current, gate, gains, out_weight, trans_up, trans_down),
         [held],
         (result, pltpu.VMEM(*held), pltpu.SemaphoreType.DMA((tokens // chunk,))),

time: 74.1 us -> 71.1 us (0.960)
  blocking collectives: 65.7 us -> 62.5 us
    all_to_all x4, blocking collectives: 65.7 us -> 62.5 us  [exchange(): lax.all_to_all(values, axes, split_axis=0, concat_axis=0, axis_index_grou...]
where the time goes in v17:
time: 71.1 us; the launch traced here: 70.6 us
  blocking collectives  62.5 us (88%)
  Pallas kernels  7.98 us (11%)
    all_to_all x4, blocking collectives, exchange(): lax.all_to_all(values, axes, split_axis=0, concat_axis=0, axis_index_grou...  62.5 us
    pallas_call x5, Pallas kernels, call(): pl.pallas_call(body, in_specs=[in_place if in_hbm else held] * count, out...  7.98 us

profile of v17, /device:TPU:0, one launch (start us, length us, event | category | flops | bytes accessed | tf_op | source)
XLA Modules:
  0.0 70.6 jit_solution(13401168768514508252)
XLA Ops:
  0.0 1.9 %shard_map.100 = (bf16[8,256,128]{2,1,0:T(8,128)(2,1)S(1)}, f32[128,1024]{1,0:T(8,128)S(1)}, f32[128,1024]{1,0:T(8,128)S(1)}, f32[8,128]{1,0:T(8,128)S(1)}, f32[8,128]{1,0:T(8,128)S(1)}) custom-call(f32[4,8,32,128]{3,2,1,0:T(8,128)} %bitcast.3, s32[32,32]{1,0:T(8,128)} %refs_1_.1, bf16[2,128,512]{2,1,0:T(8,128)(2,1)} %refs_5_.4, ...), custom_call_target="tpu_custom_call" | custom-call | tf_op jit(solution)/shard_map/pallas_call | solution.py:281
  1.9 13.9 %all_to_all.20.refs_0_ = bf16[8,256,128]{2,1,0:T(8,128)(2,1)S(1)} all-to-all(bf16[8,256,128]{2,1,0:T(8,128)(2,1)S(1)} %get-tuple-element.13), channel_id=1, replica_groups=mesh['grp'=2,'row'=4,'half'=2,'near'=2] {'near','row'}, dimensions={0} | all-to-all | bytes 1048576 | tf_op jit(solution)/shard_map/all_to_all | solution.py:293
  15.8 1.5 %shard_map.101 = bf16[16,128,128]{2,1,0:T(8,128)(2,1)S(1)} custom-call(bf16[8,256,128]{2,1,0:T(8,128)(2,1)S(1)} %all_to_all.20.refs_0_), custom_call_target="tpu_custom_call" | custom-call | tf_op jit(solution)/shard_map/pallas_call | solution.py:281
  17.3 0.0 copy-start
  17.3 0.0 copy-start.2
  17.3 0.0 copy-start.3
  17.3 18.9 %all_to_all.21.refs_0_ = bf16[16,128,128]{2,1,0:T(8,128)(2,1)S(1)} all-to-all(bf16[16,128,128]{2,1,0:T(8,128)(2,1)S(1)} %shard_map.101), channel_id=1, replica_groups={{1,5,9,13,0,4,8,12,2,6,10,14,3,7,11,15},{17,21,25,29,16,20,24,28,18,22,..., dimensions={0} | all-to-all | bytes 1048576 | tf_op jit(solution)/shard_map/all_to_all | solution.py:293
  36.3 0.0 copy-done
  36.3 0.0 copy-done.2
  36.3 0.0 copy-done.3
  36.3 1.1 %shard_map.102 = (bf16[16,128,128]{2,1,0:T(8,128)(2,1)S(1)}, f32[128,1024]{1,0:T(8,128)S(1)}, f32[128,1024]{1,0:T(8,128)S(1)}) custom-call(bf16[16,128,128]{2,1,0:T(8,128)(2,1)S(1)} %all_to_all.21.refs_0_, f32[128,1024]{1,0:T(8,128)S(1)} %get-tuple-element.14.refs_1_, f32[128,1024]{1,0:T(8,128)S(1)} %get-tuple-element.15.refs_2_, ...), custom_call_target="tpu_custom_call" | custom-call | tf_op jit(solution)/shard_map/pallas_call | solution.py:281
  37.4 17.5 %all_to_all.22.refs_0_ = bf16[16,128,128]{2,1,0:T(8,128)(2,1)S(1)} all-to-all(bf16[16,128,128]{2,1,0:T(8,128)(2,1)S(1)} %get-tuple-element.18), channel_id=1, replica_groups={{1,5,9,13,0,4,8,12,2,6,10,14,3,7,11,15},{17,21,25,29,16,20,24,28,18,22,..., dimensions={0} | all-to-all | bytes 1048576 | tf_op jit(solution)/shard_map/all_to_all | solution.py:293
  54.9 1.1 %shard_map.103 = bf16[16,64,128]{2,1,0:T(8,128)(2,1)S(1)} custom-call(bf16[16,128,128]{2,1,0:T(8,128)(2,1)S(1)} %all_to_all.22.refs_0_), custom_call_target="tpu_custom_call" | custom-call | tf_op jit(solution)/shard_map/pallas_call | solution.py:281
  56.0 0.0 copy-start.1
  56.0 0.0 copy-start.4
  56.0 12.2 %all_to_all.23.refs_0_ = bf16[16,64,128]{2,1,0:T(8,128)(2,1)S(1)} all-to-all(bf16[16,64,128]{2,1,0:T(8,128)(2,1)S(1)} %shard_map.103), channel_id=1, replica_groups={{1,5,9,13,0,4,8,12,2,6,10,14,3,7,11,15},{17,21,25,29,16,20,24,28,18,22,..., dimensions={0} | all-to-all | bytes 524288 | tf_op jit(solution)/shard_map/all_to_all | solution.py:293
  68.2 0.0 copy-done.1
  68.2 0.0 copy-done.4
  68.2 2.4 %shard_map.104 = f32[4,8,32,128]{3,2,1,0:T(8,128)} custom-call(bf16[16,64,128]{2,1,0:T(8,128)(2,1)S(1)} %all_to_all.23.refs_0_, f32[128,1024]{1,0:T(8,128)S(1)} %get-tuple-element.19.refs_1_, f32[128,1024]{1,0:T(8,128)S(1)} %get-tuple-element.20.refs_2_, f32[8,128]{1,0:T(8,128)S(1)} %get-tuple-element.17.refs_4_.refs_3_, bf16[2,128,128]{2,1,0:T(8,128)(2,1)S(1)} %copy-done.3, ...), custom_call_target="tpu_custom_call" | custom-call | tf_op jit(solution)/shard_map/pallas_call | solution.py:281
Async XLA Ops:
  17.3 19.0 %copy-start = (bf16[2,128,512]{2,1,0:T(8,128)(2,1)S(1)}, bf16[2,128,512]{2,1,0:T(8,128)(2,1)}, u32[]{:S(2)}) copy-start(bf16[2,128,512]{2,1,0:T(8,128)(2,1)} %refs_5_.4) | copy-start | bytes 786436
  17.3 19.0 %copy-start.2 = (bf16[2,128,128]{2,1,0:T(8,128)(2,1)S(1)}, bf16[2,128,128]{2,1,0:T(8,128)(2,1)}, u32[]{:S(2)}) copy-start(bf16[2,128,128]{2,1,0:T(8,128)(2,1)} %refs_6_.2) | copy-start | bytes 196612
  17.3 18.9 %copy-start.3 = (bf16[2,128,128]{2,1,0:T(8,128)(2,1)S(1)}, bf16[2,128,128]{2,1,0:T(8,128)(2,1)}, u32[]{:S(2)}) copy-start(bf16[2,128,128]{2,1,0:T(8,128)(2,1)} %refs_4_.3) | copy-start | bytes 196612
  56.0 12.2 %copy-start.1 = (bf16[128,1024]{1,0:T(8,128)(2,1)S(1)}, bf16[128,1024]{1,0:T(8,128)(2,1)}, u32[]{:S(2)}) copy-start(bf16[128,1024]{1,0:T(8,128)(2,1)} %refs_5_.5) | copy-start | bytes 786436
  56.0 12.2 %copy-start.4 = (bf16[512,128]{1,0:T(8,128)(2,1)S(1)}, bf16[512,128]{1,0:T(8,128)(2,1)}, u32[]{:S(2)}) copy-start(bf16[512,128]{1,0:T(8,128)(2,1)} %refs_6_.3) | copy-start | bytes 393220

commit v18 on v17

--- a/solution.py
+++ b/solution.py
@@ -288,9 +288,8 @@
     )(*[pltpu.with_memory_space_constraint(array, pltpu.HBM) if in_hbm else array for array in operands])
 
 
-def exchange(values, axes, order=None):
-    groups = [order] if order else None
-    return lax.all_to_all(values, axes, split_axis=0, concat_axis=0, axis_index_groups=groups, tiled=True)
+def exchange(values, axes, order):
+    return lax.all_to_all(values, axes, split_axis=0, concat_axis=0, axis_index_groups=[order], tiled=True)
 
 
 def per_device(
@@ -327,15 +326,21 @@
     def message(own):
         return ((hid // own, 2 * own * lines, LANES), BF16)
 
-    blocks = list(range(cols))
-    blocks.insert(0, blocks.pop((cols - 1) // 2))
-    order = [col * rows + row for col in blocks for row in range(rows)]
-    everyone = [[order.index(col * rows + row) for row in range(rows)] for col in range(cols)]
-    beside = [[near * rows + row for row in range(rows)] for near in range(nears)] if split > 1 else everyone
+    def listed(count):
+        middle = (count - 1) // 2
+        places = [(col, row) for col in range(count) for row in range(rows)]
+        places.sort(key=lambda at: (at != (middle, 0), -abs(at[0] - middle), -at[1]))
+        order = [col * rows + row for col, row in places]
+        return order, [[order.index(col * rows + row) for row in range(rows)] for col in range(count)]
+
+    order, everyone = listed(cols)
+    near_order, beside = listed(nears) if split > 1 else (order, everyone)
     single = [[n] for n in range(owners)]
-    paired = single if split == 1 else [
-        [everyone[half * nears + near][row] for half in range(halves)] for near in range(nears) for row in range(rows)
-    ]
+    paired = single
+    if split > 1:
+        paired = [
+            [everyone[half * nears + place // rows][place % rows] for half in range(halves)] for place in near_order
+        ]
 
     def combine(both, own, sources, outgoing):
         kernel = functools.partial(combine_kernel, sources, everyone, breadth, own, outgoing)
@@ -357,7 +362,7 @@
         ),
         in_hbm=True,
     )
-    both = exchange(both, NEAR_AXES) if split > 1 else exchange(both, ALL_AXES, order)
+    both = exchange(both, NEAR_AXES if split > 1 else ALL_AXES, near_order)
     combined = combine(both, first_share, beside, True)
     both, gate, current = call(
         functools.partial(middle_kernel, first_share, paired, share, tokens),

time: 71.1 us -> 71.6 us (level)
  blocking collectives: 62.5 us -> 63.3 us
    all_to_all x4, blocking collectives: 62.5 us -> 63.3 us  [exchange(): lax.all_to_all(values, axes, split_axis=0, concat_axis=0, axis_index_grou...]
where the time goes in v18:
time: 71.6 us; the launch traced here: 71.4 us
  blocking collectives  63.3 us (88%)
  Pallas kernels  7.98 us (11%)
    all_to_all x4, blocking collectives, exchange(): lax.all_to_all(values, axes, split_axis=0, concat_axis=0, axis_index_grou...  63.3 us
    pallas_call x5, Pallas kernels, call(): pl.pallas_call(body, in_specs=[in_place if in_hbm else held] * count, out...  7.98 us

profile of v18, /device:TPU:0, one launch (start us, length us, event | category | flops | bytes accessed | tf_op | source)
XLA Modules:
  0.0 71.4 jit_solution(1101595192138358140)
XLA Ops:
  0.0 1.9 %shard_map.100 = (bf16[8,256,128]{2,1,0:T(8,128)(2,1)S(1)}, f32[128,1024]{1,0:T(8,128)S(1)}, f32[128,1024]{1,0:T(8,128)S(1)}, f32[8,128]{1,0:T(8,128)S(1)}, f32[8,128]{1,0:T(8,128)S(1)}) custom-call(f32[4,8,32,128]{3,2,1,0:T(8,128)} %bitcast.3, s32[32,32]{1,0:T(8,128)} %refs_1_.1, bf16[2,128,512]{2,1,0:T(8,128)(2,1)} %refs_5_.4, ...), custom_call_target="tpu_custom_call" | custom-call | tf_op jit(solution)/shard_map/pallas_call | solution.py:281
  1.9 13.9 %all_to_all.20.refs_0_ = bf16[8,256,128]{2,1,0:T(8,128)(2,1)S(1)} all-to-all(bf16[8,256,128]{2,1,0:T(8,128)(2,1)S(1)} %get-tuple-element.13), channel_id=1, replica_groups={{0,13,9,5,1,12,8,4},{2,15,11,7,3,14,10,6},{16,29,25,21,17,28,24,20},{18..., dimensions={0} | all-to-all | bytes 1048576 | tf_op jit(solution)/shard_map/all_to_all | solution.py:292
  15.8 1.5 %shard_map.101 = bf16[16,128,128]{2,1,0:T(8,128)(2,1)S(1)} custom-call(bf16[8,256,128]{2,1,0:T(8,128)(2,1)S(1)} %all_to_all.20.refs_0_), custom_call_target="tpu_custom_call" | custom-call | tf_op jit(solution)/shard_map/pallas_call | solution.py:281
  17.3 0.0 copy-start
  17.3 0.0 copy-start.2
  17.3 0.0 copy-start.3
  17.3 18.7 %all_to_all.21.refs_0_ = bf16[16,128,128]{2,1,0:T(8,128)(2,1)S(1)} all-to-all(bf16[16,128,128]{2,1,0:T(8,128)(2,1)S(1)} %shard_map.101), channel_id=1, replica_groups={{1,15,11,7,3,12,14,8,10,4,6,0,2,13,9,5},{17,31,27,23,19,28,30,24,26,20,..., dimensions={0} | all-to-all | bytes 1048576 | tf_op jit(solution)/shard_map/all_to_all | solution.py:292
  36.0 0.0 copy-done
  36.0 0.0 copy-done.2
  36.0 0.0 copy-done.3
  36.1 1.1 %shard_map.102 = (bf16[16,128,128]{2,1,0:T(8,128)(2,1)S(1)}, f32[128,1024]{1,0:T(8,128)S(1)}, f32[128,1024]{1,0:T(8,128)S(1)}) custom-call(bf16[16,128,128]{2,1,0:T(8,128)(2,1)S(1)} %all_to_all.21.refs_0_, f32[128,1024]{1,0:T(8,128)S(1)} %get-tuple-element.14.refs_1_, f32[128,1024]{1,0:T(8,128)S(1)} %get-tuple-element.15.refs_2_, ...), custom_call_target="tpu_custom_call" | custom-call | tf_op jit(solution)/shard_map/pallas_call | solution.py:281
  37.1 17.9 %all_to_all.22.refs_0_ = bf16[16,128,128]{2,1,0:T(8,128)(2,1)S(1)} all-to-all(bf16[16,128,128]{2,1,0:T(8,128)(2,1)S(1)} %get-tuple-element.18), channel_id=1, replica_groups={{1,15,11,7,3,12,14,8,10,4,6,0,2,13,9,5},{17,31,27,23,19,28,30,24,26,20,..., dimensions={0} | all-to-all | bytes 1048576 | tf_op jit(solution)/shard_map/all_to_all | solution.py:292
  55.0 1.1 %shard_map.103 = bf16[16,64,128]{2,1,0:T(8,128)(2,1)S(1)} custom-call(bf16[16,128,128]{2,1,0:T(8,128)(2,1)S(1)} %all_to_all.22.refs_0_), custom_call_target="tpu_custom_call" | custom-call | tf_op jit(solution)/shard_map/pallas_call | solution.py:281
  56.1 0.0 copy-start.1
  56.1 0.0 copy-start.4
  56.2 12.8 %all_to_all.23.refs_0_ = bf16[16,64,128]{2,1,0:T(8,128)(2,1)S(1)} all-to-all(bf16[16,64,128]{2,1,0:T(8,128)(2,1)S(1)} %shard_map.103), channel_id=1, replica_groups={{1,15,11,7,3,12,14,8,10,4,6,0,2,13,9,5},{17,31,27,23,19,28,30,24,26,20,..., dimensions={0} | all-to-all | bytes 524288 | tf_op jit(solution)/shard_map/all_to_all | solution.py:292
  68.9 0.0 copy-done.1
  68.9 0.0 copy-done.4
  68.9 2.4 %shard_map.104 = f32[4,8,32,128]{3,2,1,0:T(8,128)} custom-call(bf16[16,64,128]{2,1,0:T(8,128)(2,1)S(1)} %all_to_all.23.refs_0_, f32[128,1024]{1,0:T(8,128)S(1)} %get-tuple-element.19.refs_1_, f32[128,1024]{1,0:T(8,128)S(1)} %get-tuple-element.20.refs_2_, f32[8,128]{1,0:T(8,128)S(1)} %get-tuple-element.17.refs_4_.refs_3_, bf16[2,128,128]{2,1,0:T(8,128)(2,1)S(1)} %copy-done.3, ...), custom_call_target="tpu_custom_call" | custom-call | tf_op jit(solution)/shard_map/pallas_call | solution.py:281
Async XLA Ops:
  17.3 18.8 %copy-start = (bf16[2,128,512]{2,1,0:T(8,128)(2,1)S(1)}, bf16[2,128,512]{2,1,0:T(8,128)(2,1)}, u32[]{:S(2)}) copy-start(bf16[2,128,512]{2,1,0:T(8,128)(2,1)} %refs_5_.4) | copy-start | bytes 786436
  17.3 18.8 %copy-start.2 = (bf16[2,128,128]{2,1,0:T(8,128)(2,1)S(1)}, bf16[2,128,128]{2,1,0:T(8,128)(2,1)}, u32[]{:S(2)}) copy-start(bf16[2,128,128]{2,1,0:T(8,128)(2,1)} %refs_6_.2) | copy-start | bytes 196612
  17.3 18.8 %copy-start.3 = (bf16[2,128,128]{2,1,0:T(8,128)(2,1)S(1)}, bf16[2,128,128]{2,1,0:T(8,128)(2,1)}, u32[]{:S(2)}) copy-start(bf16[2,128,128]{2,1,0:T(8,128)(2,1)} %refs_4_.3) | copy-start | bytes 196612
  56.1 12.8 %copy-start.1 = (bf16[128,1024]{1,0:T(8,128)(2,1)S(1)}, bf16[128,1024]{1,0:T(8,128)(2,1)}, u32[]{:S(2)}) copy-start(bf16[128,1024]{1,0:T(8,128)(2,1)} %refs_5_.5) | copy-start | bytes 786436
  56.1 12.8 %copy-start.4 = (bf16[512,128]{1,0:T(8,128)(2,1)S(1)}, bf16[512,128]{1,0:T(8,128)(2,1)}, u32[]{:S(2)}) copy-start(bf16[512,128]{1,0:T(8,128)(2,1)} %refs_6_.3) | copy-start | bytes 393220

commit v19 on v18

--- a/solution.py
+++ b/solution.py
@@ -326,15 +326,16 @@
     def message(own):
         return ((hid // own, 2 * own * lines, LANES), BF16)
 
-    def listed(count):
-        middle = (count - 1) // 2
-        places = [(col, row) for col in range(count) for row in range(rows)]
-        places.sort(key=lambda at: (at != (middle, 0), -abs(at[0] - middle), -at[1]))
+    def listed(count, rank):
+        places = sorted([(col, row) for col in range(count) for row in range(rows)], key=rank)
         order = [col * rows + row for col, row in places]
         return order, [[order.index(col * rows + row) for row in range(rows)] for col in range(count)]
 
-    order, everyone = listed(cols)
-    near_order, beside = listed(nears) if split > 1 else (order, everyone)
+    middle = (cols - 1) // 2
+    order, everyone = listed(cols, lambda at: (abs(at[0] - middle), -at[0], at[1]))
+    near_order, beside = order, everyone
+    if split > 1:
+        near_order, beside = listed(nears, lambda at: (at != (0, 0), -at[0], -at[1]))
     single = [[n] for n in range(owners)]
     paired = single
     if split > 1:

time: 71.6 us -> 72.6 us (1.014)
  blocking collectives: 63.3 us -> 64.2 us
    all_to_all x4, blocking collectives: 63.3 us -> 64.2 us  [exchange(): lax.all_to_all(values, axes, split_axis=0, concat_axis=0, axis_index_grou...]
where the time goes in v19:
time: 72.6 us; the launch traced here: 72.3 us
  blocking collectives  64.2 us (88%)
  Pallas kernels  7.98 us (11%)
    all_to_all x4, blocking collectives, exchange(): lax.all_to_all(values, axes, split_axis=0, concat_axis=0, axis_index_grou...  64.2 us
    pallas_call x5, Pallas kernels, call(): pl.pallas_call(body, in_specs=[in_place if in_hbm else held] * count, out...  7.98 us

profile of v19, /device:TPU:0, one launch (start us, length us, event | category | flops | bytes accessed | tf_op | source)
XLA Modules:
  0.0 72.3 jit_solution(8459576873997346913)
XLA Ops:
  0.0 1.9 %shard_map.100 = (bf16[8,256,128]{2,1,0:T(8,128)(2,1)S(1)}, f32[128,1024]{1,0:T(8,128)S(1)}, f32[128,1024]{1,0:T(8,128)S(1)}, f32[8,128]{1,0:T(8,128)S(1)}, f32[8,128]{1,0:T(8,128)S(1)}) custom-call(f32[4,8,32,128]{3,2,1,0:T(8,128)} %bitcast.3, s32[32,32]{1,0:T(8,128)} %refs_1_.1, bf16[2,128,512]{2,1,0:T(8,128)(2,1)} %refs_5_.4, ...), custom_call_target="tpu_custom_call" | custom-call | tf_op jit(solution)/shard_map/pallas_call | solution.py:281
  1.9 13.9 %all_to_all.20.refs_0_ = bf16[8,256,128]{2,1,0:T(8,128)(2,1)S(1)} all-to-all(bf16[8,256,128]{2,1,0:T(8,128)(2,1)S(1)} %get-tuple-element.13), channel_id=1, replica_groups={{0,13,9,5,1,12,8,4},{2,15,11,7,3,14,10,6},{16,29,25,21,17,28,24,20},{18..., dimensions={0} | all-to-all | bytes 1048576 | tf_op jit(solution)/shard_map/all_to_all | solution.py:292
  15.8 1.5 %shard_map.101 = bf16[16,128,128]{2,1,0:T(8,128)(2,1)S(1)} custom-call(bf16[8,256,128]{2,1,0:T(8,128)(2,1)S(1)} %all_to_all.20.refs_0_), custom_call_target="tpu_custom_call" | custom-call | tf_op jit(solution)/shard_map/pallas_call | solution.py:281
  17.3 0.0 copy-start
  17.3 0.0 copy-start.2
  17.3 0.0 copy-start.3
  17.3 20.0 %all_to_all.21.refs_0_ = bf16[16,128,128]{2,1,0:T(8,128)(2,1)S(1)} all-to-all(bf16[16,128,128]{2,1,0:T(8,128)(2,1)S(1)} %shard_map.101), channel_id=1, replica_groups={{1,5,9,13,2,6,10,14,0,4,8,12,3,7,11,15},{17,21,25,29,18,22,26,30,16,20,..., dimensions={0} | all-to-all | bytes 1048576 | tf_op jit(solution)/shard_map/all_to_all | solution.py:292
  37.3 0.0 copy-done
  37.3 0.0 copy-done.2
  37.3 0.0 copy-done.3
  37.3 1.1 %shard_map.102 = (bf16[16,128,128]{2,1,0:T(8,128)(2,1)S(1)}, f32[128,1024]{1,0:T(8,128)S(1)}, f32[128,1024]{1,0:T(8,128)S(1)}) custom-call(bf16[16,128,128]{2,1,0:T(8,128)(2,1)S(1)} %all_to_all.21.refs_0_, f32[128,1024]{1,0:T(8,128)S(1)} %get-tuple-element.14.refs_1_, f32[128,1024]{1,0:T(8,128)S(1)} %get-tuple-element.15.refs_2_, ...), custom_call_target="tpu_custom_call" | custom-call | tf_op jit(solution)/shard_map/pallas_call | solution.py:281
  38.4 17.9 %all_to_all.22.refs_0_ = bf16[16,128,128]{2,1,0:T(8,128)(2,1)S(1)} all-to-all(bf16[16,128,128]{2,1,0:T(8,128)(2,1)S(1)} %get-tuple-element.18), channel_id=1, replica_groups={{1,5,9,13,2,6,10,14,0,4,8,12,3,7,11,15},{17,21,25,29,18,22,26,30,16,20,..., dimensions={0} | all-to-all | bytes 1048576 | tf_op jit(solution)/shard_map/all_to_all | solution.py:292
  56.3 1.1 %shard_map.103 = bf16[16,64,128]{2,1,0:T(8,128)(2,1)S(1)} custom-call(bf16[16,128,128]{2,1,0:T(8,128)(2,1)S(1)} %all_to_all.22.refs_0_), custom_call_target="tpu_custom_call" | custom-call | tf_op jit(solution)/shard_map/pallas_call | solution.py:281
  57.5 0.0 copy-start.1
  57.5 0.0 copy-start.4
  57.5 12.4 %all_to_all.23.refs_0_ = bf16[16,64,128]{2,1,0:T(8,128)(2,1)S(1)} all-to-all(bf16[16,64,128]{2,1,0:T(8,128)(2,1)S(1)} %shard_map.103), channel_id=1, replica_groups={{1,5,9,13,2,6,10,14,0,4,8,12,3,7,11,15},{17,21,25,29,18,22,26,30,16,20,..., dimensions={0} | all-to-all | bytes 524288 | tf_op jit(solution)/shard_map/all_to_all | solution.py:292
  69.9 0.0 copy-done.1
  69.9 0.0 copy-done.4
  69.9 2.4 %shard_map.104 = f32[4,8,32,128]{3,2,1,0:T(8,128)} custom-call(bf16[16,64,128]{2,1,0:T(8,128)(2,1)S(1)} %all_to_all.23.refs_0_, f32[128,1024]{1,0:T(8,128)S(1)} %get-tuple-element.19.refs_1_, f32[128,1024]{1,0:T(8,128)S(1)} %get-tuple-element.20.refs_2_, f32[8,128]{1,0:T(8,128)S(1)} %get-tuple-element.17.refs_4_.refs_3_, bf16[2,128,128]{2,1,0:T(8,128)(2,1)S(1)} %copy-done.3, ...), custom_call_target="tpu_custom_call" | custom-call | tf_op jit(solution)/shard_map/pallas_call | solution.py:281
Async XLA Ops:
  17.3 20.1 %copy-start = (bf16[2,128,512]{2,1,0:T(8,128)(2,1)S(1)}, bf16[2,128,512]{2,1,0:T(8,128)(2,1)}, u32[]{:S(2)}) copy-start(bf16[2,128,512]{2,1,0:T(8,128)(2,1)} %refs_5_.4) | copy-start | bytes 786436
  17.3 20.1 %copy-start.2 = (bf16[2,128,128]{2,1,0:T(8,128)(2,1)S(1)}, bf16[2,128,128]{2,1,0:T(8,128)(2,1)}, u32[]{:S(2)}) copy-start(bf16[2,128,128]{2,1,0:T(8,128)(2,1)} %refs_6_.2) | copy-start | bytes 196612
  17.3 20.0 %copy-start.3 = (bf16[2,128,128]{2,1,0:T(8,128)(2,1)S(1)}, bf16[2,128,128]{2,1,0:T(8,128)(2,1)}, u32[]{:S(2)}) copy-start(bf16[2,128,128]{2,1,0:T(8,128)(2,1)} %refs_4_.3) | copy-start | bytes 196612
  57.5 12.4 %copy-start.1 = (bf16[128,1024]{1,0:T(8,128)(2,1)S(1)}, bf16[128,1024]{1,0:T(8,128)(2,1)}, u32[]{:S(2)}) copy-start(bf16[128,1024]{1,0:T(8,128)(2,1)} %refs_5_.5) | copy-start | bytes 786436
  57.5 12.4 %copy-start.4 = (bf16[512,128]{1,0:T(8,128)(2,1)S(1)}, bf16[512,128]{1,0:T(8,128)(2,1)}, u32[]{:S(2)}) copy-start(bf16[512,128]{1,0:T(8,128)(2,1)} %refs_6_.3) | copy-start | bytes 393220

commit v20 on v19

--- a/solution.py
+++ b/solution.py
@@ -90,21 +90,24 @@
     x_in, mask_in, weight_in, gate_in, gain_in, gain_out, trans_gain = ins
     lines = x_ref.shape[1]
     pairs = [
+        (x_in, x_ref),
         (weight_in.at[0], weight_ref),
-        (x_in, x_ref),
         (gain_in, gain_in_ref),
         (mask_in, mask_ref),
         (gate_in.at[0], gate_ref),
         (gain_out, gain_out_ref),
         (trans_gain, trans_gain_ref),
     ]
-    for copy in start_all(pairs, sems):
+    large, *small = start_all(pairs, sems)
+    for copy in small:
         copy.wait()
     mask = token_mask(mask_ref[...], lines)
+    gain, weight_t, gate_t = spread_gain(gain_in_ref[0:1, :]), halved(weight_ref[...]), halved(gate_ref[...])
+    large.wait()
     current = jnp.concatenate([line_tokens(x_ref, line).T for line in range(lines)], axis=1)
-    normed = channel_norm(current, spread_gain(gain_in_ref[0:1, :]))
-    emit_message(normed, halved(weight_ref[...]), mask, 0, message_ref, stage_ref, share)
-    gate_out[...] = twice_sigmoid(dot(halved(gate_ref[...]), normed))
+    normed = channel_norm(current, gain)
+    emit_message(normed, weight_t, mask, 0, message_ref, stage_ref, share)
+    gate_out[...] = twice_sigmoid(dot(gate_t, normed))
     turned_out[...] = current
     mask_out[...] = mask
     rows = [gain_out_ref[0:1, :], gain_in_ref[1:2, :], gain_out_ref[1:2, :], trans_gain_ref[...]]
@@ -332,7 +335,7 @@
         return order, [[order.index(col * rows + row) for row in range(rows)] for col in range(count)]
 
     middle = (cols - 1) // 2
-    order, everyone = listed(cols, lambda at: (abs(at[0] - middle), -at[0], at[1]))
+    order, everyone = listed(cols, lambda at: (at[0] != middle, at))
     near_order, beside = order, everyone
     if split > 1:
         near_order, beside = listed(nears, lambda at: (at != (0, 0), -at[0], -at[1]))

time: 72.6 us -> 71.1 us (0.979)
  blocking collectives: 64.2 us -> 62.4 us
    all_to_all x4, blocking collectives: 64.2 us -> 62.4 us  [exchange(): lax.all_to_all(values, axes, split_axis=0, concat_axis=0, axis_index_grou...]
where the time goes in v20:
time: 71.1 us; the launch traced here: 70.6 us
  blocking collectives  62.4 us (88%)
  Pallas kernels  8.12 us (11%)
    all_to_all x4, blocking collectives, exchange(): lax.all_to_all(values, axes, split_axis=0, concat_axis=0, axis_index_grou...  62.4 us
    pallas_call x5, Pallas kernels, call(): pl.pallas_call(body, in_specs=[in_place if in_hbm else held] * count, out...  8.12 us

profile of v20, /device:TPU:0, one launch (start us, length us, event | category | flops | bytes accessed | tf_op | source)
XLA Modules:
  0.0 70.6 jit_solution(14009948375430076169)
XLA Ops:
  0.0 2.0 %shard_map.100 = (bf16[8,256,128]{2,1,0:T(8,128)(2,1)S(1)}, f32[128,1024]{1,0:T(8,128)S(1)}, f32[128,1024]{1,0:T(8,128)S(1)}, f32[8,128]{1,0:T(8,128)S(1)}, f32[8,128]{1,0:T(8,128)S(1)}) custom-call(f32[4,8,32,128]{3,2,1,0:T(8,128)} %bitcast.3, s32[32,32]{1,0:T(8,128)} %refs_1_.1, bf16[2,128,512]{2,1,0:T(8,128)(2,1)} %refs_5_.4, ...), custom_call_target="tpu_custom_call" | custom-call | tf_op jit(solution)/shard_map/pallas_call | solution.py:284
  2.0 13.9 %all_to_all.20.refs_0_ = bf16[8,256,128]{2,1,0:T(8,128)(2,1)S(1)} all-to-all(bf16[8,256,128]{2,1,0:T(8,128)(2,1)S(1)} %get-tuple-element.13), channel_id=1, replica_groups={{0,13,9,5,1,12,8,4},{2,15,11,7,3,14,10,6},{16,29,25,21,17,28,24,20},{18..., dimensions={0} | all-to-all | bytes 1048576 | tf_op jit(solution)/shard_map/all_to_all | solution.py:295
  15.9 1.5 %shard_map.101 = bf16[16,128,128]{2,1,0:T(8,128)(2,1)S(1)} custom-call(bf16[8,256,128]{2,1,0:T(8,128)(2,1)S(1)} %all_to_all.20.refs_0_), custom_call_target="tpu_custom_call" | custom-call | tf_op jit(solution)/shard_map/pallas_call | solution.py:284
  17.4 0.0 copy-start
  17.4 0.0 copy-start.2
  17.4 0.0 copy-start.3
  17.4 18.8 %all_to_all.21.refs_0_ = bf16[16,128,128]{2,1,0:T(8,128)(2,1)S(1)} all-to-all(bf16[16,128,128]{2,1,0:T(8,128)(2,1)S(1)} %shard_map.101), channel_id=1, replica_groups={{1,5,9,13,0,4,8,12,2,6,10,14,3,7,11,15},{17,21,25,29,16,20,24,28,18,22,..., dimensions={0} | all-to-all | bytes 1048576 | tf_op jit(solution)/shard_map/all_to_all | solution.py:295
  36.3 0.0 copy-done
  36.3 0.0 copy-done.2
  36.3 0.0 copy-done.3
  36.3 1.1 %shard_map.102 = (bf16[16,128,128]{2,1,0:T(8,128)(2,1)S(1)}, f32[128,1024]{1,0:T(8,128)S(1)}, f32[128,1024]{1,0:T(8,128)S(1)}) custom-call(bf16[16,128,128]{2,1,0:T(8,128)(2,1)S(1)} %all_to_all.21.refs_0_, f32[128,1024]{1,0:T(8,128)S(1)} %get-tuple-element.14.refs_1_, f32[128,1024]{1,0:T(8,128)S(1)} %get-tuple-element.15.refs_2_, ...), custom_call_target="tpu_custom_call" | custom-call | tf_op jit(solution)/shard_map/pallas_call | solution.py:284
  37.4 17.5 %all_to_all.22.refs_0_ = bf16[16,128,128]{2,1,0:T(8,128)(2,1)S(1)} all-to-all(bf16[16,128,128]{2,1,0:T(8,128)(2,1)S(1)} %get-tuple-element.18), channel_id=1, replica_groups={{1,5,9,13,0,4,8,12,2,6,10,14,3,7,11,15},{17,21,25,29,16,20,24,28,18,22,..., dimensions={0} | all-to-all | bytes 1048576 | tf_op jit(solution)/shard_map/all_to_all | solution.py:295
  54.9 1.1 %shard_map.103 = bf16[16,64,128]{2,1,0:T(8,128)(2,1)S(1)} custom-call(bf16[16,128,128]{2,1,0:T(8,128)(2,1)S(1)} %all_to_all.22.refs_0_), custom_call_target="tpu_custom_call" | custom-call | tf_op jit(solution)/shard_map/pallas_call | solution.py:284
  56.0 0.0 copy-start.1
  56.0 0.0 copy-start.4
  56.0 12.2 %all_to_all.23.refs_0_ = bf16[16,64,128]{2,1,0:T(8,128)(2,1)S(1)} all-to-all(bf16[16,64,128]{2,1,0:T(8,128)(2,1)S(1)} %shard_map.103), channel_id=1, replica_groups={{1,5,9,13,0,4,8,12,2,6,10,14,3,7,11,15},{17,21,25,29,16,20,24,28,18,22,..., dimensions={0} | all-to-all | bytes 524288 | tf_op jit(solution)/shard_map/all_to_all | solution.py:295
  68.2 0.0 copy-done.1
  68.2 0.0 copy-done.4
  68.2 2.4 %shard_map.104 = f32[4,8,32,128]{3,2,1,0:T(8,128)} custom-call(bf16[16,64,128]{2,1,0:T(8,128)(2,1)S(1)} %all_to_all.23.refs_0_, f32[128,1024]{1,0:T(8,128)S(1)} %get-tuple-element.19.refs_1_, f32[128,1024]{1,0:T(8,128)S(1)} %get-tuple-element.20.refs_2_, f32[8,128]{1,0:T(8,128)S(1)} %get-tuple-element.17.refs_4_.refs_3_, bf16[2,128,128]{2,1,0:T(8,128)(2,1)S(1)} %copy-done.3, ...), custom_call_target="tpu_custom_call" | custom-call | tf_op jit(solution)/shard_map/pallas_call | solution.py:284
Async XLA Ops:
  17.4 18.9 %copy-start = (bf16[2,128,512]{2,1,0:T(8,128)(2,1)S(1)}, bf16[2,128,512]{2,1,0:T(8,128)(2,1)}, u32[]{:S(2)}) copy-start(bf16[2,128,512]{2,1,0:T(8,128)(2,1)} %refs_5_.4) | copy-start | bytes 786436
  17.4 18.9 %copy-start.2 = (bf16[2,128,128]{2,1,0:T(8,128)(2,1)S(1)}, bf16[2,128,128]{2,1,0:T(8,128)(2,1)}, u32[]{:S(2)}) copy-start(bf16[2,128,128]{2,1,0:T(8,128)(2,1)} %refs_6_.2) | copy-start | bytes 196612
  17.4 18.9 %copy-start.3 = (bf16[2,128,128]{2,1,0:T(8,128)(2,1)S(1)}, bf16[2,128,128]{2,1,0:T(8,128)(2,1)}, u32[]{:S(2)}) copy-start(bf16[2,128,128]{2,1,0:T(8,128)(2,1)} %refs_4_.3) | copy-start | bytes 196612
  56.0 12.2 %copy-start.1 = (bf16[128,1024]{1,0:T(8,128)(2,1)S(1)}, bf16[128,1024]{1,0:T(8,128)(2,1)}, u32[]{:S(2)}) copy-start(bf16[128,1024]{1,0:T(8,128)(2,1)} %refs_5_.5) | copy-start | bytes 786436
  56.0 12.2 %copy-start.4 = (bf16[512,128]{1,0:T(8,128)(2,1)S(1)}, bf16[512,128]{1,0:T(8,128)(2,1)}, u32[]{:S(2)}) copy-start(bf16[512,128]{1,0:T(8,128)(2,1)} %refs_6_.3) | copy-start | bytes 393220

commit v21 on v17

--- a/solution.py
+++ b/solution.py
@@ -316,7 +316,7 @@
     owners = rows * cols
     share = hid // owners
     chunk = min(4 * LANES, tokens)
-    split = halves if share % 8 == 0 else 1
+    split = 1
     first_share = split * share
     held = ((LANES // breadth, lines, breadth, channels), F32)
     grouped = pair_map.reshape(held[0])
@@ -327,8 +327,7 @@
     def message(own):
         return ((hid // own, 2 * own * lines, LANES), BF16)
 
-    blocks = list(range(cols))
-    blocks.insert(0, blocks.pop((cols - 1) // 2))
+    blocks = [(col + cols // 2) % cols for col in range(cols)]
     order = [col * rows + row for col in blocks for row in range(rows)]
     everyone = [[order.index(col * rows + row) for row in range(rows)] for col in range(cols)]
     beside = [[near * rows + row for row in range(rows)] for near in range(nears)] if split > 1 else everyone

time: 71.1 us -> 71.6 us (level)
  blocking collectives: 62.5 us -> 63.6 us
    all_to_all x4, blocking collectives: 62.5 us -> 63.6 us  [exchange(): lax.all_to_all(values, axes, split_axis=0, concat_axis=0, axis_index_grou...]
where the time goes in v21:
time: 71.6 us; the launch traced here: 71.3 us
  blocking collectives  63.6 us (89%)
  Pallas kernels  7.63 us (11%)
    all_to_all x4, blocking collectives, exchange(): lax.all_to_all(values, axes, split_axis=0, concat_axis=0, axis_index_grou...  63.6 us
    pallas_call x5, Pallas kernels, call(): pl.pallas_call(body, in_specs=[in_place if in_hbm else held] * count, out...  7.63 us

profile of v21, /device:TPU:0, one launch (start us, length us, event | category | flops | bytes accessed | tf_op | source)
XLA Modules:
  0.0 71.3 jit_solution(6073815415121090471)
XLA Ops:
  0.0 1.9 %shard_map.100 = (bf16[16,128,128]{2,1,0:T(8,128)(2,1)S(1)}, f32[128,1024]{1,0:T(8,128)S(1)}, f32[128,1024]{1,0:T(8,128)S(1)}, f32[8,128]{1,0:T(8,128)S(1)}, f32[8,128]{1,0:T(8,128)S(1)}) custom-call(f32[4,8,32,128]{3,2,1,0:T(8,128)} %bitcast.3, s32[32,32]{1,0:T(8,128)} %refs_1_.1, bf16[2,128,512]{2,1,0:T(8,128)(2,1)} %refs_5_.4, ...), custom_call_target="tpu_custom_call" | custom-call | tf_op jit(solution)/shard_map/pallas_call | solution.py:281
  1.9 19.8 %all_to_all.20.refs_0_ = bf16[16,128,128]{2,1,0:T(8,128)(2,1)S(1)} all-to-all(bf16[16,128,128]{2,1,0:T(8,128)(2,1)S(1)} %get-tuple-element.13), channel_id=1, replica_groups={{2,6,10,14,3,7,11,15,0,4,8,12,1,5,9,13},{18,22,26,30,19,23,27,31,16,20,..., dimensions={0} | all-to-all | bytes 1048576 | tf_op jit(solution)/shard_map/all_to_all | solution.py:293
  21.7 1.2 %shard_map.101 = bf16[16,64,128]{2,1,0:T(8,128)(2,1)S(1)} custom-call(bf16[16,128,128]{2,1,0:T(8,128)(2,1)S(1)} %all_to_all.20.refs_0_), custom_call_target="tpu_custom_call" | custom-call | tf_op jit(solution)/shard_map/pallas_call | solution.py:281
  22.9 0.0 copy-start
  22.9 0.0 copy-start.2
  22.9 0.0 copy-start.3
  22.9 13.5 %all_to_all.21.refs_0_ = bf16[16,64,128]{2,1,0:T(8,128)(2,1)S(1)} all-to-all(bf16[16,64,128]{2,1,0:T(8,128)(2,1)S(1)} %shard_map.101), channel_id=1, replica_groups={{2,6,10,14,3,7,11,15,0,4,8,12,1,5,9,13},{18,22,26,30,19,23,27,31,16,20,..., dimensions={0} | all-to-all | bytes 524288 | tf_op jit(solution)/shard_map/all_to_all | solution.py:293
  36.4 0.0 copy-done
  36.4 0.0 copy-done.2
  36.4 0.0 copy-done.3
  36.4 1.1 %shard_map.102 = (bf16[16,128,128]{2,1,0:T(8,128)(2,1)S(1)}, f32[128,1024]{1,0:T(8,128)S(1)}, f32[128,1024]{1,0:T(8,128)S(1)}) custom-call(bf16[16,64,128]{2,1,0:T(8,128)(2,1)S(1)} %all_to_all.21.refs_0_, f32[128,1024]{1,0:T(8,128)S(1)} %get-tuple-element.14.refs_1_, f32[128,1024]{1,0:T(8,128)S(1)} %get-tuple-element.15.refs_2_, ...), custom_call_target="tpu_custom_call" | custom-call | tf_op jit(solution)/shard_map/pallas_call | solution.py:281
  37.5 16.7 %all_to_all.22.refs_0_ = bf16[16,128,128]{2,1,0:T(8,128)(2,1)S(1)} all-to-all(bf16[16,128,128]{2,1,0:T(8,128)(2,1)S(1)} %get-tuple-element.18), channel_id=1, replica_groups={{2,6,10,14,3,7,11,15,0,4,8,12,1,5,9,13},{18,22,26,30,19,23,27,31,16,20,..., dimensions={0} | all-to-all | bytes 1048576 | tf_op jit(solution)/shard_map/all_to_all | solution.py:293
  54.2 1.1 %shard_map.103 = bf16[16,64,128]{2,1,0:T(8,128)(2,1)S(1)} custom-call(bf16[16,128,128]{2,1,0:T(8,128)(2,1)S(1)} %all_to_all.22.refs_0_), custom_call_target="tpu_custom_call" | custom-call | tf_op jit(solution)/shard_map/pallas_call | solution.py:281
  55.3 0.0 copy-start.1
  55.3 0.0 copy-start.4
  55.3 13.6 %all_to_all.23.refs_0_ = bf16[16,64,128]{2,1,0:T(8,128)(2,1)S(1)} all-to-all(bf16[16,64,128]{2,1,0:T(8,128)(2,1)S(1)} %shard_map.103), channel_id=1, replica_groups={{2,6,10,14,3,7,11,15,0,4,8,12,1,5,9,13},{18,22,26,30,19,23,27,31,16,20,..., dimensions={0} | all-to-all | bytes 524288 | tf_op jit(solution)/shard_map/all_to_all | solution.py:293
  68.9 0.0 copy-done.1
  68.9 0.0 copy-done.4
  68.9 2.4 %shard_map.104 = f32[4,8,32,128]{3,2,1,0:T(8,128)} custom-call(bf16[16,64,128]{2,1,0:T(8,128)(2,1)S(1)} %all_to_all.23.refs_0_, f32[128,1024]{1,0:T(8,128)S(1)} %get-tuple-element.19.refs_1_, f32[128,1024]{1,0:T(8,128)S(1)} %get-tuple-element.20.refs_2_, f32[8,128]{1,0:T(8,128)S(1)} %get-tuple-element.17.refs_4_.refs_3_, bf16[2,128,128]{2,1,0:T(8,128)(2,1)S(1)} %copy-done.3, ...), custom_call_target="tpu_custom_call" | custom-call | tf_op jit(solution)/shard_map/pallas_call | solution.py:281
Async XLA Ops:
  22.9 13.6 %copy-start = (bf16[2,128,512]{2,1,0:T(8,128)(2,1)S(1)}, bf16[2,128,512]{2,1,0:T(8,128)(2,1)}, u32[]{:S(2)}) copy-start(bf16[2,128,512]{2,1,0:T(8,128)(2,1)} %refs_5_.4) | copy-start | bytes 786436
  22.9 13.6 %copy-start.2 = (bf16[2,128,128]{2,1,0:T(8,128)(2,1)S(1)}, bf16[2,128,128]{2,1,0:T(8,128)(2,1)}, u32[]{:S(2)}) copy-start(bf16[2,128,128]{2,1,0:T(8,128)(2,1)} %refs_6_.2) | copy-start | bytes 196612
  22.9 13.5 %copy-start.3 = (bf16[2,128,128]{2,1,0:T(8,128)(2,1)S(1)}, bf16[2,128,128]{2,1,0:T(8,128)(2,1)}, u32[]{:S(2)}) copy-start(bf16[2,128,128]{2,1,0:T(8,128)(2,1)} %refs_4_.3) | copy-start | bytes 196612
  55.3 13.6 %copy-start.1 = (bf16[128,1024]{1,0:T(8,128)(2,1)S(1)}, bf16[128,1024]{1,0:T(8,128)(2,1)}, u32[]{:S(2)}) copy-start(bf16[128,1024]{1,0:T(8,128)(2,1)} %refs_5_.5) | copy-start | bytes 786436
  55.3 13.6 %copy-start.4 = (bf16[512,128]{1,0:T(8,128)(2,1)S(1)}, bf16[512,128]{1,0:T(8,128)(2,1)}, u32[]{:S(2)}) copy-start(bf16[512,128]{1,0:T(8,128)(2,1)} %refs_6_.3) | copy-start | bytes 393220

commit v22 on v17

--- a/solution.py
+++ b/solution.py
@@ -253,7 +253,7 @@
     hidden = channel_norm(combined, gain_out)
     current = x_ref[...] + gate_ref[...] * dot(out_t, hidden)
     trans_in = channel_norm(current, gain)
-    block = min(256, half)
+    block = half
     for base in range(0, half, block):
         gate_part = dot(gate_t[base : base + block], trans_in)
         up_part = dot(up_t[base : base + block], trans_in)
@@ -327,8 +327,7 @@
     def message(own):
         return ((hid // own, 2 * own * lines, LANES), BF16)
 
-    blocks = list(range(cols))
-    blocks.insert(0, blocks.pop((cols - 1) // 2))
+    blocks = [half * nears + near for half in range(halves) for near in reversed(range(nears))]
     order = [col * rows + row for col in blocks for row in range(rows)]
     everyone = [[order.index(col * rows + row) for row in range(rows)] for col in range(cols)]
     beside = [[near * rows + row for row in range(rows)] for near in range(nears)] if split > 1 else everyone

time: 71.1 us -> 71.5 us (level)
  no operation moved by 1% of the time
where the time goes in v22:
time: 71.5 us; the launch traced here: 70.5 us
  blocking collectives  62.6 us (88%)
  Pallas kernels  7.83 us (11%)
    all_to_all x4, blocking collectives, exchange(): lax.all_to_all(values, axes, split_axis=0, concat_axis=0, axis_index_grou...  62.6 us
    pallas_call x5, Pallas kernels, call(): pl.pallas_call(body, in_specs=[in_place if in_hbm else held] * count, out...  7.83 us

profile of v22, /device:TPU:0, one launch (start us, length us, event | category | flops | bytes accessed | tf_op | source)
XLA Modules:
  0.0 70.5 jit_solution(1365756029528628928)
XLA Ops:
  0.0 1.9 %shard_map.100 = (bf16[8,256,128]{2,1,0:T(8,128)(2,1)S(1)}, f32[128,1024]{1,0:T(8,128)S(1)}, f32[128,1024]{1,0:T(8,128)S(1)}, f32[8,128]{1,0:T(8,128)S(1)}, f32[8,128]{1,0:T(8,128)S(1)}) custom-call(f32[4,8,32,128]{3,2,1,0:T(8,128)} %bitcast.3, s32[32,32]{1,0:T(8,128)} %refs_1_.1, bf16[2,128,512]{2,1,0:T(8,128)(2,1)} %refs_5_.4, ...), custom_call_target="tpu_custom_call" | custom-call | tf_op jit(solution)/shard_map/pallas_call | solution.py:281
  1.9 13.9 %all_to_all.20.refs_0_ = bf16[8,256,128]{2,1,0:T(8,128)(2,1)S(1)} all-to-all(bf16[8,256,128]{2,1,0:T(8,128)(2,1)S(1)} %get-tuple-element.13), channel_id=1, replica_groups=mesh['grp'=2,'row'=4,'half'=2,'near'=2] {'near','row'}, dimensions={0} | all-to-all | bytes 1048576 | tf_op jit(solution)/shard_map/all_to_all | solution.py:293
  15.8 1.5 %shard_map.101 = bf16[16,128,128]{2,1,0:T(8,128)(2,1)S(1)} custom-call(bf16[8,256,128]{2,1,0:T(8,128)(2,1)S(1)} %all_to_all.20.refs_0_), custom_call_target="tpu_custom_call" | custom-call | tf_op jit(solution)/shard_map/pallas_call | solution.py:281
  17.3 0.0 copy-start
  17.3 0.0 copy-start.2
  17.3 0.0 copy-start.3
  17.3 18.2 %all_to_all.21.refs_0_ = bf16[16,128,128]{2,1,0:T(8,128)(2,1)S(1)} all-to-all(bf16[16,128,128]{2,1,0:T(8,128)(2,1)S(1)} %shard_map.101), channel_id=1, replica_groups={{1,5,9,13,0,4,8,12,3,7,11,15,2,6,10,14},{17,21,25,29,16,20,24,28,19,23,..., dimensions={0} | all-to-all | bytes 1048576 | tf_op jit(solution)/shard_map/all_to_all | solution.py:293
  35.6 0.0 copy-done
  35.6 0.0 copy-done.2
  35.6 0.0 copy-done.3
  35.6 1.1 %shard_map.102 = (bf16[16,128,128]{2,1,0:T(8,128)(2,1)S(1)}, f32[128,1024]{1,0:T(8,128)S(1)}, f32[128,1024]{1,0:T(8,128)S(1)}) custom-call(bf16[16,128,128]{2,1,0:T(8,128)(2,1)S(1)} %all_to_all.21.refs_0_, f32[128,1024]{1,0:T(8,128)S(1)} %get-tuple-element.14.refs_1_, f32[128,1024]{1,0:T(8,128)S(1)} %get-tuple-element.15.refs_2_, ...), custom_call_target="tpu_custom_call" | custom-call | tf_op jit(solution)/shard_map/pallas_call | solution.py:281
  36.7 17.9 %all_to_all.22.refs_0_ = bf16[16,128,128]{2,1,0:T(8,128)(2,1)S(1)} all-to-all(bf16[16,128,128]{2,1,0:T(8,128)(2,1)S(1)} %get-tuple-element.18), channel_id=1, replica_groups={{1,5,9,13,0,4,8,12,3,7,11,15,2,6,10,14},{17,21,25,29,16,20,24,28,19,23,..., dimensions={0} | all-to-all | bytes 1048576 | tf_op jit(solution)/shard_map/all_to_all | solution.py:293
  54.6 1.1 %shard_map.103 = bf16[16,64,128]{2,1,0:T(8,128)(2,1)S(1)} custom-call(bf16[16,128,128]{2,1,0:T(8,128)(2,1)S(1)} %all_to_all.22.refs_0_), custom_call_target="tpu_custom_call" | custom-call | tf_op jit(solution)/shard_map/pallas_call | solution.py:281
  55.7 0.0 copy-start.1
  55.7 0.0 copy-start.4
  55.7 12.5 %all_to_all.23.refs_0_ = bf16[16,64,128]{2,1,0:T(8,128)(2,1)S(1)} all-to-all(bf16[16,64,128]{2,1,0:T(8,128)(2,1)S(1)} %shard_map.103), channel_id=1, replica_groups={{1,5,9,13,0,4,8,12,3,7,11,15,2,6,10,14},{17,21,25,29,16,20,24,28,19,23,..., dimensions={0} | all-to-all | bytes 524288 | tf_op jit(solution)/shard_map/all_to_all | solution.py:293
  68.2 0.0 copy-done.1
  68.2 0.0 copy-done.4
  68.2 2.3 %shard_map.104 = f32[4,8,32,128]{3,2,1,0:T(8,128)} custom-call(bf16[16,64,128]{2,1,0:T(8,128)(2,1)S(1)} %all_to_all.23.refs_0_, f32[128,1024]{1,0:T(8,128)S(1)} %get-tuple-element.19.refs_1_, f32[128,1024]{1,0:T(8,128)S(1)} %get-tuple-element.20.refs_2_, f32[8,128]{1,0:T(8,128)S(1)} %get-tuple-element.17.refs_4_.refs_3_, bf16[2,128,128]{2,1,0:T(8,128)(2,1)S(1)} %copy-done.3, ...), custom_call_target="tpu_custom_call" | custom-call | tf_op jit(solution)/shard_map/pallas_call | solution.py:281
Async XLA Ops:
  17.3 18.3 %copy-start = (bf16[2,128,512]{2,1,0:T(8,128)(2,1)S(1)}, bf16[2,128,512]{2,1,0:T(8,128)(2,1)}, u32[]{:S(2)}) copy-start(bf16[2,128,512]{2,1,0:T(8,128)(2,1)} %refs_5_.4) | copy-start | bytes 786436
  17.3 18.3 %copy-start.2 = (bf16[2,128,128]{2,1,0:T(8,128)(2,1)S(1)}, bf16[2,128,128]{2,1,0:T(8,128)(2,1)}, u32[]{:S(2)}) copy-start(bf16[2,128,128]{2,1,0:T(8,128)(2,1)} %refs_6_.2) | copy-start | bytes 196612
  17.3 18.2 %copy-start.3 = (bf16[2,128,128]{2,1,0:T(8,128)(2,1)S(1)}, bf16[2,128,128]{2,1,0:T(8,128)(2,1)}, u32[]{:S(2)}) copy-start(bf16[2,128,128]{2,1,0:T(8,128)(2,1)} %refs_4_.3) | copy-start | bytes 196612
  55.7 12.6 %copy-start.1 = (bf16[128,1024]{1,0:T(8,128)(2,1)S(1)}, bf16[128,1024]{1,0:T(8,128)(2,1)}, u32[]{:S(2)}) copy-start(bf16[128,1024]{1,0:T(8,128)(2,1)} %refs_5_.5) | copy-start | bytes 786436
  55.7 12.6 %copy-start.4 = (bf16[512,128]{1,0:T(8,128)(2,1)S(1)}, bf16[512,128]{1,0:T(8,128)(2,1)}, u32[]{:S(2)}) copy-start(bf16[512,128]{1,0:T(8,128)(2,1)} %refs_6_.3) | copy-start | bytes 393220

commit v23 on v22

--- a/solution.py
+++ b/solution.py
@@ -253,12 +253,9 @@
     hidden = channel_norm(combined, gain_out)
     current = x_ref[...] + gate_ref[...] * dot(out_t, hidden)
     trans_in = channel_norm(current, gain)
-    block = half
-    for base in range(0, half, block):
-        gate_part = dot(gate_t[base : base + block], trans_in)
-        up_part = dot(up_t[base : base + block], trans_in)
-        trans_hidden = (gate_part * twice_sigmoid(gate_part) * up_part).astype(BF16)
-        current = current + dot(down_t[:, base : base + block], trans_hidden)
+    gate_part, up_part = dot(gate_t, trans_in), dot(up_t, trans_in)
+    trans_hidden = (gate_part * twice_sigmoid(gate_part) * up_part).astype(BF16)
+    current = current + dot(down_t, trans_hidden)
     writes = []
     for first in range(0, lines, count):
         for line in range(first, first + count):
@@ -327,7 +324,7 @@
     def message(own):
         return ((hid // own, 2 * own * lines, LANES), BF16)
 
-    blocks = [half * nears + near for half in range(halves) for near in reversed(range(nears))]
+    blocks = [(col + (cols - 1) // 2) % cols for col in range(cols)]
     order = [col * rows + row for col in blocks for row in range(rows)]
     everyone = [[order.index(col * rows + row) for row in range(rows)] for col in range(cols)]
     beside = [[near * rows + row for row in range(rows)] for near in range(nears)] if split > 1 else everyone

time: 71.5 us -> 71.3 us (level)
  no operation moved by 1% of the time
where the time goes in v23:
time: 71.3 us; the launch traced here: 71 us
  blocking collectives  63.1 us (88%)
  Pallas kernels  7.84 us (11%)
    all_to_all x4, blocking collectives, exchange(): lax.all_to_all(values, axes, split_axis=0, concat_axis=0, axis_index_grou...  63.1 us
    pallas_call x5, Pallas kernels, call(): pl.pallas_call(body, in_specs=[in_place if in_hbm else held] * count, out...  7.84 us

profile of v23, /device:TPU:0, one launch (start us, length us, event | category | flops | bytes accessed | tf_op | source)
XLA Modules:
  0.0 71.0 jit_solution(15800344354990569963)
XLA Ops:
  0.0 1.9 %shard_map.100 = (bf16[8,256,128]{2,1,0:T(8,128)(2,1)S(1)}, f32[128,1024]{1,0:T(8,128)S(1)}, f32[128,1024]{1,0:T(8,128)S(1)}, f32[8,128]{1,0:T(8,128)S(1)}, f32[8,128]{1,0:T(8,128)S(1)}) custom-call(f32[4,8,32,128]{3,2,1,0:T(8,128)} %bitcast.3, s32[32,32]{1,0:T(8,128)} %refs_1_.1, bf16[2,128,512]{2,1,0:T(8,128)(2,1)} %refs_5_.4, ...), custom_call_target="tpu_custom_call" | custom-call | tf_op jit(solution)/shard_map/pallas_call | solution.py:278
  1.9 13.9 %all_to_all.20.refs_0_ = bf16[8,256,128]{2,1,0:T(8,128)(2,1)S(1)} all-to-all(bf16[8,256,128]{2,1,0:T(8,128)(2,1)S(1)} %get-tuple-element.13), channel_id=1, replica_groups=mesh['grp'=2,'row'=4,'half'=2,'near'=2] {'near','row'}, dimensions={0} | all-to-all | bytes 1048576 | tf_op jit(solution)/shard_map/all_to_all | solution.py:290
  15.8 1.5 %shard_map.101 = bf16[16,128,128]{2,1,0:T(8,128)(2,1)S(1)} custom-call(bf16[8,256,128]{2,1,0:T(8,128)(2,1)S(1)} %all_to_all.20.refs_0_), custom_call_target="tpu_custom_call" | custom-call | tf_op jit(solution)/shard_map/pallas_call | solution.py:278
  17.3 0.0 copy-start
  17.3 0.0 copy-start.2
  17.3 0.0 copy-start.3
  17.3 18.4 %all_to_all.21.refs_0_ = bf16[16,128,128]{2,1,0:T(8,128)(2,1)S(1)} all-to-all(bf16[16,128,128]{2,1,0:T(8,128)(2,1)S(1)} %shard_map.101), channel_id=1, replica_groups={{1,5,9,13,2,6,10,14,3,7,11,15,0,4,8,12},{17,21,25,29,18,22,26,30,19,23,..., dimensions={0} | all-to-all | bytes 1048576 | tf_op jit(solution)/shard_map/all_to_all | solution.py:290
  35.8 0.0 copy-done
  35.8 0.0 copy-done.2
  35.8 0.0 copy-done.3
  35.8 1.1 %shard_map.102 = (bf16[16,128,128]{2,1,0:T(8,128)(2,1)S(1)}, f32[128,1024]{1,0:T(8,128)S(1)}, f32[128,1024]{1,0:T(8,128)S(1)}) custom-call(bf16[16,128,128]{2,1,0:T(8,128)(2,1)S(1)} %all_to_all.21.refs_0_, f32[128,1024]{1,0:T(8,128)S(1)} %get-tuple-element.14.refs_1_, f32[128,1024]{1,0:T(8,128)S(1)} %get-tuple-element.15.refs_2_, ...), custom_call_target="tpu_custom_call" | custom-call | tf_op jit(solution)/shard_map/pallas_call | solution.py:278
  36.9 17.5 %all_to_all.22.refs_0_ = bf16[16,128,128]{2,1,0:T(8,128)(2,1)S(1)} all-to-all(bf16[16,128,128]{2,1,0:T(8,128)(2,1)S(1)} %get-tuple-element.18), channel_id=1, replica_groups={{1,5,9,13,2,6,10,14,3,7,11,15,0,4,8,12},{17,21,25,29,18,22,26,30,19,23,..., dimensions={0} | all-to-all | bytes 1048576 | tf_op jit(solution)/shard_map/all_to_all | solution.py:290
  54.4 1.1 %shard_map.103 = bf16[16,64,128]{2,1,0:T(8,128)(2,1)S(1)} custom-call(bf16[16,128,128]{2,1,0:T(8,128)(2,1)S(1)} %all_to_all.22.refs_0_), custom_call_target="tpu_custom_call" | custom-call | tf_op jit(solution)/shard_map/pallas_call | solution.py:278
  55.5 0.0 copy-start.1
  55.5 0.0 copy-start.4
  55.5 13.2 %all_to_all.23.refs_0_ = bf16[16,64,128]{2,1,0:T(8,128)(2,1)S(1)} all-to-all(bf16[16,64,128]{2,1,0:T(8,128)(2,1)S(1)} %shard_map.103), channel_id=1, replica_groups={{1,5,9,13,2,6,10,14,3,7,11,15,0,4,8,12},{17,21,25,29,18,22,26,30,19,23,..., dimensions={0} | all-to-all | bytes 524288 | tf_op jit(solution)/shard_map/all_to_all | solution.py:290
  68.7 0.0 copy-done.1
  68.7 0.0 copy-done.4
  68.7 2.3 %shard_map.104 = f32[4,8,32,128]{3,2,1,0:T(8,128)} custom-call(bf16[16,64,128]{2,1,0:T(8,128)(2,1)S(1)} %all_to_all.23.refs_0_, f32[128,1024]{1,0:T(8,128)S(1)} %get-tuple-element.19.refs_1_, f32[128,1024]{1,0:T(8,128)S(1)} %get-tuple-element.20.refs_2_, f32[8,128]{1,0:T(8,128)S(1)} %get-tuple-element.17.refs_4_.refs_3_, bf16[2,128,128]{2,1,0:T(8,128)(2,1)S(1)} %copy-done.3, ...), custom_call_target="tpu_custom_call" | custom-call | tf_op jit(solution)/shard_map/pallas_call | solution.py:278
Async XLA Ops:
  17.3 18.4 %copy-start = (bf16[2,128,512]{2,1,0:T(8,128)(2,1)S(1)}, bf16[2,128,512]{2,1,0:T(8,128)(2,1)}, u32[]{:S(2)}) copy-start(bf16[2,128,512]{2,1,0:T(8,128)(2,1)} %refs_5_.4) | copy-start | bytes 786436
  17.3 18.4 %copy-start.2 = (bf16[2,128,128]{2,1,0:T(8,128)(2,1)S(1)}, bf16[2,128,128]{2,1,0:T(8,128)(2,1)}, u32[]{:S(2)}) copy-start(bf16[2,128,128]{2,1,0:T(8,128)(2,1)} %refs_6_.2) | copy-start | bytes 196612
  17.3 18.4 %copy-start.3 = (bf16[2,128,128]{2,1,0:T(8,128)(2,1)S(1)}, bf16[2,128,128]{2,1,0:T(8,128)(2,1)}, u32[]{:S(2)}) copy-start(bf16[2,128,128]{2,1,0:T(8,128)(2,1)} %refs_4_.3) | copy-start | bytes 196612
  55.5 13.2 %copy-start.1 = (bf16[128,1024]{1,0:T(8,128)(2,1)S(1)}, bf16[128,1024]{1,0:T(8,128)(2,1)}, u32[]{:S(2)}) copy-start(bf16[128,1024]{1,0:T(8,128)(2,1)} %refs_5_.5) | copy-start | bytes 786436
  55.5 13.2 %copy-start.4 = (bf16[512,128]{1,0:T(8,128)(2,1)S(1)}, bf16[512,128]{1,0:T(8,128)(2,1)}, u32[]{:S(2)}) copy-start(bf16[512,128]{1,0:T(8,128)(2,1)} %refs_6_.3) | copy-start | bytes 393220

commit v24 on v23

--- a/solution.py
+++ b/solution.py
@@ -162,12 +162,14 @@
     products = [None] * share
     for group in range(groups):
         left, right = whole(0, group), whole(1, group)
+        if pack > 1:
+            lane = lax.broadcasted_iota(jnp.int32, left.shape, 1) // (near * breadth)
+            left = [jnp.where(lane == place, left, jnp.zeros_like(left)) for place in range(pack)]
+            left = jnp.concatenate(left, axis=0)
+        product = dot(left, right, (1, 1) if outgoing else (0, 0))
+        tokens = product.shape[0] // pack
         for place in range(pack):
-            mine = left
-            if pack > 1:
-                lane = lax.broadcasted_iota(jnp.int32, left.shape, 1)
-                mine = jnp.where(lane // (near * breadth) == place, left, jnp.zeros_like(left))
-            products[place * groups + group] = dot(mine, right, (1, 1) if outgoing else (0, 0))
+            products[place * groups + group] = product[place * tokens : (place + 1) * tokens]
 
     for high in range(cols // slots):
         lanes = slice(high * LANES, (high + 1) * LANES)
@@ -324,7 +326,8 @@
     def message(own):
         return ((hid // own, 2 * own * lines, LANES), BF16)
 
-    blocks = [(col + (cols - 1) // 2) % cols for col in range(cols)]
+    blocks = list(range(cols))
+    blocks.insert(0, blocks.pop((cols - 1) // 2))
     order = [col * rows + row for col in blocks for row in range(rows)]
     everyone = [[order.index(col * rows + row) for row in range(rows)] for col in range(cols)]
     beside = [[near * rows + row for row in range(rows)] for near in range(nears)] if split > 1 else everyone

time: 71.3 us -> 70.8 us (level)
  no operation moved by 1% of the time
where the time goes in v24:
time: 70.8 us; the launch traced here: 70.3 us
  blocking collectives  62.5 us (88%)
  Pallas kernels  7.63 us (11%)
    all_to_all x4, blocking collectives, exchange(): lax.all_to_all(values, axes, split_axis=0, concat_axis=0, axis_index_grou...  62.5 us
    pallas_call x5, Pallas kernels, call(): pl.pallas_call(body, in_specs=[in_place if in_hbm else held] * count, out...  7.63 us

profile of v24, /device:TPU:0, one launch (start us, length us, event | category | flops | bytes accessed | tf_op | source)
XLA Modules:
  0.0 70.3 jit_solution(10711336117032138762)
XLA Ops:
  0.0 1.9 %shard_map.100 = (bf16[8,256,128]{2,1,0:T(8,128)(2,1)S(1)}, f32[128,1024]{1,0:T(8,128)S(1)}, f32[128,1024]{1,0:T(8,128)S(1)}, f32[8,128]{1,0:T(8,128)S(1)}, f32[8,128]{1,0:T(8,128)S(1)}) custom-call(f32[4,8,32,128]{3,2,1,0:T(8,128)} %bitcast.3, s32[32,32]{1,0:T(8,128)} %refs_1_.1, bf16[2,128,512]{2,1,0:T(8,128)(2,1)} %refs_5_.4, ...), custom_call_target="tpu_custom_call" | custom-call | tf_op jit(solution)/shard_map/pallas_call | solution.py:280
  1.9 13.9 %all_to_all.20.refs_0_ = bf16[8,256,128]{2,1,0:T(8,128)(2,1)S(1)} all-to-all(bf16[8,256,128]{2,1,0:T(8,128)(2,1)S(1)} %get-tuple-element.13), channel_id=1, replica_groups=mesh['grp'=2,'row'=4,'half'=2,'near'=2] {'near','row'}, dimensions={0} | all-to-all | bytes 1048576 | tf_op jit(solution)/shard_map/all_to_all | solution.py:292
  15.8 1.3 %shard_map.101 = bf16[16,128,128]{2,1,0:T(8,128)(2,1)S(1)} custom-call(bf16[8,256,128]{2,1,0:T(8,128)(2,1)S(1)} %all_to_all.20.refs_0_), custom_call_target="tpu_custom_call" | custom-call | tf_op jit(solution)/shard_map/pallas_call | solution.py:280
  17.1 0.0 copy-start
  17.1 0.0 copy-start.2
  17.1 0.0 copy-start.3
  17.2 18.9 %all_to_all.21.refs_0_ = bf16[16,128,128]{2,1,0:T(8,128)(2,1)S(1)} all-to-all(bf16[16,128,128]{2,1,0:T(8,128)(2,1)S(1)} %shard_map.101), channel_id=1, replica_groups={{1,5,9,13,0,4,8,12,2,6,10,14,3,7,11,15},{17,21,25,29,16,20,24,28,18,22,..., dimensions={0} | all-to-all | bytes 1048576 | tf_op jit(solution)/shard_map/all_to_all | solution.py:292
  36.1 0.0 copy-done
  36.1 0.0 copy-done.2
  36.1 0.0 copy-done.3
  36.1 1.1 %shard_map.102 = (bf16[16,128,128]{2,1,0:T(8,128)(2,1)S(1)}, f32[128,1024]{1,0:T(8,128)S(1)}, f32[128,1024]{1,0:T(8,128)S(1)}) custom-call(bf16[16,128,128]{2,1,0:T(8,128)(2,1)S(1)} %all_to_all.21.refs_0_, f32[128,1024]{1,0:T(8,128)S(1)} %get-tuple-element.14.refs_1_, f32[128,1024]{1,0:T(8,128)S(1)} %get-tuple-element.15.refs_2_, ...), custom_call_target="tpu_custom_call" | custom-call | tf_op jit(solution)/shard_map/pallas_call | solution.py:280
  37.2 17.5 %all_to_all.22.refs_0_ = bf16[16,128,128]{2,1,0:T(8,128)(2,1)S(1)} all-to-all(bf16[16,128,128]{2,1,0:T(8,128)(2,1)S(1)} %get-tuple-element.18), channel_id=1, replica_groups={{1,5,9,13,0,4,8,12,2,6,10,14,3,7,11,15},{17,21,25,29,16,20,24,28,18,22,..., dimensions={0} | all-to-all | bytes 1048576 | tf_op jit(solution)/shard_map/all_to_all | solution.py:292
  54.7 1.1 %shard_map.103 = bf16[16,64,128]{2,1,0:T(8,128)(2,1)S(1)} custom-call(bf16[16,128,128]{2,1,0:T(8,128)(2,1)S(1)} %all_to_all.22.refs_0_), custom_call_target="tpu_custom_call" | custom-call | tf_op jit(solution)/shard_map/pallas_call | solution.py:280
  55.8 0.0 copy-start.1
  55.8 0.0 copy-start.4
  55.8 12.2 %all_to_all.23.refs_0_ = bf16[16,64,128]{2,1,0:T(8,128)(2,1)S(1)} all-to-all(bf16[16,64,128]{2,1,0:T(8,128)(2,1)S(1)} %shard_map.103), channel_id=1, replica_groups={{1,5,9,13,0,4,8,12,2,6,10,14,3,7,11,15},{17,21,25,29,16,20,24,28,18,22,..., dimensions={0} | all-to-all | bytes 524288 | tf_op jit(solution)/shard_map/all_to_all | solution.py:292
  68.0 0.0 copy-done.1
  68.0 0.0 copy-done.4
  68.0 2.3 %shard_map.104 = f32[4,8,32,128]{3,2,1,0:T(8,128)} custom-call(bf16[16,64,128]{2,1,0:T(8,128)(2,1)S(1)} %all_to_all.23.refs_0_, f32[128,1024]{1,0:T(8,128)S(1)} %get-tuple-element.19.refs_1_, f32[128,1024]{1,0:T(8,128)S(1)} %get-tuple-element.20.refs_2_, f32[8,128]{1,0:T(8,128)S(1)} %get-tuple-element.17.refs_4_.refs_3_, bf16[2,128,128]{2,1,0:T(8,128)(2,1)S(1)} %copy-done.3, ...), custom_call_target="tpu_custom_call" | custom-call | tf_op jit(solution)/shard_map/pallas_call | solution.py:280
Async XLA Ops:
  17.1 19.0 %copy-start = (bf16[2,128,512]{2,1,0:T(8,128)(2,1)S(1)}, bf16[2,128,512]{2,1,0:T(8,128)(2,1)}, u32[]{:S(2)}) copy-start(bf16[2,128,512]{2,1,0:T(8,128)(2,1)} %refs_5_.4) | copy-start | bytes 786436
  17.1 18.9 %copy-start.2 = (bf16[2,128,128]{2,1,0:T(8,128)(2,1)S(1)}, bf16[2,128,128]{2,1,0:T(8,128)(2,1)}, u32[]{:S(2)}) copy-start(bf16[2,128,128]{2,1,0:T(8,128)(2,1)} %refs_6_.2) | copy-start | bytes 196612
  17.1 18.9 %copy-start.3 = (bf16[2,128,128]{2,1,0:T(8,128)(2,1)S(1)}, bf16[2,128,128]{2,1,0:T(8,128)(2,1)}, u32[]{:S(2)}) copy-start(bf16[2,128,128]{2,1,0:T(8,128)(2,1)} %refs_4_.3) | copy-start | bytes 196612
  55.8 12.2 %copy-start.1 = (bf16[128,1024]{1,0:T(8,128)(2,1)S(1)}, bf16[128,1024]{1,0:T(8,128)(2,1)}, u32[]{:S(2)}) copy-start(bf16[128,1024]{1,0:T(8,128)(2,1)} %refs_5_.5) | copy-start | bytes 786436
  55.8 12.2 %copy-start.4 = (bf16[512,128]{1,0:T(8,128)(2,1)S(1)}, bf16[512,128]{1,0:T(8,128)(2,1)}, u32[]{:S(2)}) copy-start(bf16[512,128]{1,0:T(8,128)(2,1)} %refs_6_.3) | copy-start | bytes 393220

commit v25 on v24

--- a/solution.py
+++ b/solution.py
@@ -140,10 +140,11 @@
         return row % lines * (2 * share) + row // (groups * lines) % 2 * share + channel
 
     order = one_hot(span, span, source)
+    blocks = [both_ref[sources[col][row]] for row in range(rows) for col in range(near)]
+    ordered = dot(order, jnp.concatenate(blocks, axis=1)).astype(BF16)
     wide = []
     for row in range(rows):
-        here = jnp.concatenate([both_ref[sources[col][row]] for col in range(near)], axis=1)
-        here = dot(order, here).astype(BF16)
+        here = ordered[:, row * near * LANES : (row + 1) * near * LANES]
         wide.append(jnp.concatenate([here[n * size : (n + 1) * size] for n in range(pack)], axis=1))
     wide = jnp.concatenate(wide, axis=0)
     block = slots * LANES
@@ -195,14 +196,10 @@
     lines = span // share
     order = one_hot(span, span, lambda row: row % share * lines + row // share)
     order = jnp.concatenate([order] * len(sources[0]), axis=1)
-    for first in range(0, len(sources), 2):
-        blocks = [
-            jnp.concatenate([combined_ref[source] for source in sources[owner]], axis=0)
-            for owner in (first, first + 1)
-        ]
-        ordered = dot(order, jnp.concatenate(blocks, axis=1))
-        for n in range(2):
-            stage_ref[(first + n) * span : (first + n + 1) * span, :] = ordered[:, n * LANES : (n + 1) * LANES]
+    blocks = [jnp.concatenate([combined_ref[source] for source in held], axis=0) for held in sources]
+    ordered = dot(order, jnp.concatenate(blocks, axis=1))
+    for owner in range(len(sources)):
+        stage_ref[owner * span : (owner + 1) * span, :] = ordered[:, owner * LANES : (owner + 1) * LANES]
 
 
 def read_combined(stage_ref, owners, lines, share, first, count):

time: 70.8 us -> 70.8 us (level)
  no operation moved by 1% of the time
where the time goes in v25:
time: 70.8 us; the launch traced here: 70.3 us
  blocking collectives  62.5 us (88%)
  Pallas kernels  7.63 us (11%)
    all_to_all x4, blocking collectives, exchange(): lax.all_to_all(values, axes, split_axis=0, concat_axis=0, axis_index_grou...  62.5 us
    pallas_call x5, Pallas kernels, call(): pl.pallas_call(body, in_specs=[in_place if in_hbm else held] * count, out...  7.63 us

profile of v25, /device:TPU:0, one launch (start us, length us, event | category | flops | bytes accessed | tf_op | source)
XLA Modules:
  0.0 70.3 jit_solution(10711336117032138762)
XLA Ops:
  0.0 1.9 %shard_map.100 = (bf16[8,256,128]{2,1,0:T(8,128)(2,1)S(1)}, f32[128,1024]{1,0:T(8,128)S(1)}, f32[128,1024]{1,0:T(8,128)S(1)}, f32[8,128]{1,0:T(8,128)S(1)}, f32[8,128]{1,0:T(8,128)S(1)}) custom-call(f32[4,8,32,128]{3,2,1,0:T(8,128)} %bitcast.3, s32[32,32]{1,0:T(8,128)} %refs_1_.1, bf16[2,128,512]{2,1,0:T(8,128)(2,1)} %refs_5_.4, ...), custom_call_target="tpu_custom_call" | custom-call | tf_op jit(solution)/shard_map/pallas_call | solution.py:277
  1.9 13.9 %all_to_all.20.refs_0_ = bf16[8,256,128]{2,1,0:T(8,128)(2,1)S(1)} all-to-all(bf16[8,256,128]{2,1,0:T(8,128)(2,1)S(1)} %get-tuple-element.13), channel_id=1, replica_groups=mesh['grp'=2,'row'=4,'half'=2,'near'=2] {'near','row'}, dimensions={0} | all-to-all | bytes 1048576 | tf_op jit(solution)/shard_map/all_to_all | solution.py:289
  15.8 1.3 %shard_map.101 = bf16[16,128,128]{2,1,0:T(8,128)(2,1)S(1)} custom-call(bf16[8,256,128]{2,1,0:T(8,128)(2,1)S(1)} %all_to_all.20.refs_0_), custom_call_target="tpu_custom_call" | custom-call | tf_op jit(solution)/shard_map/pallas_call | solution.py:277
  17.1 0.0 copy-start
  17.1 0.0 copy-start.2
  17.1 0.0 copy-start.3
  17.2 18.9 %all_to_all.21.refs_0_ = bf16[16,128,128]{2,1,0:T(8,128)(2,1)S(1)} all-to-all(bf16[16,128,128]{2,1,0:T(8,128)(2,1)S(1)} %shard_map.101), channel_id=1, replica_groups={{1,5,9,13,0,4,8,12,2,6,10,14,3,7,11,15},{17,21,25,29,16,20,24,28,18,22,..., dimensions={0} | all-to-all | bytes 1048576 | tf_op jit(solution)/shard_map/all_to_all | solution.py:289
  36.1 0.0 copy-done
  36.1 0.0 copy-done.2
  36.1 0.0 copy-done.3
  36.1 1.1 %shard_map.102 = (bf16[16,128,128]{2,1,0:T(8,128)(2,1)S(1)}, f32[128,1024]{1,0:T(8,128)S(1)}, f32[128,1024]{1,0:T(8,128)S(1)}) custom-call(bf16[16,128,128]{2,1,0:T(8,128)(2,1)S(1)} %all_to_all.21.refs_0_, f32[128,1024]{1,0:T(8,128)S(1)} %get-tuple-element.14.refs_1_, f32[128,1024]{1,0:T(8,128)S(1)} %get-tuple-element.15.refs_2_, ...), custom_call_target="tpu_custom_call" | custom-call | tf_op jit(solution)/shard_map/pallas_call | solution.py:277
  37.2 17.5 %all_to_all.22.refs_0_ = bf16[16,128,128]{2,1,0:T(8,128)(2,1)S(1)} all-to-all(bf16[16,128,128]{2,1,0:T(8,128)(2,1)S(1)} %get-tuple-element.18), channel_id=1, replica_groups={{1,5,9,13,0,4,8,12,2,6,10,14,3,7,11,15},{17,21,25,29,16,20,24,28,18,22,..., dimensions={0} | all-to-all | bytes 1048576 | tf_op jit(solution)/shard_map/all_to_all | solution.py:289
  54.7 1.1 %shard_map.103 = bf16[16,64,128]{2,1,0:T(8,128)(2,1)S(1)} custom-call(bf16[16,128,128]{2,1,0:T(8,128)(2,1)S(1)} %all_to_all.22.refs_0_), custom_call_target="tpu_custom_call" | custom-call | tf_op jit(solution)/shard_map/pallas_call | solution.py:277
  55.8 0.0 copy-start.1
  55.8 0.0 copy-start.4
  55.8 12.2 %all_to_all.23.refs_0_ = bf16[16,64,128]{2,1,0:T(8,128)(2,1)S(1)} all-to-all(bf16[16,64,128]{2,1,0:T(8,128)(2,1)S(1)} %shard_map.103), channel_id=1, replica_groups={{1,5,9,13,0,4,8,12,2,6,10,14,3,7,11,15},{17,21,25,29,16,20,24,28,18,22,..., dimensions={0} | all-to-all | bytes 524288 | tf_op jit(solution)/shard_map/all_to_all | solution.py:289
  68.0 0.0 copy-done.1
  68.0 0.0 copy-done.4
  68.0 2.3 %shard_map.104 = f32[4,8,32,128]{3,2,1,0:T(8,128)} custom-call(bf16[16,64,128]{2,1,0:T(8,128)(2,1)S(1)} %all_to_all.23.refs_0_, f32[128,1024]{1,0:T(8,128)S(1)} %get-tuple-element.19.refs_1_, f32[128,1024]{1,0:T(8,128)S(1)} %get-tuple-element.20.refs_2_, f32[8,128]{1,0:T(8,128)S(1)} %get-tuple-element.17.refs_4_.refs_3_, bf16[2,128,128]{2,1,0:T(8,128)(2,1)S(1)} %copy-done.3, ...), custom_call_target="tpu_custom_call" | custom-call | tf_op jit(solution)/shard_map/pallas_call | solution.py:277
Async XLA Ops:
  17.1 19.0 %copy-start = (bf16[2,128,512]{2,1,0:T(8,128)(2,1)S(1)}, bf16[2,128,512]{2,1,0:T(8,128)(2,1)}, u32[]{:S(2)}) copy-start(bf16[2,128,512]{2,1,0:T(8,128)(2,1)} %refs_5_.4) | copy-start | bytes 786436
  17.1 18.9 %copy-start.2 = (bf16[2,128,128]{2,1,0:T(8,128)(2,1)S(1)}, bf16[2,128,128]{2,1,0:T(8,128)(2,1)}, u32[]{:S(2)}) copy-start(bf16[2,128,128]{2,1,0:T(8,128)(2,1)} %refs_6_.2) | copy-start | bytes 196612
  17.1 18.9 %copy-start.3 = (bf16[2,128,128]{2,1,0:T(8,128)(2,1)S(1)}, bf16[2,128,128]{2,1,0:T(8,128)(2,1)}, u32[]{:S(2)}) copy-start(bf16[2,128,128]{2,1,0:T(8,128)(2,1)} %refs_4_.3) | copy-start | bytes 196612
  55.8 12.2 %copy-start.1 = (bf16[128,1024]{1,0:T(8,128)(2,1)S(1)}, bf16[128,1024]{1,0:T(8,128)(2,1)}, u32[]{:S(2)}) copy-start(bf16[128,1024]{1,0:T(8,128)(2,1)} %refs_5_.5) | copy-start | bytes 786436
  55.8 12.2 %copy-start.4 = (bf16[512,128]{1,0:T(8,128)(2,1)S(1)}, bf16[512,128]{1,0:T(8,128)(2,1)}, u32[]{:S(2)}) copy-start(bf16[512,128]{1,0:T(8,128)(2,1)} %refs_6_.3) | copy-start | bytes 393220

commit v26 on v25

--- a/solution.py
+++ b/solution.py
@@ -284,9 +284,8 @@
     )(*[pltpu.with_memory_space_constraint(array, pltpu.HBM) if in_hbm else array for array in operands])
 
 
-def exchange(values, axes, order=None):
-    groups = [order] if order else None
-    return lax.all_to_all(values, axes, split_axis=0, concat_axis=0, axis_index_groups=groups, tiled=True)
+def exchange(values, axes, order):
+    return lax.all_to_all(values, axes, split_axis=0, concat_axis=0, axis_index_groups=[order], tiled=True)
 
 
 def per_device(
@@ -323,18 +322,27 @@
     def message(own):
         return ((hid // own, 2 * own * lines, LANES), BF16)
 
+    def listed(places):
+        order = [col * rows + row for col, row in places]
+        count = len(places) // rows
+        return order, [[order.index(col * rows + row) for row in range(rows)] for col in range(count)]
+
+    middle = (cols - 1) // 2
     blocks = list(range(cols))
-    blocks.insert(0, blocks.pop((cols - 1) // 2))
-    order = [col * rows + row for col in blocks for row in range(rows)]
-    everyone = [[order.index(col * rows + row) for row in range(rows)] for col in range(cols)]
-    beside = [[near * rows + row for row in range(rows)] for near in range(nears)] if split > 1 else everyone
-    single = [[n] for n in range(owners)]
-    paired = single if split == 1 else [
-        [everyone[half * nears + near][row] for half in range(halves)] for near in range(nears) for row in range(rows)
+    blocks.insert(0, blocks.pop(middle))
+    order, everyone = listed([(col, row) for col in blocks for row in range(rows)])
+    turned = [(col + middle) % cols for col in range(cols)]
+    last_order, last_everyone = listed([(col, row) for col in turned for row in range(rows)])
+    near_order, beside = order, everyone
+    if split > 1:
+        near_order, beside = listed([(near, row) for row in range(rows) for near in range(nears)])
+    single = [[last_order.index(device)] for device in order]
+    paired = [
+        [everyone[half * nears + device // rows][device % rows] for half in range(split)] for device in near_order
     ]
 
-    def combine(both, own, sources, outgoing):
-        kernel = functools.partial(combine_kernel, sources, everyone, breadth, own, outgoing)
+    def combine(both, own, sources, outgoing, order, owners_at):
+        kernel = functools.partial(combine_kernel, sources, owners_at, breadth, own, outgoing)
         answer = ((owners, own * lines, LANES), BF16)
         return exchange(call(kernel, (both,), [answer])[0], ALL_AXES, order)
 
@@ -353,15 +361,15 @@
         ),
         in_hbm=True,
     )
-    both = exchange(both, NEAR_AXES) if split > 1 else exchange(both, ALL_AXES, order)
-    combined = combine(both, first_share, beside, True)
+    both = exchange(both, NEAR_AXES if split > 1 else ALL_AXES, near_order)
+    combined = combine(both, first_share, beside, True, order, everyone)
     both, gate, current = call(
         functools.partial(middle_kernel, first_share, paired, share, tokens),
         (combined, current, gate, mask, gains, proj_weight, gate_weight, out_weight),
         [message(share), wide, wide],
         (result, spare),
     )
-    combined = combine(exchange(both, ALL_AXES, order), share, everyone, False)
+    combined = combine(exchange(both, ALL_AXES, order), share, everyone, False, last_order, last_everyone)
     (pair_out,) = call(
         functools.partial(last_kernel, share, single, chunk),
         (combined, current, gate, gains, out_weight, trans_up, trans_down),

time: 70.8 us -> 71 us (level)
  no operation moved by 1% of the time
where the time goes in v26:
time: 71 us; the launch traced here: 70.7 us
  blocking collectives  63 us (89%)
  Pallas kernels  7.64 us (11%)
    all_to_all x4, blocking collectives, exchange(): lax.all_to_all(values, axes, split_axis=0, concat_axis=0, axis_index_grou...  63 us
    pallas_call x5, Pallas kernels, call(): pl.pallas_call(body, in_specs=[in_place if in_hbm else held] * count, out...  7.64 us

profile of v26, /device:TPU:0, one launch (start us, length us, event | category | flops | bytes accessed | tf_op | source)
XLA Modules:
  0.0 70.7 jit_solution(11553543584895120059)
XLA Ops:
  0.0 1.9 %shard_map.100 = (bf16[8,256,128]{2,1,0:T(8,128)(2,1)S(1)}, f32[128,1024]{1,0:T(8,128)S(1)}, f32[128,1024]{1,0:T(8,128)S(1)}, f32[8,128]{1,0:T(8,128)S(1)}, f32[8,128]{1,0:T(8,128)S(1)}) custom-call(f32[4,8,32,128]{3,2,1,0:T(8,128)} %bitcast.3, s32[32,32]{1,0:T(8,128)} %refs_1_.1, bf16[2,128,512]{2,1,0:T(8,128)(2,1)} %refs_5_.4, ...), custom_call_target="tpu_custom_call" | custom-call | tf_op jit(solution)/shard_map/pallas_call | solution.py:277
  1.9 14.3 %all_to_all.20.refs_0_ = bf16[8,256,128]{2,1,0:T(8,128)(2,1)S(1)} all-to-all(bf16[8,256,128]{2,1,0:T(8,128)(2,1)S(1)} %get-tuple-element.13), channel_id=1, replica_groups={{0,1,4,5,8,9,12,13},{2,3,6,7,10,11,14,15},{16,17,20,21,24,25,28,29},{18..., dimensions={0} | all-to-all | bytes 1048576 | tf_op jit(solution)/shard_map/all_to_all | solution.py:288
  16.2 1.3 %shard_map.101 = bf16[16,128,128]{2,1,0:T(8,128)(2,1)S(1)} custom-call(bf16[8,256,128]{2,1,0:T(8,128)(2,1)S(1)} %all_to_all.20.refs_0_), custom_call_target="tpu_custom_call" | custom-call | tf_op jit(solution)/shard_map/pallas_call | solution.py:277
  17.5 0.0 copy-start
  17.5 0.0 copy-start.2
  17.5 0.0 copy-start.3
  17.5 18.5 %all_to_all.21.refs_0_ = bf16[16,128,128]{2,1,0:T(8,128)(2,1)S(1)} all-to-all(bf16[16,128,128]{2,1,0:T(8,128)(2,1)S(1)} %shard_map.101), channel_id=1, replica_groups={{1,5,9,13,0,4,8,12,2,6,10,14,3,7,11,15},{17,21,25,29,16,20,24,28,18,22,..., dimensions={0} | all-to-all | bytes 1048576 | tf_op jit(solution)/shard_map/all_to_all | solution.py:288
  36.0 0.0 copy-done
  36.0 0.0 copy-done.2
  36.0 0.0 copy-done.3
  36.0 1.1 %shard_map.102 = (bf16[16,128,128]{2,1,0:T(8,128)(2,1)S(1)}, f32[128,1024]{1,0:T(8,128)S(1)}, f32[128,1024]{1,0:T(8,128)S(1)}) custom-call(bf16[16,128,128]{2,1,0:T(8,128)(2,1)S(1)} %all_to_all.21.refs_0_, f32[128,1024]{1,0:T(8,128)S(1)} %get-tuple-element.14.refs_1_, f32[128,1024]{1,0:T(8,128)S(1)} %get-tuple-element.15.refs_2_, ...), custom_call_target="tpu_custom_call" | custom-call | tf_op jit(solution)/shard_map/pallas_call | solution.py:277
  37.1 17.5 %all_to_all.22.refs_0_ = bf16[16,128,128]{2,1,0:T(8,128)(2,1)S(1)} all-to-all(bf16[16,128,128]{2,1,0:T(8,128)(2,1)S(1)} %get-tuple-element.18), channel_id=1, replica_groups={{1,5,9,13,0,4,8,12,2,6,10,14,3,7,11,15},{17,21,25,29,16,20,24,28,18,22,..., dimensions={0} | all-to-all | bytes 1048576 | tf_op jit(solution)/shard_map/all_to_all | solution.py:288
  54.6 1.1 %shard_map.103 = bf16[16,64,128]{2,1,0:T(8,128)(2,1)S(1)} custom-call(bf16[16,128,128]{2,1,0:T(8,128)(2,1)S(1)} %all_to_all.22.refs_0_), custom_call_target="tpu_custom_call" | custom-call | tf_op jit(solution)/shard_map/pallas_call | solution.py:277
  55.7 0.0 copy-start.1
  55.7 0.0 copy-start.4
  55.7 12.7 %all_to_all.23.refs_0_ = bf16[16,64,128]{2,1,0:T(8,128)(2,1)S(1)} all-to-all(bf16[16,64,128]{2,1,0:T(8,128)(2,1)S(1)} %shard_map.103), channel_id=1, replica_groups={{1,5,9,13,2,6,10,14,3,7,11,15,0,4,8,12},{17,21,25,29,18,22,26,30,19,23,..., dimensions={0} | all-to-all | bytes 524288 | tf_op jit(solution)/shard_map/all_to_all | solution.py:288
  68.4 0.0 copy-done.1
  68.4 0.0 copy-done.4
  68.4 2.3 %shard_map.104 = f32[4,8,32,128]{3,2,1,0:T(8,128)} custom-call(bf16[16,64,128]{2,1,0:T(8,128)(2,1)S(1)} %all_to_all.23.refs_0_, f32[128,1024]{1,0:T(8,128)S(1)} %get-tuple-element.19.refs_1_, f32[128,1024]{1,0:T(8,128)S(1)} %get-tuple-element.20.refs_2_, f32[8,128]{1,0:T(8,128)S(1)} %get-tuple-element.17.refs_4_.refs_3_, bf16[2,128,128]{2,1,0:T(8,128)(2,1)S(1)} %copy-done.3, ...), custom_call_target="tpu_custom_call" | custom-call | tf_op jit(solution)/shard_map/pallas_call | solution.py:277
Async XLA Ops:
  17.5 18.5 %copy-start = (bf16[2,128,512]{2,1,0:T(8,128)(2,1)S(1)}, bf16[2,128,512]{2,1,0:T(8,128)(2,1)}, u32[]{:S(2)}) copy-start(bf16[2,128,512]{2,1,0:T(8,128)(2,1)} %refs_5_.4) | copy-start | bytes 786436
  17.5 18.5 %copy-start.2 = (bf16[2,128,128]{2,1,0:T(8,128)(2,1)S(1)}, bf16[2,128,128]{2,1,0:T(8,128)(2,1)}, u32[]{:S(2)}) copy-start(bf16[2,128,128]{2,1,0:T(8,128)(2,1)} %refs_6_.2) | copy-start | bytes 196612
  17.5 18.5 %copy-start.3 = (bf16[2,128,128]{2,1,0:T(8,128)(2,1)S(1)}, bf16[2,128,128]{2,1,0:T(8,128)(2,1)}, u32[]{:S(2)}) copy-start(bf16[2,128,128]{2,1,0:T(8,128)(2,1)} %refs_4_.3) | copy-start | bytes 196612
  55.7 12.7 %copy-start.1 = (bf16[128,1024]{1,0:T(8,128)(2,1)S(1)}, bf16[128,1024]{1,0:T(8,128)(2,1)}, u32[]{:S(2)}) copy-start(bf16[128,1024]{1,0:T(8,128)(2,1)} %refs_5_.5) | copy-start | bytes 786436
  55.7 12.7 %copy-start.4 = (bf16[512,128]{1,0:T(8,128)(2,1)S(1)}, bf16[512,128]{1,0:T(8,128)(2,1)}, u32[]{:S(2)}) copy-start(bf16[512,128]{1,0:T(8,128)(2,1)} %refs_6_.3) | copy-start | bytes 393220

commit v27 on v25

--- a/solution.py
+++ b/solution.py
@@ -312,7 +312,7 @@
     owners = rows * cols
     share = hid // owners
     chunk = min(4 * LANES, tokens)
-    split = halves if share % 8 == 0 else 1
+    split = 1
     first_share = split * share
     held = ((LANES // breadth, lines, breadth, channels), F32)
     grouped = pair_map.reshape(held[0])

time: 70.8 us -> 71 us (level)
  no operation moved by 1% of the time
where the time goes in v27:
time: 71 us; the launch traced here: 70.5 us
  blocking collectives  63 us (89%)
  Pallas kernels  7.44 us (10%)
    all_to_all x4, blocking collectives, exchange(): lax.all_to_all(values, axes, split_axis=0, concat_axis=0, axis_index_grou...  63 us
    pallas_call x5, Pallas kernels, call(): pl.pallas_call(body, in_specs=[in_place if in_hbm else held] * count, out...  7.44 us

profile of v27, /device:TPU:0, one launch (start us, length us, event | category | flops | bytes accessed | tf_op | source)
XLA Modules:
  0.0 70.5 jit_solution(15409110779200606214)
XLA Ops:
  0.0 1.9 %shard_map.100 = (bf16[16,128,128]{2,1,0:T(8,128)(2,1)S(1)}, f32[128,1024]{1,0:T(8,128)S(1)}, f32[128,1024]{1,0:T(8,128)S(1)}, f32[8,128]{1,0:T(8,128)S(1)}, f32[8,128]{1,0:T(8,128)S(1)}) custom-call(f32[4,8,32,128]{3,2,1,0:T(8,128)} %bitcast.3, s32[32,32]{1,0:T(8,128)} %refs_1_.1, bf16[2,128,512]{2,1,0:T(8,128)(2,1)} %refs_5_.4, ...), custom_call_target="tpu_custom_call" | custom-call | tf_op jit(solution)/shard_map/pallas_call | solution.py:277
  1.9 21.2 %all_to_all.20.refs_0_ = bf16[16,128,128]{2,1,0:T(8,128)(2,1)S(1)} all-to-all(bf16[16,128,128]{2,1,0:T(8,128)(2,1)S(1)} %get-tuple-element.13), channel_id=1, replica_groups={{1,5,9,13,0,4,8,12,2,6,10,14,3,7,11,15},{17,21,25,29,16,20,24,28,18,22,..., dimensions={0} | all-to-all | bytes 1048576 | tf_op jit(solution)/shard_map/all_to_all | solution.py:289
  23.1 1.1 %shard_map.101 = bf16[16,64,128]{2,1,0:T(8,128)(2,1)S(1)} custom-call(bf16[16,128,128]{2,1,0:T(8,128)(2,1)S(1)} %all_to_all.20.refs_0_), custom_call_target="tpu_custom_call" | custom-call | tf_op jit(solution)/shard_map/pallas_call | solution.py:277
  24.3 0.0 copy-start
  24.3 0.0 copy-start.2
  24.3 0.0 copy-start.3
  24.3 12.2 %all_to_all.21.refs_0_ = bf16[16,64,128]{2,1,0:T(8,128)(2,1)S(1)} all-to-all(bf16[16,64,128]{2,1,0:T(8,128)(2,1)S(1)} %shard_map.101), channel_id=1, replica_groups={{1,5,9,13,0,4,8,12,2,6,10,14,3,7,11,15},{17,21,25,29,16,20,24,28,18,22,..., dimensions={0} | all-to-all | bytes 524288 | tf_op jit(solution)/shard_map/all_to_all | solution.py:289
  36.5 0.0 copy-done
  36.5 0.0 copy-done.2
  36.5 0.0 copy-done.3
  36.5 1.1 %shard_map.102 = (bf16[16,128,128]{2,1,0:T(8,128)(2,1)S(1)}, f32[128,1024]{1,0:T(8,128)S(1)}, f32[128,1024]{1,0:T(8,128)S(1)}) custom-call(bf16[16,64,128]{2,1,0:T(8,128)(2,1)S(1)} %all_to_all.21.refs_0_, f32[128,1024]{1,0:T(8,128)S(1)} %get-tuple-element.14.refs_1_, f32[128,1024]{1,0:T(8,128)S(1)} %get-tuple-element.15.refs_2_, ...), custom_call_target="tpu_custom_call" | custom-call | tf_op jit(solution)/shard_map/pallas_call | solution.py:277
  37.6 17.4 %all_to_all.22.refs_0_ = bf16[16,128,128]{2,1,0:T(8,128)(2,1)S(1)} all-to-all(bf16[16,128,128]{2,1,0:T(8,128)(2,1)S(1)} %get-tuple-element.18), channel_id=1, replica_groups={{1,5,9,13,0,4,8,12,2,6,10,14,3,7,11,15},{17,21,25,29,16,20,24,28,18,22,..., dimensions={0} | all-to-all | bytes 1048576 | tf_op jit(solution)/shard_map/all_to_all | solution.py:289
  54.9 1.1 %shard_map.103 = bf16[16,64,128]{2,1,0:T(8,128)(2,1)S(1)} custom-call(bf16[16,128,128]{2,1,0:T(8,128)(2,1)S(1)} %all_to_all.22.refs_0_), custom_call_target="tpu_custom_call" | custom-call | tf_op jit(solution)/shard_map/pallas_call | solution.py:277
  56.0 0.0 copy-start.1
  56.0 0.0 copy-start.4
  56.1 12.2 %all_to_all.23.refs_0_ = bf16[16,64,128]{2,1,0:T(8,128)(2,1)S(1)} all-to-all(bf16[16,64,128]{2,1,0:T(8,128)(2,1)S(1)} %shard_map.103), channel_id=1, replica_groups={{1,5,9,13,0,4,8,12,2,6,10,14,3,7,11,15},{17,21,25,29,16,20,24,28,18,22,..., dimensions={0} | all-to-all | bytes 524288 | tf_op jit(solution)/shard_map/all_to_all | solution.py:289
  68.2 0.0 copy-done.1
  68.2 0.0 copy-done.4
  68.2 2.3 %shard_map.104 = f32[4,8,32,128]{3,2,1,0:T(8,128)} custom-call(bf16[16,64,128]{2,1,0:T(8,128)(2,1)S(1)} %all_to_all.23.refs_0_, f32[128,1024]{1,0:T(8,128)S(1)} %get-tuple-element.19.refs_1_, f32[128,1024]{1,0:T(8,128)S(1)} %get-tuple-element.20.refs_2_, f32[8,128]{1,0:T(8,128)S(1)} %get-tuple-element.17.refs_4_.refs_3_, bf16[2,128,128]{2,1,0:T(8,128)(2,1)S(1)} %copy-done.3, ...), custom_call_target="tpu_custom_call" | custom-call | tf_op jit(solution)/shard_map/pallas_call | solution.py:277
Async XLA Ops:
  24.3 12.2 %copy-start = (bf16[2,128,512]{2,1,0:T(8,128)(2,1)S(1)}, bf16[2,128,512]{2,1,0:T(8,128)(2,1)}, u32[]{:S(2)}) copy-start(bf16[2,128,512]{2,1,0:T(8,128)(2,1)} %refs_5_.4) | copy-start | bytes 786436
  24.3 12.2 %copy-start.2 = (bf16[2,128,128]{2,1,0:T(8,128)(2,1)S(1)}, bf16[2,128,128]{2,1,0:T(8,128)(2,1)}, u32[]{:S(2)}) copy-start(bf16[2,128,128]{2,1,0:T(8,128)(2,1)} %refs_6_.2) | copy-start | bytes 196612
  24.3 12.2 %copy-start.3 = (bf16[2,128,128]{2,1,0:T(8,128)(2,1)S(1)}, bf16[2,128,128]{2,1,0:T(8,128)(2,1)}, u32[]{:S(2)}) copy-start(bf16[2,128,128]{2,1,0:T(8,128)(2,1)} %refs_4_.3) | copy-start | bytes 196612
  56.0 12.2 %copy-start.1 = (bf16[128,1024]{1,0:T(8,128)(2,1)S(1)}, bf16[128,1024]{1,0:T(8,128)(2,1)}, u32[]{:S(2)}) copy-start(bf16[128,1024]{1,0:T(8,128)(2,1)} %refs_5_.5) | copy-start | bytes 786436
  56.0 12.2 %copy-start.4 = (bf16[512,128]{1,0:T(8,128)(2,1)S(1)}, bf16[512,128]{1,0:T(8,128)(2,1)}, u32[]{:S(2)}) copy-start(bf16[512,128]{1,0:T(8,128)(2,1)} %refs_6_.3) | copy-start | bytes 393220

commit v28 on v25

--- a/solution.py
+++ b/solution.py
@@ -51,26 +51,24 @@
     return dot((source % lines == line).astype(BF16), wide)
 
 
-def emit_message(normed, weight_t, mask, line, message_ref, stage_ref, share):
+def emit_message(normed, weight_t, mask, message_ref, stage_ref, share):
     projected = dot(weight_t, normed)
     hid = weight_t.shape[0] // 4
-    owners = hid // share
-    for part in range(normed.shape[1] // LANES):
-        here = projected[:, part * LANES : (part + 1) * LANES]
-        at = line + part
-        keep = mask[at : at + 1]
+    owners, lines = hid // share, mask.shape[0]
+    for line in range(lines):
+        here = projected[:, line * LANES : (line + 1) * LANES]
+        keep = mask[line : line + 1]
         left = twice_sigmoid(here[:hid]) * here[hid : 2 * hid] * keep
         right = twice_sigmoid(here[2 * hid : 3 * hid]) * here[3 * hid :] * keep
         if share % 8 == 0:
             for owner in range(owners):
                 rows = slice(owner * share, (owner + 1) * share)
                 both = jnp.concatenate([left[rows], right[rows]], axis=0).astype(BF16)
-                message_ref[owner, 2 * share * at : 2 * share * (at + 1), :] = both
+                message_ref[owner, 2 * share * line : 2 * share * (line + 1), :] = both
         else:
-            lines = message_ref.shape[1] // 2
-            stage_ref[pl.ds(2 * at, owners, stride=2 * lines), :] = left
-            stage_ref[pl.ds(2 * at + 1, owners, stride=2 * lines), :] = right
-    if share % 8 and line + normed.shape[1] // LANES == mask.shape[0]:
+            stage_ref[pl.ds(2 * line, owners, stride=2 * lines), :] = left
+            stage_ref[pl.ds(2 * line + 1, owners, stride=2 * lines), :] = right
+    if share % 8:
         message_ref[...] = stage_ref[...].astype(BF16).reshape(message_ref.shape)
 
 
@@ -90,8 +88,8 @@
     x_in, mask_in, weight_in, gate_in, gain_in, gain_out, trans_gain = ins
     lines = x_ref.shape[1]
     pairs = [
+        (x_in, x_ref),
         (weight_in.at[0], weight_ref),
-        (x_in, x_ref),
         (gain_in, gain_in_ref),
         (mask_in, mask_ref),
         (gate_in.at[0], gate_ref),
@@ -103,7 +101,7 @@
     mask = token_mask(mask_ref[...], lines)
     current = jnp.concatenate([line_tokens(x_ref, line).T for line in range(lines)], axis=1)
     normed = channel_norm(current, spread_gain(gain_in_ref[0:1, :]))
-    emit_message(normed, halved(weight_ref[...]), mask, 0, message_ref, stage_ref, share)
+    emit_message(normed, halved(weight_ref[...]), mask, message_ref, stage_ref, share)
     gate_out[...] = twice_sigmoid(dot(halved(gate_ref[...]), normed))
     turned_out[...] = current
     mask_out[...] = mask
@@ -191,65 +189,49 @@
                 ]
 
 
-def hold_combined(combined_ref, stage_ref, share, sources):
+def read_combined(combined_ref, stage_ref, share, sources):
     span = combined_ref.shape[1]
-    lines = span // share
+    lines, owners = span // share, len(sources)
     order = one_hot(span, span, lambda row: row % share * lines + row // share)
     order = jnp.concatenate([order] * len(sources[0]), axis=1)
     blocks = [jnp.concatenate([combined_ref[source] for source in held], axis=0) for held in sources]
     ordered = dot(order, jnp.concatenate(blocks, axis=1))
-    for owner in range(len(sources)):
-        stage_ref[owner * span : (owner + 1) * span, :] = ordered[:, owner * LANES : (owner + 1) * LANES]
-
-
-def read_combined(stage_ref, owners, lines, share, first, count):
-    columns = []
-    for line in range(first, first + count):
-        if share % 8 == 0:
-            held = [
-                stage_ref[(owner * lines + line) * share : (owner * lines + line + 1) * share, :]
-                for owner in range(owners)
-            ]
-            columns.append(jnp.concatenate(held, axis=0))
-        else:
-            columns.append(stage_ref[pl.ds(line, owners, stride=lines), :])
+    parts = [ordered[:, owner * LANES : (owner + 1) * LANES] for owner in range(owners)]
+    if share % 8 == 0:
+        columns = [
+            jnp.concatenate([part[line * share : (line + 1) * share] for part in parts], axis=0)
+            for line in range(lines)
+        ]
+    else:
+        for owner, part in enumerate(parts):
+            stage_ref[owner * span : (owner + 1) * span, :] = part
+        columns = [stage_ref[pl.ds(line, owners, stride=lines), :] for line in range(lines)]
     return jnp.concatenate(columns, axis=1)
 
 
-def middle_kernel(share, sources, next_share, chunk, ins, outs, stage_ref, message_stage_ref):
+def middle_kernel(share, sources, next_share, ins, outs, stage_ref, message_stage_ref):
     combined_ref, x_ref, gate_ref, mask_ref, gains_ref, proj_ref, gate_weight_ref, out_ref = ins
     message_ref, gate_out, next_ref = outs
-    tokens = x_ref.shape[1]
-    lines = tokens // LANES
-    owners = x_ref.shape[0] // share
-    hold_combined(combined_ref, stage_ref, share, sources)
-    mask = mask_ref[...]
     gain_out, gain = [spread_gain(gains_ref[n : n + 1, :]) for n in (0, 1)]
     out_t, proj_t, gate_t = halved(out_ref[0]), halved(proj_ref[1]), halved(gate_weight_ref[1])
-    for start in range(0, tokens, chunk):
-        here = slice(start, start + chunk)
-        combined = read_combined(stage_ref, owners, lines, share, start // LANES, chunk // LANES)
-        hidden = channel_norm(combined, gain_out)
-        current = x_ref[:, here] + gate_ref[:, here] * dot(out_t, hidden)
-        next_ref[:, here] = current
-        normed = channel_norm(current, gain)
-        emit_message(normed, proj_t, mask, start // LANES, message_ref, message_stage_ref, next_share)
-        gate_out[:, here] = twice_sigmoid(dot(gate_t, normed))
+    hidden = channel_norm(read_combined(combined_ref, stage_ref, share, sources), gain_out)
+    current = x_ref[...] + gate_ref[...] * dot(out_t, hidden)
+    next_ref[...] = current
+    normed = channel_norm(current, gain)
+    emit_message(normed, proj_t, mask_ref[...], message_ref, message_stage_ref, next_share)
+    gate_out[...] = twice_sigmoid(dot(gate_t, normed))
 
 
 def last_kernel(share, sources, chunk, ins, outs, stage_ref, result_ref, sems):
     combined_ref, x_ref, gate_ref, gains_ref, out_ref, up_ref, down_ref = ins
     (result_out,) = outs
     slots, lines, breadth, channels = result_ref.shape
-    owners = x_ref.shape[0] // share
     half = down_ref.shape[0]
     count = chunk // LANES
     gain_out, gain = [spread_gain(gains_ref[n : n + 1, :]) for n in (2, 3)]
     out_t, down_t = halved(out_ref[1]), down_ref[...].T
     gate_t, up_t = halved(up_ref[:, :half]), up_ref[:, half:].T
-    hold_combined(combined_ref, stage_ref, share, sources)
-    combined = read_combined(stage_ref, owners, lines, share, 0, lines)
-    hidden = channel_norm(combined, gain_out)
+    hidden = channel_norm(read_combined(combined_ref, stage_ref, share, sources), gain_out)
     current = x_ref[...] + gate_ref[...] * dot(out_t, hidden)
     trans_in = channel_norm(current, gain)
     gate_part, up_part = dot(gate_t, trans_in), dot(up_t, trans_in)
@@ -356,7 +338,7 @@
     both = exchange(both, NEAR_AXES) if split > 1 else exchange(both, ALL_AXES, order)
     combined = combine(both, first_share, beside, True)
     both, gate, current = call(
-        functools.partial(middle_kernel, first_share, paired, share, tokens),
+        functools.partial(middle_kernel, first_share, paired, share),
         (combined, current, gate, mask, gains, proj_weight, gate_weight, out_weight),
         [message(share), wide, wide],
         (result, spare),

time: 70.8 us -> 70.7 us (level)
  no operation moved by 1% of the time
where the time goes in v28:
time: 70.7 us; the launch traced here: 70.2 us
  blocking collectives  62.5 us (88%)
  Pallas kernels  7.57 us (11%)
    all_to_all x4, blocking collectives, exchange(): lax.all_to_all(values, axes, split_axis=0, concat_axis=0, axis_index_grou...  62.5 us
    pallas_call x5, Pallas kernels, call(): pl.pallas_call(body, in_specs=[in_place if in_hbm else held] * count, out...  7.57 us

profile of v28, /device:TPU:0, one launch (start us, length us, event | category | flops | bytes accessed | tf_op | source)
XLA Modules:
  0.0 70.2 jit_solution(4083449000350415314)
XLA Ops:
  0.0 1.8 %shard_map.100 = (bf16[8,256,128]{2,1,0:T(8,128)(2,1)S(1)}, f32[128,1024]{1,0:T(8,128)S(1)}, f32[128,1024]{1,0:T(8,128)S(1)}, f32[8,128]{1,0:T(8,128)S(1)}, f32[8,128]{1,0:T(8,128)S(1)}) custom-call(f32[4,8,32,128]{3,2,1,0:T(8,128)} %bitcast.3, s32[32,32]{1,0:T(8,128)} %refs_1_.1, bf16[2,128,512]{2,1,0:T(8,128)(2,1)} %refs_5_.4, ...), custom_call_target="tpu_custom_call" | custom-call | tf_op jit(solution)/shard_map/pallas_call | solution.py:259
  1.8 13.9 %all_to_all.20.refs_0_ = bf16[8,256,128]{2,1,0:T(8,128)(2,1)S(1)} all-to-all(bf16[8,256,128]{2,1,0:T(8,128)(2,1)S(1)} %get-tuple-element.13), channel_id=1, replica_groups=mesh['grp'=2,'row'=4,'half'=2,'near'=2] {'near','row'}, dimensions={0} | all-to-all | bytes 1048576 | tf_op jit(solution)/shard_map/all_to_all | solution.py:271
  15.8 1.3 %shard_map.101 = bf16[16,128,128]{2,1,0:T(8,128)(2,1)S(1)} custom-call(bf16[8,256,128]{2,1,0:T(8,128)(2,1)S(1)} %all_to_all.20.refs_0_), custom_call_target="tpu_custom_call" | custom-call | tf_op jit(solution)/shard_map/pallas_call | solution.py:259
  17.1 0.0 copy-start
  17.1 0.0 copy-start.2
  17.1 0.0 copy-start.3
  17.1 18.9 %all_to_all.21.refs_0_ = bf16[16,128,128]{2,1,0:T(8,128)(2,1)S(1)} all-to-all(bf16[16,128,128]{2,1,0:T(8,128)(2,1)S(1)} %shard_map.101), channel_id=1, replica_groups={{1,5,9,13,0,4,8,12,2,6,10,14,3,7,11,15},{17,21,25,29,16,20,24,28,18,22,..., dimensions={0} | all-to-all | bytes 1048576 | tf_op jit(solution)/shard_map/all_to_all | solution.py:271
  36.0 0.0 copy-done
  36.0 0.0 copy-done.2
  36.0 0.0 copy-done.3
  36.0 1.1 %shard_map.102 = (bf16[16,128,128]{2,1,0:T(8,128)(2,1)S(1)}, f32[128,1024]{1,0:T(8,128)S(1)}, f32[128,1024]{1,0:T(8,128)S(1)}) custom-call(bf16[16,128,128]{2,1,0:T(8,128)(2,1)S(1)} %all_to_all.21.refs_0_, f32[128,1024]{1,0:T(8,128)S(1)} %get-tuple-element.14.refs_1_, f32[128,1024]{1,0:T(8,128)S(1)} %get-tuple-element.15.refs_2_, ...), custom_call_target="tpu_custom_call" | custom-call | tf_op jit(solution)/shard_map/pallas_call | solution.py:259
  37.1 17.5 %all_to_all.22.refs_0_ = bf16[16,128,128]{2,1,0:T(8,128)(2,1)S(1)} all-to-all(bf16[16,128,128]{2,1,0:T(8,128)(2,1)S(1)} %get-tuple-element.18), channel_id=1, replica_groups={{1,5,9,13,0,4,8,12,2,6,10,14,3,7,11,15},{17,21,25,29,16,20,24,28,18,22,..., dimensions={0} | all-to-all | bytes 1048576 | tf_op jit(solution)/shard_map/all_to_all | solution.py:271
  54.6 1.1 %shard_map.103 = bf16[16,64,128]{2,1,0:T(8,128)(2,1)S(1)} custom-call(bf16[16,128,128]{2,1,0:T(8,128)(2,1)S(1)} %all_to_all.22.refs_0_), custom_call_target="tpu_custom_call" | custom-call | tf_op jit(solution)/shard_map/pallas_call | solution.py:259
  55.7 0.0 copy-start.1
  55.8 0.0 copy-start.4
  55.8 12.2 %all_to_all.23.refs_0_ = bf16[16,64,128]{2,1,0:T(8,128)(2,1)S(1)} all-to-all(bf16[16,64,128]{2,1,0:T(8,128)(2,1)S(1)} %shard_map.103), channel_id=1, replica_groups={{1,5,9,13,0,4,8,12,2,6,10,14,3,7,11,15},{17,21,25,29,16,20,24,28,18,22,..., dimensions={0} | all-to-all | bytes 524288 | tf_op jit(solution)/shard_map/all_to_all | solution.py:271
  67.9 0.0 copy-done.1
  68.0 0.0 copy-done.4
  68.0 2.3 %shard_map.104 = f32[4,8,32,128]{3,2,1,0:T(8,128)} custom-call(bf16[16,64,128]{2,1,0:T(8,128)(2,1)S(1)} %all_to_all.23.refs_0_, f32[128,1024]{1,0:T(8,128)S(1)} %get-tuple-element.19.refs_1_, f32[128,1024]{1,0:T(8,128)S(1)} %get-tuple-element.20.refs_2_, f32[8,128]{1,0:T(8,128)S(1)} %get-tuple-element.17.refs_4_.refs_3_, bf16[2,128,128]{2,1,0:T(8,128)(2,1)S(1)} %copy-done.3, ...), custom_call_target="tpu_custom_call" | custom-call | tf_op jit(solution)/shard_map/pallas_call | solution.py:259
Async XLA Ops:
  17.1 19.0 %copy-start = (bf16[2,128,512]{2,1,0:T(8,128)(2,1)S(1)}, bf16[2,128,512]{2,1,0:T(8,128)(2,1)}, u32[]{:S(2)}) copy-start(bf16[2,128,512]{2,1,0:T(8,128)(2,1)} %refs_5_.4) | copy-start | bytes 786436
  17.1 19.0 %copy-start.2 = (bf16[2,128,128]{2,1,0:T(8,128)(2,1)S(1)}, bf16[2,128,128]{2,1,0:T(8,128)(2,1)}, u32[]{:S(2)}) copy-start(bf16[2,128,128]{2,1,0:T(8,128)(2,1)} %refs_6_.2) | copy-start | bytes 196612
  17.1 18.9 %copy-start.3 = (bf16[2,128,128]{2,1,0:T(8,128)(2,1)S(1)}, bf16[2,128,128]{2,1,0:T(8,128)(2,1)}, u32[]{:S(2)}) copy-start(bf16[2,128,128]{2,1,0:T(8,128)(2,1)} %refs_4_.3) | copy-start | bytes 196612
  55.7 12.2 %copy-start.1 = (bf16[128,1024]{1,0:T(8,128)(2,1)S(1)}, bf16[128,1024]{1,0:T(8,128)(2,1)}, u32[]{:S(2)}) copy-start(bf16[128,1024]{1,0:T(8,128)(2,1)} %refs_5_.5) | copy-start | bytes 786436
  55.8 12.2 %copy-start.4 = (bf16[512,128]{1,0:T(8,128)(2,1)S(1)}, bf16[512,128]{1,0:T(8,128)(2,1)}, u32[]{:S(2)}) copy-start(bf16[512,128]{1,0:T(8,128)(2,1)} %refs_6_.3) | copy-start | bytes 393220

commit v29 on v28

--- a/solution.py
+++ b/solution.py
@@ -148,7 +148,7 @@
     block = slots * LANES
     swapped = [dot(wide[:, first : first + block], swap) for first in range(0, wide.shape[1], block)]
 
-    def whole(side, group):
+    def whole(side, group, turned=False):
         columns = []
         for part in swapped:
             held = []
@@ -156,16 +156,18 @@
                 first = row * size + (side * groups + group) * lines
                 held += [part[first : first + lines, slot * LANES : (slot + 1) * LANES] for slot in range(slots)]
             columns.append(jnp.concatenate(held, axis=0))
+        if turned:
+            return jnp.concatenate([column.T for column in columns], axis=0).astype(BF16)
         return jnp.concatenate(columns, axis=1).astype(BF16)
 
     products = [None] * share
     for group in range(groups):
-        left, right = whole(0, group), whole(1, group)
+        left, right = whole(0, group, not outgoing), whole(1, group)
         if pack > 1:
             lane = lax.broadcasted_iota(jnp.int32, left.shape, 1) // (near * breadth)
             left = [jnp.where(lane == place, left, jnp.zeros_like(left)) for place in range(pack)]
             left = jnp.concatenate(left, axis=0)
-        product = dot(left, right, (1, 1) if outgoing else (0, 0))
+        product = dot(left, right, (1, 1) if outgoing else (1, 0))
         tokens = product.shape[0] // pack
         for place in range(pack):
             products[place * groups + group] = product[place * tokens : (place + 1) * tokens]

time: 70.7 us -> 70.8 us (level)
  no operation moved by 1% of the time
where the time goes in v29:
time: 70.8 us; the launch traced here: 70.3 us
  blocking collectives  62.5 us (88%)
  Pallas kernels  7.61 us (11%)
    all_to_all x4, blocking collectives, exchange(): lax.all_to_all(values, axes, split_axis=0, concat_axis=0, axis_index_grou...  62.5 us
    pallas_call x5, Pallas kernels, call(): pl.pallas_call(body, in_specs=[in_place if in_hbm else held] * count, out...  7.61 us

profile of v29, /device:TPU:0, one launch (start us, length us, event | category | flops | bytes accessed | tf_op | source)
XLA Modules:
  0.0 70.3 jit_solution(9413585854095002466)
XLA Ops:
  0.0 1.8 %shard_map.100 = (bf16[8,256,128]{2,1,0:T(8,128)(2,1)S(1)}, f32[128,1024]{1,0:T(8,128)S(1)}, f32[128,1024]{1,0:T(8,128)S(1)}, f32[8,128]{1,0:T(8,128)S(1)}, f32[8,128]{1,0:T(8,128)S(1)}) custom-call(f32[4,8,32,128]{3,2,1,0:T(8,128)} %bitcast.3, s32[32,32]{1,0:T(8,128)} %refs_1_.1, bf16[2,128,512]{2,1,0:T(8,128)(2,1)} %refs_5_.4, ...), custom_call_target="tpu_custom_call" | custom-call | tf_op jit(solution)/shard_map/pallas_call | solution.py:261
  1.8 13.9 %all_to_all.20.refs_0_ = bf16[8,256,128]{2,1,0:T(8,128)(2,1)S(1)} all-to-all(bf16[8,256,128]{2,1,0:T(8,128)(2,1)S(1)} %get-tuple-element.13), channel_id=1, replica_groups=mesh['grp'=2,'row'=4,'half'=2,'near'=2] {'near','row'}, dimensions={0} | all-to-all | bytes 1048576 | tf_op jit(solution)/shard_map/all_to_all | solution.py:273
  15.8 1.3 %shard_map.101 = bf16[16,128,128]{2,1,0:T(8,128)(2,1)S(1)} custom-call(bf16[8,256,128]{2,1,0:T(8,128)(2,1)S(1)} %all_to_all.20.refs_0_), custom_call_target="tpu_custom_call" | custom-call | tf_op jit(solution)/shard_map/pallas_call | solution.py:261
  17.1 0.0 copy-start
  17.1 0.0 copy-start.2
  17.1 0.0 copy-start.3
  17.1 18.9 %all_to_all.21.refs_0_ = bf16[16,128,128]{2,1,0:T(8,128)(2,1)S(1)} all-to-all(bf16[16,128,128]{2,1,0:T(8,128)(2,1)S(1)} %shard_map.101), channel_id=1, replica_groups={{1,5,9,13,0,4,8,12,2,6,10,14,3,7,11,15},{17,21,25,29,16,20,24,28,18,22,..., dimensions={0} | all-to-all | bytes 1048576 | tf_op jit(solution)/shard_map/all_to_all | solution.py:273
  36.0 0.0 copy-done
  36.0 0.0 copy-done.2
  36.0 0.0 copy-done.3
  36.0 1.1 %shard_map.102 = (bf16[16,128,128]{2,1,0:T(8,128)(2,1)S(1)}, f32[128,1024]{1,0:T(8,128)S(1)}, f32[128,1024]{1,0:T(8,128)S(1)}) custom-call(bf16[16,128,128]{2,1,0:T(8,128)(2,1)S(1)} %all_to_all.21.refs_0_, f32[128,1024]{1,0:T(8,128)S(1)} %get-tuple-element.14.refs_1_, f32[128,1024]{1,0:T(8,128)S(1)} %get-tuple-element.15.refs_2_, ...), custom_call_target="tpu_custom_call" | custom-call | tf_op jit(solution)/shard_map/pallas_call | solution.py:261
  37.1 17.5 %all_to_all.22.refs_0_ = bf16[16,128,128]{2,1,0:T(8,128)(2,1)S(1)} all-to-all(bf16[16,128,128]{2,1,0:T(8,128)(2,1)S(1)} %get-tuple-element.18), channel_id=1, replica_groups={{1,5,9,13,0,4,8,12,2,6,10,14,3,7,11,15},{17,21,25,29,16,20,24,28,18,22,..., dimensions={0} | all-to-all | bytes 1048576 | tf_op jit(solution)/shard_map/all_to_all | solution.py:273
  54.6 1.1 %shard_map.103 = bf16[16,64,128]{2,1,0:T(8,128)(2,1)S(1)} custom-call(bf16[16,128,128]{2,1,0:T(8,128)(2,1)S(1)} %all_to_all.22.refs_0_), custom_call_target="tpu_custom_call" | custom-call | tf_op jit(solution)/shard_map/pallas_call | solution.py:261
  55.8 0.0 copy-start.1
  55.8 0.0 copy-start.4
  55.8 12.2 %all_to_all.23.refs_0_ = bf16[16,64,128]{2,1,0:T(8,128)(2,1)S(1)} all-to-all(bf16[16,64,128]{2,1,0:T(8,128)(2,1)S(1)} %shard_map.103), channel_id=1, replica_groups={{1,5,9,13,0,4,8,12,2,6,10,14,3,7,11,15},{17,21,25,29,16,20,24,28,18,22,..., dimensions={0} | all-to-all | bytes 524288 | tf_op jit(solution)/shard_map/all_to_all | solution.py:273
  68.0 0.0 copy-done.1
  68.0 0.0 copy-done.4
  68.0 2.3 %shard_map.104 = f32[4,8,32,128]{3,2,1,0:T(8,128)} custom-call(bf16[16,64,128]{2,1,0:T(8,128)(2,1)S(1)} %all_to_all.23.refs_0_, f32[128,1024]{1,0:T(8,128)S(1)} %get-tuple-element.19.refs_1_, f32[128,1024]{1,0:T(8,128)S(1)} %get-tuple-element.20.refs_2_, f32[8,128]{1,0:T(8,128)S(1)} %get-tuple-element.17.refs_4_.refs_3_, bf16[2,128,128]{2,1,0:T(8,128)(2,1)S(1)} %copy-done.3, ...), custom_call_target="tpu_custom_call" | custom-call | tf_op jit(solution)/shard_map/pallas_call | solution.py:261
Async XLA Ops:
  17.1 19.0 %copy-start = (bf16[2,128,512]{2,1,0:T(8,128)(2,1)S(1)}, bf16[2,128,512]{2,1,0:T(8,128)(2,1)}, u32[]{:S(2)}) copy-start(bf16[2,128,512]{2,1,0:T(8,128)(2,1)} %refs_5_.4) | copy-start | bytes 786436
  17.1 19.0 %copy-start.2 = (bf16[2,128,128]{2,1,0:T(8,128)(2,1)S(1)}, bf16[2,128,128]{2,1,0:T(8,128)(2,1)}, u32[]{:S(2)}) copy-start(bf16[2,128,128]{2,1,0:T(8,128)(2,1)} %refs_6_.2) | copy-start | bytes 196612
  17.1 18.9 %copy-start.3 = (bf16[2,128,128]{2,1,0:T(8,128)(2,1)S(1)}, bf16[2,128,128]{2,1,0:T(8,128)(2,1)}, u32[]{:S(2)}) copy-start(bf16[2,128,128]{2,1,0:T(8,128)(2,1)} %refs_4_.3) | copy-start | bytes 196612
  55.8 12.2 %copy-start.1 = (bf16[128,1024]{1,0:T(8,128)(2,1)S(1)}, bf16[128,1024]{1,0:T(8,128)(2,1)}, u32[]{:S(2)}) copy-start(bf16[128,1024]{1,0:T(8,128)(2,1)} %refs_5_.5) | copy-start | bytes 786436
  55.8 12.2 %copy-start.4 = (bf16[512,128]{1,0:T(8,128)(2,1)S(1)}, bf16[512,128]{1,0:T(8,128)(2,1)}, u32[]{:S(2)}) copy-start(bf16[512,128]{1,0:T(8,128)(2,1)} %refs_6_.3) | copy-start | bytes 393220

commit v30 on v29

--- a/solution.py
+++ b/solution.py
@@ -295,7 +295,7 @@
     cols = halves * nears
     owners = rows * cols
     share = hid // owners
-    chunk = min(4 * LANES, tokens)
+    chunk = tokens
     split = halves if share % 8 == 0 else 1
     first_share = split * share
     held = ((LANES // breadth, lines, breadth, channels), F32)

time: 70.8 us -> 70.9 us (level)
  no operation moved by 1% of the time
where the time goes in v30:
time: 70.9 us; the launch traced here: 70.3 us
  blocking collectives  62.5 us (88%)
  Pallas kernels  7.69 us (11%)
    all_to_all x4, blocking collectives, exchange(): lax.all_to_all(values, axes, split_axis=0, concat_axis=0, axis_index_grou...  62.5 us
    pallas_call x5, Pallas kernels, call(): pl.pallas_call(body, in_specs=[in_place if in_hbm else held] * count, out...  7.69 us

profile of v30, /device:TPU:0, one launch (start us, length us, event | category | flops | bytes accessed | tf_op | source)
XLA Modules:
  0.0 70.3 jit_solution(4351415435047201976)
XLA Ops:
  0.0 1.8 %shard_map.100 = (bf16[8,256,128]{2,1,0:T(8,128)(2,1)S(1)}, f32[128,1024]{1,0:T(8,128)S(1)}, f32[128,1024]{1,0:T(8,128)S(1)}, f32[8,128]{1,0:T(8,128)S(1)}, f32[8,128]{1,0:T(8,128)S(1)}) custom-call(f32[4,8,32,128]{3,2,1,0:T(8,128)} %bitcast.3, s32[32,32]{1,0:T(8,128)} %refs_1_.1, bf16[2,128,512]{2,1,0:T(8,128)(2,1)} %refs_5_.4, ...), custom_call_target="tpu_custom_call" | custom-call | tf_op jit(solution)/shard_map/pallas_call | solution.py:261
  1.8 13.9 %all_to_all.20.refs_0_ = bf16[8,256,128]{2,1,0:T(8,128)(2,1)S(1)} all-to-all(bf16[8,256,128]{2,1,0:T(8,128)(2,1)S(1)} %get-tuple-element.13), channel_id=1, replica_groups=mesh['grp'=2,'row'=4,'half'=2,'near'=2] {'near','row'}, dimensions={0} | all-to-all | bytes 1048576 | tf_op jit(solution)/shard_map/all_to_all | solution.py:273
  15.8 1.3 %shard_map.101 = bf16[16,128,128]{2,1,0:T(8,128)(2,1)S(1)} custom-call(bf16[8,256,128]{2,1,0:T(8,128)(2,1)S(1)} %all_to_all.20.refs_0_), custom_call_target="tpu_custom_call" | custom-call | tf_op jit(solution)/shard_map/pallas_call | solution.py:261
  17.1 0.0 copy-start
  17.1 0.0 copy-start.2
  17.1 0.0 copy-start.3
  17.1 18.9 %all_to_all.21.refs_0_ = bf16[16,128,128]{2,1,0:T(8,128)(2,1)S(1)} all-to-all(bf16[16,128,128]{2,1,0:T(8,128)(2,1)S(1)} %shard_map.101), channel_id=1, replica_groups={{1,5,9,13,0,4,8,12,2,6,10,14,3,7,11,15},{17,21,25,29,16,20,24,28,18,22,..., dimensions={0} | all-to-all | bytes 1048576 | tf_op jit(solution)/shard_map/all_to_all | solution.py:273
  36.0 0.0 copy-done
  36.0 0.0 copy-done.2
  36.0 0.0 copy-done.3
  36.0 1.1 %shard_map.102 = (bf16[16,128,128]{2,1,0:T(8,128)(2,1)S(1)}, f32[128,1024]{1,0:T(8,128)S(1)}, f32[128,1024]{1,0:T(8,128)S(1)}) custom-call(bf16[16,128,128]{2,1,0:T(8,128)(2,1)S(1)} %all_to_all.21.refs_0_, f32[128,1024]{1,0:T(8,128)S(1)} %get-tuple-element.14.refs_1_, f32[128,1024]{1,0:T(8,128)S(1)} %get-tuple-element.15.refs_2_, ...), custom_call_target="tpu_custom_call" | custom-call | tf_op jit(solution)/shard_map/pallas_call | solution.py:261
  37.1 17.5 %all_to_all.22.refs_0_ = bf16[16,128,128]{2,1,0:T(8,128)(2,1)S(1)} all-to-all(bf16[16,128,128]{2,1,0:T(8,128)(2,1)S(1)} %get-tuple-element.18), channel_id=1, replica_groups={{1,5,9,13,0,4,8,12,2,6,10,14,3,7,11,15},{17,21,25,29,16,20,24,28,18,22,..., dimensions={0} | all-to-all | bytes 1048576 | tf_op jit(solution)/shard_map/all_to_all | solution.py:273
  54.6 1.1 %shard_map.103 = bf16[16,64,128]{2,1,0:T(8,128)(2,1)S(1)} custom-call(bf16[16,128,128]{2,1,0:T(8,128)(2,1)S(1)} %all_to_all.22.refs_0_), custom_call_target="tpu_custom_call" | custom-call | tf_op jit(solution)/shard_map/pallas_call | solution.py:261
  55.8 0.0 copy-start.1
  55.8 0.0 copy-start.4
  55.8 12.2 %all_to_all.23.refs_0_ = bf16[16,64,128]{2,1,0:T(8,128)(2,1)S(1)} all-to-all(bf16[16,64,128]{2,1,0:T(8,128)(2,1)S(1)} %shard_map.103), channel_id=1, replica_groups={{1,5,9,13,0,4,8,12,2,6,10,14,3,7,11,15},{17,21,25,29,16,20,24,28,18,22,..., dimensions={0} | all-to-all | bytes 524288 | tf_op jit(solution)/shard_map/all_to_all | solution.py:273
  68.0 0.0 copy-done.1
  68.0 0.0 copy-done.4
  68.0 2.4 %shard_map.104 = f32[4,8,32,128]{3,2,1,0:T(8,128)} custom-call(bf16[16,64,128]{2,1,0:T(8,128)(2,1)S(1)} %all_to_all.23.refs_0_, f32[128,1024]{1,0:T(8,128)S(1)} %get-tuple-element.19.refs_1_, f32[128,1024]{1,0:T(8,128)S(1)} %get-tuple-element.20.refs_2_, f32[8,128]{1,0:T(8,128)S(1)} %get-tuple-element.17.refs_4_.refs_3_, bf16[2,128,128]{2,1,0:T(8,128)(2,1)S(1)} %copy-done.3, ...), custom_call_target="tpu_custom_call" | custom-call | tf_op jit(solution)/shard_map/pallas_call | solution.py:261
Async XLA Ops:
  17.1 19.0 %copy-start = (bf16[2,128,512]{2,1,0:T(8,128)(2,1)S(1)}, bf16[2,128,512]{2,1,0:T(8,128)(2,1)}, u32[]{:S(2)}) copy-start(bf16[2,128,512]{2,1,0:T(8,128)(2,1)} %refs_5_.4) | copy-start | bytes 786436
  17.1 19.0 %copy-start.2 = (bf16[2,128,128]{2,1,0:T(8,128)(2,1)S(1)}, bf16[2,128,128]{2,1,0:T(8,128)(2,1)}, u32[]{:S(2)}) copy-start(bf16[2,128,128]{2,1,0:T(8,128)(2,1)} %refs_6_.2) | copy-start | bytes 196612
  17.1 18.9 %copy-start.3 = (bf16[2,128,128]{2,1,0:T(8,128)(2,1)S(1)}, bf16[2,128,128]{2,1,0:T(8,128)(2,1)}, u32[]{:S(2)}) copy-start(bf16[2,128,128]{2,1,0:T(8,128)(2,1)} %refs_4_.3) | copy-start | bytes 196612
  55.8 12.2 %copy-start.1 = (bf16[128,1024]{1,0:T(8,128)(2,1)S(1)}, bf16[128,1024]{1,0:T(8,128)(2,1)}, u32[]{:S(2)}) copy-start(bf16[128,1024]{1,0:T(8,128)(2,1)} %refs_5_.5) | copy-start | bytes 786436
  55.8 12.2 %copy-start.4 = (bf16[512,128]{1,0:T(8,128)(2,1)S(1)}, bf16[512,128]{1,0:T(8,128)(2,1)}, u32[]{:S(2)}) copy-start(bf16[512,128]{1,0:T(8,128)(2,1)} %refs_6_.3) | copy-start | bytes 393220

commit v31 on v30

--- a/solution.py
+++ b/solution.py
@@ -295,7 +295,7 @@
     cols = halves * nears
     owners = rows * cols
     share = hid // owners
-    chunk = tokens
+    chunk = min(2 * LANES, tokens)
     split = halves if share % 8 == 0 else 1
     first_share = split * share
     held = ((LANES // breadth, lines, breadth, channels), F32)

time: 70.9 us -> 70.8 us (level)
  no operation moved by 1% of the time
where the time goes in v31:
time: 70.8 us; the launch traced here: 70.2 us
  blocking collectives  62.5 us (88%)
  Pallas kernels  7.59 us (11%)
    all_to_all x4, blocking collectives, exchange(): lax.all_to_all(values, axes, split_axis=0, concat_axis=0, axis_index_grou...  62.5 us
    pallas_call x5, Pallas kernels, call(): pl.pallas_call(body, in_specs=[in_place if in_hbm else held] * count, out...  7.59 us

profile of v31, /device:TPU:0, one launch (start us, length us, event | category | flops | bytes accessed | tf_op | source)
XLA Modules:
  0.0 70.2 jit_solution(5816132853491194737)
XLA Ops:
  0.0 1.8 %shard_map.100 = (bf16[8,256,128]{2,1,0:T(8,128)(2,1)S(1)}, f32[128,1024]{1,0:T(8,128)S(1)}, f32[128,1024]{1,0:T(8,128)S(1)}, f32[8,128]{1,0:T(8,128)S(1)}, f32[8,128]{1,0:T(8,128)S(1)}) custom-call(f32[4,8,32,128]{3,2,1,0:T(8,128)} %bitcast.3, s32[32,32]{1,0:T(8,128)} %refs_1_.1, bf16[2,128,512]{2,1,0:T(8,128)(2,1)} %refs_5_.4, ...), custom_call_target="tpu_custom_call" | custom-call | tf_op jit(solution)/shard_map/pallas_call | solution.py:261
  1.8 13.9 %all_to_all.20.refs_0_ = bf16[8,256,128]{2,1,0:T(8,128)(2,1)S(1)} all-to-all(bf16[8,256,128]{2,1,0:T(8,128)(2,1)S(1)} %get-tuple-element.13), channel_id=1, replica_groups=mesh['grp'=2,'row'=4,'half'=2,'near'=2] {'near','row'}, dimensions={0} | all-to-all | bytes 1048576 | tf_op jit(solution)/shard_map/all_to_all | solution.py:273
  15.8 1.3 %shard_map.101 = bf16[16,128,128]{2,1,0:T(8,128)(2,1)S(1)} custom-call(bf16[8,256,128]{2,1,0:T(8,128)(2,1)S(1)} %all_to_all.20.refs_0_), custom_call_target="tpu_custom_call" | custom-call | tf_op jit(solution)/shard_map/pallas_call | solution.py:261
  17.1 0.0 copy-start
  17.1 0.0 copy-start.2
  17.1 0.0 copy-start.3
  17.1 18.9 %all_to_all.21.refs_0_ = bf16[16,128,128]{2,1,0:T(8,128)(2,1)S(1)} all-to-all(bf16[16,128,128]{2,1,0:T(8,128)(2,1)S(1)} %shard_map.101), channel_id=1, replica_groups={{1,5,9,13,0,4,8,12,2,6,10,14,3,7,11,15},{17,21,25,29,16,20,24,28,18,22,..., dimensions={0} | all-to-all | bytes 1048576 | tf_op jit(solution)/shard_map/all_to_all | solution.py:273
  36.0 0.0 copy-done
  36.0 0.0 copy-done.2
  36.0 0.0 copy-done.3
  36.0 1.1 %shard_map.102 = (bf16[16,128,128]{2,1,0:T(8,128)(2,1)S(1)}, f32[128,1024]{1,0:T(8,128)S(1)}, f32[128,1024]{1,0:T(8,128)S(1)}) custom-call(bf16[16,128,128]{2,1,0:T(8,128)(2,1)S(1)} %all_to_all.21.refs_0_, f32[128,1024]{1,0:T(8,128)S(1)} %get-tuple-element.14.refs_1_, f32[128,1024]{1,0:T(8,128)S(1)} %get-tuple-element.15.refs_2_, ...), custom_call_target="tpu_custom_call" | custom-call | tf_op jit(solution)/shard_map/pallas_call | solution.py:261
  37.1 17.5 %all_to_all.22.refs_0_ = bf16[16,128,128]{2,1,0:T(8,128)(2,1)S(1)} all-to-all(bf16[16,128,128]{2,1,0:T(8,128)(2,1)S(1)} %get-tuple-element.18), channel_id=1, replica_groups={{1,5,9,13,0,4,8,12,2,6,10,14,3,7,11,15},{17,21,25,29,16,20,24,28,18,22,..., dimensions={0} | all-to-all | bytes 1048576 | tf_op jit(solution)/shard_map/all_to_all | solution.py:273
  54.6 1.1 %shard_map.103 = bf16[16,64,128]{2,1,0:T(8,128)(2,1)S(1)} custom-call(bf16[16,128,128]{2,1,0:T(8,128)(2,1)S(1)} %all_to_all.22.refs_0_), custom_call_target="tpu_custom_call" | custom-call | tf_op jit(solution)/shard_map/pallas_call | solution.py:261
  55.8 0.0 copy-start.1
  55.8 0.0 copy-start.4
  55.8 12.2 %all_to_all.23.refs_0_ = bf16[16,64,128]{2,1,0:T(8,128)(2,1)S(1)} all-to-all(bf16[16,64,128]{2,1,0:T(8,128)(2,1)S(1)} %shard_map.103), channel_id=1, replica_groups={{1,5,9,13,0,4,8,12,2,6,10,14,3,7,11,15},{17,21,25,29,16,20,24,28,18,22,..., dimensions={0} | all-to-all | bytes 524288 | tf_op jit(solution)/shard_map/all_to_all | solution.py:273
  68.0 0.0 copy-done.1
  68.0 0.0 copy-done.4
  68.0 2.3 %shard_map.104 = f32[4,8,32,128]{3,2,1,0:T(8,128)} custom-call(bf16[16,64,128]{2,1,0:T(8,128)(2,1)S(1)} %all_to_all.23.refs_0_, f32[128,1024]{1,0:T(8,128)S(1)} %get-tuple-element.19.refs_1_, f32[128,1024]{1,0:T(8,128)S(1)} %get-tuple-element.20.refs_2_, f32[8,128]{1,0:T(8,128)S(1)} %get-tuple-element.17.refs_4_.refs_3_, bf16[2,128,128]{2,1,0:T(8,128)(2,1)S(1)} %copy-done.3, ...), custom_call_target="tpu_custom_call" | custom-call | tf_op jit(solution)/shard_map/pallas_call | solution.py:261
Async XLA Ops:
  17.1 19.0 %copy-start = (bf16[2,128,512]{2,1,0:T(8,128)(2,1)S(1)}, bf16[2,128,512]{2,1,0:T(8,128)(2,1)}, u32[]{:S(2)}) copy-start(bf16[2,128,512]{2,1,0:T(8,128)(2,1)} %refs_5_.4) | copy-start | bytes 786436
  17.1 19.0 %copy-start.2 = (bf16[2,128,128]{2,1,0:T(8,128)(2,1)S(1)}, bf16[2,128,128]{2,1,0:T(8,128)(2,1)}, u32[]{:S(2)}) copy-start(bf16[2,128,128]{2,1,0:T(8,128)(2,1)} %refs_6_.2) | copy-start | bytes 196612
  17.1 18.9 %copy-start.3 = (bf16[2,128,128]{2,1,0:T(8,128)(2,1)S(1)}, bf16[2,128,128]{2,1,0:T(8,128)(2,1)}, u32[]{:S(2)}) copy-start(bf16[2,128,128]{2,1,0:T(8,128)(2,1)} %refs_4_.3) | copy-start | bytes 196612
  55.8 12.2 %copy-start.1 = (bf16[128,1024]{1,0:T(8,128)(2,1)S(1)}, bf16[128,1024]{1,0:T(8,128)(2,1)}, u32[]{:S(2)}) copy-start(bf16[128,1024]{1,0:T(8,128)(2,1)} %refs_5_.5) | copy-start | bytes 786436
  55.8 12.2 %copy-start.4 = (bf16[512,128]{1,0:T(8,128)(2,1)S(1)}, bf16[512,128]{1,0:T(8,128)(2,1)}, u32[]{:S(2)}) copy-start(bf16[512,128]{1,0:T(8,128)(2,1)} %refs_6_.3) | copy-start | bytes 393220
